TPU v7x, 32 devices: a whole 2x2x4 slice. The times are simulated.
32 devices in a mesh: dp: 2 (over x), fsdp: 16 (over z, y, core).
Axes of the slice: x: 2, y: 2, z: 4, core: 2. Of those that a mesh axis runs over, the one named last changes fastest.
Arguments:
- input_token_index: int32 [32, 1024], P(('dp', 'fsdp')), may hold values from 0 to 51199
- sentence_numbers: int32 [32, 1024], P(('dp', 'fsdp')), may hold values from 0 to 15, never falling along the last dimension, each value on 1 to 128 neighbouring positions
- label_positions: int32 [32, 128], P(('dp', 'fsdp')), may hold values from 0 to 1023
- label_target_token: int32 [32, 128], P(('dp', 'fsdp')), may hold values from 0 to 51199
- sequence_task_index: int32 [32], P(('dp', 'fsdp')), may hold values from 0 to 3
- task_loss_weight: float32 [4], replicated, may hold values from 0.5 to 2
- optimizer_step_count: int32 [1], replicated, may hold values from 2 to 20
- embed: bfloat16 [51200, 768], P('dp'), may hold values from -0.4375 to 0.4375
- position_embedding: bfloat16 [128, 768], replicated, may hold values from -0.4375 to 0.4375
- norm_gain_vector: float32 [6, 768], replicated, may hold values from 0.5 to 1.5
- norm_bias_vector: float32 [6, 768], replicated, may hold values from -2 to 2
- attention_in_weight: bfloat16 [2, 768, 2304], P(None, None, ('dp', 'fsdp')), may hold values from -0.21875 to 0.21875
- attention_out_weight: bfloat16 [2, 768, 768], P(None, None, ('dp', 'fsdp')), may hold values from -1.75 to 1.75
- feedforward_up: bfloat16 [2, 768, 3072], P(None, None, ('dp', 'fsdp')), may hold values from -0.21875 to 0.21875
- feedforward_down: bfloat16 [2, 3072, 768], P(None, ('dp', 'fsdp')), may hold values from -0.109375 to 0.109375
- layer_bias_vector: float32 [2, 6144], replicated, may hold values from -2 to 2
- head_dense_bias: float32 [768], replicated, may hold values from -2 to 2
- vocabulary_bias: float32 [51200], P(('dp', 'fsdp')), may hold values from -3 to 3
- adapter_down_matrix: bfloat16 [2, 2, 768, 8], replicated, may hold values from -0.21875 to 0.21875
- adapter_up_matrix: float32 [2, 2, 8, 768], P(None, None, None, ('dp', 'fsdp')), may hold values from -0.6 to 0.6
- adapter_moment_first: float32 [2, 2, 8, 768], P(None, None, None, ('dp', 'fsdp')), may hold values from -1.9073486e-05 to 1.9073486e-05
- adapter_moment_second: float32 [2, 2, 8, 768], P(None, None, None, ('dp', 'fsdp')), may hold values from 1.6276042e-13 to 6.5104167e-13
- head_projection: float32 [768, 768], P(('dp', 'fsdp')), may hold values from -0.21875 to 0.21875
- head_moment_first: float32 [768, 768], P(('dp', 'fsdp')), may hold values from -1.9073486e-05 to 1.9073486e-05
- head_moment_second: float32 [768, 768], P(('dp', 'fsdp')), may hold values from 1.6276042e-13 to 6.5104167e-13
Outputs:
- masked_task_loss: float32 [], replicated
- gradient_norm: float32 [], replicated
- lora_up_next: float32 [2, 2, 8, 768], P(None, None, None, ('dp', 'fsdp'))
- lora_first_next: float32 [2, 2, 8, 768], P(None, None, None, ('dp', 'fsdp'))
- lora_second_next: float32 [2, 2, 8, 768], P(None, None, None, ('dp', 'fsdp'))
- head_dense_next: float32 [768, 768], P(('dp', 'fsdp'))
- head_first_next: float32 [768, 768], P(('dp', 'fsdp'))
- head_second_next: float32 [768, 768], P(('dp', 'fsdp'))
Inputs may be any that keep to these rules, and one draw needn't show every extreme that they name: `sentence_numbers`: segment numbers never fall along a sequence; each sentence holds 1 to 128 tokens.
All inputs are finite; a program needn't handle non-finite values.
Results may differ from a plain program's by a relative error of at most 0.0044.
Values may be sent and summed in bfloat16 or wider, within the bound.
A program may use at most 448 MiB of HBM per device.

v0:
```python
import jax
import jax.numpy as jnp
from jax import lax
from jax.sharding import PartitionSpec as P

HEADS = 12
TASKS = 4


norm_eps = 1e-05
adapter_scale = 2.0
clip_limit = 0.01
learn_rate = 0.05
beta_first = 0.9
beta_second = 0.999
adam_eps = 1e-08
decay_rate = 0.01
masked_score = -1e30


def combined_all(value, axis, combine):
    everything = jax.tree.map(
        lambda part, kind: lax.all_gather(part.astype(kind), axis),
        value,
        jax.tree.map(lambda a: jnp.bfloat16 if a.dtype == jnp.float32 else a.dtype, value),
    )

    def take(k):
        return jax.tree.map(lambda part, own: part[k].astype(own.dtype), everything, value)

    return lax.fori_loop(
        1, lax.axis_size(axis), lambda k, so_far: combine(so_far, take(k)), take(0)
    )


def layer_norm(rows_in, gain, shift):
    center = rows_in - jnp.mean(rows_in, -1, keepdims=True)
    spread = jnp.mean(center * center, -1, keepdims=True)
    return center * lax.rsqrt(spread + norm_eps) * gain + shift


def gelu_exact(rows_in):
    return jax.nn.gelu(rows_in, approximate=False)


def norm_back(rows_in, gain, shift, gradient):
    unused, fetch_rows = jax.vjp(lambda value: layer_norm(value, gain, shift), rows_in)
    return fetch_rows(gradient)[0]


def gelu_back(rows_in, gradient):
    unused, fetch_rows = jax.vjp(gelu_exact, rows_in)
    return fetch_rows(gradient)[0]


def seg_positions(segments):
    index = jnp.arange(segments.shape[-1], dtype=jnp.int32)
    fresh = jnp.concatenate(
        [jnp.ones(segments.shape[:-1] + (1,), dtype=bool), segments[..., 1:] != segments[..., :-1]],
        -1,
    )
    starts = lax.cummax(jnp.where(fresh, index, jnp.zeros_like(index)), axis=segments.ndim - 1)
    return index - starts


def split_heads(matrix, head_count):
    return matrix.reshape(matrix.shape[0], head_count, matrix.shape[1] // head_count)


def block_scores(query_rows, key_rows, seg_query, seg_keys):
    score_scale = query_rows.shape[-1] ** (-0.5)
    scores = (
        jnp.einsum("qhd,khd->hqk", query_rows, key_rows, preferred_element_type=jnp.float32)
        * score_scale
    )
    return jnp.where((seg_query[:, None] == seg_keys[None, :])[None], scores, masked_score)


def attend(query_key_value_reduced, sentence_numbers, head_count):
    seq_len = query_key_value_reduced.shape[1]
    hidden_width = query_key_value_reduced.shape[2] // 3
    block_rows = min(512, seq_len)

    def one_seq(seq_item):
        merged_parts, seg_ids = seq_item
        query_rows = split_heads(merged_parts[:, :hidden_width], head_count)
        key_rows = split_heads(merged_parts[:, hidden_width : 2 * hidden_width], head_count)
        value_rows = split_heads(merged_parts[:, 2 * hidden_width :], head_count)
        contexts = []
        log_parts = []
        for row_start in range(0, seq_len, block_rows):
            block_part = slice(row_start, row_start + block_rows)
            scores = block_scores(query_rows[block_part], key_rows, seg_ids[block_part], seg_ids)
            row_max = jnp.max(scores, -1, keepdims=True)
            log_total = row_max + jnp.log(jnp.sum(jnp.exp(scores - row_max), -1, keepdims=True))
            weights = jnp.exp(scores - log_total).astype(jnp.bfloat16)
            contexts.append(
                jnp.einsum("hqk,khd->qhd", weights, value_rows, preferred_element_type=jnp.float32)
            )
            log_parts.append(log_total)
        return (
            jnp.concatenate(contexts, 0).reshape(seq_len, hidden_width),
            jnp.concatenate(log_parts, 1),
        )

    return lax.map(one_seq, (query_key_value_reduced, sentence_numbers))


def attend_back(
    query_key_value_reduced, context_grad, log_normalizers, sentence_numbers, head_count
):
    seq_len = query_key_value_reduced.shape[1]
    hidden_width = query_key_value_reduced.shape[2] // 3
    block_rows = min(512, seq_len)

    def one_seq(seq_item):
        merged_parts, grad_rows, totals_seq, seg_ids = seq_item
        query_rows = split_heads(merged_parts[:, :hidden_width], head_count)
        key_rows = split_heads(merged_parts[:, hidden_width : 2 * hidden_width], head_count)
        value_rows = split_heads(merged_parts[:, 2 * hidden_width :], head_count)
        out_grads = split_heads(grad_rows, head_count)
        score_scale = query_rows.shape[-1] ** (-0.5)
        query_parts = []
        key_grad = jnp.zeros(key_rows.shape, jnp.float32)
        value_gradient = jnp.zeros(value_rows.shape, jnp.float32)
        for row_start in range(0, seq_len, block_rows):
            block_part = slice(row_start, row_start + block_rows)
            scores = block_scores(query_rows[block_part], key_rows, seg_ids[block_part], seg_ids)
            weights = jnp.exp(scores - totals_seq[:, block_part])
            weight_grad = jnp.einsum(
                "qhd,khd->hqk",
                out_grads[block_part],
                value_rows,
                preferred_element_type=jnp.float32,
            )
            row_inner = jnp.sum(weight_grad * weights, -1, keepdims=True)
            score_grad = (weights * (weight_grad - row_inner)).astype(jnp.bfloat16)
            query_parts.append(
                jnp.einsum("hqk,khd->qhd", score_grad, key_rows, preferred_element_type=jnp.float32)
                * score_scale
            )
            key_grad = (
                key_grad
                + jnp.einsum(
                    "hqk,qhd->khd",
                    score_grad,
                    query_rows[block_part],
                    preferred_element_type=jnp.float32,
                )
                * score_scale
            )
            value_gradient = value_gradient + jnp.einsum(
                "hqk,qhd->khd",
                weights.astype(jnp.bfloat16),
                out_grads[block_part],
                preferred_element_type=jnp.float32,
            )
        members = (jnp.concatenate(query_parts, 0), key_grad, value_gradient)
        return jnp.concatenate([member.reshape(seq_len, hidden_width) for member in members], 1)

    return lax.map(
        one_seq, (query_key_value_reduced, context_grad, log_normalizers, sentence_numbers)
    )


def layer_gains(norm_gain_vector, norm_bias_vector, layer_position):
    return (
        norm_gain_vector[1 + 2 * layer_position],
        norm_bias_vector[1 + 2 * layer_position],
        norm_gain_vector[2 + 2 * layer_position],
        norm_bias_vector[2 + 2 * layer_position],
    )


def layer_forward(
    hidden, sentence_numbers, weights, biases, gains, down_weight_couple, up_weight_couple
):
    proj_w, output_w, up_w, down_w = weights
    hidden_width = hidden.shape[1]
    ff_width = up_w.shape[1]
    adapter_rank_size = down_weight_couple.shape[2]
    seq_count, seq_len = sentence_numbers.shape
    hidden_reduced = hidden.astype(jnp.bfloat16)
    down_weight_merged = jnp.concatenate([down_weight_couple[0], down_weight_couple[1]], 1)
    adapter_middle = jnp.dot(
        hidden_reduced, down_weight_merged, preferred_element_type=jnp.float32
    ).astype(jnp.bfloat16)
    adapter_query = jnp.dot(
        adapter_middle[:, :adapter_rank_size],
        up_weight_couple[0],
        preferred_element_type=jnp.float32,
    )
    adapter_value = jnp.dot(
        adapter_middle[:, adapter_rank_size:],
        up_weight_couple[1],
        preferred_element_type=jnp.float32,
    )
    bias_qkv = jnp.concatenate(
        [
            biases[:hidden_width],
            jnp.zeros((hidden_width,), jnp.float32),
            biases[hidden_width : 2 * hidden_width],
        ]
    )
    merged_parts = jnp.dot(hidden_reduced, proj_w, preferred_element_type=jnp.float32) + bias_qkv
    merged_parts = merged_parts + adapter_scale * jnp.concatenate(
        [adapter_query, jnp.zeros_like(adapter_query), adapter_value], 1
    )
    query_key_value_reduced = merged_parts.astype(jnp.bfloat16).reshape(
        seq_count, seq_len, 3 * hidden_width
    )
    context, log_normalizers = attend(query_key_value_reduced, sentence_numbers, HEADS)
    context_low = context.reshape(-1, hidden_width).astype(jnp.bfloat16)
    residual_first = hidden + (
        jnp.dot(context_low, output_w, preferred_element_type=jnp.float32)
        + biases[2 * hidden_width : 3 * hidden_width]
    )
    middle = layer_norm(residual_first, gains[0], gains[1])
    gate_preactivation = (
        jnp.dot(middle.astype(jnp.bfloat16), up_w, preferred_element_type=jnp.float32)
        + biases[3 * hidden_width : 3 * hidden_width + ff_width]
    )
    gate_low = gelu_exact(gate_preactivation).astype(jnp.bfloat16)
    residual_second = middle + (
        jnp.dot(gate_low, down_w, preferred_element_type=jnp.float32)
        + biases[3 * hidden_width + ff_width :]
    )
    saved_activations = (
        adapter_middle,
        query_key_value_reduced,
        log_normalizers,
        residual_first,
        gate_preactivation,
        residual_second,
    )
    return (layer_norm(residual_second, gains[2], gains[3]), saved_activations)


def layer_backward(
    out_grad,
    sentence_numbers,
    weights,
    gains,
    down_weight_couple,
    up_weight_couple,
    saved_activations,
):
    proj_w, output_w, up_w, down_w = weights
    (
        adapter_middle,
        query_key_value_reduced,
        log_normalizers,
        residual_first,
        gate_preactivation,
        residual_second,
    ) = saved_activations
    hidden_width = out_grad.shape[1]
    adapter_rank_size = down_weight_couple.shape[2]
    two_grad = norm_back(residual_second, gains[2], gains[3], out_grad)
    gate_grad = gelu_back(
        gate_preactivation,
        jnp.dot(two_grad.astype(jnp.bfloat16), down_w.T, preferred_element_type=jnp.float32),
    ).astype(jnp.bfloat16)
    middle_grad = two_grad + jnp.dot(gate_grad, up_w.T, preferred_element_type=jnp.float32)
    one_grad = norm_back(residual_first, gains[0], gains[1], middle_grad)
    context_grad = jnp.dot(
        one_grad.astype(jnp.bfloat16), output_w.T, preferred_element_type=jnp.float32
    ).astype(jnp.bfloat16)
    context_grad = context_grad.reshape(
        query_key_value_reduced.shape[0], query_key_value_reduced.shape[1], hidden_width
    )
    qkv_grad = (
        attend_back(query_key_value_reduced, context_grad, log_normalizers, sentence_numbers, HEADS)
        .reshape(-1, 3 * hidden_width)
        .astype(jnp.bfloat16)
    )
    query_gradient = qkv_grad[:, :hidden_width]
    value_gradient = qkv_grad[:, 2 * hidden_width :]
    middle_gradient = adapter_scale * jnp.concatenate(
        [
            jnp.dot(query_gradient, up_weight_couple[0].T, preferred_element_type=jnp.float32),
            jnp.dot(value_gradient, up_weight_couple[1].T, preferred_element_type=jnp.float32),
        ],
        1,
    )
    middle_gradient = middle_gradient.astype(jnp.bfloat16)
    down_weight_merged = jnp.concatenate([down_weight_couple[0], down_weight_couple[1]], 1)
    hidden_grad = (
        one_grad
        + jnp.dot(qkv_grad, proj_w.T, preferred_element_type=jnp.float32)
        + jnp.dot(middle_gradient, down_weight_merged.T, preferred_element_type=jnp.float32)
    )
    contract_product = (((0,), (0,)), ((), ()))
    up_gradient = adapter_scale * jnp.stack(
        [
            lax.dot_general(
                adapter_middle[:, :adapter_rank_size],
                query_gradient,
                contract_product,
                preferred_element_type=jnp.float32,
            ),
            lax.dot_general(
                adapter_middle[:, adapter_rank_size:],
                value_gradient,
                contract_product,
                preferred_element_type=jnp.float32,
            ),
        ]
    )
    return (hidden_grad, up_gradient)


def merge_stats(first_set, second_set):
    row_max = jnp.maximum(first_set[0], second_set[0])
    exp_sum = first_set[1] * jnp.exp(first_set[0] - row_max) + second_set[1] * jnp.exp(
        second_set[0] - row_max
    )
    return (row_max, exp_sum, first_set[2] + second_set[2])


def local_stats(every_feats, own_vocab, own_bias, vocab_ids, every_tokens):
    logits = (
        lax.dot_general(
            every_feats, own_vocab, (((1,), (1,)), ((), ())), preferred_element_type=jnp.float32
        )
        + own_bias
    )
    hits = every_tokens[:, None] == vocab_ids[None, :]
    row_max = jnp.max(logits, 1)
    exp_sum = jnp.sum(jnp.exp(logits - row_max[:, None]), 1)
    target = jnp.sum(jnp.where(hits, logits, 0.0), 1)
    return (logits, hits, (row_max, exp_sum, target))


def optimizer_update(weight, gradient, moment_one, moment_two, step_as_real):
    moment_one = beta_first * moment_one + (1.0 - beta_first) * gradient
    moment_two = beta_second * moment_two + (1.0 - beta_second) * gradient * gradient
    one_hat = moment_one / (1.0 - beta_first**step_as_real)
    two_hat = moment_two / (1.0 - beta_second**step_as_real)
    weight = weight - learn_rate * (one_hat / (jnp.sqrt(two_hat) + adam_eps) + decay_rate * weight)
    return (weight, moment_one, moment_two)


def per_device(
    input_token_index,
    sentence_numbers,
    label_positions,
    label_target_token,
    sequence_task_index,
    task_loss_weight,
    optimizer_step_count,
    embed,
    position_embedding,
    norm_gain_vector,
    norm_bias_vector,
    attention_in_weight,
    attention_out_weight,
    feedforward_up,
    feedforward_down,
    layer_bias_vector,
    head_dense_bias,
    vocabulary_bias,
    adapter_down_matrix,
    adapter_up_matrix,
    adapter_moment_first,
    adapter_moment_second,
    head_projection,
    head_moment_first,
    head_moment_second,
):
    adapter_collected, dense_collected = (
        lax.all_gather(adapter_up_matrix.astype(jnp.bfloat16), ("dp", "fsdp"), axis=3, tiled=True),
        lax.all_gather(head_projection.astype(jnp.bfloat16), ("dp", "fsdp"), axis=0, tiled=True),
    )
    seq_count, seq_len = input_token_index.shape
    label_count = label_positions.shape[1]
    task_range = jnp.arange(TASKS, dtype=jnp.int32)
    task_hot = (sequence_task_index[:, None] == task_range[None, :]).astype(jnp.float32)
    counts = lax.psum(jnp.sum(task_hot, 0) * label_count, ("dp", "fsdp"))
    task_table = task_loss_weight / jnp.maximum(counts, 1.0)
    row_tasks = jnp.repeat(sequence_task_index, label_count)
    flat_places = (
        label_positions + jnp.arange(seq_count, dtype=jnp.int32)[:, None] * seq_len
    ).reshape(-1)
    table_rows = embed.shape[0]
    dp_index = lax.axis_index("dp")
    table_start = dp_index * table_rows
    group_ids = (
        lax.all_gather(input_token_index.reshape(-1), "dp", axis=0, tiled=True) - table_start
    )
    inside = (group_ids >= 0) & (group_ids < table_rows)
    looked = jnp.where(
        inside[:, None], embed[jnp.clip(group_ids, 0, table_rows - 1)], jnp.zeros((), jnp.bfloat16)
    )
    embed_rows = lax.psum_scatter(looked, "dp", scatter_dimension=0, tiled=True).astype(jnp.float32)
    place_hot = (
        seg_positions(sentence_numbers).reshape(-1)[:, None]
        == jnp.arange(position_embedding.shape[0], dtype=jnp.int32)[None, :]
    ).astype(jnp.bfloat16)
    hidden = embed_rows + jnp.dot(place_hot, position_embedding, preferred_element_type=jnp.float32)
    hidden = layer_norm(hidden, norm_gain_vector[0], norm_bias_vector[0])
    layer_count = attention_in_weight.shape[0]
    saved_list = []
    weight_list = []
    for layer_position in range(layer_count):
        weights = (
            lax.all_gather(attention_in_weight[layer_position], ("dp", "fsdp"), axis=1, tiled=True),
            lax.all_gather(
                attention_out_weight[layer_position], ("dp", "fsdp"), axis=1, tiled=True
            ),
            lax.all_gather(feedforward_up[layer_position], ("dp", "fsdp"), axis=1, tiled=True),
            lax.all_gather(feedforward_down[layer_position], ("dp", "fsdp"), axis=0, tiled=True),
        )
        hidden, saved_activations = layer_forward(
            hidden,
            sentence_numbers,
            weights,
            layer_bias_vector[layer_position],
            layer_gains(norm_gain_vector, norm_bias_vector, layer_position),
            adapter_down_matrix[layer_position],
            adapter_collected[layer_position],
        )
        saved_list.append(saved_activations)
        weight_list.append(weights)
    picked = hidden[flat_places]
    picked_low = picked.astype(jnp.bfloat16)
    pre_act = (
        jnp.dot(picked_low, dense_collected, preferred_element_type=jnp.float32) + head_dense_bias
    )
    activated = gelu_exact(pre_act)
    feats_low = layer_norm(activated, norm_gain_vector[-1], norm_bias_vector[-1]).astype(
        jnp.bfloat16
    )
    fsdp_index = lax.axis_index("fsdp")
    every_tokens, every_tasks = (
        lax.all_gather(label_target_token.reshape(-1), "fsdp", axis=0, tiled=True),
        lax.all_gather(row_tasks, "fsdp", axis=0, tiled=True),
    )
    every_feats = lax.all_gather(feats_low, "fsdp", axis=0, tiled=True)
    slice_rows = vocabulary_bias.shape[0]
    fsdp_count = lax.axis_size("fsdp")
    own_slice = lax.dynamic_slice_in_dim(embed, fsdp_index * slice_rows, slice_rows, 0)
    own_vocab, own_bias = (
        lax.all_gather(own_slice, "dp", axis=0, tiled=True),
        lax.all_gather(vocabulary_bias.astype(jnp.bfloat16), "dp", axis=0, tiled=True).astype(
            vocabulary_bias.dtype
        ),
    )
    local_index = jnp.arange(own_vocab.shape[0], dtype=jnp.int32)
    vocab_ids = (
        local_index // slice_rows * fsdp_count + fsdp_index
    ) * slice_rows + local_index % slice_rows
    logits, hits, stats = local_stats(every_feats, own_vocab, own_bias, vocab_ids, every_tokens)
    row_max, exp_sum, target = combined_all(stats, "fsdp", merge_stats)
    log_total = row_max + jnp.log(exp_sum)
    row_weight = jnp.sum(
        (every_tasks[:, None] == task_range[None, :]).astype(jnp.float32) * task_table[None, :], 1
    )
    own_rows = picked.shape[0]
    own_loss = jnp.sum(
        lax.dynamic_slice_in_dim(
            row_weight * (log_total - target), fsdp_index * own_rows, own_rows, 0
        )
    )
    probability = jnp.exp(logits - log_total[:, None])
    logit_grad = (row_weight[:, None] * (probability - hits.astype(jnp.float32))).astype(
        jnp.bfloat16
    )
    feat_term = jnp.dot(logit_grad, own_vocab, preferred_element_type=jnp.float32)
    feat_grad = lax.psum_scatter(
        feat_term.astype(jnp.bfloat16), "fsdp", scatter_dimension=0, tiled=True
    ).astype(jnp.float32)
    pre_grad = gelu_back(
        pre_act, norm_back(activated, norm_gain_vector[-1], norm_bias_vector[-1], feat_grad)
    ).astype(jnp.bfloat16)
    dense_gradient = lax.dot_general(
        picked_low, pre_grad, (((0,), (0,)), ((), ())), preferred_element_type=jnp.float32
    )
    hidden_grad = (
        jnp.zeros(hidden.shape, jnp.float32)
        .at[flat_places]
        .add(jnp.dot(pre_grad, dense_collected.T, preferred_element_type=jnp.float32))
    )
    up_gradients_list = [None] * layer_count
    for layer_position in reversed(range(layer_count)):
        weights = (
            lax.all_gather(attention_in_weight[layer_position], ("dp", "fsdp"), axis=1, tiled=True),
            lax.all_gather(
                attention_out_weight[layer_position], ("dp", "fsdp"), axis=1, tiled=True
            ),
            lax.all_gather(feedforward_up[layer_position], ("dp", "fsdp"), axis=1, tiled=True),
            lax.all_gather(feedforward_down[layer_position], ("dp", "fsdp"), axis=0, tiled=True),
        )
        hidden_grad, up_gradients_list[layer_position] = layer_backward(
            hidden_grad,
            sentence_numbers,
            weights,
            layer_gains(norm_gain_vector, norm_bias_vector, layer_position),
            adapter_down_matrix[layer_position],
            adapter_collected[layer_position],
            saved_list[layer_position],
        )
    adapter_gradient = jnp.stack(up_gradients_list)
    adapter_portion, dense_portion = (
        lax.psum_scatter(adapter_gradient, ("dp", "fsdp"), scatter_dimension=3, tiled=True),
        lax.psum_scatter(dense_gradient, ("dp", "fsdp"), scatter_dimension=0, tiled=True),
    )
    squared_entries = jnp.sum(adapter_portion * adapter_portion) + jnp.sum(
        dense_portion * dense_portion
    )
    masked_task_loss, norm_square = lax.psum((own_loss, squared_entries), ("dp", "fsdp"))
    gradient_norm = jnp.sqrt(norm_square)
    scale_factor = jnp.minimum(1.0, clip_limit / (gradient_norm + 1e-06))
    step_as_real = optimizer_step_count[0].astype(jnp.float32)
    adapter_updated, adapter_first_part, adapter_second_part = optimizer_update(
        adapter_up_matrix,
        adapter_portion * scale_factor,
        adapter_moment_first,
        adapter_moment_second,
        step_as_real,
    )
    dense_updated, dense_moment_first, dense_moment_second = optimizer_update(
        head_projection,
        dense_portion * scale_factor,
        head_moment_first,
        head_moment_second,
        step_as_real,
    )
    return (
        masked_task_loss,
        gradient_norm,
        adapter_updated,
        adapter_first_part,
        adapter_second_part,
        dense_updated,
        dense_moment_first,
        dense_moment_second,
    )


def solution(mesh):
    in_specs = (
        P(("dp", "fsdp"), None),
        P(("dp", "fsdp"), None),
        P(("dp", "fsdp"), None),
        P(("dp", "fsdp"), None),
        P(("dp", "fsdp")),
        P(),
        P(),
        P("dp", None),
        P(),
        P(),
        P(),
        P(None, None, ("dp", "fsdp")),
        P(None, None, ("dp", "fsdp")),
        P(None, None, ("dp", "fsdp")),
        P(None, ("dp", "fsdp"), None),
        P(),
        P(),
        P(("dp", "fsdp")),
        P(),
        P(None, None, None, ("dp", "fsdp")),
        P(None, None, None, ("dp", "fsdp")),
        P(None, None, None, ("dp", "fsdp")),
        P(("dp", "fsdp"), None),
        P(("dp", "fsdp"), None),
        P(("dp", "fsdp"), None),
    )
    out_specs = (
        P(),
        P(),
        P(None, None, None, ("dp", "fsdp")),
        P(None, None, None, ("dp", "fsdp")),
        P(None, None, None, ("dp", "fsdp")),
        P(("dp", "fsdp"), None),
        P(("dp", "fsdp"), None),
        P(("dp", "fsdp"), None),
    )
    return jax.shard_map(
        per_device, mesh=mesh, in_specs=in_specs, out_specs=out_specs, check_vma=False
    )
```

profile of v0, /device:TPU:0, one launch (start us, length us, event | category | flops | bytes accessed | tf_op | source)
XLA Modules:
  0.0 1573.2 jit_solution(15887750265219851902)
XLA Ops:
  8.1 5.6 all-gather
  13.7 58.7 %gather_fusion = bf16[2048,768]{1,0:T(8,128)(2,1)} fusion(bf16[25600,768]{1,0:T(8,128)(2,1)} %param.34, s32[2048]{0:T(1024)S(1)} %fusion.188), kind=kCustom, calls=%fused_computation | custom fusion | bytes 6299648 | tf_op jit(solution)/shard_map/gather | solution.py:393
  95.0 59.7 %all_gather.70 = bf16[2,2,8,768]{2,1,0,3:T(2,128)(2,1)S(1)} all-gather(bf16[2,2,8,24]{2,1,0,3:T(2,128)(2,1)S(1)} %copy.139), channel_id=1, replica_groups=mesh['dp'=2,'fsdp'=16] {'dp','fsdp'}, dimensions={3}, use_global_device_ids=true | all-gather | bytes 50688 | tf_op jit(solution)/shard_map/all_gather | solution.py:372
  167.9 19.1 %all-gather.32.cloned.1.call-done = bf16[1,768,2304]{1,2,0:T(8,128)(2,1)} async-done(((bf16[1,768,72]{1,2,0:T(8,128)(2,1)}), bf16[1,768,2304]{1,2,0:T(8,128)(2,1)}) %all-gather.32.cloned.1.call-update) | async-done | bytes 3538960 | tf_op jit(solution)/shard_map/all_gather | solution.py:407
  187.3 8.3 fusion.33
  208.3 12.1 fusion.5
  220.3 12.0 exponential_reduce_fusion.3
  232.4 11.1 fusion.4
  243.5 12.0 exponential_reduce_fusion.4
  255.5 11.2 fusion.113
  266.7 11.3 fusion.112
  279.4 4.3 fusion.251
  284.1 24.6 %all-gather.36.cloned.1.call-done = bf16[1,768,3072]{1,2,0:T(8,128)(2,1)} async-done(((bf16[1,768,96]{1,2,0:T(8,128)(2,1)}), bf16[1,768,3072]{1,2,0:T(8,128)(2,1)}) %all-gather.36.cloned.1.call-update) | async-done | bytes 4718608 | tf_op jit(solution)/shard_map/all_gather | solution.py:411
  308.7 36.3 %fusion.14 = (f32[1024,3072]{1,0:T(8,128)}, f32[1024,3072]{1,0:T(8,128)}) fusion(f32[3072]{0:T(1024)S(1)} %bitcast.298, bf16[1,768,3072]{1,2,0:T(8,128)(2,1)} %all-gather.36.cloned.1.call-done, f32[1024,768]{0,1:T(8,128)S(1)} %get-tuple-element.351, f32[768]{0:T(1024)S(1)} %get-tuple-element.274, f32[768]{0:T(1024)S(1)} %get-tuple-element.268, ...), kind=kOutput, calls=%fused_computation.48 | convolution fusion | flops 5033951232 | bytes 33056768 | tf_op jit(solution)/shard_map/dot_general | solution.py:220
  345.1 28.6 %all-gather.38.cloned.1.call-done = bf16[1,3072,768]{2,1,0:T(8,128)(2,1)} async-done(((bf16[1,96,768]{2,1,0:T(8,128)(2,1)}), bf16[1,3072,768]{2,1,0:T(8,128)(2,1)}) %all-gather.38.cloned.1.call-update) | async-done | bytes 4718608 | tf_op jit(solution)/shard_map/all_gather | solution.py:412
  373.7 16.2 %fusion.252 = (f32[1024]{0:T(1024)S(1)}, f32[1024,768]{0,1:T(8,128)S(1)}) fusion(f32[768]{0:T(1024)S(1)} %copy-done.115, bf16[1,3072,768]{2,1,0:T(8,128)(2,1)} %all-gather.38.cloned.1.call-done, f32[1024,3072]{1,0:T(8,128)} %get-tuple-element.352, f32[1024,3072]{1,0:T(8,128)} %get-tuple-element.353, f32[3072]{0:T(1024)S(1)} %bitcast.299, ...), kind=kOutput, calls=%fused_computation.433 | convolution fusion | flops 4849925120 | bytes 36209664 | tf_op jit(solution)/shard_map/dot_general | solution.py:225
  394.6 40.9 %all-gather.40.cloned.1.call-done = bf16[1,768,2304]{1,2,0:T(8,128)(2,1)} async-done(((bf16[1,768,72]{1,2,0:T(8,128)(2,1)}), bf16[1,768,2304]{1,2,0:T(8,128)(2,1)}) %all-gather.40.cloned.1.call-update) | async-done | bytes 3538960 | tf_op jit(solution)/shard_map/all_gather | solution.py:407
  435.4 7.4 fusion.37
  453.1 11.1 fusion.7
  464.2 11.9 exponential_reduce_fusion.1
  476.1 10.7 fusion.6
  486.8 11.9 exponential_reduce_fusion.2
  498.8 11.3 fusion.115
  510.1 11.5 fusion.114
  528.6 28.6 %all-gather.44.cloned.1.call-done = bf16[1,768,3072]{1,2,0:T(8,128)(2,1)} async-done(((bf16[1,768,96]{1,2,0:T(8,128)(2,1)}), bf16[1,768,3072]{1,2,0:T(8,128)(2,1)}) %all-gather.44.cloned.1.call-update) | async-done | bytes 4718608 | tf_op jit(solution)/shard_map/all_gather | solution.py:411
  557.2 36.3 %fusion.15 = (f32[1024,3072]{1,0:T(8,128)}, f32[1024,3072]{1,0:T(8,128)}) fusion(f32[3072]{0:T(1024)S(1)} %bitcast.301, bf16[1,768,3072]{1,2,0:T(8,128)(2,1)} %all-gather.44.cloned.1.call-done, f32[1024,768]{0,1:T(8,128)} %copy-done.26, f32[768]{0:T(1024)S(1)} %copy-done.120, f32[768]{0:T(1024)S(1)} %copy-done.118, f32[1024]{0:T(1024)S(1)} %fusion.192, ...), kind=kOutput, calls=%fused_computation.49 | convolution fusion | flops 5033951232 | bytes 33056768 | tf_op jit(solution)/shard_map/dot_general | solution.py:220
  593.5 28.5 %all-gather.46.cloned.1.call-done = bf16[1,3072,768]{2,1,0:T(8,128)(2,1)} async-done(((bf16[1,96,768]{2,1,0:T(8,128)(2,1)}), bf16[1,3072,768]{2,1,0:T(8,128)(2,1)}) %all-gather.46.cloned.1.call-update) | async-done | bytes 4718608 | tf_op jit(solution)/shard_map/all_gather | solution.py:412
  622.0 16.1 %fusion.254 = (f32[1024]{0:T(1024)S(1)}, f32[1024,768]{0,1:T(8,128)S(1)}) fusion(f32[768]{0:T(1024)S(1)} %copy-done.113, bf16[1,3072,768]{2,1,0:T(8,128)(2,1)} %all-gather.46.cloned.1.call-done, f32[1024,3072]{1,0:T(8,128)} %get-tuple-element.362, f32[1024,3072]{1,0:T(8,128)} %get-tuple-element.363, f32[3072]{0:T(1024)S(1)} %bitcast.302, ...), kind=kOutput, calls=%fused_computation.435 | convolution fusion | flops 4849925120 | bytes 36209664 | tf_op jit(solution)/shard_map/dot_general | solution.py:225
  645.6 32.2 %all-gather.26.cloned.1.call-done = bf16[768,768]{1,0:T(8,128)(2,1)} async-done(((bf16[24,768]{1,0:T(8,128)(2,1)}), bf16[768,768]{1,0:T(8,128)(2,1)}) %all-gather.26.cloned.1.call-update) | async-done | bytes 1179664 | tf_op jit(solution)/shard_map/all_gather | solution.py:373
  683.2 39.7 %psum.21 = f32[4]{0:T(128)S(1)} all-reduce(f32[4]{0:T(128)S(1)} %compare_select_fusion.3), channel_id=1, replica_groups=mesh['dp'=2,'fsdp'=16] {'dp','fsdp'}, use_global_device_ids=true, to_apply=%region_0.0 | all-reduce | flops 4 | bytes 32 | tf_op jit(solution)/shard_map/psum | solution.py:379
  724.4 5.4 all-reduce
  729.9 20.0 %all-gather.13 = s32[16,1,128]{2,1,0:T(1,128)S(1)} all-gather(s32[1,1,128]{2,1,0:T(1,128)S(1)} %broadcast.703), channel_id=1, replica_groups=mesh['dp'=2,'fsdp'=16] {'fsdp'}, dimensions={0}, use_global_device_ids=true | all-gather | bytes 8704 | tf_op jit(solution)/shard_map/all_gather | solution.py:437
  749.8 17.3 %all-gather.11 = s32[1,2048]{1,0:T(1,128)S(1)} all-gather(s32[1,128]{1,0:T(1,128)S(1)} %copy-done.123), channel_id=13, replica_groups=mesh['dp'=2,'fsdp'=16] {'fsdp'}, dimensions={1}, use_global_device_ids=true | all-gather | bytes 8704 | tf_op jit(solution)/shard_map/all_gather | solution.py:436
  767.3 24.7 %all-gather.28.cloned.1.call-done = bf16[2048,768]{1,0:T(8,128)(2,1)} async-done(((bf16[128,768]{1,0:T(8,128)(2,1)}), bf16[2048,768]{1,0:T(8,128)(2,1)}) %all-gather.28.cloned.1.call-update) | async-done | bytes 3145744 | tf_op jit(solution)/shard_map/all_gather | solution.py:439
  792.0 19.1 %add_reduce_fusion = (f32[2048]{0:T(1024)S(1)}, f32[2048,3200]{1,0:T(8,128)}) fusion(f32[3200]{0:T(1024)S(1)} %convert_element_type.271, bf16[2048,768]{1,0:T(8,128)(2,1)} %all-gather.28.cloned.1.call-done, bf16[3200,768]{1,0:T(8,128)(2,1)} %all-gather.30.cloned.1.call-done), kind=kOutput, calls=%fused_computation.34 | convolution fusion | flops 10079434752 | bytes 34296320 | tf_op jit(solution)/shard_map/dot_general | solution.py:323
  811.0 11.6 fusion
  822.6 18.8 %all-gather.12 = bf16[32768]{0:T(1024)(128)(2,1)S(1)} all-gather(bf16[2048]{0:T(1024)(128)(2,1)S(1)} %get-tuple-element.255), channel_id=14, replica_groups=mesh['dp'=2,'fsdp'=16] {'fsdp'}, dimensions={0}, use_global_device_ids=true | all-gather | bytes 69632 | tf_op jit(solution)/shard_map/all_gather | solution.py:23
  841.5 17.7 %all-gather.9 = bf16[32768]{0:T(1024)(128)(2,1)S(1)} all-gather(bf16[2048]{0:T(1024)(128)(2,1)S(1)} %convert_element_type.272), channel_id=11, replica_groups=mesh['dp'=2,'fsdp'=16] {'fsdp'}, dimensions={0}, use_global_device_ids=true | all-gather | bytes 69632 | tf_op jit(solution)/shard_map/all_gather | solution.py:23
  859.3 18.8 %all-gather.10 = bf16[32768]{0:T(1024)(128)(2,1)S(1)} all-gather(bf16[2048]{0:T(1024)(128)(2,1)S(1)} %get-tuple-element.256), channel_id=12, replica_groups=mesh['dp'=2,'fsdp'=16] {'fsdp'}, dimensions={0}, use_global_device_ids=true | all-gather | bytes 69632 | tf_op jit(solution)/shard_map/all_gather | solution.py:23
  879.8 22.1 %fusion.75 = bf16[2048,768]{1,0:T(8,128)(2,1)} fusion(bf16[3200,768]{1,0:T(8,128)(2,1)} %all-gather.30.cloned.1.call-done, f32[2048,3200]{1,0:T(8,128)} %get-tuple-element.368, f32[2048]{0:T(1024)S(1)} %log_add_fusion.4, f32[2048]{0:T(1024)S(1)} %select_reduce_fusion, s32[3200]{0:T(1024)S(1)} %fusion.163, f32[3200]{0:T(1024)S(1)} %convert_element_type.271, ...), kind=kOutput, calls=%fused_computation.125 | convolution fusion | flops 10113777664 | bytes 34325504 | tf_op jit(solution)/shard_map/dot_general | solution.py:469
  902.2 63.3 %reduce-scatter.7.cloned.1.call-done = bf16[128,768]{1,0:T(8,128)(2,1)} async-done(((bf16[2048,768]{1,0:T(8,128)(2,1)}), bf16[128,768]{1,0:T(8,128)(2,1)}) %reduce-scatter.7.cloned.1.call-update) | async-done | bytes 196624 | tf_op jit(solution)/shard_map/reduce_scatter | solution.py:470
  972.3 3.7 scatter_custom_fusion
  983.2 24.9 %multiply_reduce_fusion.6 = (f32[1024]{0:T(1024)S(1)}, f32[1024,768]{0,1:T(8,128)}) fusion(f32[1024,768]{0,1:T(8,128)} %copy-done.26, f32[1024]{0:T(1024)S(1)} %broadcast_multiply_fusion.1, f32[768]{0:T(1024)S(1)} %copy-done.119, bf16[1,768,3072]{1,2,0:T(8,128)(2,1)} %all-gather.44.cloned.1.call-done, f32[1024,3072]{1,0:T(8,128)} %get-tuple-element.362, ...), kind=kOutput, calls=%fused_computation.134 | convolution fusion | flops 9726589952 | bytes 47228928 | tf_op jit(solution)/shard_map/dot_general | solution.py:264
  1008.1 4.1 fusion.234
  1014.0 12.0 fusion.141
  1026.1 12.2 add_convert_fusion.6
  1040.6 17.7 %multiply_reduce_fusion.2 = (f32[12,512]{1,0:T(8,128)S(1)}, f32[12,512,1024]{2,1,0:T(8,128)}) fusion(f32[12,512,1024]{2,1,0:T(8,128)} %get-tuple-element.357, f32[12,512]{1,0:T(8,128)S(1)} %copy-done.57, pred[512,1024]{1,0:T(8,128)(4,1)S(1)} %copy-done.10, bf16[512,12,64]{0,2,1:T(8,128)(2,1)} %bitcast.281, bf16[1024,12,64]{0,2,1:T(8,128)(2,1)S(1)} %bitcast.262), kind=kOutput, calls=%fused_computation.19 | convolution fusion | flops 836757504 | bytes 53264384 | tf_op jit(solution)/shard_map/while/body/eval_jaxpr/qhd,khd->hqk/dot_general | solution.py:130
  1058.3 17.7 %multiply_reduce_fusion.3 = (f32[12,512]{1,0:T(8,128)S(1)}, f32[12,512,1024]{2,1,0:T(8,128)}) fusion(f32[12,512,1024]{2,1,0:T(8,128)} %get-tuple-element.359, f32[12,512]{1,0:T(8,128)S(1)} %copy-done.59, pred[512,1024]{1,0:T(8,128)(4,1)S(1)} %copy-done.6, bf16[512,12,64]{0,2,1:T(8,128)(2,1)} %bitcast.279, bf16[1024,12,64]{0,2,1:T(8,128)(2,1)S(1)} %bitcast.263), kind=kOutput, calls=%fused_computation.21 | convolution fusion | flops 836757504 | bytes 53264384 | tf_op jit(solution)/shard_map/while/body/eval_jaxpr/qhd,khd->hqk/dot_general | solution.py:130
  1076.0 41.9 %multiply_convert_fusion.2 = (bf16[12,512,1024]{2,1,0:T(8,128)(2,1)}, bf16[12,512,1024]{2,1,0:T(8,128)(2,1)}) fusion(f32[12,512,1024]{2,1,0:T(8,128)} %get-tuple-element.372, f32[12,512,1024]{2,1,0:T(8,128)} %get-tuple-element.357, f32[12,512]{1,0:T(8,128)S(1)} %get-tuple-element.371, f32[12,512]{1,0:T(8,128)S(1)} %copy-done.57, ...), kind=kLoop, calls=%fused_computation.18 | loop fusion | flops 75497472 | bytes 126976000 | tf_op jit(solution)/shard_map/while/body/eval_jaxpr/convert_element_type | solution.py:137
  1118.0 9.5 fusion.116
  1127.6 8.9 fusion.260
  1136.5 6.2 fusion.117
  1148.5 4.2 fusion.46
  1156.7 24.9 %multiply_reduce_fusion.4 = (f32[1024]{0:T(1024)S(1)}, f32[1024,768]{0,1:T(8,128)}) fusion(f32[1024,768]{0,1:T(8,128)} %copy-done.24, f32[1024]{0:T(1024)S(1)} %copy-done.86, f32[768]{0:T(1024)S(1)} %copy-done.117, bf16[1,768,3072]{1,2,0:T(8,128)(2,1)} %all-gather.36.cloned.1.call-done, f32[1024,3072]{1,0:T(8,128)} %get-tuple-element.352, ...), kind=kOutput, calls=%fused_computation.128 | convolution fusion | flops 9725017088 | bytes 47225856 | tf_op jit(solution)/shard_map/dot_general | solution.py:264
  1181.6 3.7 fusion.125
  1191.1 13.5 fusion.146
  1204.6 17.7 %multiply_reduce_fusion.1 = (f32[12,512]{1,0:T(8,128)S(1)}, f32[12,512,1024]{2,1,0:T(8,128)}) fusion(f32[12,512,1024]{2,1,0:T(8,128)} %get-tuple-element.349, f32[12,512]{1,0:T(8,128)S(1)} %copy-done.48, pred[512,1024]{1,0:T(8,128)(4,1)S(1)} %copy-done.7, bf16[512,12,64]{0,2,1:T(8,128)(2,1)} %bitcast.285, bf16[1024,12,64]{0,2,1:T(8,128)(2,1)S(1)} %bitcast.258), kind=kOutput, calls=%fused_computation.17 | convolution fusion | flops 836757504 | bytes 53264384 | tf_op jit(solution)/shard_map/while/body/eval_jaxpr/qhd,khd->hqk/dot_general | solution.py:130
  1222.3 17.7 %multiply_reduce_fusion = (f32[12,512]{1,0:T(8,128)S(1)}, f32[12,512,1024]{2,1,0:T(8,128)}) fusion(f32[12,512,1024]{2,1,0:T(8,128)} %get-tuple-element.347, f32[12,512]{1,0:T(8,128)S(1)} %copy-done.46, pred[512,1024]{1,0:T(8,128)(4,1)S(1)} %copy-done.11, bf16[512,12,64]{0,2,1:T(8,128)(2,1)} %bitcast.282, bf16[1024,12,64]{0,2,1:T(8,128)(2,1)S(1)} %bitcast.259), kind=kOutput, calls=%fused_computation.15 | convolution fusion | flops 836757504 | bytes 53264384 | tf_op jit(solution)/shard_map/while/body/eval_jaxpr/qhd,khd->hqk/dot_general | solution.py:130
  1240.1 13.1 add_convert_fusion.4
  1253.7 18.4 %fusion.119 = bf16[512,12,64]{0,2,1:T(8,128)(2,1)S(1)} fusion(bf16[1024,12,64]{0,2,1:T(8,128)(2,1)S(1)} %bitcast.250, f32[12,512,1024]{2,1,0:T(8,128)} %get-tuple-element.380, f32[12,512,1024]{2,1,0:T(8,128)} %get-tuple-element.347, f32[12,512]{1,0:T(8,128)S(1)} %get-tuple-element.379, f32[12,512]{1,0:T(8,128)S(1)} %copy-done.46, ...), kind=kOutput, calls=%fused_computation.195 | convolution fusion | flops 843841536 | bytes 53264384 | tf_op jit(solution)/shard_map/while/body/eval_jaxpr/hqk,khd->qhd/dot_general | solution.py:139
  1272.1 18.4 %fusion.118 = bf16[512,12,64]{0,2,1:T(8,128)(2,1)S(1)} fusion(bf16[1024,12,64]{0,2,1:T(8,128)(2,1)S(1)} %bitcast.251, f32[12,512,1024]{2,1,0:T(8,128)} %get-tuple-element.382, f32[12,512,1024]{2,1,0:T(8,128)} %get-tuple-element.349, f32[12,512]{1,0:T(8,128)S(1)} %get-tuple-element.381, f32[12,512]{1,0:T(8,128)S(1)} %copy-done.48, ...), kind=kOutput, calls=%fused_computation.194 | convolution fusion | flops 843841536 | bytes 53264384 | tf_op jit(solution)/shard_map/while/body/eval_jaxpr/hqk,khd->qhd/dot_general | solution.py:139
  1296.2 115.2 %all-reduce.5.cloned.1.call-done = f32[2,2,8,768]{3,2,1,0:T(8,128)} async-done(((f32[2,2,8,768]{3,2,1,0:T(8,128)}), f32[2,2,8,768]{3,2,1,0:T(8,128)}) %all-reduce.5.cloned.1.call-update) | async-done | bytes 98320
  1412.9 104.5 %reduce-scatter.9.cloned.1.call-done = f32[24,768]{1,0:T(8,128)} async-done(((f32[768,768]{1,0:T(8,128)}), f32[24,768]{1,0:T(8,128)}) %reduce-scatter.9.cloned.1.call-update) | async-done | bytes 73744 | tf_op jit(solution)/shard_map/reduce_scatter | solution.py:506
  1520.1 40.3 %all-reduce.2 = (f32[]{:T(128)}, f32[]{:T(128)}) all-reduce(f32[]{:T(128)} %fusion.195, f32[]{:T(128)S(6)} %add.567), channel_id=1, replica_groups=mesh['dp'=2,'fsdp'=16] {'dp','fsdp'}, use_global_device_ids=true, to_apply=%region_31.32 | all-reduce | flops 2 | bytes 16 | tf_op jit(solution)/shard_map/psum | solution.py:511
  (513 shorter events, 132.7 us)
Async XLA Ops:
  8.0 151.5 %copy-start = (bf16[128,768]{1,0:T(8,128)(2,1)S(1)}, bf16[128,768]{1,0:T(8,128)(2,1)}, u32[]{:S(2)}) copy-start(bf16[128,768]{1,0:T(8,128)(2,1)} %param.35) | copy-start | bytes 589828
  8.0 151.5 %reduce-scatter.5.cloned.1.call-start = ((), (), s32[]{:S(2)}) async-start(), calls=%async_computation.3 | async-start | bytes 4718592 | tf_op jit(solution)/shard_map/reduce_scatter | solution.py:395
  77.6 109.4 %all-gather.32.cloned.1.call-start = ((), (), s32[]{:S(2)}) async-start(), calls=%async_computation.9 | async-start | bytes 3649536 | tf_op jit(solution)/shard_map/all_gather | solution.py:407
  79.3 200.1 %all-gather.34.cloned.1.call-start = ((), (), s32[]{:S(2)}) async-start(), calls=%async_computation.10 | async-start | bytes 1216512 | tf_op jit(solution)/shard_map/all_gather | solution.py:408
  80.1 228.6 %all-gather.36.cloned.1.call-start = ((), (), s32[]{:S(2)}) async-start(), calls=%async_computation.11 | async-start | bytes 4866048 | tf_op jit(solution)/shard_map/all_gather | solution.py:411
  81.9 291.8 %all-gather.38.cloned.1.call-start = ((), (), s32[]{:S(2)}) async-start(), calls=%async_computation.12 | async-start | bytes 4866048 | tf_op jit(solution)/shard_map/all_gather | solution.py:412
  82.7 352.7 %all-gather.40.cloned.1.call-start = ((), (), s32[]{:S(2)}) async-start(), calls=%async_computation.13 | async-start | bytes 3649536 | tf_op jit(solution)/shard_map/all_gather | solution.py:407
  83.5 439.5 %all-gather.42.cloned.1.call-start = ((), (), s32[]{:S(2)}) async-start(), calls=%async_computation.14 | async-start | bytes 1216512 | tf_op jit(solution)/shard_map/all_gather | solution.py:408
  84.2 472.9 %all-gather.44.cloned.1.call-start = ((), (), s32[]{:S(2)}) async-start(), calls=%async_computation.15 | async-start | bytes 4866048 | tf_op jit(solution)/shard_map/all_gather | solution.py:411
  84.8 537.2 %all-gather.46.cloned.1.call-start = ((), (), s32[]{:S(2)}) async-start(), calls=%async_computation.16 | async-start | bytes 4866048 | tf_op jit(solution)/shard_map/all_gather | solution.py:412
  85.4 592.3 %all-gather.26.cloned.1.call-start = ((), (), s32[]{:S(2)}) async-start(), calls=%async_computation.4 | async-start | bytes 1216512 | tf_op jit(solution)/shard_map/all_gather | solution.py:373
  86.1 681.2 %all-gather.30.cloned.1.call-start = ((), (), s32[]{:S(2)}) async-start(), calls=%async_computation.6 | async-start | bytes 7372800 | tf_op jit(solution)/shard_map/all_gather | solution.py:444
  89.6 702.4 %all-gather.28.cloned.1.call-start = ((), (), s32[]{:S(2)}) async-start(), calls=%async_computation.5 | async-start | bytes 3342336 | tf_op jit(solution)/shard_map/all_gather | solution.py:439
  90.3 283.3 %copy-start.106 = (f32[1,3072]{1,0:T(1,128)}, f32[1,3072]{1,0:T(1,128)S(1)}, u32[]{:S(2)}) copy-start(f32[1,3072]{1,0:T(1,128)S(1)} %get-tuple-element.333) | copy-start | bytes 36868
  93.8 279.9 %copy-start.116 = (f32[768]{0:T(1024)}, f32[768]{0:T(1024)S(1)}, u32[]{:S(2)}) copy-start(f32[768]{0:T(1024)S(1)} %get-tuple-element.268) | copy-start | bytes 9220
  158.8 96.7 %copy-start.8 = (pred[512,1024]{1,0:T(8,128)(4,1)}, pred[512,1024]{1,0:T(8,128)(4,1)S(1)}, u32[]{:S(2)}) copy-start(pred[512,1024]{1,0:T(8,128)(4,1)S(1)} %get-tuple-element.341) | copy-start | bytes 1572868
  158.8 107.9 %copy-start.4 = (pred[512,1024]{1,0:T(8,128)(4,1)}, pred[512,1024]{1,0:T(8,128)(4,1)S(1)}, u32[]{:S(2)}) copy-start(pred[512,1024]{1,0:T(8,128)(4,1)S(1)} %get-tuple-element.340) | copy-start | bytes 1572868
  163.3 23.9 %copy-start.52 = (bf16[1024,16]{0,1:T(8,128)(2,1)}, bf16[1024,16]{0,1:T(8,128)(2,1)S(1)}, u32[]{:S(2)}) copy-start(bf16[1024,16]{0,1:T(8,128)(2,1)S(1)} %convolution_convert_fusion.7) | copy-start | bytes 98308
  200.5 31.9 %copy-start.2 = (bf16[1024,768]{0,1:T(8,128)(2,1)}, bf16[1024,768]{0,1:T(8,128)(2,1)S(1)}, u32[]{:S(2)}) copy-start(bf16[1024,768]{0,1:T(8,128)(2,1)S(1)} %copy.146) | copy-start | bytes 4718596
  232.3 23.1 %copy-start.45 = (f32[12,512]{1,0:T(8,128)}, f32[12,512]{1,0:T(8,128)S(1)}, u32[]{:S(2)}) copy-start(f32[12,512]{1,0:T(8,128)S(1)} %log_add_fusion.2) | copy-start | bytes 73732
  283.7 61.3 %copy-start.24 = (f32[1024,768]{0,1:T(8,128)}, f32[1024,768]{0,1:T(8,128)S(1)}, u32[]{:S(2)}) copy-start(f32[1024,768]{0,1:T(8,128)S(1)} %get-tuple-element.351) | copy-start | bytes 9437188
  283.7 90.0 %copy-start.85 = (f32[1024]{0:T(1024)}, f32[1024]{0:T(1024)S(1)}, u32[]{:S(2)}) copy-start(f32[1024]{0:T(1024)S(1)} %broadcast_multiply_fusion.3) | copy-start | bytes 12292
  284.1 60.9 %copy-start.91 = (f32[1024]{0:T(1024)}, f32[1024]{0:T(1024)S(1)}, u32[]{:S(2)}) copy-start(f32[1024]{0:T(1024)S(1)} %multiply_reduce_fusion.11) | copy-start | bytes 12292
  284.1 89.5 %copy-start.97 = (f32[1024]{0:T(1024)}, f32[1024]{0:T(1024)S(1)}, u32[]{:S(2)}) copy-start(f32[1024]{0:T(1024)S(1)} %fusion.190) | copy-start | bytes 12292
  308.7 65.0 %copy-start.115 = (f32[768]{0:T(1024)S(1)}, f32[768]{0:T(1024)}, u32[]{:S(2)}) copy-start(f32[768]{0:T(1024)} %get-tuple-element.261) | copy-start | bytes 9220
  389.9 133.1 %copy-start.71 = (f32[1024]{0:T(1024)}, f32[1024]{0:T(1024)S(1)}, u32[]{:S(2)}) copy-start(f32[1024]{0:T(1024)S(1)} %broadcast_multiply_fusion.2) | copy-start | bytes 12292
  390.4 132.6 %copy-start.87 = (f32[1024]{0:T(1024)}, f32[1024]{0:T(1024)S(1)}, u32[]{:S(2)}) copy-start(f32[1024]{0:T(1024)S(1)} %fusion.191) | copy-start | bytes 12292
  390.9 44.5 %copy-start.109 = (f32[2304]{0:T(1024)S(1)}, f32[2304]{0:T(1024)}, u32[]{:S(2)}) copy-start(f32[2304]{0:T(1024)} %get-tuple-element.338) | copy-start | bytes 27652
  391.6 51.1 %copy-start.54 = (bf16[1024,16]{0,1:T(8,128)(2,1)}, bf16[1024,16]{0,1:T(8,128)(2,1)S(1)}, u32[]{:S(2)}) copy-start(bf16[1024,16]{0,1:T(8,128)(2,1)S(1)} %convolution_convert_fusion.6) | copy-start | bytes 98308
  447.4 28.6 %copy-start.15 = (bf16[1024,768]{0,1:T(8,128)(2,1)}, bf16[1024,768]{0,1:T(8,128)(2,1)S(1)}, u32[]{:S(2)}) copy-start(bf16[1024,768]{0,1:T(8,128)(2,1)S(1)} %copy.154) | copy-start | bytes 4718596
  476.1 22.7 %copy-start.56 = (f32[12,512]{1,0:T(8,128)}, f32[12,512]{1,0:T(8,128)S(1)}, u32[]{:S(2)}) copy-start(f32[12,512]{1,0:T(8,128)S(1)} %log_add_fusion) | copy-start | bytes 73732
  523.0 34.1 %copy-start.108 = (f32[1,3072]{1,0:T(1,128)S(1)}, f32[1,3072]{1,0:T(1,128)}, u32[]{:S(2)}) copy-start(f32[1,3072]{1,0:T(1,128)} %get-tuple-element.332) | copy-start | bytes 36868
  523.0 34.1 %copy-start.118 = (f32[768]{0:T(1024)S(1)}, f32[768]{0:T(1024)}, u32[]{:S(2)}) copy-start(f32[768]{0:T(1024)} %get-tuple-element.266) | copy-start | bytes 9220
  523.0 34.1 %copy-start.120 = (f32[768]{0:T(1024)S(1)}, f32[768]{0:T(1024)}, u32[]{:S(2)}) copy-start(f32[768]{0:T(1024)} %get-tuple-element.272) | copy-start | bytes 9220
  528.6 64.9 %copy-start.95 = (f32[1024]{0:T(1024)}, f32[1024]{0:T(1024)S(1)}, u32[]{:S(2)}) copy-start(f32[1024]{0:T(1024)S(1)} %multiply_reduce_fusion.9) | copy-start | bytes 12292
  557.2 64.8 %copy-start.113 = (f32[768]{0:T(1024)S(1)}, f32[768]{0:T(1024)}, u32[]{:S(2)}) copy-start(f32[768]{0:T(1024)} %get-tuple-element.257) | copy-start | bytes 9220
  638.6 39.2 %copy-start.127 = (f32[768]{0:T(1024)S(1)}, f32[768]{0:T(1024)}, u32[]{:S(2)}) copy-start(f32[768]{0:T(1024)} %param.43) | copy-start | bytes 9220
  645.5 35.3 %copy-start.49 = (bf16[128,768]{1,0:T(8,128)(2,1)}, bf16[128,768]{1,0:T(8,128)(2,1)S(1)}, u32[]{:S(2)}) copy-start(bf16[128,768]{1,0:T(8,128)(2,1)S(1)} %gather_fusion.1) | copy-start | bytes 589828
  645.5 36.1 %copy-start.73 = (f32[768]{0:T(1024)S(1)}, f32[768]{0:T(1024)}, u32[]{:S(2)}) copy-start(f32[768]{0:T(1024)} %get-tuple-element.265) | copy-start | bytes 9220
  645.5 36.1 %copy-start.99 = (f32[768]{0:T(1024)S(1)}, f32[768]{0:T(1024)}, u32[]{:S(2)}) copy-start(f32[768]{0:T(1024)} %get-tuple-element.271) | copy-start | bytes 9220
  645.6 77.3 %copy-start.112 = (f32[1600]{0:T(1024)S(1)}, f32[1600]{0:T(1024)}, u32[]{:S(2)}) copy-start(f32[1600]{0:T(1024)} %param.44) | copy-start | bytes 19204
  645.6 77.3 %copy-start.130 = (u32[32]{0:T(128)S(1)}, u32[32]{0:T(128)}, u32[]{:S(2)}) copy-start(u32[32]{0:T(128)} %constant.355) | copy-start | bytes 388
  645.6 104.2 %copy-start.123 = (s32[1,128]{1,0:T(1,128)S(1)}, s32[1,128]{1,0:T(1,128)}, u32[]{:S(2)}) copy-start(s32[1,128]{1,0:T(1,128)} %param.30) | copy-start | bytes 1540
  645.6 121.5 %copy-start.129 = (f32[4]{0:T(128)S(1)}, f32[4]{0:T(128)}, u32[]{:S(2)}) copy-start(f32[4]{0:T(128)} %param.32) | copy-start | bytes 52
  681.1 41.8 %copy-start.121 = (f32[128]{0:T(128)}, f32[128]{0:T(128)S(1)}, u32[]{:S(2)}) copy-start(f32[128]{0:T(128)S(1)} %multiply_reduce_fusion.14) | copy-start | bytes 1540
  682.4 283.0 %reduce-scatter.7.cloned.1.call-start = ((), (), s32[]{:S(2)}) async-start(), calls=%async_computation.7 | async-start | bytes 3342336 | tf_op jit(solution)/shard_map/reduce_scatter | solution.py:470
  767.2 112.5 %copy-start.111 = (f32[2048]{0:T(1024)}, f32[2048]{0:T(1024)S(1)}, u32[]{:S(2)}) copy-start(f32[2048]{0:T(1024)S(1)} %select_reduce_fusion) | copy-start | bytes 24580
  879.7 22.2 %copy-start.51 = (f32[2048]{0:T(1024)}, f32[2048]{0:T(1024)S(1)}, u32[]{:S(2)}) copy-start(f32[2048]{0:T(1024)S(1)} %get-tuple-element.254) | copy-start | bytes 24580
  879.8 22.1 %copy-start.110 = (f32[2048]{0:T(1024)}, f32[2048]{0:T(1024)S(1)}, u32[]{:S(2)}) copy-start(f32[2048]{0:T(1024)S(1)} %log_add_fusion.4) | copy-start | bytes 24580
  879.8 86.9 %copy-start.122 = (f32[128]{0:T(128)S(1)}, f32[128]{0:T(128)}, u32[]{:S(2)}) copy-start(f32[128]{0:T(128)} %copy-done.121) | copy-start | bytes 1540
  901.9 509.5 %all-reduce.5.cloned.1.call-start = ((), (), s32[]{:S(2)}) async-start(), calls=%async_computation.17 | async-start | bytes 196608
  983.2 24.9 %copy-start.96 = (f32[1024]{0:T(1024)S(1)}, f32[1024]{0:T(1024)}, u32[]{:S(2)}) copy-start(f32[1024]{0:T(1024)} %copy-done.95) | copy-start | bytes 12292
  1076.0 42.0 %copy-start.16 = (bf16[1024,768]{0,1:T(8,128)(2,1)S(1)}, bf16[1024,768]{0,1:T(8,128)(2,1)}, u32[]{:S(2)}) copy-start(bf16[1024,768]{0,1:T(8,128)(2,1)} %copy-done.15) | copy-start | bytes 4718596
  1118.0 18.5 %slice-start = ((s8[12582912]{0:T(1024)(128)(4,1)}), s8[4194304]{0:T(1024)(128)(4,1)S(1)}, s32[]{:S(2)}) async-start(s8[12582912]{0:T(1024)(128)(4,1)} %bitcast.246), calls=%async_computation.18 | async-start | bytes 8388608
  1156.7 24.9 %copy-start.92 = (f32[1024]{0:T(1024)S(1)}, f32[1024]{0:T(1024)}, u32[]{:S(2)}) copy-start(f32[1024]{0:T(1024)} %copy-done.91) | copy-start | bytes 12292
  1156.7 24.9 %copy-start.98 = (f32[1024]{0:T(1024)S(1)}, f32[1024]{0:T(1024)}, u32[]{:S(2)}) copy-start(f32[1024]{0:T(1024)} %copy-done.97) | copy-start | bytes 12292
  1290.6 270.6 %copy-start.81 = (f32[2,2,8,24]{3,2,1,0:T(8,128)S(1)}, f32[2,2,8,24]{3,2,1,0:T(8,128)}, u32[]{:S(2)}) copy-start(f32[2,2,8,24]{3,2,1,0:T(8,128)} %param.46) | copy-start | bytes 9220
  1290.6 270.6 %copy-start.102 = (f32[2,2,8,24]{3,2,1,0:T(8,128)S(1)}, f32[2,2,8,24]{3,2,1,0:T(8,128)}, u32[]{:S(2)}) copy-start(f32[2,2,8,24]{3,2,1,0:T(8,128)} %param.48) | copy-start | bytes 9220
  1290.6 270.6 %copy-start.103 = (f32[2,2,8,24]{3,2,1,0:T(8,128)S(1)}, f32[2,2,8,24]{3,2,1,0:T(8,128)}, u32[]{:S(2)}) copy-start(f32[2,2,8,24]{3,2,1,0:T(8,128)} %param.47) | copy-start | bytes 9220
  1290.6 272.0 %copy-start.61 = (f32[24,768]{1,0:T(8,128)S(1)}, f32[24,768]{1,0:T(8,128)}, u32[]{:S(2)}) copy-start(f32[24,768]{1,0:T(8,128)} %param.49) | copy-start | bytes 221188
  1290.6 272.0 %copy-start.76 = (f32[24,768]{1,0:T(8,128)S(1)}, f32[24,768]{1,0:T(8,128)}, u32[]{:S(2)}) copy-start(f32[24,768]{1,0:T(8,128)} %param.51) | copy-start | bytes 221188
  1290.7 272.0 %copy-start.77 = (f32[24,768]{1,0:T(8,128)S(1)}, f32[24,768]{1,0:T(8,128)}, u32[]{:S(2)}) copy-start(f32[24,768]{1,0:T(8,128)} %param.50) | copy-start | bytes 221188
  1290.7 273.6 %copy-start.1 = (bf16[128,768]{1,0:T(8,128)(2,1)S(1)}, bf16[128,768]{1,0:T(8,128)(2,1)}, u32[]{:S(2)}) copy-start(bf16[128,768]{1,0:T(8,128)(2,1)} %param.35) | copy-start | bytes 589828
  1292.1 225.2 %reduce-scatter.9.cloned.1.call-start = ((), (), s32[]{:S(2)}) async-start(), calls=%async_computation.8 | async-start | bytes 2433024 | tf_op jit(solution)/shard_map/reduce_scatter | solution.py:506
  (85 other events, 614.9 us)
Sparse Core Ops, SparseCore 0:
  77.7 60.0 reduce-scatter.4
Sparse Core Ops, SparseCore 1:
  81.0 106.0 all-gather.31
  190.4 52.7 all-gather.33
  245.9 62.7 all-gather.35
  311.6 62.0 all-gather.37
  376.6 58.7 all-gather.39
  438.9 52.7 all-gather.41
  494.4 62.7 all-gather.43
  559.9 62.0 all-gather.45
  625.3 52.4 all-gather.25
  679.3 64.8 all-gather.29
  746.6 45.3 all-gather.27
  902.0 63.4 reduce-scatter.6
  1292.2 119.2 all-reduce.4
  1417.6 99.7 reduce-scatter.8
where the time goes:
time: 1580 us; the launch traced here: 1570 us
  matrix products  527 us (33%)
  waiting for transfers between devices  513 us (32%)
  blocking collectives  243 us (15%)
  other arithmetic  146 us (9%)
  local copies, waits for them, and re-layouts  120 us (8%)
  between operations  23.2 us (1%)
    unnamed x16, waiting for transfers between devices  118 us
    reduce_scatter x1, waiting for transfers between devices, per_device(): lax.psum_scatter(dense_gradient, ('dp', 'fsdp'), scatter_dimension=0, til...  104 us
    dot_general x2, matrix products, layer_forward(): jnp.dot(middle.astype(jnp.bfloat16), up_w, preferred_element_type=jnp.flo...  72.6 us
    dot_general x4, matrix products, one_seq(): jnp.einsum('qhd,khd->hqk', out_grads[block_part], value_rows, preferred_e...  70.9 us
    reduce_scatter x1, waiting for transfers between devices, per_device(): lax.psum_scatter(feat_term.astype(jnp.bfloat16), 'fsdp', scatter_dimensio...  63.3 us
    gather x2, local copies, waits for them, and re-layouts, per_device(): embed[jnp.clip(group_ids, 0, table_rows - 1)]  61.9 us
    all_gather x2, waiting for transfers between devices, per_device(): lax.all_gather(attention_in_weight[layer_position], ('dp', 'fsdp'), axis=...  60 us
    all_gather x1, blocking collectives, per_device(): lax.all_gather(adapter_up_matrix.astype(jnp.bfloat16), ('dp', 'fsdp'), ax...  59.7 us
  transfers between devices with their start and end apart: 15, of which 11 were waited for; matrix products, arithmetic and copies ran while one was open for 22% of the time, Pallas kernels for 0%

commit v1 on v0

v1 whole, which is shorter than its diff:
```python
import functools

import jax
import jax.numpy as jnp
from jax import lax
from jax.experimental import pallas as pl
from jax.experimental.pallas import tpu as pltpu
from jax.sharding import PartitionSpec as P

HEADS = 12
TASKS = 4
REACH = 128

norm_eps = 1e-05
adapter_scale = 2.0
clip_limit = 0.01
learn_rate = 0.05
beta_first = 0.9
beta_second = 0.999
adam_eps = 1e-08
decay_rate = 0.01
masked_score = -1e30

BF = jnp.bfloat16
F32 = jnp.float32
BOTH = ("dp", "fsdp")
VMEM_BYTES = 60 * 1024 * 1024


def mm(a, b):
    return lax.dot_general(a, b, (((1,), (0,)), ((), ())), preferred_element_type=F32)


def mm_nt(a, b):
    return lax.dot_general(a, b, (((1,), (1,)), ((), ())), preferred_element_type=F32)


def mm_tn(a, b):
    return lax.dot_general(a, b, (((0,), (0,)), ((), ())), preferred_element_type=F32)


def layer_norm(rows_in, gain, shift):
    center = rows_in - jnp.mean(rows_in, -1, keepdims=True)
    spread = jnp.mean(center * center, -1, keepdims=True)
    return center * lax.rsqrt(spread + norm_eps) * gain + shift


def norm_back(rows_in, gain, gradient):
    center = rows_in - jnp.mean(rows_in, -1, keepdims=True)
    inverse = lax.rsqrt(jnp.mean(center * center, -1, keepdims=True) + norm_eps)
    unit = center * inverse
    scaled = gradient * gain
    return inverse * (
        scaled
        - jnp.mean(scaled, -1, keepdims=True)
        - unit * jnp.mean(scaled * unit, -1, keepdims=True)
    )


def gelu_pair(v):
    size = jnp.abs(v) * 0.7071067811865476
    base = 1.0 + 0.3275911 * size
    t = pl.reciprocal(base, approx=True)
    t = t * (2.0 - base * t)
    bell = jnp.exp(-0.5 * v * v)
    poly = t * (
        0.127414796 + t * (-0.142248368 + t * (0.7107068705 + t * (-0.7265760135 + t * 0.5307027145)))
    )
    tail = poly * bell
    phi = jnp.where(v >= 0.0, 1.0 - tail, tail)
    return v * phi, phi + v * (bell * 0.3989422804014327)


def params(**more):
    return pltpu.CompilerParams(vmem_limit_bytes=VMEM_BYTES, **more)


def full(shape):
    return pl.BlockSpec(shape, lambda *_: (0,) * len(shape))


def split_of(total, most, step):
    size = (min(most, total) // step) * step
    while size > step and total % size:
        size -= step
    return size if size and total % size == 0 else total


def pair_rows(block, width):
    first = lax.broadcasted_iota(jnp.int32, block.shape, 1) < width
    return jnp.concatenate([jnp.where(first, block, 0.0), jnp.where(first, 0.0, block)], 0).astype(BF)


def pair_join(wide, width):
    rows = wide.shape[1] // 2
    return jnp.concatenate([wide[:width, :rows], wide[width:, rows:]], 0)


def masked(scores, same):
    rows = scores.shape[1] // 2
    return jnp.concatenate(
        [
            jnp.where(same, scores[:, :rows], masked_score),
            jnp.where(same, scores[:, rows:], masked_score),
        ],
        1,
    )


def project_body(x_ref, down_ref, w_ref, up_ref, bias_ref, out_ref, mid_ref):
    low = x_ref[...].astype(BF)
    mid = mm(low, down_ref[...]).astype(BF)
    mid_ref[...] = mid
    total = w_ref.shape[0]
    step = split_of(total, 768, 128)
    for start in range(0, total, step):
        part = slice(start, start + step)
        out_ref[:, part] = (
            mm_nt(low, w_ref[part, :]) + mm(mid, up_ref[:, part]) + bias_ref[:, part]
        ).astype(BF)


def project(x, down, w, up, bias):
    rows, width = x.shape
    tile = split_of(rows, 256, 16)
    total = w.shape[0]
    return pl.pallas_call(
        project_body,
        grid=(rows // tile,),
        in_specs=[
            pl.BlockSpec((tile, width), lambda i: (i, 0)),
            full(down.shape),
            full(w.shape),
            full(up.shape),
            full(bias.shape),
        ],
        out_specs=[
            pl.BlockSpec((tile, total), lambda i: (i, 0)),
            pl.BlockSpec((tile, down.shape[1]), lambda i: (i, 0)),
        ],
        out_shape=[
            jax.ShapeDtypeStruct((rows, total), BF),
            jax.ShapeDtypeStruct((rows, down.shape[1]), BF),
        ],
        compiler_params=params(),
        name="project",
    )(x, down, w, up, bias)


def attend_body(q_ref, k_ref, v_ref, seg_ref, seg_row_ref, ctx_ref, log_ref):
    rows = q_ref.shape[0]
    width = q_ref.shape[1] // 2
    scale = width**-0.5
    for start in range(0, rows, REACH):
        own = slice(start, start + REACH)
        near = slice(max(0, start - REACH), min(rows, start + 2 * REACH))
        queries = pair_rows(q_ref[own, :].astype(F32) * scale, width)
        same = seg_ref[near, :] == seg_row_ref[:, own]
        scores = masked(mm_nt(k_ref[near, :], queries), same)
        top = jnp.max(scores, 0, keepdims=True)
        weights = jnp.exp(scores - top)
        total = jnp.sum(weights, 0, keepdims=True)
        context = mm_tn(v_ref[near, :], weights.astype(BF)) * (1.0 / total)
        ctx_ref[own, :] = pair_join(context, width).T.astype(BF)
        log_ref[0, :, 2 * start : 2 * start + 2 * REACH] = top + jnp.log(total)


def attend(qkv, seg_wide, seg_row):
    rows, total = qkv.shape
    hidden = total // 3
    lanes = 2 * (hidden // HEADS)
    pairs = hidden // lanes
    column = lambda kind: pl.BlockSpec((rows, lanes), lambda p: (0, kind * pairs + p))
    return pl.pallas_call(
        attend_body,
        grid=(pairs,),
        in_specs=[column(0), column(1), column(2), full(seg_wide.shape), full(seg_row.shape)],
        out_specs=[
            pl.BlockSpec((rows, lanes), lambda p: (0, p)),
            pl.BlockSpec((1, 1, 2 * rows), lambda p: (p, 0, 0)),
        ],
        out_shape=[
            jax.ShapeDtypeStruct((rows, hidden), BF),
            jax.ShapeDtypeStruct((pairs, 1, 2 * rows), F32),
        ],
        compiler_params=params(),
        name="attend",
    )(qkv, qkv, qkv, seg_wide, seg_row)


def flat(ref):
    whole = ref[...]
    return whole.reshape(-1, whole.shape[-1])


def rows_of(ref, start, size):
    each = ref.shape[1]
    if size % each == 0 and start % each == 0 and each % 16 == 0:
        part = ref[start // each : (start + size) // each, :, :]
        return part.reshape(size, part.shape[-1])
    return flat(ref)[start : start + size, :]


def feed_step(ref):
    units = ref.shape[0] * ref.shape[1]
    step = ref.shape[1]
    while units % (2 * step) == 0 and 2 * step <= 768 and ref.shape[0] > 1:
        step *= 2
    return units, (step if ref.shape[0] > 1 else split_of(units, 768, 128))


def after_body(
    ctx_ref, x_ref, wo_ref, up_ref, down_ref, bo_ref, b1_ref, b2_ref, norm_ref,
    out_ref, one_ref, two_ref, slope_ref,
):
    one = x_ref[...] + (mm_nt(ctx_ref[...], wo_ref[...]) + bo_ref[...])
    one_ref[...] = one
    middle = layer_norm(one, norm_ref[0:1, :], norm_ref[1:2, :])
    low = middle.astype(BF)
    total = middle + b2_ref[...]
    units, step = feed_step(up_ref)
    for start in range(0, units, step):
        part = slice(start, start + step)
        act, slope = gelu_pair(mm_nt(low, rows_of(up_ref, start, step)) + b1_ref[:, part])
        slope_ref[:, part] = slope.astype(BF)
        total = total + mm(act.astype(BF), rows_of(down_ref, start, step))
    two_ref[...] = total
    out_ref[...] = layer_norm(total, norm_ref[2:3, :], norm_ref[3:4, :])


def slab_spec(slab):
    array, place, rows = slab
    return pl.BlockSpec((array.shape[0], rows, array.shape[2]), lambda *_: (0, place, 0))


def after(ctx, x, wo, up, down, bo, b1, b2, norms):
    rows, width = x.shape
    tile = split_of(rows, 256, 16)
    units = b1.shape[1]
    row = lambda n: pl.BlockSpec((tile, n), lambda i: (i, 0))
    return pl.pallas_call(
        after_body,
        grid=(rows // tile,),
        in_specs=[row(width), row(width), full(wo.shape), slab_spec(up), slab_spec(down)]
        + [full(a.shape) for a in (bo, b1, b2, norms)],
        out_specs=[row(width), row(width), row(width), row(units)],
        out_shape=[jax.ShapeDtypeStruct((rows, width), F32)] * 3
        + [jax.ShapeDtypeStruct((rows, units), BF)],
        compiler_params=params(),
        name="after",
    )(ctx, x, wo, up[0], down[0], bo, b1, b2, norms)


def exact_rows(choose, matrix):
    high = matrix.astype(BF)
    rest = matrix - high.astype(F32)
    middle = rest.astype(BF)
    low = (rest - middle.astype(F32)).astype(BF)
    return mm(choose, high) + mm(choose, middle) + mm(choose, low)


def last_forward_body(
    x_ref, place_ref, place_row_ref, seg_ref, down_ref, w_ref, adapt_ref, bias_ref, wo_ref, up_any, dn_any,
    bo_ref, b1_ref, b2_ref, norm_ref, hb_ref, hbias_ref,
    kv_ref, q_ref, mid_ref, log_ref, one_ref, slope_ref, two_ref, low_ref, act_ref, hslope_ref, feat_ref,
    up_ref, dn_ref, ctx_ref, sems, *, places,
):
    copies = []
    for k, (source, target, place) in enumerate(
        ((up_any, up_ref, places[0]), (dn_any, dn_ref, places[1]))
    ):
        rows = target.shape[1]
        copies.append(
            pltpu.make_async_copy(
                source.at[:, pl.ds(place * rows, rows), :], target, sems.at[k]
            )
        )
        copies[-1].start()
    rows, hidden = x_ref.shape
    labels = place_ref.shape[0]
    lanes = 2 * (hidden // HEADS)
    width = lanes // 2
    low = x_ref[...].astype(BF)
    mid = mm(low, down_ref[...]).astype(BF)
    mid_ref[...] = mid
    step = split_of(2 * hidden, 512, 128)
    for start in range(hidden, 3 * hidden, step):
        part = slice(start, start + step)
        kv_ref[:, start - hidden : start - hidden + step] = (
            mm_nt(low, w_ref[part, :]) + mm(mid, adapt_ref[:, part]) + bias_ref[:, part]
        ).astype(BF)
    choose = (
        lax.broadcasted_iota(jnp.int32, (labels, rows), 1) == place_ref[...][:, 0:1]
    ).astype(F32).astype(BF)
    own = exact_rows(choose, x_ref[...])
    own_low = own.astype(BF)
    own_mid = mm(choose, mid).astype(BF)
    q_ref[...] = (
        mm_nt(own_low, w_ref[:hidden, :]) + mm(own_mid, adapt_ref[:, :hidden]) + bias_ref[:, :hidden]
    ).astype(BF)
    seg = seg_ref[...]
    seg_own = jnp.sum(
        jnp.where(
            lax.broadcasted_iota(jnp.int32, (rows, labels), 0) == place_row_ref[...], seg, 0.0
        ),
        0,
        keepdims=True,
    )
    same = seg == seg_own
    for p in range(hidden // lanes):
        part = slice(p * lanes, (p + 1) * lanes)
        queries = pair_rows(q_ref[:, part].astype(F32) * width**-0.5, width)
        scores = masked(mm_nt(kv_ref[:, part], queries), same)
        top = jnp.max(scores, 0, keepdims=True)
        weights = jnp.exp(scores - top)
        total = jnp.sum(weights, 0, keepdims=True)
        context = mm_tn(
            kv_ref[:, hidden + p * lanes : hidden + (p + 1) * lanes], weights.astype(BF)
        ) * (1.0 / total)
        ctx_ref[:, part] = pair_join(context, width).T.astype(BF)
        log_ref[p : p + 1, :] = top + jnp.log(total)
    one = own + (mm_nt(ctx_ref[...], wo_ref[...]) + bo_ref[...])
    one_ref[...] = one
    middle = layer_norm(one, norm_ref[0:1, :], norm_ref[1:2, :])
    middle_low = middle.astype(BF)
    sum_two = middle + b2_ref[...]
    units, step = feed_step(up_ref)
    for copy in copies:
        copy.wait()
    for start in range(0, units, step):
        part = slice(start, start + step)
        act, slope = gelu_pair(mm_nt(middle_low, rows_of(up_ref, start, step)) + b1_ref[:, part])
        slope_ref[:, part] = slope.astype(BF)
        sum_two = sum_two + mm(act.astype(BF), rows_of(dn_ref, start, step))
    two_ref[...] = sum_two
    out_low = layer_norm(sum_two, norm_ref[2:3, :], norm_ref[3:4, :]).astype(BF)
    low_ref[...] = out_low
    act, slope = gelu_pair(mm(out_low, hb_ref[...]) + hbias_ref[...])
    act_ref[...] = act
    hslope_ref[...] = slope
    feat_ref[...] = layer_norm(act, norm_ref[4:5, :], norm_ref[5:6, :]).astype(BF)


def slab_scratch(slab):
    array, place, rows = slab
    return pltpu.VMEM((array.shape[0], rows, array.shape[2]), BF)


def last_forward(x, place_col, place_row, seg_wide, down, w, adapt, bias, wo, up, dn, bo, b1, b2, norms, hb, hbias):
    rows, hidden = x.shape
    labels = place_col.shape[0]
    units = b1.shape[1]
    whole = pl.BlockSpec(memory_space=pltpu.VMEM)
    anywhere = pl.BlockSpec(memory_space=pl.ANY)
    shape = jax.ShapeDtypeStruct
    pairs = HEADS // 2
    return pl.pallas_call(
        functools.partial(last_forward_body, places=(up[1], dn[1])),
        in_specs=[whole] * 9 + [anywhere] * 2 + [whole] * 6,
        out_specs=[whole] * 11,
        out_shape=[
            shape((rows, 2 * hidden), BF),
            shape((labels, hidden), BF),
            shape((rows, down.shape[1]), BF),
            shape((pairs, 2 * labels), F32),
            shape((labels, hidden), F32),
            shape((labels, units), BF),
            shape((labels, hidden), F32),
            shape((labels, hidden), BF),
            shape((labels, hidden), F32),
            shape((labels, hidden), F32),
            shape((labels, hidden), BF),
        ],
        scratch_shapes=[
            slab_scratch(up),
            slab_scratch(dn),
            pltpu.VMEM((labels, hidden), BF),
            pltpu.SemaphoreType.DMA((2,)),
        ],
        compiler_params=params(),
        name="last_forward",
    )(x, place_col, place_row, seg_wide, down, w, adapt, bias, wo, up[0], dn[0], bo, b1, b2, norms, hb, hbias)


def vocab_body(u_ref, e_ref, et_ref, bias_ref, num_ref, log_ref, scores, weights):
    count = e_ref.shape[0]
    step = split_of(count, 640, 16)
    u = u_ref[...]
    rows = u.shape[0]
    labels = num_ref.shape[2]
    top = jnp.full((1, rows), -jnp.inf, F32)
    for start in range(0, count, step):
        part = slice(start, start + step)
        bias = bias_ref[part, :]
        logits = mm_nt(e_ref[part, :], u) + jnp.concatenate([bias] * (rows // bias.shape[1]), 1)
        scores[part, :] = logits
        top = jnp.maximum(top, jnp.max(logits, 0, keepdims=True))
    total = jnp.zeros((1, rows), F32)
    for start in range(0, count, step):
        part = slice(start, start + step)
        grown = jnp.exp(scores[part, :] - top)
        total = total + jnp.sum(grown, 0, keepdims=True)
        weights[part, :] = grown.astype(BF)
    mean = mm(et_ref[...], weights[...]) * (1.0 / total)
    logs = top + jnp.log(total)
    for k in range(rows // labels):
        num_ref[k, :, :] = mean[:, k * labels : (k + 1) * labels]
        log_ref[k, :, :] = logs[:, k * labels : (k + 1) * labels]


def vocab(u, e, et, bias_wide, labels):
    rows, hidden = u.shape
    count = e.shape[0]
    tile = 2 * labels
    return pl.pallas_call(
        vocab_body,
        grid=(rows // tile,),
        in_specs=[
            pl.BlockSpec((tile, hidden), lambda i: (i, 0)),
            full(e.shape),
            full(et.shape),
            full(bias_wide.shape),
        ],
        out_specs=[
            pl.BlockSpec((2, hidden, labels), lambda i: (i, 0, 0)),
            pl.BlockSpec((2, 1, labels), lambda i: (i, 0, 0)),
        ],
        out_shape=[
            jax.ShapeDtypeStruct((rows // labels, hidden, labels), F32),
            jax.ShapeDtypeStruct((rows // labels, 1, labels), F32),
        ],
        scratch_shapes=[pltpu.VMEM((count, tile), F32), pltpu.VMEM((count, tile), BF)],
        compiler_params=params(),
        name="vocab",
    )(u, e, et, bias_wide)


def last_backward_body(
    du_ref, kv_ref, q_ref, mid_ref, log_ref, one_ref, slope_ref, two_ref, low_ref, act_ref, hslope_ref,
    place_ref, place_row_ref, seg_ref, down_ref, w_ref, adapt_ref, wo_ref, up_any, dn_any, norm_ref, hb_ref,
    dx_ref, gh_ref, gq_ref, gv_ref,
    up_ref, dn_ref, dkv_ref, dq_ref, sems, *, places, rank,
):
    copies = []
    for k, (source, target, place) in enumerate(
        ((up_any, up_ref, places[0]), (dn_any, dn_ref, places[1]))
    ):
        rows = target.shape[1]
        copies.append(
            pltpu.make_async_copy(
                source.at[:, pl.ds(place * rows, rows), :], target, sems.at[k]
            )
        )
        copies[-1].start()
    rows = kv_ref.shape[0]
    labels, hidden = du_ref.shape
    lanes = 2 * (hidden // HEADS)
    width = lanes // 2
    scale = width**-0.5
    dact = norm_back(act_ref[...], norm_ref[4:5, :], du_ref[...])
    dz = (hslope_ref[...] * dact).astype(BF)
    gh_ref[...] = mm_tn(low_ref[...], dz)
    dtwo = norm_back(two_ref[...], norm_ref[2:3, :], mm_nt(dz, hb_ref[...]))
    dtwo_low = dtwo.astype(BF)
    dmiddle = dtwo
    units, step = feed_step(up_ref)
    for copy in copies:
        copy.wait()
    for start in range(0, units, step):
        part = slice(start, start + step)
        dgate = (
            slope_ref[:, part].astype(F32) * mm_nt(dtwo_low, rows_of(dn_ref, start, step))
        ).astype(BF)
        dmiddle = dmiddle + mm(dgate, rows_of(up_ref, start, step))
    done = norm_back(one_ref[...], norm_ref[0:1, :], dmiddle)
    dctx = mm(done.astype(BF), wo_ref[...]).astype(BF)
    seg = seg_ref[...]
    choose_t = lax.broadcasted_iota(jnp.int32, (rows, labels), 0) == place_row_ref[...]
    same = seg == jnp.sum(jnp.where(choose_t, seg, 0.0), 0, keepdims=True)
    for p in range(hidden // lanes):
        part = slice(p * lanes, (p + 1) * lanes)
        later = slice(hidden + p * lanes, hidden + (p + 1) * lanes)
        queries = pair_rows(q_ref[:, part].astype(F32) * scale, width)
        outs = pair_rows(dctx[:, part].astype(F32), width)
        keys = kv_ref[:, part]
        weights = jnp.exp(masked(mm_nt(keys, queries), same) - log_ref[p : p + 1, :])
        dweights = mm_nt(kv_ref[:, later], outs)
        inner = jnp.sum(dweights * weights, 0, keepdims=True)
        dscores = (weights * (dweights - inner)).astype(BF)
        dkv_ref[:, part] = mm(dscores, queries).astype(BF)
        dkv_ref[:, later] = mm(weights.astype(BF), outs).astype(BF)
        dq_ref[:, part] = (pair_join(mm_tn(keys, dscores), width) * scale).T.astype(BF)
    dq = dq_ref[...]
    own_mid = mm(
        (lax.broadcasted_iota(jnp.int32, (labels, rows), 1) == place_ref[...][:, 0:1]).astype(F32).astype(BF),
        mid_ref[...],
    ).astype(BF)
    gq_ref[...] = adapter_scale * mm_tn(own_mid, dq)[:rank, :]
    gv_ref[...] = adapter_scale * mm_tn(mid_ref[...], dkv_ref[:, hidden:])[rank : 2 * rank, :]
    dmid_own = mm_nt(dq, adapt_ref[:, :hidden]).astype(BF)
    own = done + mm(dq, w_ref[:hidden, :]) + mm_nt(dmid_own, down_ref[...])
    spread = choose_t.astype(F32).astype(BF)
    own_high = own.astype(BF)
    own_rest = (own - own_high.astype(F32)).astype(BF)
    dmid = mm_nt(dkv_ref[:, hidden:], adapt_ref[:, 2 * hidden :]).astype(BF)
    step = split_of(hidden, 256, 128)
    for start in range(0, hidden, step):
        part = slice(start, start + step)
        dx_ref[:, part] = (
            mm(dkv_ref[...], w_ref[hidden:, part])
            + mm_nt(dmid, down_ref[part, :])
            + mm(spread, own_high[:, part])
            + mm(spread, own_rest[:, part])
        )


def last_backward(du, saved, place_col, place_row, seg_wide, down, w, adapt, wo, up, dn, norms, hb, rank):
    kv = saved[0]
    rows = kv.shape[0]
    labels, hidden = du.shape
    whole = pl.BlockSpec(memory_space=pltpu.VMEM)
    anywhere = pl.BlockSpec(memory_space=pl.ANY)
    shape = jax.ShapeDtypeStruct
    return pl.pallas_call(
        functools.partial(last_backward_body, places=(up[1], dn[1]), rank=rank),
        in_specs=[whole] * 18 + [anywhere] * 2 + [whole] * 2,
        out_specs=[whole] * 4,
        out_shape=[
            shape((rows, hidden), F32),
            shape((hidden, hidden), F32),
            shape((rank, hidden), F32),
            shape((rank, hidden), F32),
        ],
        scratch_shapes=[
            slab_scratch(up),
            slab_scratch(dn),
            pltpu.VMEM(kv.shape, BF),
            pltpu.VMEM((labels, hidden), BF),
            pltpu.SemaphoreType.DMA((2,)),
        ],
        compiler_params=params(),
        name="last_backward",
    )(du, *saved, place_col, place_row, seg_wide, down, w, adapt, wo, up[0], dn[0], norms, hb)


def after_back_body(dout_ref, one_ref, two_ref, slope_ref, wo_ref, up_ref, down_ref, norm_ref, dctx_ref):
    dtwo = norm_back(two_ref[...], norm_ref[2:3, :], dout_ref[...])
    low = dtwo.astype(BF)
    dmiddle = dtwo
    units, step = feed_step(up_ref)
    for start in range(0, units, step):
        part = slice(start, start + step)
        dgate = (
            slope_ref[:, part].astype(F32) * mm_nt(low, rows_of(down_ref, start, step))
        ).astype(BF)
        dmiddle = dmiddle + mm(dgate, rows_of(up_ref, start, step))
    done = norm_back(one_ref[...], norm_ref[0:1, :], dmiddle)
    dctx_ref[...] = mm(done.astype(BF), wo_ref[...]).astype(BF)


def after_back(dout, one, two, slope, wo, up, down, norms):
    rows, width = dout.shape
    tile = split_of(rows, 256, 16)
    row = lambda n: pl.BlockSpec((tile, n), lambda i: (i, 0))
    return pl.pallas_call(
        after_back_body,
        grid=(rows // tile,),
        in_specs=[row(width), row(width), row(width), row(slope.shape[1]), full(wo.shape)]
        + [slab_spec(up), slab_spec(down), full(norms.shape)],
        out_specs=row(width),
        out_shape=jax.ShapeDtypeStruct((rows, width), BF),
        compiler_params=params(),
        name="after_back",
    )(dout, one, two, slope, wo, up[0], down[0], norms)


def attend_back_body(
    q_ref, k_ref, v_ref, dctx_ref, log_ref, seg_ref, seg_row_ref, mid_ref, gq_ref, gv_ref, dv_ref
):
    rows = q_ref.shape[0]
    width = q_ref.shape[1] // 2
    scale = width**-0.5
    rank = gq_ref.shape[0]
    dv_ref[...] = jnp.zeros_like(dv_ref)
    gq = jnp.zeros((2 * width, mid_ref.shape[1]), F32)
    for start in range(0, rows, REACH):
        own = slice(start, start + REACH)
        near = slice(max(0, start - REACH), min(rows, start + 2 * REACH))
        queries = pair_rows(q_ref[own, :].astype(F32) * scale, width)
        outs = pair_rows(dctx_ref[own, :].astype(F32), width)
        same = seg_ref[near, :] == seg_row_ref[:, own]
        keys = k_ref[near, :]
        logs = log_ref[0, :, 2 * start : 2 * start + 2 * REACH]
        weights = jnp.exp(masked(mm_nt(keys, queries), same) - logs)
        dweights = mm_nt(v_ref[near, :], outs)
        inner = jnp.sum(dweights * weights, 0, keepdims=True)
        dscores = (weights * (dweights - inner)).astype(BF)
        dv_ref[near, :] += mm(weights.astype(BF), outs)
        dq = (pair_join(mm_tn(keys, dscores), width) * scale).astype(BF)
        gq = gq + mm(dq, mid_ref[own, :])
    gq_ref[...] = adapter_scale * gq.T[:rank, :]
    gv_ref[...] = adapter_scale * mm_tn(mid_ref[...], dv_ref[...].astype(BF))[rank : 2 * rank, :]


def attend_back(qkv, dctx, logs, seg_wide, seg_row, mid, rank):
    rows, total = qkv.shape
    hidden = total // 3
    lanes = 2 * (hidden // HEADS)
    pairs = hidden // lanes
    column = lambda kind: pl.BlockSpec((rows, lanes), lambda p: (0, kind * pairs + p))
    return pl.pallas_call(
        attend_back_body,
        grid=(pairs,),
        in_specs=[
            column(0),
            column(1),
            column(2),
            column(0),
            pl.BlockSpec((1, 1, 2 * rows), lambda p: (p, 0, 0)),
            full(seg_wide.shape),
            full(seg_row.shape),
            full(mid.shape),
        ],
        out_specs=[pl.BlockSpec((rank, lanes), lambda p: (0, p))] * 2,
        out_shape=[jax.ShapeDtypeStruct((rank, hidden), F32)] * 2,
        scratch_shapes=[pltpu.VMEM((rows, lanes), F32)],
        compiler_params=params(),
        name="attend_back",
    )(qkv, qkv, qkv, dctx, logs, seg_wide, seg_row, mid)


def seg_positions(segments):
    index = jnp.arange(segments.shape[-1], dtype=jnp.int32)
    fresh = jnp.concatenate([jnp.ones((1,), dtype=bool), segments[1:] != segments[:-1]], -1)
    starts = lax.cummax(jnp.where(fresh, index, jnp.zeros_like(index)), axis=0)
    return index - starts


def optimizer_update(weight, gradient, moment_one, moment_two, step_as_real):
    moment_one = beta_first * moment_one + (1.0 - beta_first) * gradient
    moment_two = beta_second * moment_two + (1.0 - beta_second) * gradient * gradient
    one_hat = moment_one / (1.0 - beta_first**step_as_real)
    two_hat = moment_two / (1.0 - beta_second**step_as_real)
    weight = weight - learn_rate * (one_hat / (jnp.sqrt(two_hat) + adam_eps) + decay_rate * weight)
    return (weight, moment_one, moment_two)


def pad_rows(matrix, multiple):
    return jnp.pad(matrix, ((0, -matrix.shape[0] % multiple), (0, 0)))


def slab_of(gathered, start, rows):
    if rows % 16 == 0 and start % rows == 0:
        return (gathered, start // rows, rows)
    part = gathered[:, start : start + rows].reshape(1, -1, gathered.shape[2])
    return (part, 0, part.shape[1])


def per_device(
    input_token_index,
    sentence_numbers,
    label_positions,
    label_target_token,
    sequence_task_index,
    task_loss_weight,
    optimizer_step_count,
    embed,
    position_embedding,
    norm_gain_vector,
    norm_bias_vector,
    attention_in_weight,
    attention_out_weight,
    feedforward_up,
    feedforward_down,
    layer_bias_vector,
    head_dense_bias,
    vocabulary_bias,
    adapter_down_matrix,
    adapter_up_matrix,
    adapter_moment_first,
    adapter_moment_second,
    head_projection,
    head_moment_first,
    head_moment_second,
):
    shards = lax.axis_size("dp") * lax.axis_size("fsdp")
    dp_index = lax.axis_index("dp")
    fsdp_index = lax.axis_index("fsdp")
    layers, unused, rank, up_part = adapter_up_matrix.shape
    hidden = embed.shape[1]
    tokens = input_token_index.shape[1]
    labels = label_positions.shape[1]
    qkv_rows = attention_in_weight.shape[2]
    out_rows = attention_out_weight.shape[2]
    ff_rows = feedforward_up.shape[2]
    head_rows = head_projection.shape[0]

    pieces = []
    for layer in range(layers):
        pieces += [feedforward_up[layer].T, feedforward_down[layer]]
    for layer in range(layers):
        pieces += [attention_in_weight[layer].T, attention_out_weight[layer].T]
    pieces += [head_projection.astype(BF)]
    ups = adapter_up_matrix.astype(BF).reshape(-1)
    up_rows = -(-ups.size // hidden)
    pieces += [jnp.pad(ups, (0, up_rows * hidden - ups.size)).reshape(up_rows, hidden)]
    chunk = pad_rows(jnp.concatenate(pieces, 0), 32)
    gathered = lax.all_gather(chunk, BOTH, axis=0, tiled=False)
    slabs = [
        (
            slab_of(gathered, 2 * layer * ff_rows, ff_rows),
            slab_of(gathered, (2 * layer + 1) * ff_rows, ff_rows),
        )
        for layer in range(layers)
    ]
    at = 2 * layers * ff_rows
    in_weights, out_weights = [], []
    for layer in range(layers):
        in_weights.append(gathered[:, at : at + qkv_rows].reshape(-1, hidden))
        at += qkv_rows
        out_weights.append(gathered[:, at : at + out_rows].reshape(-1, hidden))
        at += out_rows
    head_full = gathered[:, at : at + head_rows].reshape(-1, hidden)
    at += head_rows
    ups_full = (
        gathered[:, at : at + up_rows]
        .reshape(shards, -1)[:, : ups.size]
        .reshape(shards, layers, 2, rank, up_part)
        .transpose(1, 2, 3, 0, 4)
        .reshape(layers, 2, rank, hidden)
    )
    adapters = [
        jnp.zeros((128, 3 * hidden), BF)
        .at[:rank, :hidden]
        .set(2 * ups_full[layer, 0])
        .at[rank : 2 * rank, 2 * hidden :]
        .set(2 * ups_full[layer, 1])
        for layer in range(layers)
    ]
    downs = [
        jnp.zeros((hidden, 128), BF)
        .at[:, :rank]
        .set(adapter_down_matrix[layer, 0])
        .at[:, rank : 2 * rank]
        .set(adapter_down_matrix[layer, 1])
        for layer in range(layers)
    ]
    bias_of = []
    for layer in range(layers):
        b = layer_bias_vector[layer][None, :]
        ff = b.shape[1] - 4 * hidden
        bias_of.append(
            (
                jnp.concatenate(
                    [b[:, :hidden], jnp.zeros((1, hidden), F32), b[:, hidden : 2 * hidden]], 1
                ),
                b[:, 2 * hidden : 3 * hidden],
                b[:, 3 * hidden : 3 * hidden + ff],
                b[:, 3 * hidden + ff :],
            )
        )
    norms_of = [
        jnp.concatenate(
            [
                norm_gain_vector[1 + 2 * layer][None],
                norm_bias_vector[1 + 2 * layer][None],
                norm_gain_vector[2 + 2 * layer][None],
                norm_bias_vector[2 + 2 * layer][None],
                norm_gain_vector[-1][None],
                norm_bias_vector[-1][None],
            ],
            0,
        )
        for layer in range(layers)
    ]

    table_rows = embed.shape[0]
    wanted = jnp.concatenate([input_token_index[0], label_target_token[0]])
    group_ids = lax.all_gather(wanted, "dp", axis=0, tiled=True) - dp_index * table_rows
    inside = (group_ids >= 0) & (group_ids < table_rows)
    looked = jnp.where(
        inside[:, None], embed[jnp.clip(group_ids, 0, table_rows - 1)], jnp.zeros((), BF)
    )
    rows = lax.psum_scatter(looked, "dp", scatter_dimension=0, tiled=True)
    target_rows = rows[tokens:].astype(F32)
    segments = sentence_numbers[0]
    place_hot = (
        seg_positions(segments)[:, None]
        == jnp.arange(position_embedding.shape[0], dtype=jnp.int32)[None, :]
    ).astype(BF)
    hidden_rows = layer_norm(
        rows[:tokens].astype(F32)
        + jnp.dot(place_hot, position_embedding, preferred_element_type=F32),
        norm_gain_vector[0],
        norm_bias_vector[0],
    )
    seg_real = segments.astype(F32)
    seg_wide = jnp.broadcast_to(seg_real[:, None], (tokens, 128))
    seg_row = seg_real[None, :]
    place_row = label_positions
    place_col = jnp.broadcast_to(label_positions.reshape(labels, 1), (labels, 128))

    slice_rows = vocabulary_bias.shape[0]
    own_slice = lax.dynamic_slice_in_dim(embed, fsdp_index * slice_rows, slice_rows, 0)
    parts = [own_slice]
    dp_count = lax.axis_size("dp")
    for shift in range(1, dp_count):
        parts.append(
            lax.ppermute(own_slice, "dp", [(k, (k + shift) % dp_count) for k in range(dp_count)])
        )
    own_vocab = jnp.concatenate(parts, 0)
    all_bias = lax.all_gather(vocabulary_bias, BOTH, axis=0, tiled=True)
    own_bias = jnp.concatenate(
        [
            lax.dynamic_slice_in_dim(
                all_bias,
                ((dp_index - shift) % dp_count) * table_rows + fsdp_index * slice_rows,
                slice_rows,
                0,
            )
            for shift in range(dp_count)
        ]
    )
    bias_wide = jnp.broadcast_to(own_bias[:, None], (own_bias.shape[0], 128))
    target_bias = all_bias[label_target_token[0]]

    task_range = jnp.arange(TASKS, dtype=jnp.int32)
    task_hot = (sequence_task_index[:, None] == task_range[None, :]).astype(F32)
    counts = lax.psum(jnp.sum(task_hot, 0) * labels, BOTH)
    row_weight = jnp.sum(task_hot[0] * (task_loss_weight / jnp.maximum(counts, 1.0)))

    qkv, mid = project(hidden_rows, downs[0], in_weights[0], adapters[0], bias_of[0][0])
    context, logs = attend(qkv, seg_wide, seg_row)
    x_last, one, two, slope = after(
        context, hidden_rows, out_weights[0], *slabs[0], *bias_of[0][1:], norms_of[0]
    )
    *saved, features = last_forward(
        x_last, place_col, place_row, seg_wide, downs[1], in_weights[1], adapters[1], bias_of[1][0],
        out_weights[1], *slabs[1], *bias_of[1][1:], norms_of[1], head_full, head_dense_bias[None, :],
    )
    every = lax.all_gather(features, "fsdp", axis=0, tiled=True)
    means, local_logs = vocab(every, own_vocab, own_vocab.T, bias_wide, labels)
    local_logs = local_logs.reshape(-1, labels)
    all_logs = lax.all_gather(local_logs, "fsdp", axis=0, tiled=False)
    whole_logs = jax.nn.logsumexp(all_logs, axis=0)
    scaled = (means * jnp.exp(local_logs - whole_logs)[:, None, :]).astype(BF)
    mean_rows = lax.psum_scatter(scaled, "fsdp", scatter_dimension=0, tiled=True)[0]
    own_logs = lax.dynamic_index_in_dim(whole_logs, fsdp_index, 0, keepdims=False)
    targets = jnp.sum(features.astype(F32) * target_rows, 1) + target_bias
    own_loss = row_weight * jnp.sum(own_logs - targets)
    feat_grad = row_weight * (mean_rows.astype(F32).T - target_rows)

    hidden_grad, dense_gradient, gq_last, gv_last = last_backward(
        feat_grad, saved, place_col, place_row, seg_wide, downs[1], in_weights[1], adapters[1],
        out_weights[1], *slabs[1], norms_of[1], head_full, rank,
    )
    dctx = after_back(hidden_grad, one, two, slope, out_weights[0], *slabs[0], norms_of[0])
    gq_first, gv_first = attend_back(qkv, dctx, logs, seg_wide, seg_row, mid, rank)
    adapter_gradient = jnp.stack(
        [jnp.stack([gq_first, gv_first]), jnp.stack([gq_last, gv_last])]
    )
    adapter_portion, dense_portion = (
        lax.psum_scatter(adapter_gradient, BOTH, scatter_dimension=3, tiled=True),
        lax.psum_scatter(dense_gradient, BOTH, scatter_dimension=0, tiled=True),
    )
    squared_entries = jnp.sum(adapter_portion * adapter_portion) + jnp.sum(
        dense_portion * dense_portion
    )
    masked_task_loss, norm_square = lax.psum((own_loss, squared_entries), BOTH)
    gradient_norm = jnp.sqrt(norm_square)
    scale_factor = jnp.minimum(1.0, clip_limit / (gradient_norm + 1e-06))
    step_as_real = optimizer_step_count[0].astype(F32)
    adapter_new = optimizer_update(
        adapter_up_matrix,
        adapter_portion * scale_factor,
        adapter_moment_first,
        adapter_moment_second,
        step_as_real,
    )
    dense_new = optimizer_update(
        head_projection,
        dense_portion * scale_factor,
        head_moment_first,
        head_moment_second,
        step_as_real,
    )
    return (masked_task_loss, gradient_norm, *adapter_new, *dense_new)


def solution(mesh):
    rows = P(BOTH, None)
    in_specs = (
        rows,
        rows,
        rows,
        rows,
        P(BOTH),
        P(),
        P(),
        P("dp", None),
        P(),
        P(),
        P(),
        P(None, None, BOTH),
        P(None, None, BOTH),
        P(None, None, BOTH),
        P(None, BOTH, None),
        P(),
        P(),
        P(BOTH),
        P(),
        P(None, None, None, BOTH),
        P(None, None, None, BOTH),
        P(None, None, None, BOTH),
        rows,
        rows,
        rows,
    )
    adapter = P(None, None, None, BOTH)
    out_specs = (P(), P(), adapter, adapter, adapter, rows, rows, rows)
    return jax.shard_map(
        per_device, mesh=mesh, in_specs=in_specs, out_specs=out_specs, check_vma=False
    )
```

time: 1580 us -> 953 us (0.60)
  matrix products: 527 us -> 2.11 us
  Pallas kernels: 0 us -> 190 us
  blocking collectives: 243 us -> 103 us
  other arithmetic: 146 us -> 38.9 us
  waiting for transfers between devices: 513 us -> 490 us
  local copies, waits for them, and re-layouts: 120 us -> 98.7 us
    dot_general x54 -> x1, matrix products: 527 us -> 2.11 us  [per_device(): jnp.dot(place_hot, position_embedding, preferred_element_type=F32)]
    pallas_call x0 -> x8, Pallas kernels: none -> 190 us  [the longest x1 37.7 us: vocab(): pl.pallas_call(vocab_body, grid=(rows // tile,), in_specs=[pl.BlockSpec((...]
    all_gather x7 -> x2, blocking collectives: 158 us -> 24.9 us  [the longest x1 19.6 us: per_device(): all_logs = lax.all_gather(local_logs, 'fsdp', axis=0, tiled=False)]
    reduce_sum x14 -> x3, other arithmetic: 75.3 us -> 1.25 us  [the longest x1 0.61 us: per_device(): own_loss = row_weight * jnp.sum(own_logs - targets)]
    all_gather x11 -> x2, waiting for transfers between devices: 227 us -> 155 us  [the longest x1 155 us: per_device(): gathered = lax.all_gather(chunk, BOTH, axis=0, tiled=False)]
    convert_element_type x43 -> x3, other arithmetic: 46.6 us -> 4.89 us  [the longest x1 4.88 us: per_device(): scaled = (means * jnp.exp(local_logs - whole_logs)[:, None, :]).astype(BF)]
    unnamed x16 -> x9, waiting for transfers between devices: 118 us -> 143 us
    ppermute x0 -> x1, waiting for transfers between devices: none -> 23.1 us  [per_device(): lax.ppermute(own_slice, 'dp', [(k, (k + shift) % dp_count) for k in range...]
  transfers between devices with their start and end apart: 15 -> 8, of which waited for: 11 -> 7; matrix products, arithmetic and copies ran while one was open for 22% -> 7% of each run, Pallas kernels for 0% -> 8%
where the time goes in v1:
time: 953 us; the launch traced here: 947 us
  waiting for transfers between devices  490 us (51%)
  Pallas kernels  190 us (20%)
  blocking collectives  103 us (11%)
  local copies, waits for them, and re-layouts  98.7 us (10%)
  other arithmetic  38.9 us (4%)
  between operations  22.4 us (2%)
    all_gather x1, waiting for transfers between devices, per_device(): gathered = lax.all_gather(chunk, BOTH, axis=0, tiled=False)  155 us
    unnamed x9, waiting for transfers between devices  143 us
    reduce_scatter x1, waiting for transfers between devices, per_device(): lax.psum_scatter(dense_gradient, BOTH, scatter_dimension=0, tiled=True)  104 us
    gather x1, local copies, waits for them, and re-layouts, per_device(): embed[jnp.clip(group_ids, 0, table_rows - 1)]  42.7 us
    reduce_scatter x1, waiting for transfers between devices, per_device(): rows = lax.psum_scatter(looked, 'dp', scatter_dimension=0, tiled=True)  40.4 us
    psum x1, blocking collectives, per_device(): masked_task_loss, norm_square = lax.psum((own_loss, squared_entries), BOTH)  40 us
    pallas_call x1, Pallas kernels, vocab(): pl.pallas_call(vocab_body, grid=(rows // tile,), in_specs=[pl.BlockSpec((...  37.7 us
    psum x1, blocking collectives, per_device(): counts = lax.psum(jnp.sum(task_hot, 0) * labels, BOTH)  37.7 us
  transfers between devices with their start and end apart: 8, of which 7 were waited for; matrix products, arithmetic and copies ran while one was open for 7% of the time, Pallas kernels for 8%

profile of v1, /device:TPU:0, one launch (start us, length us, event | category | flops | bytes accessed | tf_op | source)
XLA Modules:
  0.0 947.3 jit_solution(13963760744875029650)
XLA Ops:
  8.1 0.7 pad_add_fusion
  8.8 5.2 all-gather.2
  14.2 42.7 %gather_fusion = bf16[2304,768]{1,0:T(8,128)(2,1)} fusion(bf16[25600,768]{1,0:T(8,128)(2,1)} %param.48, s32[3072]{0:T(1024)S(1)} %pad_clamp_fusion), kind=kCustom, calls=%fused_computation | custom fusion | bytes 7087104 | tf_op jit(solution)/shard_map/gather | solution.py:782
  56.9 3.9 broadcast_select_fusion
  62.1 1.0 pad.33
  63.5 0.7 copy-done.6
  64.4 0.6 compare_reduce_fusion.2
  65.1 0.6 compare_reduce_fusion.1
  65.9 0.6 fusion.27
  66.5 0.6 fusion.28
  68.7 0.7 select_bitcast_fusion
  69.4 0.7 select_bitcast_fusion.2
  70.4 0.7 select_bitcast_fusion.1
  71.3 2.4 scatter.35.down_ref
  73.7 2.4 scatter.29.down_ref
  76.1 0.7 concatenate.52.norm_ref
  76.8 0.6 concatenate.50.norm_ref
  77.4 0.6 pad_maximum_fusion.4
  78.1 40.4 %reduce-scatter.5.cloned.1.call-done = bf16[1152,768]{1,0:T(8,128)(2,1)} async-done(((bf16[2304,768]{1,0:T(8,128)(2,1)}), bf16[1152,768]{1,0:T(8,128)(2,1)}) %reduce-scatter.5.cloned.1.call-update) | async-done | bytes 1769488 | tf_op jit(solution)/shard_map/reduce_scatter | solution.py:784
  118.5 2.1 fusion.32
  121.2 2.2 multiply_add_fusion.x_ref
  123.4 154.9 %all-gather.8.cloned.1.call-done = bf16[19456,768]{1,0:T(8,128)(2,1)} async-done(((bf16[608,768]{1,0:T(8,128)(2,1)}), bf16[19456,768]{1,0:T(8,128)(2,1)}) %all-gather.8.cloned.1.call-update) | async-done | bytes 29884432 | tf_op jit(solution)/shard_map/all_gather | solution.py:708
  278.3 1.2 slice_reduce_fusion
  279.5 3.9 fusion.24
  283.5 6.5 fusion.25
  290.9 0.8 copy-done.3
  291.7 10.6 %project.1 = (bf16[1024,2304]{1,0:T(8,128)(2,1)}, bf16[1024,128]{1,0:T(8,128)(2,1)}) custom-call(f32[1024,768]{1,0:T(8,128)} %multiply_add_fusion.x_ref, bf16[768,128]{1,0:T(8,128)(2,1)} %copy-done.8, bf16[2304,768]{1,0:T(8,128)(2,1)} %bitcast.131, bf16[128,2304]{1,0:T(8,128)(2,1)} %copy-done.3, f32[1,2304]{1,0:T(1,128)} %get-tuple-element.206.bias_ref), custom_call_target="tpu_custom_call" | custom-call | tf_op jit(solution)/shard_map/project/pallas_call | solution.py:127
  302.3 1.0 broadcast_in_dim.60.seg_ref
  303.3 20.2 %attend.1 = (bf16[1024,768]{1,0:T(8,128)(2,1)}, f32[6,1,2048]{2,1,0:T(1,128)}) custom-call(bf16[1024,2304]{1,0:T(8,128)(2,1)} %get-tuple-element.131.q_ref.k_ref.v_ref, bf16[1024,2304]{1,0:T(8,128)(2,1)} %get-tuple-element.131.q_ref.k_ref.v_ref, bf16[1024,2304]{1,0:T(8,128)(2,1)} %get-tuple-element.131.q_ref.k_ref.v_ref, ...), custom_call_target="tpu_custom_call" | custom-call | tf_op jit(solution)/shard_map/attend/pallas_call | solution.py:174
  323.5 29.2 %after.1 = (f32[1024,768]{1,0:T(8,128)}, f32[1024,768]{1,0:T(8,128)}, f32[1024,768]{1,0:T(8,128)}, bf16[1024,3072]{1,0:T(8,128)(2,1)}) custom-call(bf16[1024,768]{1,0:T(8,128)(2,1)} %get-tuple-element.132.ctx_ref, f32[1024,768]{1,0:T(8,128)} %multiply_add_fusion.x_ref, bf16[768,768]{1,0:T(8,128)(2,1)} %bitcast.132, bf16[32,608,768]{2,1,0:T(8,128)(2,1)} %bitcast.121, ...), custom_call_target="tpu_custom_call" | custom-call | tf_op jit(solution)/shard_map/after/pallas_call | solution.py:241
  352.7 0.7 broadcast_in_dim.62.place_ref
  353.4 19.9 %last_forward.1 = (bf16[1024,1536]{1,0:T(8,128)(2,1)}, bf16[128,768]{1,0:T(8,128)(2,1)}, bf16[1024,128]{1,0:T(8,128)(2,1)}, f32[6,256]{1,0:T(8,128)}, f32[128,76...) custom-call(f32[1024,768]{1,0:T(8,128)} %get-tuple-element.133.x_ref, ...), custom_call_target="tpu_custom_call" | custom-call | tf_op jit(solution)/shard_map/last_forward/pallas_call | solution.py:357
  373.6 3.3 constant_dynamic-slice_fusion.2
  376.9 1.4 collective-permute-start
  378.4 3.3 copy.68
  381.7 27.6 %all-reduce.11.cloned.1.call-done = f32[51200]{0:T(1024)} async-done(((f32[51200]{0:T(1024)}), f32[51200]{0:T(1024)}) %all-reduce.11.cloned.1.call-update) | async-done | bytes 204816
  409.3 0.8 fusion.26
  410.2 23.1 %collective-permute-done = bf16[1600,768]{1,0:T(8,128)(2,1)} collective-permute-done((bf16[1600,768]{1,0:T(8,128)(2,1)}, bf16[1600,768]{1,0:T(8,128)(2,1)}, u32[]{:S(2)}, u32[]{:S(2)}) %collective-permute-start) | collective-permute-done | bytes 2457632 | tf_op jit(solution)/shard_map/ppermute | solution.py:809
  433.3 4.5 copy.61
  437.7 5.3 pad_maximum_fusion
  443.0 7.5 copy.62.e_ref
  450.5 5.3 fusion.34.et_ref
  455.8 1.7 broadcast_in_dim.64.bias_ref
  457.4 37.7 %vocab.1 = (f32[16,768,128]{2,1,0:T(8,128)}, f32[16,1,128]{2,1,0:T(1,128)}) custom-call(bf16[2048,768]{1,0:T(8,128)(2,1)} %all-gather.6.cloned.1.call-done.u_ref, bf16[3200,768]{1,0:T(8,128)(2,1)} %copy.62.e_ref, bf16[768,3200]{1,0:T(8,128)(2,1)} %fusion.34.et_ref, f32[3200,128]{1,0:T(8,128)} %broadcast_in_dim.64.bias_ref), custom_call_target="tpu_custom_call" | custom-call | tf_op jit(solution)/shard_map/vocab/pallas_call | solution.py:415
  495.2 6.6 copy.64
  501.8 19.6 %all-gather.1 = f32[256,1,128]{2,1,0:T(1,128)S(1)} all-gather(f32[16,1,128]{2,1,0:T(1,128)S(1)} %copy-done.22), channel_id=3, replica_groups=mesh['dp'=2,'fsdp'=16] {'fsdp'}, dimensions={0}, use_global_device_ids=true | all-gather | bytes 139264 | tf_op jit(solution)/shard_map/all_gather | solution.py:844
  521.5 4.9 multiply_convert_fusion
  527.2 37.7 %psum.21 = f32[4]{0:T(128)S(1)} all-reduce(f32[4]{0:T(128)S(1)} %compare_select_fusion.3), channel_id=1, replica_groups=mesh['dp'=2,'fsdp'=16] {'dp','fsdp'}, use_global_device_ids=true, to_apply=%region_0.1 | all-reduce | flops 4 | bytes 32 | tf_op jit(solution)/shard_map/psum | solution.py:829
  565.5 24.3 %reduce-scatter.7.cloned.1.call-done = bf16[1,768,128]{1,2,0:T(8,128)(2,1)} async-done(((bf16[16,768,128]{1,2,0:T(8,128)(2,1)}), bf16[1,768,128]{1,2,0:T(8,128)(2,1)}) %reduce-scatter.7.cloned.1.call-update) | async-done | bytes 196624 | tf_op jit(solution)/shard_map/reduce_scatter | solution.py:847
  589.7 2.5 fusion.1
  592.3 26.1 %last_backward.1 = (f32[1024,768]{1,0:T(8,128)}, f32[768,768]{1,0:T(8,128)}, f32[8,768]{1,0:T(8,128)}, f32[8,768]{1,0:T(8,128)}) custom-call(f32[128,768]{1,0:T(8,128)} %get-tuple-element.171.du_ref, bf16[1024,1536]{1,0:T(8,128)(2,1)} %get-tuple-element.137.kv_ref, bf16[128,768]{1,0:T(8,128)(2,1)} %get-tuple-element.138.q_ref, ...), custom_call_target="tpu_custom_call" | custom-call | tf_op jit(solution)/shard_map/last_backward/pallas_call | solution.py:524
  618.4 21.0 %after_back.1.dctx_ref = bf16[1024,768]{1,0:T(8,128)(2,1)} custom-call(f32[1024,768]{1,0:T(8,128)} %get-tuple-element.147.dout_ref, f32[1024,768]{1,0:T(8,128)} %get-tuple-element.148.one_ref, f32[1024,768]{1,0:T(8,128)} %get-tuple-element.149.two_ref, bf16[1024,3072]{1,0:T(8,128)(2,1)} %get-tuple-element.150.slope_ref, bf16[768,768]{1,0:T(8,128)(2,1)} %bitcast.133, ...), custom_call_target="tpu_custom_call" | custom-call | tf_op jit(solution)/shard_map/after_back/pallas_call | solution.py:565
  639.4 25.4 %attend_back.1 = (f32[8,768]{1,0:T(8,128)}, f32[8,768]{1,0:T(8,128)}) custom-call(bf16[1024,2304]{1,0:T(8,128)(2,1)} %get-tuple-element.131.q_ref.k_ref.v_ref, bf16[1024,2304]{1,0:T(8,128)(2,1)} %get-tuple-element.131.q_ref.k_ref.v_ref, bf16[1024,2304]{1,0:T(8,128)(2,1)} %get-tuple-element.131.q_ref.k_ref.v_ref, bf16[1024,768]{1,0:T(8,128)(2,1)} %after_back.1.dctx_ref, ...), custom_call_target="tpu_custom_call" | custom-call | tf_op jit(solution)/shard_map/attend_back/pallas_call | solution.py:611
  664.9 0.9 maximum_bitcast_fusion
  665.8 0.6 pad_maximum_fusion.1
  666.5 0.7 reduce-scatter.9.cloned.1.call-update
  668.0 1.1 gather_fusion.1
  671.1 114.9 %all-reduce.13.cloned.1.call-done = f32[2,2,8,768]{3,2,1,0:T(8,128)} async-done(((f32[2,2,8,768]{3,2,1,0:T(8,128)}), f32[2,2,8,768]{3,2,1,0:T(8,128)}) %all-reduce.13.cloned.1.call-update) | async-done | bytes 98320
  785.9 1.4 multiply_reduce_fusion.2
  787.4 104.5 %reduce-scatter.9.cloned.1.call-done = f32[24,768]{1,0:T(8,128)} async-done(((f32[768,768]{1,0:T(8,128)}), f32[24,768]{1,0:T(8,128)}) %reduce-scatter.9.cloned.1.call-update) | async-done | bytes 73744 | tf_op jit(solution)/shard_map/reduce_scatter | solution.py:864
  891.8 1.5 multiply_reduce_fusion.1
  894.7 40.0 %all-reduce.7 = (f32[]{:T(128)}, f32[]{:T(128)}) all-reduce(f32[]{:T(128)S(6)} %mul.204, f32[]{:T(128)S(6)} %add.179), channel_id=1, replica_groups=mesh['dp'=2,'fsdp'=16] {'dp','fsdp'}, use_global_device_ids=true, to_apply=%region_13.14 | all-reduce | flops 2 | bytes 16 | tf_op jit(solution)/shard_map/psum | solution.py:869
  935.4 1.5 multiply_subtract_fusion.1
  936.9 1.6 multiply_subtract_fusion
  (142 shorter events, 7.4 us)
Async XLA Ops:
  8.0 110.5 %copy-start = (bf16[128,768]{1,0:T(8,128)(2,1)S(1)}, bf16[128,768]{1,0:T(8,128)(2,1)}, u32[]{:S(2)}) copy-start(bf16[128,768]{1,0:T(8,128)(2,1)} %param.49) | copy-start | bytes 589828
  8.0 110.4 %reduce-scatter.5.cloned.1.call-start = ((), (), s32[]{:S(2)}) async-start(), calls=%async_computation.3 | async-start | bytes 5308416 | tf_op jit(solution)/shard_map/reduce_scatter | solution.py:784
  60.8 0.7 copy-start.17
  60.8 1.0 copy-start.11
  60.8 1.1 copy-start.12
  60.8 1.1 copy-start.13
  60.8 1.1 copy-start.16
  60.8 1.2 copy-start.9
  60.9 2.3 copy-start.29
  60.9 4.9 copy-start.21
  60.9 5.0 copy-start.19
  60.9 6.2 copy-start.31
  60.9 7.4 copy-start.20
  60.9 217.4 %all-gather.8.cloned.1.call-start = ((), (), s32[]{:S(2)}) async-start(), calls=%async_computation.7 | async-start | bytes 30818304 | tf_op jit(solution)/shard_map/all_gather | solution.py:708
  62.0 9.2 copy-start.27
  62.1 9.2 copy-start.28
  63.1 346.2 %all-reduce.11.cloned.1.call-start = ((), (), s32[]{:S(2)}) async-start(), calls=%async_computation.8 | async-start | bytes 409600
  63.5 0.7 copy-start.6
  64.2 391.5 %all-gather.6.cloned.1.call-start = ((), (), s32[]{:S(2)}) async-start(), calls=%async_computation.4 | async-start | bytes 3342336 | tf_op jit(solution)/shard_map/all_gather | solution.py:841
  65.8 236.5 %copy-start.18 = (f32[1,1024]{1,0:T(1,128)}, f32[1,1024]{1,0:T(1,128)S(1)}, u32[]{:S(2)}) copy-start(f32[1,1024]{1,0:T(1,128)S(1)} %convert_element_type.48.seg_row_ref) | copy-start | bytes 12292
  73.7 47.4 %copy-start.4 = (bf16[768,128]{1,0:T(8,128)(2,1)}, bf16[768,128]{1,0:T(8,128)(2,1)S(1)}, u32[]{:S(2)}) copy-start(bf16[768,128]{1,0:T(8,128)(2,1)S(1)} %scatter.35.down_ref) | copy-start | bytes 589828
  76.1 45.0 %copy-start.8 = (bf16[768,128]{1,0:T(8,128)(2,1)}, bf16[768,128]{1,0:T(8,128)(2,1)S(1)}, u32[]{:S(2)}) copy-start(bf16[768,128]{1,0:T(8,128)(2,1)S(1)} %scatter.29.down_ref) | copy-start | bytes 589828
  290.9 0.8 copy-start.3
  290.9 11.4 %copy-start.2 = (bf16[128,2304]{1,0:T(8,128)(2,1)}, bf16[128,2304]{1,0:T(8,128)(2,1)S(1)}, u32[]{:S(2)}) copy-start(bf16[128,2304]{1,0:T(8,128)(2,1)S(1)} %get-tuple-element.185.adapt_ref) | copy-start | bytes 1769476
  323.5 29.2 %copy-start.30 = (s32[1,128]{1,0:T(1,128)S(1)}, s32[1,128]{1,0:T(1,128)}, u32[]{:S(2)}) copy-start(s32[1,128]{1,0:T(1,128)} %place_row_ref.3) | copy-start | bytes 1540
  373.4 216.4 %reduce-scatter.7.cloned.1.call-start = ((), (), s32[]{:S(2)}) async-start(), calls=%async_computation.5 | async-start | bytes 3342336 | tf_op jit(solution)/shard_map/reduce_scatter | solution.py:847
  376.9 56.3 %collective-permute-start = (bf16[1600,768]{1,0:T(8,128)(2,1)}, bf16[1600,768]{1,0:T(8,128)(2,1)}, u32[]{:S(2)}, u32[]{:S(2)}) collective-permute-start(bf16[1600,768]{1,0:T(8,128)(2,1)} %constant_dynamic-slice_fusion.2), channel_id=1, source_target_pairs={{0,16},{16,0},{1,17},{17,1},{2,18},{18,2},{3,19},{19,3},{4,20},{20... | collective-permute-start | bytes 7372808 | tf_op jit(solution)/shard_map/ppermute | solution.py:809
  495.2 6.6 copy-start.22
  526.4 38.4 %copy-start.33 = (f32[4]{0:T(128)S(1)}, f32[4]{0:T(128)}, u32[]{:S(2)}) copy-start(f32[4]{0:T(128)} %param.46) | copy-start | bytes 52
  526.4 63.3 %copy-start.7 = (bf16[128,768]{1,0:T(8,128)(2,1)S(1)}, bf16[128,768]{1,0:T(8,128)(2,1)}, u32[]{:S(2)}) copy-start(bf16[128,768]{1,0:T(8,128)(2,1)} %get-tuple-element.134) | copy-start | bytes 589828
  526.4 259.5 %all-reduce.13.cloned.1.call-start = ((), (), s32[]{:S(2)}) async-start(), calls=%async_computation.9 | async-start | bytes 196608
  639.4 26.4 %copy-start.23 = (f32[8,768]{1,0:T(8,128)S(1)}, f32[8,768]{1,0:T(8,128)}, u32[]{:S(2)}) copy-start(f32[8,768]{1,0:T(8,128)} %get-tuple-element.155) | copy-start | bytes 73732
  639.4 26.4 %copy-start.24 = (f32[8,768]{1,0:T(8,128)S(1)}, f32[8,768]{1,0:T(8,128)}, u32[]{:S(2)}) copy-start(f32[8,768]{1,0:T(8,128)} %get-tuple-element.156) | copy-start | bytes 73732
  639.4 28.6 %copy-start.32 = (s32[1,128]{1,0:T(1,128)S(1)}, s32[1,128]{1,0:T(1,128)}, u32[]{:S(2)}) copy-start(s32[1,128]{1,0:T(1,128)} %param.44) | copy-start | bytes 1540
  639.4 299.1 %copy-start.1 = (bf16[128,768]{1,0:T(8,128)(2,1)S(1)}, bf16[128,768]{1,0:T(8,128)(2,1)}, u32[]{:S(2)}) copy-start(bf16[128,768]{1,0:T(8,128)(2,1)} %param.49) | copy-start | bytes 589828
  664.8 3.1 copy-start.5
  664.8 270.6 %copy-start.25 = (f32[2,2,8,24]{3,2,1,0:T(8,128)S(1)}, f32[2,2,8,24]{3,2,1,0:T(8,128)}, u32[]{:S(2)}) copy-start(f32[2,2,8,24]{3,2,1,0:T(8,128)} %param.62) | copy-start | bytes 9220
  664.9 270.6 %copy-start.26 = (f32[2,2,8,24]{3,2,1,0:T(8,128)S(1)}, f32[2,2,8,24]{3,2,1,0:T(8,128)}, u32[]{:S(2)}) copy-start(f32[2,2,8,24]{3,2,1,0:T(8,128)} %param.61) | copy-start | bytes 9220
  664.9 272.0 %copy-start.10 = (f32[24,768]{1,0:T(8,128)S(1)}, f32[24,768]{1,0:T(8,128)}, u32[]{:S(2)}) copy-start(f32[24,768]{1,0:T(8,128)} %param.63) | copy-start | bytes 221188
  664.9 272.0 %copy-start.14 = (f32[24,768]{1,0:T(8,128)S(1)}, f32[24,768]{1,0:T(8,128)}, u32[]{:S(2)}) copy-start(f32[24,768]{1,0:T(8,128)} %param.65) | copy-start | bytes 221188
  664.9 272.0 %copy-start.15 = (f32[24,768]{1,0:T(8,128)S(1)}, f32[24,768]{1,0:T(8,128)}, u32[]{:S(2)}) copy-start(f32[24,768]{1,0:T(8,128)} %param.64) | copy-start | bytes 221188
  666.5 225.4 %reduce-scatter.9.cloned.1.call-start = ((), (), s32[]{:S(2)}) async-start(), calls=%async_computation.6 | async-start | bytes 2433024 | tf_op jit(solution)/shard_map/reduce_scatter | solution.py:864
Sparse Core Ops, SparseCore 0:
  61.0 57.4 reduce-scatter.4
  373.5 43.6 all-gather.5
  526.5 63.1 reduce-scatter.6
Sparse Core Ops, SparseCore 1:
  64.7 213.5 all-gather.7
  284.6 124.6 all-reduce.10
  666.6 119.3 all-reduce.12
  792.1 99.7 reduce-scatter.8

commit v2 on v1

--- a/solution.py
+++ b/solution.py
@@ -543,6 +543,32 @@
     )(du, *saved, place_col, place_row, seg_wide, down, w, adapt, wo, up[0], dn[0], norms, hb)
 
 
+def after_back_sum_body(shards, *refs):
+    *plain, parts, dctx_ref, sum_ref, got, sends, gets = refs
+    step, last = pl.program_id(0), pl.num_programs(0) - 1
+    me = number_of(position())
+
+    @pl.when(step == 0)
+    def _():
+        greet_all(shards)
+        got[me] = parts[me]
+
+    @pl.when(step == jnp.minimum(1, last))
+    def _():
+        await_all(shards)
+        spread(lambda peer: parts.at[peer], got, sends, gets, me, shards)
+
+    after_back_body(*plain, dctx_ref)
+
+    @pl.when(step == last)
+    def _():
+        collect(lambda peer: parts.at[peer], got, sends, gets, me, shards)
+        total = got[0].astype(F32)
+        for k in range(1, shards):
+            total = total + got[k].astype(F32)
+        sum_ref[...] = total
+
+
 def after_back_body(dout_ref, one_ref, two_ref, slope_ref, wo_ref, up_ref, down_ref, norm_ref, dctx_ref):
     dtwo = norm_back(two_ref[...], norm_ref[2:3, :], dout_ref[...])
     low = dtwo.astype(BF)
@@ -556,6 +582,27 @@
         dmiddle = dmiddle + mm(dgate, rows_of(up_ref, start, step))
     done = norm_back(one_ref[...], norm_ref[0:1, :], dmiddle)
     dctx_ref[...] = mm(done.astype(BF), wo_ref[...]).astype(BF)
+
+
+def after_back_sum(dout, one, two, slope, wo, up, down, norms, parts, shards):
+    rows, width = dout.shape
+    tile = split_of(rows, 256, 16)
+    row = lambda n: pl.BlockSpec((tile, n), lambda i: (i, 0))
+    sems = pltpu.SemaphoreType.DMA
+    return pl.pallas_call(
+        functools.partial(after_back_sum_body, shards),
+        grid=(rows // tile,),
+        in_specs=[row(width), row(width), row(width), row(slope.shape[1]), full(wo.shape)]
+        + [slab_spec(up), slab_spec(down), full(norms.shape), full(parts.shape)],
+        out_specs=[row(width), full(parts.shape[1:])],
+        out_shape=[
+            jax.ShapeDtypeStruct((rows, width), BF),
+            jax.ShapeDtypeStruct(parts.shape[1:], F32),
+        ],
+        scratch_shapes=[pltpu.VMEM(parts.shape, BF), sems((shards,)), sems((shards,))],
+        compiler_params=params(collective_id=3, has_side_effects=True),
+        name="after_back_sum",
+    )(dout, one, two, slope, wo, up[0], down[0], norms, parts)
 
 
 def after_back(dout, one, two, slope, wo, up, down, norms):
@@ -627,6 +674,307 @@
         compiler_params=params(),
         name="attend_back",
     )(qkv, qkv, qkv, dctx, logs, seg_wide, seg_row, mid)
+
+
+MESH = pl.DeviceIdType.MESH
+LINES = {"x": 2, "z": 4, "y": 2}
+
+
+def position():
+    dp, fsdp = lax.axis_index("dp"), lax.axis_index("fsdp")
+    return {"x": dp, "z": fsdp // 4, "y": (fsdp // 2) % 2, "c": fsdp % 2}
+
+
+def device_of(place):
+    return (place["x"], (place["z"] * 2 + place["y"]) * 2 + place["c"])
+
+
+def number_of(place):
+    return place["x"] * 16 + (place["z"] * 2 + place["y"]) * 2 + place["c"]
+
+
+def rank_device(number):
+    return (number // 16, number % 16)
+
+
+def greet_all(shards):
+    barrier = pltpu.get_barrier_semaphore()
+    me = lax.axis_index("dp") * 16 + lax.axis_index("fsdp")
+
+    @pl.loop(1, shards)
+    def _(k):
+        pl.semaphore_signal(
+            barrier, inc=1, device_id=rank_device((me + k) % shards), device_id_type=MESH
+        )
+
+
+def await_all(shards):
+    pl.semaphore_wait(pltpu.get_barrier_semaphore(), shards - 1)
+
+
+def direct_copy(source, target, sends, receives, me, k, shards):
+    return pltpu.make_async_remote_copy(
+        src_ref=source,
+        dst_ref=target,
+        send_sem=sends.at[k],
+        recv_sem=receives.at[me],
+        device_id=rank_device((me + k) % shards),
+        device_id_type=MESH,
+    )
+
+
+def spread(piece_of, buffer, sends, receives, me, shards):
+    @pl.loop(1, shards)
+    def _(k):
+        direct_copy(piece_of((me + k) % shards), buffer.at[me], sends, receives, me, k, shards).start()
+
+
+def collect(piece_of, buffer, sends, receives, me, shards):
+    @pl.loop(1, shards)
+    def _(k):
+        source = (me + shards - k) % shards
+        direct_copy(buffer.at[source], buffer.at[source], sends, receives, source, k, shards).wait_recv()
+
+    @pl.loop(1, shards)
+    def _(k):
+        direct_copy(piece_of((me + k) % shards), buffer.at[me], sends, receives, me, k, shards).wait_send()
+
+
+def relative_places(order):
+    places = [
+        {"x": dx, "z": dz, "y": dy} for dx in (0, 1) for dz in range(-3, 4) for dy in (0, 1)
+    ]
+    return sorted(places, key=lambda p: (abs(p["x"]) + abs(p["z"]) + abs(p["y"]), [abs(p[a]) for a in order]))
+
+
+class Gather:
+    def __init__(self, chunk, full_buffer, start, rows, order, sends, receives, hands, hands_got):
+        self.chunk, self.full, self.order = chunk, full_buffer, order
+        self.part = pl.ds(start, rows)
+        self.sends, self.receives, self.hands, self.hands_got = sends, receives, hands, hands_got
+        self.here = position()
+        self.items = relative_places(order)
+        self.pending = []
+
+    def origin(self, item):
+        here = self.here
+        return {"x": (here["x"] + item["x"]) % 2, "z": here["z"] - item["z"], "y": (here["y"] + item["y"]) % 2, "c": here["c"]}
+
+    def key(self, place):
+        return (place["x"] * 4 + place["z"]) * 2 + place["y"]
+
+    def outward(self, item):
+        deepest = max([k for k, axis in enumerate(self.order) if item[axis]], default=-1)
+        ways = []
+        if deepest >= 0 and self.order[deepest] == "z":
+            ways.append(("z", 1 if item["z"] > 0 else -1))
+        for axis in self.order[deepest + 1 :]:
+            ways += [("z", 1), ("z", -1)] if axis == "z" else [(axis, 1)]
+        return ways
+
+    def copy(self, index, way, slot, item):
+        here = self.here
+        place = self.origin(item)
+        number, key = number_of(place), self.key(place)
+        mine = not any(item.values())
+        source = self.chunk.at[self.part, :] if mine else self.full.at[number, self.part, :]
+        if way is None:
+            target = dict(here, c=1 - here["c"])
+            sends, receives = self.hands.at[index], self.hands_got.at[key]
+        else:
+            axis, step = way
+            target = dict(here)
+            target[axis] = here["z"] + step if axis == "z" else 1 - here[axis]
+            sends, receives = self.sends.at[index * 4 + slot], self.receives.at[key]
+        return pltpu.make_async_remote_copy(
+            src_ref=source,
+            dst_ref=self.full.at[number, self.part, :],
+            send_sem=sends,
+            recv_sem=receives,
+            device_id=device_of(target),
+            device_id_type=MESH,
+        )
+
+    def valid(self, item):
+        z = self.here["z"] - item["z"]
+        return (z >= 0) & (z <= 3)
+
+    def step(self, index):
+        item = self.items[index]
+
+        @pl.when(self.valid(item))
+        def _():
+            if any(item.values()):
+                self.arrived(index, item)
+            for slot, way in enumerate(self.outward(item)):
+                self.when_way(way, lambda way=way, slot=slot: self.copy(index, way, slot, item).start())
+            self.copy(index, None, 0, item).start()
+
+    def when_way(self, way, act):
+        axis, step = way
+        if axis == "z":
+            z = self.here["z"] + step
+            pl.when((z >= 0) & (z <= 3))(act)
+        else:
+            act()
+
+    def arrived(self, index, item):
+        place = self.origin(item)
+        spot = self.full.at[number_of(place), self.part, :]
+        pltpu.make_async_remote_copy(
+            src_ref=spot,
+            dst_ref=spot,
+            send_sem=self.sends.at[index * 4],
+            recv_sem=self.receives.at[self.key(place)],
+            device_id=device_of(dict(self.here, c=1 - self.here["c"])),
+            device_id_type=MESH,
+        ).wait_recv()
+
+    def finish(self):
+        for index, item in enumerate(self.items):
+
+            @pl.when(self.valid(item))
+            def _(index=index, item=item):
+                for slot, way in enumerate(self.outward(item)):
+                    self.when_way(way, lambda way=way, slot=slot: self.copy(index, way, slot, item).wait_send())
+                self.copy(index, None, 0, item).wait_send()
+                place = dict(self.origin(item), c=1 - self.here["c"])
+                spot = self.full.at[number_of(place), self.part, :]
+                pltpu.make_async_remote_copy(
+                    src_ref=spot,
+                    dst_ref=spot,
+                    send_sem=self.hands.at[index],
+                    recv_sem=self.hands_got.at[self.key(place)],
+                    device_id=device_of(dict(self.here, c=1 - self.here["c"])),
+                    device_id_type=MESH,
+                ).wait_recv()
+
+
+ITEMS = 28
+
+
+def start_body(
+    streams, shards, chunk, rows, note, bias, full_chunk, got, notes, biases,
+    sends, receives, hands, hands_got, row_sems, note_sends, note_gets, bias_sends, bias_gets, own_sems,
+):
+    here = position()
+    me = number_of(here)
+    greet_all(shards)
+    own = pltpu.make_async_copy(chunk, full_chunk.at[me], own_sems.at[0])
+    own.start()
+    own_note = pltpu.make_async_copy(note, notes.at[me], own_sems.at[1])
+    own_note.start()
+    own_bias = pltpu.make_async_copy(bias, biases.at[me], own_sems.at[2])
+    own_bias.start()
+    await_all(shards)
+    gathers = [
+        Gather(
+            chunk, full_chunk, start, size, order, sends.at[k], receives.at[k], hands.at[k], hands_got.at[k]
+        )
+        for k, (start, size, order) in enumerate(streams)
+    ]
+    across = pltpu.make_async_remote_copy(
+        src_ref=rows,
+        dst_ref=got,
+        send_sem=row_sems.at[0],
+        recv_sem=row_sems.at[1],
+        device_id=device_of(dict(here, x=1 - here["x"])),
+        device_id_type=MESH,
+    )
+    for gather in gathers:
+        gather.step(0)
+    spread(lambda peer: note, notes, note_sends, note_gets, me, shards)
+    spread(lambda peer: bias, biases, bias_sends, bias_gets, me, shards)
+    across.start()
+    for index in range(1, ITEMS):
+        for gather in gathers:
+            gather.step(index)
+    for gather in gathers:
+        gather.finish()
+    collect(lambda peer: note, notes, note_sends, note_gets, me, shards)
+    collect(lambda peer: bias, biases, bias_sends, bias_gets, me, shards)
+    across.wait()
+    own.wait()
+    own_note.wait()
+    own_bias.wait()
+
+
+def start_exchange(chunk, rows, note, bias, shards):
+    anywhere = pl.BlockSpec(memory_space=pl.ANY)
+    cut = (chunk.shape[0] * 5 // 6 + 15) // 16 * 16
+    streams = ((0, cut, "xzy"), (cut, chunk.shape[0] - cut, "xyz"))
+    shape = jax.ShapeDtypeStruct
+    sems = pltpu.SemaphoreType.DMA
+    return pl.pallas_call(
+        functools.partial(start_body, streams, shards),
+        in_specs=[anywhere] * 4,
+        out_specs=[anywhere] * 4,
+        out_shape=[
+            shape((shards, *chunk.shape), chunk.dtype),
+            shape(rows.shape, rows.dtype),
+            shape((shards, *note.shape), note.dtype),
+            shape((shards, *bias.shape), bias.dtype),
+        ],
+        scratch_shapes=[
+            sems((2, 4 * ITEMS)),
+            sems((2, 16)),
+            sems((2, ITEMS)),
+            sems((2, 16)),
+            sems((2,)),
+            sems((shards,)),
+            sems((shards,)),
+            sems((shards,)),
+            sems((shards,)),
+            sems((3,)),
+        ],
+        compiler_params=params(collective_id=1, has_side_effects=True),
+        name="start_exchange",
+    )(chunk, rows, note, bias)
+
+
+def tail_body(shards, parts, dense, loss, total_ref, sums_ref, got, note, notes, send_a, get_a, send_b, get_b):
+    me = number_of(position())
+    greet_all(shards)
+    got[me] = parts[me]
+    await_all(shards)
+    spread(lambda peer: parts.at[peer], got, send_a, get_a, me, shards)
+    dense_square = jnp.sum(dense[...] * dense[...], keepdims=True)
+    collect(lambda peer: parts.at[peer], got, send_a, get_a, me, shards)
+    total = got[0]
+    for k in range(1, shards):
+        total = total + got[k]
+    total_ref[...] = total
+    square = dense_square + jnp.sum(total * total, keepdims=True)
+    row = lax.broadcasted_iota(jnp.int32, note.shape, 0)
+    note[...] = jnp.where(row == 0, loss[...], jnp.where(row == 1, square, 0.0))
+    notes[me] = note[...]
+    spread(lambda peer: note, notes, send_b, get_b, me, shards)
+    collect(lambda peer: note, notes, send_b, get_b, me, shards)
+    total = notes[0]
+    for k in range(1, shards):
+        total = total + notes[k]
+    sums_ref[...] = total
+
+
+def tail(parts, dense, loss, shards):
+    whole = pl.BlockSpec(memory_space=pltpu.VMEM)
+    block = parts.shape[1:]
+    shape = jax.ShapeDtypeStruct
+    sems = pltpu.SemaphoreType.DMA
+    return pl.pallas_call(
+        functools.partial(tail_body, shards),
+        in_specs=[whole] * 3,
+        out_specs=[whole] * 2,
+        out_shape=[shape(block, F32), shape((8, 128), F32)],
+        scratch_shapes=[
+            pltpu.VMEM(parts.shape, F32),
+            pltpu.VMEM((8, 128), F32),
+            pltpu.VMEM((shards, 8, 128), F32),
+        ]
+        + [sems((shards,))] * 4,
+        compiler_params=params(collective_id=2, has_side_effects=True),
+        name="tail",
+    )(parts, dense, loss)
 
 
 def seg_positions(segments):
@@ -695,35 +1043,80 @@
     ff_rows = feedforward_up.shape[2]
     head_rows = head_projection.shape[0]
 
-    pieces = []
-    for layer in range(layers):
-        pieces += [feedforward_up[layer].T, feedforward_down[layer]]
-    for layer in range(layers):
-        pieces += [attention_in_weight[layer].T, attention_out_weight[layer].T]
-    pieces += [head_projection.astype(BF)]
+    grouped = (lax.axis_size("dp"), lax.axis_size("fsdp")) == (2, 16)
+    chunks = [
+        [
+            feedforward_up[layer].T,
+            feedforward_down[layer],
+            attention_in_weight[layer].T,
+            attention_out_weight[layer].T,
+        ]
+        for layer in range(layers)
+    ]
     ups = adapter_up_matrix.astype(BF).reshape(-1)
     up_rows = -(-ups.size // hidden)
-    pieces += [jnp.pad(ups, (0, up_rows * hidden - ups.size)).reshape(up_rows, hidden)]
-    chunk = pad_rows(jnp.concatenate(pieces, 0), 32)
-    gathered = lax.all_gather(chunk, BOTH, axis=0, tiled=False)
+    chunks[0] += [
+        head_projection.astype(BF),
+        jnp.pad(ups, (0, up_rows * hidden - ups.size)).reshape(up_rows, hidden),
+    ]
+    chunks = [pad_rows(jnp.concatenate(pieces, 0), 32) for pieces in chunks]
+
+    table_rows = embed.shape[0]
+    wanted = jnp.concatenate([input_token_index[0], label_target_token[0]])
+    dp_count = lax.axis_size("dp")
+    group_ids = lax.all_gather(wanted, "dp", axis=0, tiled=False) - dp_index * table_rows
+    later_full = [lax.all_gather(chunk, BOTH, axis=0, tiled=False) for chunk in chunks[1:]]
+
+    def look(ids):
+        inside = (ids >= 0) & (ids < table_rows)
+        found = embed[jnp.clip(ids, 0, table_rows - 1)]
+        return jnp.where(inside[:, None], found, jnp.zeros((), BF)), inside
+
+    task_range = jnp.arange(TASKS, dtype=jnp.int32)
+    slice_rows = vocabulary_bias.shape[0]
+    if grouped:
+        pair_ids = jnp.concatenate(
+            [
+                lax.dynamic_index_in_dim(group_ids, 1 - dp_index, 0, keepdims=False),
+                lax.dynamic_index_in_dim(group_ids, dp_index, 0, keepdims=False),
+            ]
+        )
+        looked, inside = look(pair_ids)
+        note = jnp.broadcast_to(sequence_task_index.astype(F32)[:, None], (8, 128))
+        bias_rows = -(-slice_rows // 1024) * 8
+        bias_block = jnp.pad(vocabulary_bias, (0, bias_rows * 128 - slice_rows)).reshape(bias_rows, 128)
+        first_full, got, notes, biases = start_exchange(
+            chunks[0], looked[: wanted.size], note, bias_block, shards
+        )
+        rows = jnp.where(inside[wanted.size :, None], looked[wanted.size :], got)
+        every_task = notes[:, 0, 0].astype(jnp.int32)
+        all_bias = biases.reshape(shards, -1)[:, :slice_rows].reshape(-1)
+    else:
+        looked, inside = look(group_ids.reshape(-1))
+        first_full = lax.all_gather(chunks[0], BOTH, axis=0, tiled=False)
+        rows = lax.psum_scatter(looked, "dp", scatter_dimension=0, tiled=True)
+        every_task = lax.all_gather(sequence_task_index, BOTH, axis=0, tiled=True)
+        all_bias = lax.all_gather(vocabulary_bias, BOTH, axis=0, tiled=True)
+    counts = labels * jnp.sum((every_task[:, None] == task_range[None, :]).astype(F32), 0)
+    task_hot = (sequence_task_index[:, None] == task_range[None, :]).astype(F32)
+    row_weight = jnp.sum(task_hot[0] * (task_loss_weight / jnp.maximum(counts, 1.0)))
+
+    gathered = [first_full, *later_full]
     slabs = [
-        (
-            slab_of(gathered, 2 * layer * ff_rows, ff_rows),
-            slab_of(gathered, (2 * layer + 1) * ff_rows, ff_rows),
-        )
+        (slab_of(gathered[layer], 0, ff_rows), slab_of(gathered[layer], ff_rows, ff_rows))
         for layer in range(layers)
     ]
-    at = 2 * layers * ff_rows
     in_weights, out_weights = [], []
     for layer in range(layers):
-        in_weights.append(gathered[:, at : at + qkv_rows].reshape(-1, hidden))
+        at = 2 * ff_rows
+        in_weights.append(gathered[layer][:, at : at + qkv_rows].reshape(-1, hidden))
         at += qkv_rows
-        out_weights.append(gathered[:, at : at + out_rows].reshape(-1, hidden))
-        at += out_rows
-    head_full = gathered[:, at : at + head_rows].reshape(-1, hidden)
+        out_weights.append(gathered[layer][:, at : at + out_rows].reshape(-1, hidden))
+    at = 2 * ff_rows + qkv_rows + out_rows
+    head_full = first_full[:, at : at + head_rows].reshape(-1, hidden)
     at += head_rows
     ups_full = (
-        gathered[:, at : at + up_rows]
+        first_full[:, at : at + up_rows]
         .reshape(shards, -1)[:, : ups.size]
         .reshape(shards, layers, 2, rank, up_part)
         .transpose(1, 2, 3, 0, 4)
@@ -774,14 +1167,6 @@
         for layer in range(layers)
     ]
 
-    table_rows = embed.shape[0]
-    wanted = jnp.concatenate([input_token_index[0], label_target_token[0]])
-    group_ids = lax.all_gather(wanted, "dp", axis=0, tiled=True) - dp_index * table_rows
-    inside = (group_ids >= 0) & (group_ids < table_rows)
-    looked = jnp.where(
-        inside[:, None], embed[jnp.clip(group_ids, 0, table_rows - 1)], jnp.zeros((), BF)
-    )
-    rows = lax.psum_scatter(looked, "dp", scatter_dimension=0, tiled=True)
     target_rows = rows[tokens:].astype(F32)
     segments = sentence_numbers[0]
     place_hot = (
@@ -800,34 +1185,18 @@
     place_row = label_positions
     place_col = jnp.broadcast_to(label_positions.reshape(labels, 1), (labels, 128))
 
-    slice_rows = vocabulary_bias.shape[0]
     own_slice = lax.dynamic_slice_in_dim(embed, fsdp_index * slice_rows, slice_rows, 0)
-    parts = [own_slice]
-    dp_count = lax.axis_size("dp")
-    for shift in range(1, dp_count):
-        parts.append(
-            lax.ppermute(own_slice, "dp", [(k, (k + shift) % dp_count) for k in range(dp_count)])
-        )
-    own_vocab = jnp.concatenate(parts, 0)
-    all_bias = lax.all_gather(vocabulary_bias, BOTH, axis=0, tiled=True)
+    own_vocab = lax.all_gather(own_slice, "dp", axis=0, tiled=True)
     own_bias = jnp.concatenate(
         [
             lax.dynamic_slice_in_dim(
-                all_bias,
-                ((dp_index - shift) % dp_count) * table_rows + fsdp_index * slice_rows,
-                slice_rows,
-                0,
+                all_bias, part * table_rows + fsdp_index * slice_rows, slice_rows, 0
             )
-            for shift in range(dp_count)
+            for part in range(dp_count)
         ]
     )
     bias_wide = jnp.broadcast_to(own_bias[:, None], (own_bias.shape[0], 128))
     target_bias = all_bias[label_target_token[0]]
-
-    task_range = jnp.arange(TASKS, dtype=jnp.int32)
-    task_hot = (sequence_task_index[:, None] == task_range[None, :]).astype(F32)
-    counts = lax.psum(jnp.sum(task_hot, 0) * labels, BOTH)
-    row_weight = jnp.sum(task_hot[0] * (task_loss_weight / jnp.maximum(counts, 1.0)))
 
     qkv, mid = project(hidden_rows, downs[0], in_weights[0], adapters[0], bias_of[0][0])
     context, logs = attend(qkv, seg_wide, seg_row)
@@ -854,19 +1223,32 @@
         feat_grad, saved, place_col, place_row, seg_wide, downs[1], in_weights[1], adapters[1],
         out_weights[1], *slabs[1], norms_of[1], head_full, rank,
     )
-    dctx = after_back(hidden_grad, one, two, slope, out_weights[0], *slabs[0], norms_of[0])
+    back = (hidden_grad, one, two, slope, out_weights[0], *slabs[0], norms_of[0])
+    if grouped:
+        block = -(-head_rows * hidden // 2048) * 2048
+        dense_parts = jnp.pad(
+            dense_gradient.reshape(shards, -1).astype(BF), ((0, 0), (0, block - head_rows * hidden))
+        ).reshape(shards, 16, block // 16)
+        dctx, dense_sum = after_back_sum(*back, dense_parts, shards)
+        dense_portion = dense_sum.reshape(-1)[: head_rows * hidden].reshape(head_rows, hidden)
+    else:
+        dctx = after_back(*back)
+        dense_portion = lax.psum_scatter(dense_gradient, BOTH, scatter_dimension=0, tiled=True)
     gq_first, gv_first = attend_back(qkv, dctx, logs, seg_wide, seg_row, mid, rank)
-    adapter_gradient = jnp.stack(
-        [jnp.stack([gq_first, gv_first]), jnp.stack([gq_last, gv_last])]
-    )
-    adapter_portion, dense_portion = (
-        lax.psum_scatter(adapter_gradient, BOTH, scatter_dimension=3, tiled=True),
-        lax.psum_scatter(dense_gradient, BOTH, scatter_dimension=0, tiled=True),
-    )
-    squared_entries = jnp.sum(adapter_portion * adapter_portion) + jnp.sum(
-        dense_portion * dense_portion
-    )
-    masked_task_loss, norm_square = lax.psum((own_loss, squared_entries), BOTH)
+    adapter_gradient = jnp.stack([gq_first, gv_first, gq_last, gv_last]).reshape(layers, 2, rank, hidden)
+    if grouped:
+        parts = adapter_gradient.reshape(-1, shards, up_part).transpose(1, 0, 2).reshape(shards, -1)
+        block = -(-ups.size // 1024) * 1024
+        parts = jnp.pad(parts, ((0, 0), (0, block - ups.size))).reshape(shards, block // 128, 128)
+        own_parts, sums = tail(parts, dense_portion, jnp.broadcast_to(own_loss, (8, 128)), shards)
+        adapter_portion = own_parts.reshape(-1)[: ups.size].reshape(adapter_up_matrix.shape)
+        masked_task_loss, norm_square = sums[0, 0], sums[1, 0]
+    else:
+        adapter_portion = lax.psum_scatter(adapter_gradient, BOTH, scatter_dimension=3, tiled=True)
+        squared_entries = jnp.sum(adapter_portion * adapter_portion) + jnp.sum(
+            dense_portion * dense_portion
+        )
+        masked_task_loss, norm_square = lax.psum((own_loss, squared_entries), BOTH)
     gradient_norm = jnp.sqrt(norm_square)
     scale_factor = jnp.minimum(1.0, clip_limit / (gradient_norm + 1e-06))
     step_as_real = optimizer_step_count[0].astype(F32)

time: 953 us -> 639 us (0.67)
  waiting for transfers between devices: 490 us -> 96.1 us
  Pallas kernels: 190 us -> 346 us
  blocking collectives: 103 us -> 24.8 us
  local copies, waits for them, and re-layouts: 98.7 us -> 118 us
  other arithmetic: 38.9 us -> 28.8 us
    pallas_call x1 -> x3, Pallas kernels: 21 us -> 177 us  [the longest x1 121 us: start_exchange(): pl.pallas_call(functools.partial(start_body, streams, shards), in_specs=[...]
    all_gather x1 -> x2, waiting for transfers between devices: 155 us -> 0.02 us  [the longest x1 0.02 us: per_device(): lax.all_gather(chunk, BOTH, axis=0, tiled=False)]
    reduce_scatter x2 -> x0, waiting for transfers between devices: 145 us -> none  [the longest x1 104 us: per_device(): lax.psum_scatter(dense_gradient, BOTH, scatter_dimension=0, tiled=True)]
    unnamed x9 -> x4, waiting for transfers between devices: 143 us -> 0.07 us
    psum x2 -> x0, blocking collectives: 77.7 us -> none  [the longest x1 40 us: per_device(): masked_task_loss, norm_square = lax.psum((own_loss, squared_entries), BOTH)]
    all_gather x1, waiting for transfers between devices: 0.01 us -> 36.6 us  [per_device(): every = lax.all_gather(features, 'fsdp', axis=0, tiled=True)]
    reduce_scatter x1, waiting for transfers between devices: 24.3 us -> 59.4 us  [per_device(): lax.psum_scatter(scaled, 'fsdp', scatter_dimension=0, tiled=True)[0]]
    ppermute x1 -> x0, waiting for transfers between devices: 23.1 us -> none  [per_device(): lax.ppermute(own_slice, 'dp', [(k, (k + shift) % dp_count) for k in range...]
  transfers between devices with their start and end apart: 8 -> 4, of which waited for: 7 -> 2; matrix products, arithmetic and copies ran while one was open for 7% -> 18% of each run, Pallas kernels for 8% -> 32%
where the time goes in v2:
time: 639 us; the launch traced here: 634 us
  Pallas kernels  346 us (54%)
  local copies, waits for them, and re-layouts  118 us (18%)
  waiting for transfers between devices  96.1 us (15%)
  other arithmetic  28.8 us (5%)
  blocking collectives  24.8 us (4%)
  between operations  19.5 us (3%)
    pallas_call x1, Pallas kernels, start_exchange(): pl.pallas_call(functools.partial(start_body, streams, shards), in_specs=[...  121 us
    reduce_scatter x1, waiting for transfers between devices, per_device(): lax.psum_scatter(scaled, 'fsdp', scatter_dimension=0, tiled=True)[0]  59.4 us
    gather x1, local copies, waits for them, and re-layouts, look(): found = embed[jnp.clip(ids, 0, table_rows - 1)]  53.1 us
    pallas_call x1, Pallas kernels, vocab(): pl.pallas_call(vocab_body, grid=(rows // tile,), in_specs=[pl.BlockSpec((...  37.7 us
    all_gather x1, waiting for transfers between devices, per_device(): every = lax.all_gather(features, 'fsdp', axis=0, tiled=True)  36.6 us
    pallas_call x1, Pallas kernels, after_back_sum(): pl.pallas_call(functools.partial(after_back_sum_body, shards), grid=(rows...  34.2 us
    pallas_call x1, Pallas kernels, after(): pl.pallas_call(after_body, grid=(rows // tile,), in_specs=[row(width), ro...  29.2 us
    pallas_call x1, Pallas kernels, last_backward(): pl.pallas_call(functools.partial(last_backward_body, places=(up[1], dn[1]...  26.1 us
  transfers between devices with their start and end apart: 4, of which 2 were waited for; matrix products, arithmetic and copies ran while one was open for 18% of the time, Pallas kernels for 32%

profile of v2, /device:TPU:0, one launch (start us, length us, event | category | flops | bytes accessed | tf_op | source)
XLA Modules:
  0.0 633.7 jit_solution(11928424740561738375)
XLA Ops:
  7.2 0.8 slice_bitcast_fusion.3
  8.0 0.9 slice_bitcast_fusion.2
  8.9 0.9 slice_bitcast_fusion.1
  9.9 0.9 slice_bitcast_fusion
  10.8 0.8 pad_maximum_fusion
  11.8 3.4 constant_dynamic-slice_fusion.1
  15.3 0.6 compare_reduce_fusion.2
  15.9 0.6 compare_reduce_fusion.1
  18.0 5.2 all-gather.3
  24.7 53.1 %gather_fusion = bf16[2304,768]{1,0:T(8,128)(2,1)} fusion(bf16[25600,768]{1,0:T(8,128)(2,1)} %param.48, s32[3072]{0:T(1024)S(1)} %pad_clamp_fusion), kind=kCustom, calls=%fused_computation | custom fusion | bytes 7087104 | tf_op jit(solution)/shard_map/gather | solution.py:1072
  77.9 2.7 broadcast_select_fusion
  80.6 1.7 copy-done.2
  82.3 1.3 slice.406.rows
  83.7 0.8 pad.41.chunk
  85.1 121.2 %start_exchange.1 = (bf16[32,320,768]{2,1,0:T(8,128)(2,1)}, bf16[1152,768]{1,0:T(8,128)(2,1)}, f32[32,8,128]{2,1,0:T(8,128)}, f32[32,16,128]{2,1,0:T(8,128)}) custom-call(bf16[320,768]{1,0:T(8,128)(2,1)} %pad.41.chunk, bf16[1152,768]{1,0:T(8,128)(2,1)} %slice.406.rows, f32[8,128]{1,0:T(8,128)} %broadcast_in_dim.46.note, f32[16,128]{1,0:T(8,128)} %pad_bitcast_fusion.1.bias), custom_call_target="tpu_custom_call" | custom-call | tf_op jit(solution)/shard_map/start_exchange/pallas_call | solution.py:908
  206.3 1.2 slice_reduce_fusion
  207.6 4.0 slice.358
  213.4 0.7 select_bitcast_fusion.1
  216.3 0.7 select_bitcast_fusion
  216.9 2.4 scatter.35.down_ref
  219.4 0.7 select_bitcast_fusion.2
  220.1 2.4 scatter.29.down_ref
  222.7 2.3 slice_select_fusion
  225.0 0.7 fusion.33
  226.3 0.6 fusion.27
  227.0 0.7 pad_maximum_fusion.4
  227.8 2.2 multiply_add_fusion.x_ref
  230.0 10.6 %project.1 = (bf16[1024,2304]{1,0:T(8,128)(2,1)}, bf16[1024,128]{1,0:T(8,128)(2,1)}) custom-call(f32[1024,768]{1,0:T(8,128)} %multiply_add_fusion.x_ref, bf16[768,128]{1,0:T(8,128)(2,1)} %copy-done.7, bf16[2304,768]{1,0:T(8,128)(2,1)} %bitcast.136, bf16[128,2304]{1,0:T(8,128)(2,1)} %copy-done.4, f32[1,2304]{1,0:T(1,128)} %get-tuple-element.219.bias_ref), custom_call_target="tpu_custom_call" | custom-call | tf_op jit(solution)/shard_map/project/pallas_call | solution.py:127
  240.6 1.0 broadcast_in_dim.82.seg_ref
  241.6 20.2 %attend.1 = (bf16[1024,768]{1,0:T(8,128)(2,1)}, f32[6,1,2048]{2,1,0:T(1,128)}) custom-call(bf16[1024,2304]{1,0:T(8,128)(2,1)} %get-tuple-element.141.q_ref.k_ref.v_ref, bf16[1024,2304]{1,0:T(8,128)(2,1)} %get-tuple-element.141.q_ref.k_ref.v_ref, bf16[1024,2304]{1,0:T(8,128)(2,1)} %get-tuple-element.141.q_ref.k_ref.v_ref, ...), custom_call_target="tpu_custom_call" | custom-call | tf_op jit(solution)/shard_map/attend/pallas_call | solution.py:174
  261.8 0.6 concatenate.80.norm_ref
  262.4 0.6 concatenate.77.norm_ref.refs_7_
  263.0 3.3 fusion.25
  266.3 0.6 fusion.28
  266.9 29.2 %after.1 = (f32[1024,768]{1,0:T(8,128)}, f32[1024,768]{1,0:T(8,128)}, f32[1024,768]{1,0:T(8,128)}, bf16[1024,3072]{1,0:T(8,128)(2,1)}) custom-call(bf16[1024,768]{1,0:T(8,128)(2,1)} %get-tuple-element.143.ctx_ref, f32[1024,768]{1,0:T(8,128)} %multiply_add_fusion.x_ref, bf16[768,768]{1,0:T(8,128)(2,1)} %bitcast.139, ...), custom_call_target="tpu_custom_call" | custom-call | tf_op jit(solution)/shard_map/after/pallas_call | solution.py:241
  296.2 2.4 slice.414
  298.6 4.0 slice.411
  302.6 0.7 broadcast_in_dim.84.place_ref
  303.3 20.1 %last_forward.1 = (bf16[1024,1536]{1,0:T(8,128)(2,1)}, bf16[128,768]{1,0:T(8,128)(2,1)}, bf16[1024,128]{1,0:T(8,128)(2,1)}, f32[6,256]{1,0:T(8,128)}, f32[128,76...) custom-call(f32[1024,768]{1,0:T(8,128)} %get-tuple-element.144.x_ref, ...), custom_call_target="tpu_custom_call" | custom-call | tf_op jit(solution)/shard_map/last_forward/pallas_call | solution.py:357
  323.9 7.5 %copy.71 = bf16[3200,768]{0,1:T(8,128)(2,1)} copy(bf16[3200,768]{1,0:T(8,128)(2,1)} %all-gather.10.cloned.1.call-done.e_ref) | data formatting | bytes 9830400 | tf_op jit(solution)/shard_map/all_gather | solution.py:1189
  331.4 36.6 %all-gather.8.cloned.1.call-done.u_ref = bf16[2048,768]{1,0:T(8,128)(2,1)} async-done(((bf16[128,768]{1,0:T(8,128)(2,1)}), bf16[2048,768]{1,0:T(8,128)(2,1)}) %all-gather.8.cloned.1.call-update) | async-done | bytes 3145744 | tf_op jit(solution)/shard_map/all_gather | solution.py:1210
  368.0 1.6 broadcast_in_dim.86.bias_ref
  369.6 37.7 %vocab.1 = (f32[16,768,128]{2,1,0:T(8,128)}, f32[16,1,128]{2,1,0:T(1,128)}) custom-call(bf16[2048,768]{1,0:T(8,128)(2,1)} %all-gather.8.cloned.1.call-done.u_ref, bf16[3200,768]{1,0:T(8,128)(2,1)} %all-gather.10.cloned.1.call-done.e_ref, bf16[768,3200]{1,0:T(8,128)(2,1)} %bitcast.135, f32[3200,128]{1,0:T(8,128)} %broadcast_in_dim.86.bias_ref), custom_call_target="tpu_custom_call" | custom-call | tf_op jit(solution)/shard_map/vocab/pallas_call | solution.py:415
  407.4 6.6 %copy.73 = f32[16,768,128]{1,2,0:T(8,128)} copy(f32[16,768,128]{2,1,0:T(8,128)} %get-tuple-element.147) | data formatting | bytes 12582912 | tf_op jit(solution)/shard_map/vocab/pallas_call | solution.py:415
  414.0 19.6 %all-gather.2 = f32[256,1,128]{2,1,0:T(1,128)S(1)} all-gather(f32[16,1,128]{2,1,0:T(1,128)S(1)} %copy-done.27), channel_id=4, replica_groups=mesh['dp'=2,'fsdp'=16] {'fsdp'}, dimensions={0}, use_global_device_ids=true | all-gather | bytes 139264 | tf_op jit(solution)/shard_map/all_gather | solution.py:1213
  433.7 4.8 multiply_convert_fusion
  439.4 1.1 gather_fusion.1
  440.5 1.6 convert_reduce_fusion
  442.3 0.6 fusion.20
  442.9 59.4 %reduce-scatter.2.cloned.1.call-done = bf16[1,768,128]{1,2,0:T(8,128)(2,1)} async-done(((bf16[16,768,128]{1,2,0:T(8,128)(2,1)}), bf16[1,768,128]{1,2,0:T(8,128)(2,1)}) %reduce-scatter.2.cloned.1.call-update) | async-done | bytes 196624 | tf_op jit(solution)/shard_map/reduce_scatter | solution.py:1216
  502.3 2.4 fusion.1
  506.6 26.1 %last_backward.1 = (f32[1024,768]{1,0:T(8,128)}, f32[768,768]{1,0:T(8,128)}, f32[8,768]{1,0:T(8,128)}, f32[8,768]{1,0:T(8,128)}) custom-call(f32[128,768]{1,0:T(8,128)} %get-tuple-element.185.du_ref, bf16[1024,1536]{1,0:T(8,128)(2,1)} %get-tuple-element.149.kv_ref, bf16[128,768]{1,0:T(8,128)(2,1)} %get-tuple-element.150.q_ref, ...), custom_call_target="tpu_custom_call" | custom-call | tf_op jit(solution)/shard_map/last_backward/pallas_call | solution.py:524
  532.7 1.8 convert_element_type.83
  534.5 1.6 convert_element_type.84.refs_8_
  536.0 34.2 %after_back_sum.1 = (bf16[1024,768]{1,0:T(8,128)(2,1)}, f32[16,1152]{1,0:T(8,128)}) custom-call(f32[1024,768]{1,0:T(8,128)} %get-tuple-element.159.refs_0_, f32[1024,768]{1,0:T(8,128)} %get-tuple-element.160.refs_1_, f32[1024,768]{1,0:T(8,128)} %get-tuple-element.161.refs_2_, bf16[1024,3072]{1,0:T(8,128)(2,1)} %get-tuple-element.162.refs_3_, ...), custom_call_target="tpu_custom_call" | custom-call | tf_op jit(solution)/shard_map/after_back_sum/pallas_call | solution.py:592
  570.3 1.5 reshape_reshape.11.dense
  571.8 25.4 %attend_back.1 = (f32[8,768]{1,0:T(8,128)}, f32[8,768]{1,0:T(8,128)}) custom-call(bf16[1024,2304]{1,0:T(8,128)(2,1)} %get-tuple-element.141.q_ref.k_ref.v_ref, bf16[1024,2304]{1,0:T(8,128)(2,1)} %get-tuple-element.141.q_ref.k_ref.v_ref, bf16[1024,2304]{1,0:T(8,128)(2,1)} %get-tuple-element.141.q_ref.k_ref.v_ref, ...), custom_call_target="tpu_custom_call" | custom-call | tf_op jit(solution)/shard_map/attend_back/pallas_call | solution.py:658
  597.3 0.8 pad_maximum_fusion.1
  599.1 0.7 copy.77
  600.4 21.3 %tail.1 = (f32[8,128]{1,0:T(8,128)}, f32[8,128]{1,0:T(8,128)}) custom-call(f32[32,8,128]{2,1,0:T(8,128)} %bitcast.148, f32[24,768]{1,0:T(8,128)} %reshape_reshape.11.dense, f32[8,128]{1,0:T(8,128)} %broadcast_in_dim.89.loss), custom_call_target="tpu_custom_call" | custom-call | tf_op jit(solution)/shard_map/tail/pallas_call | solution.py:964
  621.7 1.3 fusion.32
  623.7 0.7 slice_multiply_fusion.4
  624.5 0.7 multiply_subtract_fusion
  625.2 0.6 multiply_subtract_fusion.1
  (158 shorter events, 10.6 us)
Async XLA Ops:
  7.2 217.8 %copy-start = (bf16[128,768]{1,0:T(8,128)(2,1)S(1)}, bf16[128,768]{1,0:T(8,128)(2,1)}, u32[]{:S(2)}) copy-start(bf16[128,768]{1,0:T(8,128)(2,1)} %param.49) | copy-start | bytes 589828
  7.2 289.0 %all-gather.12.cloned.1.call-start = ((), (), s32[]{:S(2)}) async-start(), calls=%async_computation.4 | async-start | bytes 14598144 | tf_op jit(solution)/shard_map/all_gather | solution.py:1068
  11.6 312.3 %all-gather.10.cloned.1.call-start = ((), (), s32[]{:S(2)}) async-start(), calls=%async_computation.2 | async-start | bytes 7372800 | tf_op jit(solution)/shard_map/all_gather | solution.py:1189
  11.7 4.9 copy-start.26
  11.7 5.6 copy-start.11
  11.7 6.2 copy-start.36
  11.7 6.2 copy-start.38
  11.7 11.5 %copy-start.34 = (f32[1600]{0:T(1024)S(1)}, f32[1600]{0:T(1024)}, u32[]{:S(2)}) copy-start(f32[1600]{0:T(1024)} %param.58) | copy-start | bytes 19204
  11.7 12.1 %copy-start.20 = (f32[2,2,8,24]{3,2,1,0:T(8,128)S(1)}, f32[2,2,8,24]{3,2,1,0:T(8,128)}, u32[]{:S(2)}) copy-start(f32[2,2,8,24]{3,2,1,0:T(8,128)} %param.60) | copy-start | bytes 9220
  11.7 12.9 %copy-start.12 = (bf16[2,96,768]{2,1,0:T(8,128)(2,1)S(1)}, bf16[2,96,768]{2,1,0:T(8,128)(2,1)}, u32[]{:S(2)}) copy-start(bf16[2,96,768]{2,1,0:T(8,128)(2,1)} %param.55) | copy-start | bytes 884740
  11.8 12.9 %copy-start.14 = (bf16[2,768,72]{1,2,0:T(8,128)(2,1)S(1)}, bf16[2,768,72]{1,2,0:T(8,128)(2,1)}, u32[]{:S(2)}) copy-start(bf16[2,768,72]{1,2,0:T(8,128)(2,1)} %param.52) | copy-start | bytes 663556
  11.8 13.0 %copy-start.19 = (bf16[2,768,24]{1,2,0:T(8,128)(2,1)S(1)}, bf16[2,768,24]{1,2,0:T(8,128)(2,1)}, u32[]{:S(2)}) copy-start(bf16[2,768,24]{1,2,0:T(8,128)(2,1)} %param.53) | copy-start | bytes 221188
  15.2 352.7 %all-gather.8.cloned.1.call-start = ((), (), s32[]{:S(2)}) async-start(), calls=%async_computation.1 | async-start | bytes 3342336 | tf_op jit(solution)/shard_map/all_gather | solution.py:1210
  80.6 1.7 copy-start.2
  82.3 1.3 copy-start.9
  207.6 4.1 copy-start.37
  207.6 5.1 copy-start.22
  215.0 0.6 copy-start.15
  219.3 6.4 %copy-start.5 = (bf16[768,128]{1,0:T(8,128)(2,1)}, bf16[768,128]{1,0:T(8,128)(2,1)S(1)}, u32[]{:S(2)}) copy-start(bf16[768,128]{1,0:T(8,128)(2,1)S(1)} %scatter.35.down_ref) | copy-start | bytes 589828
  222.5 3.2 copy-start.7
  224.9 1.3 copy-start.23
  224.9 1.9 copy-start.16
  225.0 1.9 copy-start.32
  225.0 1.9 copy-start.33
  225.0 2.0 copy-start.25
  226.9 3.0 copy-start.3
  226.9 3.0 copy-start.4
  230.0 10.6 %copy-start.21 = (f32[1,1024]{1,0:T(1,128)S(1)}, f32[1,1024]{1,0:T(1,128)}, u32[]{:S(2)}) copy-start(f32[1,1024]{1,0:T(1,128)} %convert_element_type.78.seg_row_ref) | copy-start | bytes 12292
  261.8 4.5 copy-start.24
  298.6 4.0 copy-start.35
  303.3 20.2 %copy-start.13 = (f32[32,16,128]{2,1,0:T(8,128)S(1)}, f32[32,16,128]{2,1,0:T(8,128)}, u32[]{:S(2)}) copy-start(f32[32,16,128]{2,1,0:T(8,128)} %get-tuple-element.146) | copy-start | bytes 786436
  323.4 178.8 %reduce-scatter.2.cloned.1.call-start = ((), (), s32[]{:S(2)}) async-start(), calls=%async_computation.3 | async-start | bytes 3342336 | tf_op jit(solution)/shard_map/reduce_scatter | solution.py:1216
  407.4 6.6 %copy-start.27 = (f32[16,1,128]{2,1,0:T(1,128)S(1)}, f32[16,1,128]{2,1,0:T(1,128)}, u32[]{:S(2)}) copy-start(f32[16,1,128]{2,1,0:T(1,128)} %get-tuple-element.148) | copy-start | bytes 24580
  438.5 0.8 copy-start.39
  438.5 3.7 copy-start.40
  438.5 63.7 %copy-start.6 = (bf16[128,768]{1,0:T(8,128)(2,1)S(1)}, bf16[128,768]{1,0:T(8,128)(2,1)}, u32[]{:S(2)}) copy-start(bf16[128,768]{1,0:T(8,128)(2,1)} %get-tuple-element.145) | copy-start | bytes 589828
  571.8 25.5 %copy-start.28 = (f32[8,768]{1,0:T(8,128)S(1)}, f32[8,768]{1,0:T(8,128)}, u32[]{:S(2)}) copy-start(f32[8,768]{1,0:T(8,128)} %get-tuple-element.169) | copy-start | bytes 73732
  571.8 25.5 %copy-start.29 = (f32[8,768]{1,0:T(8,128)S(1)}, f32[8,768]{1,0:T(8,128)}, u32[]{:S(2)}) copy-start(f32[8,768]{1,0:T(8,128)} %get-tuple-element.170) | copy-start | bytes 73732
  571.8 54.0 %copy-start.1 = (bf16[128,768]{1,0:T(8,128)(2,1)S(1)}, bf16[128,768]{1,0:T(8,128)(2,1)}, u32[]{:S(2)}) copy-start(bf16[128,768]{1,0:T(8,128)(2,1)} %param.49) | copy-start | bytes 589828
  597.2 27.2 %copy-start.8 = (f32[24,768]{1,0:T(8,128)S(1)}, f32[24,768]{1,0:T(8,128)}, u32[]{:S(2)}) copy-start(f32[24,768]{1,0:T(8,128)} %reshape_reshape.11.dense) | copy-start | bytes 221188
  597.2 27.3 %copy-start.10 = (f32[24,768]{1,0:T(8,128)S(1)}, f32[24,768]{1,0:T(8,128)}, u32[]{:S(2)}) copy-start(f32[24,768]{1,0:T(8,128)} %param.63) | copy-start | bytes 221188
  597.2 27.3 %copy-start.17 = (f32[24,768]{1,0:T(8,128)S(1)}, f32[24,768]{1,0:T(8,128)}, u32[]{:S(2)}) copy-start(f32[24,768]{1,0:T(8,128)} %param.65) | copy-start | bytes 221188
  597.2 27.2 %copy-start.18 = (f32[24,768]{1,0:T(8,128)S(1)}, f32[24,768]{1,0:T(8,128)}, u32[]{:S(2)}) copy-start(f32[24,768]{1,0:T(8,128)} %param.64) | copy-start | bytes 221188
  597.2 28.0 %copy-start.30 = (f32[2,2,8,24]{3,2,1,0:T(8,128)S(1)}, f32[2,2,8,24]{3,2,1,0:T(8,128)}, u32[]{:S(2)}) copy-start(f32[2,2,8,24]{3,2,1,0:T(8,128)} %param.62) | copy-start | bytes 9220
  597.3 28.0 %copy-start.31 = (f32[2,2,8,24]{3,2,1,0:T(8,128)S(1)}, f32[2,2,8,24]{3,2,1,0:T(8,128)}, u32[]{:S(2)}) copy-start(f32[2,2,8,24]{3,2,1,0:T(8,128)} %param.61) | copy-start | bytes 9220
Sparse Core Ops, SparseCore 0:
  11.7 123.4 all-gather.11
  136.8 67.7 all-gather.9
  323.6 44.3 all-gather.7
  438.7 63.5 reduce-scatter.1

commit v3 on v2

--- a/solution.py
+++ b/solution.py
@@ -677,7 +677,6 @@
 
 
 MESH = pl.DeviceIdType.MESH
-LINES = {"x": 2, "z": 4, "y": 2}
 
 
 def position():
@@ -740,139 +739,18 @@
         direct_copy(piece_of((me + k) % shards), buffer.at[me], sends, receives, me, k, shards).wait_send()
 
 
-def relative_places(order):
-    places = [
-        {"x": dx, "z": dz, "y": dy} for dx in (0, 1) for dz in range(-3, 4) for dy in (0, 1)
-    ]
-    return sorted(places, key=lambda p: (abs(p["x"]) + abs(p["z"]) + abs(p["y"]), [abs(p[a]) for a in order]))
-
-
-class Gather:
-    def __init__(self, chunk, full_buffer, start, rows, order, sends, receives, hands, hands_got):
-        self.chunk, self.full, self.order = chunk, full_buffer, order
-        self.part = pl.ds(start, rows)
-        self.sends, self.receives, self.hands, self.hands_got = sends, receives, hands, hands_got
-        self.here = position()
-        self.items = relative_places(order)
-        self.pending = []
-
-    def origin(self, item):
-        here = self.here
-        return {"x": (here["x"] + item["x"]) % 2, "z": here["z"] - item["z"], "y": (here["y"] + item["y"]) % 2, "c": here["c"]}
-
-    def key(self, place):
-        return (place["x"] * 4 + place["z"]) * 2 + place["y"]
-
-    def outward(self, item):
-        deepest = max([k for k, axis in enumerate(self.order) if item[axis]], default=-1)
-        ways = []
-        if deepest >= 0 and self.order[deepest] == "z":
-            ways.append(("z", 1 if item["z"] > 0 else -1))
-        for axis in self.order[deepest + 1 :]:
-            ways += [("z", 1), ("z", -1)] if axis == "z" else [(axis, 1)]
-        return ways
-
-    def copy(self, index, way, slot, item):
-        here = self.here
-        place = self.origin(item)
-        number, key = number_of(place), self.key(place)
-        mine = not any(item.values())
-        source = self.chunk.at[self.part, :] if mine else self.full.at[number, self.part, :]
-        if way is None:
-            target = dict(here, c=1 - here["c"])
-            sends, receives = self.hands.at[index], self.hands_got.at[key]
-        else:
-            axis, step = way
-            target = dict(here)
-            target[axis] = here["z"] + step if axis == "z" else 1 - here[axis]
-            sends, receives = self.sends.at[index * 4 + slot], self.receives.at[key]
-        return pltpu.make_async_remote_copy(
-            src_ref=source,
-            dst_ref=self.full.at[number, self.part, :],
-            send_sem=sends,
-            recv_sem=receives,
-            device_id=device_of(target),
-            device_id_type=MESH,
-        )
-
-    def valid(self, item):
-        z = self.here["z"] - item["z"]
-        return (z >= 0) & (z <= 3)
-
-    def step(self, index):
-        item = self.items[index]
-
-        @pl.when(self.valid(item))
-        def _():
-            if any(item.values()):
-                self.arrived(index, item)
-            for slot, way in enumerate(self.outward(item)):
-                self.when_way(way, lambda way=way, slot=slot: self.copy(index, way, slot, item).start())
-            self.copy(index, None, 0, item).start()
-
-    def when_way(self, way, act):
-        axis, step = way
-        if axis == "z":
-            z = self.here["z"] + step
-            pl.when((z >= 0) & (z <= 3))(act)
-        else:
-            act()
-
-    def arrived(self, index, item):
-        place = self.origin(item)
-        spot = self.full.at[number_of(place), self.part, :]
-        pltpu.make_async_remote_copy(
-            src_ref=spot,
-            dst_ref=spot,
-            send_sem=self.sends.at[index * 4],
-            recv_sem=self.receives.at[self.key(place)],
-            device_id=device_of(dict(self.here, c=1 - self.here["c"])),
-            device_id_type=MESH,
-        ).wait_recv()
-
-    def finish(self):
-        for index, item in enumerate(self.items):
-
-            @pl.when(self.valid(item))
-            def _(index=index, item=item):
-                for slot, way in enumerate(self.outward(item)):
-                    self.when_way(way, lambda way=way, slot=slot: self.copy(index, way, slot, item).wait_send())
-                self.copy(index, None, 0, item).wait_send()
-                place = dict(self.origin(item), c=1 - self.here["c"])
-                spot = self.full.at[number_of(place), self.part, :]
-                pltpu.make_async_remote_copy(
-                    src_ref=spot,
-                    dst_ref=spot,
-                    send_sem=self.hands.at[index],
-                    recv_sem=self.hands_got.at[self.key(place)],
-                    device_id=device_of(dict(self.here, c=1 - self.here["c"])),
-                    device_id_type=MESH,
-                ).wait_recv()
-
-
-ITEMS = 28
-
-
 def start_body(
-    streams, shards, chunk, rows, note, bias, full_chunk, got, notes, biases,
-    sends, receives, hands, hands_got, row_sems, note_sends, note_gets, bias_sends, bias_gets, own_sems,
+    shards, rows, note, bias, got, notes, biases,
+    row_sems, note_sends, note_gets, bias_sends, bias_gets, own_sems,
 ):
     here = position()
     me = number_of(here)
     greet_all(shards)
-    own = pltpu.make_async_copy(chunk, full_chunk.at[me], own_sems.at[0])
-    own.start()
-    own_note = pltpu.make_async_copy(note, notes.at[me], own_sems.at[1])
+    own_note = pltpu.make_async_copy(note, notes.at[me], own_sems.at[0])
     own_note.start()
-    own_bias = pltpu.make_async_copy(bias, biases.at[me], own_sems.at[2])
+    own_bias = pltpu.make_async_copy(bias, biases.at[me], own_sems.at[1])
     own_bias.start()
     await_all(shards)
-    gathers = [
-        Gather(
-            chunk, full_chunk, start, size, order, sends.at[k], receives.at[k], hands.at[k], hands_got.at[k]
-        )
-        for k, (start, size, order) in enumerate(streams)
-    ]
     across = pltpu.make_async_remote_copy(
         src_ref=rows,
         dst_ref=got,
@@ -881,55 +759,33 @@
         device_id=device_of(dict(here, x=1 - here["x"])),
         device_id_type=MESH,
     )
-    for gather in gathers:
-        gather.step(0)
+    across.start()
     spread(lambda peer: note, notes, note_sends, note_gets, me, shards)
     spread(lambda peer: bias, biases, bias_sends, bias_gets, me, shards)
-    across.start()
-    for index in range(1, ITEMS):
-        for gather in gathers:
-            gather.step(index)
-    for gather in gathers:
-        gather.finish()
     collect(lambda peer: note, notes, note_sends, note_gets, me, shards)
     collect(lambda peer: bias, biases, bias_sends, bias_gets, me, shards)
     across.wait()
-    own.wait()
     own_note.wait()
     own_bias.wait()
 
 
-def start_exchange(chunk, rows, note, bias, shards):
+def start_exchange(rows, note, bias, shards):
     anywhere = pl.BlockSpec(memory_space=pl.ANY)
-    cut = (chunk.shape[0] * 5 // 6 + 15) // 16 * 16
-    streams = ((0, cut, "xzy"), (cut, chunk.shape[0] - cut, "xyz"))
     shape = jax.ShapeDtypeStruct
     sems = pltpu.SemaphoreType.DMA
     return pl.pallas_call(
-        functools.partial(start_body, streams, shards),
-        in_specs=[anywhere] * 4,
-        out_specs=[anywhere] * 4,
+        functools.partial(start_body, shards),
+        in_specs=[anywhere] * 3,
+        out_specs=[anywhere] * 3,
         out_shape=[
-            shape((shards, *chunk.shape), chunk.dtype),
             shape(rows.shape, rows.dtype),
             shape((shards, *note.shape), note.dtype),
             shape((shards, *bias.shape), bias.dtype),
         ],
-        scratch_shapes=[
-            sems((2, 4 * ITEMS)),
-            sems((2, 16)),
-            sems((2, ITEMS)),
-            sems((2, 16)),
-            sems((2,)),
-            sems((shards,)),
-            sems((shards,)),
-            sems((shards,)),
-            sems((shards,)),
-            sems((3,)),
-        ],
+        scratch_shapes=[sems((2,))] + [sems((shards,))] * 4 + [sems((2,))],
         compiler_params=params(collective_id=1, has_side_effects=True),
         name="start_exchange",
-    )(chunk, rows, note, bias)
+    )(rows, note, bias)
 
 
 def tail_body(shards, parts, dense, loss, total_ref, sums_ref, got, note, notes, send_a, get_a, send_b, get_b):
@@ -975,6 +831,320 @@
         compiler_params=params(collective_id=2, has_side_effects=True),
         name="tail",
     )(parts, dense, loss)
+
+
+HOPS = 3
+LOG_ROWS = 16
+
+
+def flip(z, k):
+    return (z % 2 + k % 2) % 2 + 2 * ((z // 2 + k // 2) % 2)
+
+
+def pack_log(log_row, rows):
+    high = log_row.astype(BF).astype(F32)
+    middle = (log_row - high).astype(BF).astype(F32)
+    low = log_row - high - middle
+    row = lax.broadcasted_iota(jnp.int32, (rows, log_row.shape[1]), 0)
+    return jnp.where(
+        row == 0, high, jnp.where(row == 1, middle, jnp.where(row == 2, low, 0.0))
+    ).astype(BF)
+
+
+def unpack(block, hidden):
+    logs = block[hidden : hidden + LOG_ROWS, :].astype(F32)
+    return block[:hidden, :].astype(F32), jnp.sum(logs, 0, keepdims=True)
+
+
+def merged(one, two):
+    top = jnp.maximum(one[1], two[1])
+    first, second = jnp.exp(one[1] - top), jnp.exp(two[1] - top)
+    total = first + second
+    inverse = 1.0 / total
+    return one[0] * (first * inverse) + two[0] * (second * inverse), top + jnp.log(total)
+
+
+def store_packed(ref, pair, hidden):
+    ref[:hidden, :] = pair[0].astype(BF)
+    ref[hidden : hidden + LOG_ROWS, :] = pack_log(pair[1], LOG_ROWS)
+
+
+def head_body(
+    u_ref, e_any, et_any, bias_any, mean_ref, log_ref,
+    e_ref, et_ref, bias_ref, feats, packs, handed, crossed, kept, lined, zouts,
+    loads, z_send, z_get, y_send, y_get, c_send, c_get, h_send, h_get, p_send, p_get, l_send, l_get,
+):
+    here = position()
+    z, y, c = here["z"], here["y"], here["c"]
+    labels, hidden = u_ref.shape
+    slot_of = lambda zz, yy, cc: (zz * 2 + yy) * 2 + cc
+    me = slot_of(z, y, c)
+    sibling = device_of(dict(here, c=1 - c))
+    beside = device_of(dict(here, y=1 - y))
+    at_z = lambda zz: device_of(dict(here, z=zz))
+    inside = lambda zz: (zz >= 0) & (zz <= HOPS)
+
+    fills = [
+        pltpu.make_async_copy(source, target, loads.at[k])
+        for k, (source, target) in enumerate(((e_any, e_ref), (bias_any, bias_ref), (et_any, et_ref)))
+    ]
+    for fill in fills:
+        fill.start()
+    barrier = pltpu.get_barrier_semaphore()
+    for target in (sibling, beside):
+        pl.semaphore_signal(barrier, inc=1, device_id=target, device_id_type=MESH)
+    for k in range(1, 4):
+        pl.semaphore_signal(barrier, inc=1, device_id=at_z(flip(z, k)), device_id_type=MESH)
+    feats[me] = u_ref[...]
+    pl.semaphore_wait(barrier, 5)
+
+    def move(slot, device, send, get):
+        return pltpu.make_async_remote_copy(
+            src_ref=feats.at[slot],
+            dst_ref=feats.at[slot],
+            send_sem=send,
+            recv_sem=get,
+            device_id=device,
+            device_id_type=MESH,
+        )
+
+    def hand(zz, other):
+        slot = slot_of(zz, (y + other) % 2, c)
+        return move(slot, sibling, c_send.at[other * 4 + zz], c_get.at[other * 4 + zz])
+
+    def handed_here(zz, other):
+        slot = slot_of(zz, (y + other) % 2, 1 - c)
+        return move(slot, sibling, c_send.at[other * 4 + zz], c_get.at[other * 4 + zz])
+
+    def cross(zz):
+        return move(slot_of(zz, y, c), beside, y_send.at[zz], y_get.at[zz])
+
+    def crossed_here(zz):
+        return move(slot_of(zz, 1 - y, c), beside, y_send.at[zz], y_get.at[zz])
+
+    def along(zz, to, way):
+        return move(slot_of(zz, y, c), at_z(to), z_send.at[way * 4 + zz], z_get.at[zz])
+
+    def own_round():
+        for way, to in ((0, z + 1), (1, z - 1)):
+
+            @pl.when(inside(to))
+            def _(way=way, to=to):
+                along(z, to, way).start()
+
+        cross(z).start()
+        hand(z, 0).start()
+
+    def later_round(r):
+        if r <= HOPS:
+            for way, origin, to in ((0, z - r, z + 1), (1, z + r, z - 1)):
+
+                @pl.when(inside(origin))
+                def _(way=way, origin=origin, to=to):
+                    along(origin, to, way).wait_recv()
+
+                    @pl.when(inside(to))
+                    def _():
+                        along(origin, to, way).start()
+
+                    cross(origin).start()
+                    hand(origin, 0).start()
+
+        for origin in (z - (r - 1), z + (r - 1))[: 1 if r == 1 else 2]:
+
+            @pl.when(inside(origin))
+            def _(origin=origin):
+                crossed_here(origin).wait_recv()
+                hand(origin, 1).start()
+
+    own_round()
+    fills[0].wait()
+    fills[1].wait()
+    fills[2].wait()
+    count = e_ref.shape[0]
+    step = split_of(count, 640, 128)
+
+    def hand_part(s):
+        return pltpu.make_async_remote_copy(
+            src_ref=packs.at[s, 1 - c],
+            dst_ref=handed.at[s],
+            send_sem=h_send.at[s],
+            recv_sem=h_get.at[s],
+            device_id=sibling,
+            device_id_type=MESH,
+        )
+
+    def cross_part(k):
+        return pltpu.make_async_remote_copy(
+            src_ref=packs.at[2 * k + 1, c],
+            dst_ref=crossed.at[k],
+            send_sem=p_send.at[k],
+            recv_sem=p_get.at[k],
+            device_id=beside,
+            device_id_type=MESH,
+        )
+
+    def line_part(k):
+        return pltpu.make_async_remote_copy(
+            src_ref=zouts.at[k],
+            dst_ref=lined.at[k],
+            send_sem=l_send.at[k],
+            recv_sem=l_get.at[k],
+            device_id=at_z(flip(z, k)),
+            device_id_type=MESH,
+        )
+
+    def compute(s):
+        zt, yt = flip(z, s // 2), (y + s % 2) % 2
+
+        handed_here(zt, s % 2).wait_recv()
+        first = slot_of(zt, yt, 0)
+        u = feats[pl.ds(first, 2)].reshape(2 * labels, hidden)
+        top = total = mean = None
+        for start in range(0, count, step):
+            part = slice(start, start + step)
+            bias = bias_ref[part, :]
+            logits = mm_nt(e_ref[part, :], u) + jnp.concatenate([bias, bias], 1)
+            high = jnp.max(logits, 0, keepdims=True)
+            new = high if top is None else jnp.maximum(top, high)
+            grown = jnp.exp(logits - new)
+            sums = jnp.sum(grown, 0, keepdims=True)
+            product = mm(et_ref[:, part], grown.astype(BF))
+            if top is None:
+                total, mean = sums, product
+            else:
+                shrink = jnp.exp(top - new)
+                total, mean = total * shrink + sums, mean * shrink + product
+            top = new
+        mean = mean * (1.0 / total)
+        logs = top + jnp.log(total)
+        for k in range(2):
+            half = slice(k * labels, (k + 1) * labels)
+            packs[s, k, :hidden, :] = mean[:, half].astype(BF)
+            packs[s, k, hidden : hidden + LOG_ROWS, :] = pack_log(logs[:, half], LOG_ROWS)
+        hand_part(s).start()
+
+    def settle(s):
+        hand_part(s).wait_recv()
+        pair = merged(unpack(packs[s, c], hidden), unpack(handed[s], hidden))
+
+        @pl.when(s % 2 == 1)
+        def _():
+            store_packed(packs.at[s, c], pair, hidden)
+            cross_part(s // 2).start()
+
+        @pl.when(s % 2 == 0)
+        def _():
+            store_packed(kept.at[s // 2], pair, hidden)
+
+    def finish(k):
+        cross_part(k).wait_recv()
+        pair = merged(unpack(kept[k], hidden), unpack(crossed[k], hidden))
+
+        @pl.when(k > 0)
+        def _():
+            store_packed(zouts.at[k], pair, hidden)
+            line_part(k).start()
+
+        @pl.when(k == 0)
+        def _():
+            store_packed(zouts.at[k], pair, hidden)
+
+    steps = 8
+
+    @pl.loop(0, steps)
+    def _(s):
+        for r in range(1, HOPS + 2):
+            pl.when(s == r)(functools.partial(later_round, r))
+        compute(s)
+
+        @pl.when(s > 0)
+        def _():
+            settle(s - 1)
+
+        @pl.when((s >= 3) & (s % 2 == 1))
+        def _():
+            finish((s - 3) // 2)
+
+    settle(steps - 1)
+    finish(steps // 2 - 1)
+    total = unpack(zouts[0], hidden)
+    for k in range(1, 4):
+        line_part(k).wait_recv()
+        total = merged(total, unpack(lined[k], hidden))
+    mean_ref[...] = total[0]
+    log_ref[...] = total[1]
+
+    for way, to in ((0, z + 1), (1, z - 1)):
+
+        @pl.when(inside(to))
+        def _(way=way, to=to):
+            along(z, to, way).wait_send()
+
+    cross(z).wait_send()
+    hand(z, 0).wait_send()
+    for r in range(1, HOPS + 1):
+        for way, origin, to in ((0, z - r, z + 1), (1, z + r, z - 1)):
+
+            @pl.when(inside(origin))
+            def _(way=way, origin=origin, to=to):
+                @pl.when(inside(to))
+                def _():
+                    along(origin, to, way).wait_send()
+
+                cross(origin).wait_send()
+                hand(origin, 0).wait_send()
+
+    for origin in range(4):
+        hand(origin, 1).wait_send()
+    for s in range(steps):
+        hand_part(s).wait_send()
+    for k in range(4):
+        cross_part(k).wait_send()
+    for k in range(1, 4):
+        line_part(k).wait_send()
+
+
+def head(u, e, et, bias_wide):
+    labels, hidden = u.shape
+    whole = pl.BlockSpec(memory_space=pltpu.VMEM)
+    anywhere = pl.BlockSpec(memory_space=pl.ANY)
+    shape = jax.ShapeDtypeStruct
+    sems = pltpu.SemaphoreType.DMA
+    block = (hidden + LOG_ROWS, labels)
+    return pl.pallas_call(
+        head_body,
+        in_specs=[whole] + [anywhere] * 3,
+        out_specs=[whole] * 2,
+        out_shape=[shape((hidden, labels), F32), shape((1, labels), F32)],
+        scratch_shapes=[
+            pltpu.VMEM(e.shape, BF),
+            pltpu.VMEM(et.shape, BF),
+            pltpu.VMEM(bias_wide.shape, F32),
+            pltpu.VMEM((16, labels, hidden), BF),
+            pltpu.VMEM((8, 2, *block), BF),
+            pltpu.VMEM((8, *block), BF),
+            pltpu.VMEM((4, *block), BF),
+            pltpu.VMEM((4, *block), BF),
+            pltpu.VMEM((4, *block), BF),
+            pltpu.VMEM((4, *block), BF),
+            sems((3,)),
+            sems((8,)),
+            sems((4,)),
+            sems((4,)),
+            sems((4,)),
+            sems((8,)),
+            sems((8,)),
+            sems((8,)),
+            sems((8,)),
+            sems((4,)),
+            sems((4,)),
+            sems((4,)),
+            sems((4,)),
+        ],
+        compiler_params=params(collective_id=4, has_side_effects=True),
+        name="head",
+    )(u, e, et, bias_wide)
 
 
 def seg_positions(segments):
@@ -1065,7 +1235,12 @@
     wanted = jnp.concatenate([input_token_index[0], label_target_token[0]])
     dp_count = lax.axis_size("dp")
     group_ids = lax.all_gather(wanted, "dp", axis=0, tiled=False) - dp_index * table_rows
-    later_full = [lax.all_gather(chunk, BOTH, axis=0, tiled=False) for chunk in chunks[1:]]
+    gathered = []
+    for chunk in chunks:
+        if gathered:
+            chunk, gathered[-1] = lax.optimization_barrier((chunk, gathered[-1]))
+        gathered.append(lax.all_gather(chunk, BOTH, axis=0, tiled=False))
+    first_full = gathered[0]
 
     def look(ids):
         inside = (ids >= 0) & (ids < table_rows)
@@ -1085,15 +1260,12 @@
         note = jnp.broadcast_to(sequence_task_index.astype(F32)[:, None], (8, 128))
         bias_rows = -(-slice_rows // 1024) * 8
         bias_block = jnp.pad(vocabulary_bias, (0, bias_rows * 128 - slice_rows)).reshape(bias_rows, 128)
-        first_full, got, notes, biases = start_exchange(
-            chunks[0], looked[: wanted.size], note, bias_block, shards
-        )
+        got, notes, biases = start_exchange(looked[: wanted.size], note, bias_block, shards)
         rows = jnp.where(inside[wanted.size :, None], looked[wanted.size :], got)
         every_task = notes[:, 0, 0].astype(jnp.int32)
         all_bias = biases.reshape(shards, -1)[:, :slice_rows].reshape(-1)
     else:
         looked, inside = look(group_ids.reshape(-1))
-        first_full = lax.all_gather(chunks[0], BOTH, axis=0, tiled=False)
         rows = lax.psum_scatter(looked, "dp", scatter_dimension=0, tiled=True)
         every_task = lax.all_gather(sequence_task_index, BOTH, axis=0, tiled=True)
         all_bias = lax.all_gather(vocabulary_bias, BOTH, axis=0, tiled=True)
@@ -1101,7 +1273,6 @@
     task_hot = (sequence_task_index[:, None] == task_range[None, :]).astype(F32)
     row_weight = jnp.sum(task_hot[0] * (task_loss_weight / jnp.maximum(counts, 1.0)))
 
-    gathered = [first_full, *later_full]
     slabs = [
         (slab_of(gathered[layer], 0, ff_rows), slab_of(gathered[layer], ff_rows, ff_rows))
         for layer in range(layers)
@@ -1186,17 +1357,32 @@
     place_col = jnp.broadcast_to(label_positions.reshape(labels, 1), (labels, 128))
 
     own_slice = lax.dynamic_slice_in_dim(embed, fsdp_index * slice_rows, slice_rows, 0)
-    own_vocab = lax.all_gather(own_slice, "dp", axis=0, tiled=True)
+    own_vocab = jnp.concatenate(
+        [own_slice]
+        + [
+            lax.ppermute(own_slice, "dp", [(k, (k + shift) % dp_count) for k in range(dp_count)])
+            for shift in range(1, dp_count)
+        ],
+        0,
+    )
     own_bias = jnp.concatenate(
         [
             lax.dynamic_slice_in_dim(
-                all_bias, part * table_rows + fsdp_index * slice_rows, slice_rows, 0
+                all_bias,
+                ((dp_index - shift) % dp_count) * table_rows + fsdp_index * slice_rows,
+                slice_rows,
+                0,
             )
-            for part in range(dp_count)
+            for shift in range(dp_count)
         ]
     )
-    bias_wide = jnp.broadcast_to(own_bias[:, None], (own_bias.shape[0], 128))
+    vocab_block = (
+        own_vocab,
+        own_vocab.T,
+        jnp.broadcast_to(own_bias[:, None], (own_bias.shape[0], 128)),
+    )
     target_bias = all_bias[label_target_token[0]]
+    hidden_rows, vocab_block = lax.optimization_barrier((hidden_rows, vocab_block))
 
     qkv, mid = project(hidden_rows, downs[0], in_weights[0], adapters[0], bias_of[0][0])
     context, logs = attend(qkv, seg_wide, seg_row)
@@ -1207,17 +1393,20 @@
         x_last, place_col, place_row, seg_wide, downs[1], in_weights[1], adapters[1], bias_of[1][0],
         out_weights[1], *slabs[1], *bias_of[1][1:], norms_of[1], head_full, head_dense_bias[None, :],
     )
-    every = lax.all_gather(features, "fsdp", axis=0, tiled=True)
-    means, local_logs = vocab(every, own_vocab, own_vocab.T, bias_wide, labels)
-    local_logs = local_logs.reshape(-1, labels)
-    all_logs = lax.all_gather(local_logs, "fsdp", axis=0, tiled=False)
-    whole_logs = jax.nn.logsumexp(all_logs, axis=0)
-    scaled = (means * jnp.exp(local_logs - whole_logs)[:, None, :]).astype(BF)
-    mean_rows = lax.psum_scatter(scaled, "fsdp", scatter_dimension=0, tiled=True)[0]
-    own_logs = lax.dynamic_index_in_dim(whole_logs, fsdp_index, 0, keepdims=False)
+    if grouped:
+        mean_t, own_logs = head(features, *vocab_block)
+    else:
+        every = lax.all_gather(features, "fsdp", axis=0, tiled=True)
+        means, local_logs = vocab(every, *vocab_block, labels)
+        local_logs = local_logs.reshape(-1, labels)
+        all_logs = lax.all_gather(local_logs, "fsdp", axis=0, tiled=False)
+        whole_logs = jax.nn.logsumexp(all_logs, axis=0)
+        scaled = (means * jnp.exp(local_logs - whole_logs)[:, None, :]).astype(BF)
+        mean_t = lax.psum_scatter(scaled, "fsdp", scatter_dimension=0, tiled=True)[0].astype(F32)
+        own_logs = lax.dynamic_index_in_dim(whole_logs, fsdp_index, 0, keepdims=False)
     targets = jnp.sum(features.astype(F32) * target_rows, 1) + target_bias
     own_loss = row_weight * jnp.sum(own_logs - targets)
-    feat_grad = row_weight * (mean_rows.astype(F32).T - target_rows)
+    feat_grad = row_weight * (mean_t.T - target_rows)
 
     hidden_grad, dense_gradient, gq_last, gv_last = last_backward(
         feat_grad, saved, place_col, place_row, seg_wide, downs[1], in_weights[1], adapters[1],

time: 639 us -> 687 us (1.075)
  blocking collectives: 24.8 us -> 69 us
  Pallas kernels: 346 us -> 315 us
  waiting for transfers between devices: 96.1 us -> 109 us
  other arithmetic: 28.8 us -> 39.1 us
    all_gather x3 -> x2, waiting for transfers between devices: 36.6 us -> 109 us  [per_device(): gathered.append(lax.all_gather(chunk, BOTH, axis=0, tiled=False))]
    all_gather x1, blocking collectives: 5.23 us -> 69 us  [per_device(): lax.all_gather(wanted, 'dp', axis=0, tiled=False) - dp_index * table_rows]
    reduce_scatter x1 -> x0, waiting for transfers between devices: 59.4 us -> none  [per_device(): lax.psum_scatter(scaled, 'fsdp', scatter_dimension=0, tiled=True)[0]]
    pallas_call x2, Pallas kernels: 159 us -> 124 us  [the longest x1 66 us: head(): pl.pallas_call(head_body, in_specs=[whole] + [anywhere] * 3, out_specs=[w...]
    all_gather x1 -> x0, blocking collectives: 19.6 us -> none  [per_device(): all_logs = lax.all_gather(local_logs, 'fsdp', axis=0, tiled=False)]
    gather x1, local copies, waits for them, and re-layouts: 53.1 us -> 41.4 us  [look(): found = embed[jnp.clip(ids, 0, table_rows - 1)]]
    unnamed x90 -> x83, local copies, waits for them, and re-layouts: 3.25 us -> 13.8 us
    optimization_barrier x0 -> x1, local copies, waits for them, and re-layouts: none -> 7.65 us  [per_device(): lax.optimization_barrier((hidden_rows, vocab_block))]
  transfers between devices with their start and end apart: 4 -> 3, of which waited for: 2 -> 1; matrix products, arithmetic and copies ran while one was open for 18% -> 19% of each run, Pallas kernels for 32% -> 18%
where the time goes in v3:
time: 687 us; the launch traced here: 676 us
  Pallas kernels  315 us (46%)
  local copies, waits for them, and re-layouts  121 us (18%)
  waiting for transfers between devices  109 us (16%)
  blocking collectives  69 us (10%)
  other arithmetic  39.1 us (6%)
  between operations  19.6 us (3%)
    all_gather x2, waiting for transfers between devices, per_device(): gathered.append(lax.all_gather(chunk, BOTH, axis=0, tiled=False))  109 us
    all_gather x1, blocking collectives, per_device(): lax.all_gather(wanted, 'dp', axis=0, tiled=False) - dp_index * table_rows  69 us
    pallas_call x1, Pallas kernels, head(): pl.pallas_call(head_body, in_specs=[whole] + [anywhere] * 3, out_specs=[w...  66 us
    pallas_call x1, Pallas kernels, start_exchange(): pl.pallas_call(functools.partial(start_body, shards), in_specs=[anywhere]...  58.5 us
    gather x1, local copies, waits for them, and re-layouts, look(): found = embed[jnp.clip(ids, 0, table_rows - 1)]  41.4 us
    pallas_call x1, Pallas kernels, after_back_sum(): pl.pallas_call(functools.partial(after_back_sum_body, shards), grid=(rows...  35.9 us
    pallas_call x1, Pallas kernels, after(): pl.pallas_call(after_body, grid=(rows // tile,), in_specs=[row(width), ro...  29.2 us
    pallas_call x1, Pallas kernels, last_backward(): pl.pallas_call(functools.partial(last_backward_body, places=(up[1], dn[1]...  26.2 us
  transfers between devices with their start and end apart: 3, of which 1 were waited for; matrix products, arithmetic and copies ran while one was open for 19% of the time, Pallas kernels for 18%

profile of v3, /device:TPU:0, one launch (start us, length us, event | category | flops | bytes accessed | tf_op | source)
XLA Modules:
  0.0 676.2 jit_solution(14247812107002943559)
XLA Ops:
  8.1 0.9 bitcast_dynamic-update-slice_fusion
  9.1 0.9 bitcast_dynamic-update-slice_fusion.1
  10.0 0.9 bitcast_dynamic-update-slice_fusion.2
  11.7 0.9 convert_dynamic-update-slice_fusion
  12.6 0.8 pad.42
  14.3 0.9 slice_bitcast_fusion.2
  15.2 0.9 slice_bitcast_fusion.1
  17.0 109.4 %all-gather.7.cloned.1.call-done = bf16[10240,768]{1,0:T(8,128)(2,1)} async-done(((bf16[320,768]{1,0:T(8,128)(2,1)}), bf16[10240,768]{1,0:T(8,128)(2,1)}) %all-gather.7.cloned.1.call-update) | async-done | bytes 15728656 | tf_op jit(solution)/shard_map/all_gather | solution.py:1242
  126.4 3.3 constant_dynamic-slice_fusion
  129.7 1.4 collective-permute-start
  132.4 69.0 %all-gather.3 = s32[2,1,1152]{2,1,0:T(1,128)S(1)} all-gather(s32[1,1,1152]{2,1,0:T(1,128)S(1)} %reshape.524), channel_id=2, replica_groups=mesh['dp'=2,'fsdp'=16] {'dp'}, dimensions={0}, use_global_device_ids=true | all-gather | bytes 13824 | tf_op jit(solution)/shard_map/all_gather | solution.py:1237
  202.2 41.4 %gather_fusion = bf16[2304,768]{1,0:T(8,128)(2,1)} fusion(bf16[25600,768]{1,0:T(8,128)(2,1)} %param.48, s32[3072]{0:T(1024)S(1)} %pad_clamp_fusion), kind=kCustom, calls=%fused_computation | custom fusion | bytes 7087104 | tf_op jit(solution)/shard_map/gather | solution.py:1247
  243.7 2.8 broadcast_select_fusion
  246.5 1.7 copy-done.4
  248.3 1.3 slice.406.rows
  250.8 58.5 %start_exchange.1 = (bf16[1152,768]{1,0:T(8,128)(2,1)}, f32[32,8,128]{2,1,0:T(8,128)}, f32[32,16,128]{2,1,0:T(8,128)}) custom-call(bf16[1152,768]{1,0:T(8,128)(2,1)} %slice.406.rows, f32[8,128]{1,0:T(8,128)} %broadcast_in_dim.42.note, f32[16,128]{1,0:T(8,128)} %pad_bitcast_fusion.1.bias), custom_call_target="tpu_custom_call" | custom-call | tf_op jit(solution)/shard_map/start_exchange/pallas_call | solution.py:776
  309.3 1.2 copy.82
  313.4 1.6 convert_reduce_fusion
  315.0 1.2 fusion.22
  316.3 1.3 select_bitcast_fusion
  317.6 1.3 select_bitcast_fusion.2
  318.9 1.4 select_bitcast_fusion.1
  320.3 1.7 slice_select_fusion
  322.1 1.2 copy-done.5
  323.3 1.3 fusion.25
  325.3 4.5 copy.78
  331.1 1.0 scatter.34
  332.1 1.7 scatter.26
  333.7 1.8 gather_fusion.1
  335.5 3.3 scatter.35.down_ref
  338.8 3.3 scatter.29.down_ref
  342.1 1.3 concatenate.85.norm_ref
  343.5 1.3 concatenate.83.norm_ref.refs_7_
  344.8 1.3 fusion.12
  348.5 2.2 multiply_add_fusion.x_ref
  351.4 4.6 copy.68
  356.0 5.4 fusion.27.et_any
  361.4 3.6 pad_maximum_fusion
  365.0 1.7 broadcast_in_dim.44.bias_any
  366.7 7.6 %copy.74.e_any = bf16[3200,768]{1,0:T(8,128)(2,1)} copy(bf16[3200,768]{0,1:T(8,128)(2,1)} %pad_maximum_fusion) | data formatting | bytes 9830400 | tf_op jit(solution)/shard_map/optimization_barrier | solution.py:1385
  374.3 4.0 slice.363
  378.3 1.2 slice_reduce_fusion
  380.5 0.8 copy-done.7
  381.3 10.6 %project.1 = (bf16[1024,2304]{1,0:T(8,128)(2,1)}, bf16[1024,128]{1,0:T(8,128)(2,1)}) custom-call(f32[1024,768]{1,0:T(8,128)} %multiply_add_fusion.x_ref, bf16[768,128]{1,0:T(8,128)(2,1)} %scatter.29.down_ref, bf16[2304,768]{1,0:T(8,128)(2,1)} %bitcast.123, bf16[128,2304]{1,0:T(8,128)(2,1)} %copy-done.7, f32[1,2304]{1,0:T(1,128)} %get-tuple-element.229.bias_ref), custom_call_target="tpu_custom_call" | custom-call | tf_op jit(solution)/shard_map/project/pallas_call | solution.py:127
  391.9 1.0 broadcast_in_dim.45.seg_ref
  393.0 20.2 %attend.1 = (bf16[1024,768]{1,0:T(8,128)(2,1)}, f32[6,1,2048]{2,1,0:T(1,128)}) custom-call(bf16[1024,2304]{1,0:T(8,128)(2,1)} %get-tuple-element.148.q_ref.k_ref.v_ref, bf16[1024,2304]{1,0:T(8,128)(2,1)} %get-tuple-element.148.q_ref.k_ref.v_ref, bf16[1024,2304]{1,0:T(8,128)(2,1)} %get-tuple-element.148.q_ref.k_ref.v_ref, ...), custom_call_target="tpu_custom_call" | custom-call | tf_op jit(solution)/shard_map/attend/pallas_call | solution.py:174
  413.1 3.2 fusion.17
  416.4 29.2 %after.1 = (f32[1024,768]{1,0:T(8,128)}, f32[1024,768]{1,0:T(8,128)}, f32[1024,768]{1,0:T(8,128)}, bf16[1024,3072]{1,0:T(8,128)(2,1)}) custom-call(bf16[1024,768]{1,0:T(8,128)(2,1)} %get-tuple-element.150.ctx_ref, f32[1024,768]{1,0:T(8,128)} %multiply_add_fusion.x_ref, bf16[768,768]{1,0:T(8,128)(2,1)} %bitcast.126, bf16[32,320,768]{2,1,0:T(8,128)(2,1)} %bitcast.111, ...), custom_call_target="tpu_custom_call" | custom-call | tf_op jit(solution)/shard_map/after/pallas_call | solution.py:241
  445.6 2.4 slice.415
  448.0 4.1 slice.412
  452.8 20.0 %last_forward.1 = (bf16[1024,1536]{1,0:T(8,128)(2,1)}, bf16[128,768]{1,0:T(8,128)(2,1)}, bf16[1024,128]{1,0:T(8,128)(2,1)}, f32[6,256]{1,0:T(8,128)}, f32[128,76...) custom-call(f32[1024,768]{1,0:T(8,128)} %get-tuple-element.151.x_ref, ...), custom_call_target="tpu_custom_call" | custom-call | tf_op jit(solution)/shard_map/last_forward/pallas_call | solution.py:357
  472.9 66.0 %head.1 = (f32[768,128]{1,0:T(8,128)}, f32[1,128]{1,0:T(1,128)}) custom-call(bf16[128,768]{1,0:T(8,128)(2,1)} %get-tuple-element.153.u_ref, bf16[3200,768]{1,0:T(8,128)(2,1)} %copy.74.e_any, bf16[768,3200]{1,0:T(8,128)(2,1)} %fusion.27.et_any, f32[3200,128]{1,0:T(8,128)} %broadcast_in_dim.44.bias_any), custom_call_target="tpu_custom_call" | custom-call | tf_op jit(solution)/shard_map/head/pallas_call | solution.py:1115
  538.8 1.2 copy.75
  540.0 2.3 fusion.1
  542.4 1.3 fusion.14
  544.9 26.2 %last_backward.1 = (f32[1024,768]{1,0:T(8,128)}, f32[768,768]{1,0:T(8,128)}, f32[8,768]{1,0:T(8,128)}, f32[8,768]{1,0:T(8,128)}) custom-call(f32[128,768]{1,0:T(8,128)} %get-tuple-element.195.du_ref, bf16[1024,1536]{1,0:T(8,128)(2,1)} %get-tuple-element.158.kv_ref, bf16[128,768]{1,0:T(8,128)(2,1)} %get-tuple-element.159.q_ref, ...), custom_call_target="tpu_custom_call" | custom-call | tf_op jit(solution)/shard_map/last_backward/pallas_call | solution.py:524
  571.1 1.8 convert_element_type.74
  572.9 1.5 convert_element_type.75.refs_8_
  574.4 35.9 %after_back_sum.1 = (bf16[1024,768]{1,0:T(8,128)(2,1)}, f32[16,1152]{1,0:T(8,128)}) custom-call(f32[1024,768]{1,0:T(8,128)} %get-tuple-element.168.refs_0_, f32[1024,768]{1,0:T(8,128)} %get-tuple-element.169.refs_1_, f32[1024,768]{1,0:T(8,128)} %get-tuple-element.170.refs_2_, bf16[1024,3072]{1,0:T(8,128)(2,1)} %get-tuple-element.171.refs_3_, ...), custom_call_target="tpu_custom_call" | custom-call | tf_op jit(solution)/shard_map/after_back_sum/pallas_call | solution.py:592
  610.3 1.5 reshape_reshape.11.dense
  611.9 25.4 %attend_back.1 = (f32[8,768]{1,0:T(8,128)}, f32[8,768]{1,0:T(8,128)}) custom-call(bf16[1024,2304]{1,0:T(8,128)(2,1)} %get-tuple-element.148.q_ref.k_ref.v_ref, bf16[1024,2304]{1,0:T(8,128)(2,1)} %get-tuple-element.148.q_ref.k_ref.v_ref, bf16[1024,2304]{1,0:T(8,128)(2,1)} %get-tuple-element.148.q_ref.k_ref.v_ref, ...), custom_call_target="tpu_custom_call" | custom-call | tf_op jit(solution)/shard_map/attend_back/pallas_call | solution.py:658
  637.3 0.9 pad_maximum_fusion.2
  640.4 23.2 %tail.1 = (f32[8,128]{1,0:T(8,128)}, f32[8,128]{1,0:T(8,128)}) custom-call(f32[32,8,128]{2,1,0:T(8,128)} %bitcast.133, f32[24,768]{1,0:T(8,128)} %reshape_reshape.11.dense, f32[8,128]{1,0:T(8,128)} %broadcast_in_dim.81.loss), custom_call_target="tpu_custom_call" | custom-call | tf_op jit(solution)/shard_map/tail/pallas_call | solution.py:820
  663.6 1.3 fusion.24
  (143 shorter events, 19.3 us)
Async XLA Ops:
  7.2 316.1 %copy-start = (bf16[128,768]{1,0:T(8,128)(2,1)S(1)}, bf16[128,768]{1,0:T(8,128)(2,1)}, u32[]{:S(2)}) copy-start(bf16[128,768]{1,0:T(8,128)(2,1)} %param.49) | copy-start | bytes 589828
  7.2 8.9 %copy-start.13 = (bf16[2,96,768]{2,1,0:T(8,128)(2,1)S(1)}, bf16[2,96,768]{2,1,0:T(8,128)(2,1)}, u32[]{:S(2)}) copy-start(bf16[2,96,768]{2,1,0:T(8,128)(2,1)} %param.55) | copy-start | bytes 884740
  7.2 119.2 %all-gather.7.cloned.1.call-start = ((), (), s32[]{:S(2)}) async-start(), calls=%async_computation | async-start | bytes 16220160 | tf_op jit(solution)/shard_map/all_gather | solution.py:1242
  13.4 432.2 %all-gather.9.cloned.1.call-start = ((), (), s32[]{:S(2)}) async-start(), calls=%async_computation.1 | async-start | bytes 14598144 | tf_op jit(solution)/shard_map/all_gather | solution.py:1242
  16.1 115.6 %copy-start.21 = (s32[1,1024]{1,0:T(1,128)S(1)}, s32[1,1024]{1,0:T(1,128)}, u32[]{:S(2)}) copy-start(s32[1,1024]{1,0:T(1,128)} %param.42) | copy-start | bytes 12292
  16.1 116.2 %copy-start.33 = (s32[1,1024]{1,0:T(1,128)S(1)}, s32[1,1024]{1,0:T(1,128)}, u32[]{:S(2)}) copy-start(s32[1,1024]{1,0:T(1,128)} %param.41) | copy-start | bytes 12292
  16.1 116.2 %copy-start.36 = (s32[1,128]{1,0:T(1,128)S(1)}, s32[1,128]{1,0:T(1,128)}, u32[]{:S(2)}) copy-start(s32[1,128]{1,0:T(1,128)} %param.44) | copy-start | bytes 1540
  16.2 185.3 %copy-start.19 = (bf16[2,2,768,8]{2,3,1,0:T(8,128)(2,1)S(1)}, bf16[2,2,768,8]{2,3,1,0:T(8,128)(2,1)}, u32[]{:S(2)}) copy-start(bf16[2,2,768,8]{2,3,1,0:T(8,128)(2,1)} %param.59) | copy-start | bytes 147460
  129.7 221.7 %collective-permute-start = (bf16[1600,768]{1,0:T(8,128)(2,1)}, bf16[1600,768]{1,0:T(8,128)(2,1)}, u32[]{:S(2)}, u32[]{:S(2)}) collective-permute-start(bf16[1600,768]{1,0:T(8,128)(2,1)} %constant_dynamic-slice_fusion), channel_id=1, source_target_pairs={{0,16},{16,0},{1,17},{17,1},{2,18},{18,2},{3,19},{19,3},{4,20},{20... | collective-permute-start | bytes 7372808 | tf_op jit(solution)/shard_map/ppermute | solution.py:1363
  246.5 1.7 copy-start.4
  248.3 1.3 copy-start.31
  248.3 66.7 %copy-start.29 = (f32[6,768]{1,0:T(8,128)S(1)}, f32[6,768]{1,0:T(8,128)}, u32[]{:S(2)}) copy-start(f32[6,768]{1,0:T(8,128)} %param.51) | copy-start | bytes 55300
  248.3 66.7 %copy-start.30 = (f32[6,768]{1,0:T(8,128)S(1)}, f32[6,768]{1,0:T(8,128)}, u32[]{:S(2)}) copy-start(f32[6,768]{1,0:T(8,128)} %param.50) | copy-start | bytes 55300
  309.3 11.1 %copy-start.9 = (bf16[1152,768]{1,0:T(8,128)(2,1)S(1)}, bf16[1152,768]{1,0:T(8,128)(2,1)}, u32[]{:S(2)}) copy-start(bf16[1152,768]{1,0:T(8,128)(2,1)} %get-tuple-element.144) | copy-start | bytes 5308420
  322.1 1.2 copy-start.5
  324.6 5.9 copy-start.34
  325.2 66.7 %copy-start.18 = (f32[1,1024]{1,0:T(1,128)}, f32[1,1024]{1,0:T(1,128)S(1)}, u32[]{:S(2)}) copy-start(f32[1,1024]{1,0:T(1,128)S(1)} %convert_element_type.71.seg_row_ref) | copy-start | bytes 12292
  325.2 16.9 %copy-start.22 = (f32[1,768]{1,0:T(1,128)S(1)}, f32[1,768]{1,0:T(1,128)}, u32[]{:S(2)}) copy-start(f32[1,768]{1,0:T(1,128)} %get-tuple-element.217) | copy-start | bytes 9220
  335.5 11.8 %copy-start.20 = (f32[2,6144]{1,0:T(2,128)S(1)}, f32[2,6144]{1,0:T(2,128)}, u32[]{:S(2)}) copy-start(f32[2,6144]{1,0:T(2,128)} %param.56) | copy-start | bytes 147460
  335.5 13.0 %copy-start.25 = (f32[768]{0:T(1024)S(1)}, f32[768]{0:T(1024)}, u32[]{:S(2)}) copy-start(f32[768]{0:T(1024)} %get-tuple-element.220) | copy-start | bytes 9220
  335.5 13.0 %copy-start.26 = (f32[768]{0:T(1024)S(1)}, f32[768]{0:T(1024)}, u32[]{:S(2)}) copy-start(f32[768]{0:T(1024)} %get-tuple-element.237) | copy-start | bytes 9220
  338.8 11.9 %copy-start.8 = (bf16[768,128]{1,0:T(8,128)(2,1)}, bf16[768,128]{1,0:T(8,128)(2,1)S(1)}, u32[]{:S(2)}) copy-start(bf16[768,128]{1,0:T(8,128)(2,1)S(1)} %scatter.35.down_ref) | copy-start | bytes 589828
  350.7 5.3 copy-start.2
  356.0 5.4 copy-start.3
  361.4 3.6 copy-start.16
  380.5 0.8 copy-start.7
  380.5 11.4 %copy-start.6 = (bf16[128,2304]{1,0:T(8,128)(2,1)}, bf16[128,2304]{1,0:T(8,128)(2,1)S(1)}, u32[]{:S(2)}) copy-start(bf16[128,2304]{1,0:T(8,128)(2,1)S(1)} %get-tuple-element.208.adapt_ref) | copy-start | bytes 1769476
  448.0 4.1 copy-start.32
  472.9 67.2 %copy-start.10 = (bf16[128,768]{1,0:T(8,128)(2,1)S(1)}, bf16[128,768]{1,0:T(8,128)(2,1)}, u32[]{:S(2)}) copy-start(bf16[128,768]{1,0:T(8,128)(2,1)} %get-tuple-element.153.u_ref) | copy-start | bytes 589828
  472.9 69.5 %copy-start.35 = (f32[128]{0:T(128)S(1)}, f32[128]{0:T(128)}, u32[]{:S(2)}) copy-start(f32[128]{0:T(128)} %gather_fusion.1) | copy-start | bytes 1540
  611.9 25.5 %copy-start.23 = (f32[8,768]{1,0:T(8,128)S(1)}, f32[8,768]{1,0:T(8,128)}, u32[]{:S(2)}) copy-start(f32[8,768]{1,0:T(8,128)} %get-tuple-element.178) | copy-start | bytes 73732
  611.9 25.5 %copy-start.24 = (f32[8,768]{1,0:T(8,128)S(1)}, f32[8,768]{1,0:T(8,128)}, u32[]{:S(2)}) copy-start(f32[8,768]{1,0:T(8,128)} %get-tuple-element.179) | copy-start | bytes 73732
  611.9 56.0 %copy-start.1 = (bf16[128,768]{1,0:T(8,128)(2,1)S(1)}, bf16[128,768]{1,0:T(8,128)(2,1)}, u32[]{:S(2)}) copy-start(bf16[128,768]{1,0:T(8,128)(2,1)} %param.49) | copy-start | bytes 589828
  637.2 29.2 %copy-start.11 = (f32[24,768]{1,0:T(8,128)S(1)}, f32[24,768]{1,0:T(8,128)}, u32[]{:S(2)}) copy-start(f32[24,768]{1,0:T(8,128)} %reshape_reshape.11.dense) | copy-start | bytes 221188
  637.2 29.2 %copy-start.12 = (f32[24,768]{1,0:T(8,128)S(1)}, f32[24,768]{1,0:T(8,128)}, u32[]{:S(2)}) copy-start(f32[24,768]{1,0:T(8,128)} %param.63) | copy-start | bytes 221188
  637.3 29.2 %copy-start.14 = (f32[24,768]{1,0:T(8,128)S(1)}, f32[24,768]{1,0:T(8,128)}, u32[]{:S(2)}) copy-start(f32[24,768]{1,0:T(8,128)} %param.65) | copy-start | bytes 221188
  637.3 29.2 %copy-start.15 = (f32[24,768]{1,0:T(8,128)S(1)}, f32[24,768]{1,0:T(8,128)}, u32[]{:S(2)}) copy-start(f32[24,768]{1,0:T(8,128)} %param.64) | copy-start | bytes 221188
  637.3 29.9 %copy-start.17 = (f32[2,2,8,24]{3,2,1,0:T(8,128)S(1)}, f32[2,2,8,24]{3,2,1,0:T(8,128)}, u32[]{:S(2)}) copy-start(f32[2,2,8,24]{3,2,1,0:T(8,128)} %param.60) | copy-start | bytes 9220
  637.3 29.9 %copy-start.27 = (f32[2,2,8,24]{3,2,1,0:T(8,128)S(1)}, f32[2,2,8,24]{3,2,1,0:T(8,128)}, u32[]{:S(2)}) copy-start(f32[2,2,8,24]{3,2,1,0:T(8,128)} %param.62) | copy-start | bytes 9220
  637.3 29.9 %copy-start.28 = (f32[2,2,8,24]{3,2,1,0:T(8,128)S(1)}, f32[2,2,8,24]{3,2,1,0:T(8,128)}, u32[]{:S(2)}) copy-start(f32[2,2,8,24]{3,2,1,0:T(8,128)} %param.61) | copy-start | bytes 9220
Sparse Core Ops, SparseCore 0:
  13.6 112.7 all-gather.6
  129.3 116.7 all-gather.8

commit v4 on v3

--- a/solution.py
+++ b/solution.py
@@ -107,8 +107,17 @@
     )
 
 
-def project_body(x_ref, down_ref, w_ref, up_ref, bias_ref, out_ref, mid_ref):
-    low = x_ref[...].astype(BF)
+def project_body(
+    own_ref, got_ref, mine_ref, spot_ref, spots_ref, norm_ref, down_ref, w_ref, up_ref, bias_ref,
+    out_ref, mid_ref, x_ref,
+):
+    choose = lax.broadcasted_iota(jnp.int32, (own_ref.shape[0], spots_ref.shape[0]), 1) == spot_ref[...]
+    summed = jnp.where(
+        mine_ref[...] > 0, own_ref[...].astype(F32), got_ref[...].astype(F32)
+    ) + mm(choose.astype(F32).astype(BF), spots_ref[...])
+    x = layer_norm(summed, norm_ref[0:1, :], norm_ref[1:2, :])
+    x_ref[...] = x
+    low = x.astype(BF)
     mid = mm(low, down_ref[...]).astype(BF)
     mid_ref[...] = mid
     total = w_ref.shape[0]
@@ -120,31 +129,25 @@
         ).astype(BF)
 
 
-def project(x, down, w, up, bias):
-    rows, width = x.shape
+def project(own, got, mine, spot, spots, norms, down, w, up, bias):
+    rows, width = mine.shape[0], own.shape[1]
     tile = split_of(rows, 256, 16)
     total = w.shape[0]
+    row = lambda n: pl.BlockSpec((tile, n), lambda i: (i, 0))
     return pl.pallas_call(
         project_body,
         grid=(rows // tile,),
-        in_specs=[
-            pl.BlockSpec((tile, width), lambda i: (i, 0)),
-            full(down.shape),
-            full(w.shape),
-            full(up.shape),
-            full(bias.shape),
-        ],
-        out_specs=[
-            pl.BlockSpec((tile, total), lambda i: (i, 0)),
-            pl.BlockSpec((tile, down.shape[1]), lambda i: (i, 0)),
-        ],
+        in_specs=[row(width), row(width), row(1), row(1)]
+        + [full(a.shape) for a in (spots, norms, down, w, up, bias)],
+        out_specs=[row(total), row(down.shape[1]), row(width)],
         out_shape=[
             jax.ShapeDtypeStruct((rows, total), BF),
             jax.ShapeDtypeStruct((rows, down.shape[1]), BF),
+            jax.ShapeDtypeStruct((rows, width), F32),
         ],
         compiler_params=params(),
         name="project",
-    )(x, down, w, up, bias)
+    )(own, got, mine, spot, spots, norms, down, w, up, bias)
 
 
 def attend_body(q_ref, k_ref, v_ref, seg_ref, seg_row_ref, ctx_ref, log_ref):
@@ -739,53 +742,291 @@
         direct_copy(piece_of((me + k) % shards), buffer.at[me], sends, receives, me, k, shards).wait_send()
 
 
+def relative_places(order):
+    places = [
+        {"x": dx, "z": dz, "y": dy} for dx in (0, 1) for dz in range(-3, 4) for dy in (0, 1)
+    ]
+    return sorted(places, key=lambda p: (abs(p["x"]) + abs(p["z"]) + abs(p["y"]), [abs(p[a]) for a in order]))
+
+
+class Gather:
+    def __init__(self, chunk, full_buffer, start, rows, order, sends, receives, hands, hands_got):
+        self.chunk, self.full, self.order = chunk, full_buffer, order
+        self.part = pl.ds(start, rows)
+        self.sends, self.receives, self.hands, self.hands_got = sends, receives, hands, hands_got
+        self.here = position()
+        self.items = relative_places(order)
+        self.pending = []
+
+    def origin(self, item):
+        here = self.here
+        return {"x": (here["x"] + item["x"]) % 2, "z": here["z"] - item["z"], "y": (here["y"] + item["y"]) % 2, "c": here["c"]}
+
+    def key(self, place):
+        return (place["x"] * 4 + place["z"]) * 2 + place["y"]
+
+    def outward(self, item):
+        deepest = max([k for k, axis in enumerate(self.order) if item[axis]], default=-1)
+        ways = []
+        if deepest >= 0 and self.order[deepest] == "z":
+            ways.append(("z", 1 if item["z"] > 0 else -1))
+        for axis in self.order[deepest + 1 :]:
+            ways += [("z", 1), ("z", -1)] if axis == "z" else [(axis, 1)]
+        return ways
+
+    def copy(self, index, way, slot, item):
+        here = self.here
+        place = self.origin(item)
+        number, key = number_of(place), self.key(place)
+        mine = not any(item.values())
+        source = self.chunk.at[self.part, :] if mine else self.full.at[number, self.part, :]
+        if way is None:
+            target = dict(here, c=1 - here["c"])
+            sends, receives = self.hands.at[index], self.hands_got.at[key]
+        else:
+            axis, step = way
+            target = dict(here)
+            target[axis] = here["z"] + step if axis == "z" else 1 - here[axis]
+            sends, receives = self.sends.at[index * 4 + slot], self.receives.at[key]
+        return pltpu.make_async_remote_copy(
+            src_ref=source,
+            dst_ref=self.full.at[number, self.part, :],
+            send_sem=sends,
+            recv_sem=receives,
+            device_id=device_of(target),
+            device_id_type=MESH,
+        )
+
+    def valid(self, item):
+        z = self.here["z"] - item["z"]
+        return (z >= 0) & (z <= 3)
+
+    def step(self, index):
+        item = self.items[index]
+
+        @pl.when(self.valid(item))
+        def _():
+            if any(item.values()):
+                self.arrived(index, item)
+            for slot, way in enumerate(self.outward(item)):
+                self.when_way(way, lambda way=way, slot=slot: self.copy(index, way, slot, item).start())
+            self.copy(index, None, 0, item).start()
+
+    def when_way(self, way, act):
+        axis, step = way
+        if axis == "z":
+            z = self.here["z"] + step
+            pl.when((z >= 0) & (z <= 3))(act)
+        else:
+            act()
+
+    def arrived(self, index, item):
+        place = self.origin(item)
+        spot = self.full.at[number_of(place), self.part, :]
+        pltpu.make_async_remote_copy(
+            src_ref=spot,
+            dst_ref=spot,
+            send_sem=self.sends.at[index * 4],
+            recv_sem=self.receives.at[self.key(place)],
+            device_id=device_of(dict(self.here, c=1 - self.here["c"])),
+            device_id_type=MESH,
+        ).wait_recv()
+
+    def finish(self):
+        for index, item in enumerate(self.items):
+
+            @pl.when(self.valid(item))
+            def _(index=index, item=item):
+                for slot, way in enumerate(self.outward(item)):
+                    self.when_way(way, lambda way=way, slot=slot: self.copy(index, way, slot, item).wait_send())
+                self.copy(index, None, 0, item).wait_send()
+                place = dict(self.origin(item), c=1 - self.here["c"])
+                spot = self.full.at[number_of(place), self.part, :]
+                pltpu.make_async_remote_copy(
+                    src_ref=spot,
+                    dst_ref=spot,
+                    send_sem=self.hands.at[index],
+                    recv_sem=self.hands_got.at[self.key(place)],
+                    device_id=device_of(dict(self.here, c=1 - self.here["c"])),
+                    device_id_type=MESH,
+                ).wait_recv()
+
+
+ITEMS = 28
+
+
+ITEMS = 28
+PICK = 64
+GROUP = 16
+
+
 def start_body(
-    shards, rows, note, bias, got, notes, biases,
-    row_sems, note_sends, note_gets, bias_sends, bias_gets, own_sems,
+    streams, shards, ids, low_ref, groups_any, table_any, chunk, note, bias,
+    full_chunk, own_rows, got, notes, biases, e_out, et_out,
+    table, stage, rows, e_ref, et_ref,
+    sends, receives, hands, hands_got, row_sends, row_gets, note_sends, note_gets, bias_sends, bias_gets,
+    own_sems, e_sems, out_sems,
 ):
     here = position()
     me = number_of(here)
+    across = device_of(dict(here, x=1 - here["x"]))
+    slice_rows = e_ref.shape[0] // 2
+    half = own_rows.shape[0]
+    batches = half // PICK
+    fill = pltpu.make_async_copy(groups_any, table, own_sems.at[3])
+    fill.start()
     greet_all(shards)
-    own_note = pltpu.make_async_copy(note, notes.at[me], own_sems.at[0])
-    own_note.start()
-    own_bias = pltpu.make_async_copy(bias, biases.at[me], own_sems.at[1])
-    own_bias.start()
-    await_all(shards)
-    across = pltpu.make_async_remote_copy(
-        src_ref=rows,
-        dst_ref=got,
-        send_sem=row_sems.at[0],
-        recv_sem=row_sems.at[1],
-        device_id=device_of(dict(here, x=1 - here["x"])),
+    plain = [
+        pltpu.make_async_copy(source, target, own_sems.at[k])
+        for k, (source, target) in enumerate(
+            ((chunk, full_chunk.at[me]), (note, notes.at[me]), (bias, biases.at[me]))
+        )
+    ]
+    for copy in plain:
+        copy.start()
+    own_slice = table_any.at[
+        pl.ds(pl.multiple_of((me % 16) * slice_rows, 16), slice_rows), :
+    ]
+    keep = pltpu.make_async_copy(own_slice, e_ref.at[pl.ds(0, slice_rows), :], own_sems.at[4])
+    keep.start()
+    swap = pltpu.make_async_remote_copy(
+        src_ref=own_slice,
+        dst_ref=e_ref.at[pl.ds(slice_rows, slice_rows), :],
+        send_sem=e_sems.at[0],
+        recv_sem=e_sems.at[1],
+        device_id=across,
         device_id_type=MESH,
     )
-    across.start()
+    await_all(shards)
+    gathers = [
+        Gather(
+            chunk, full_chunk, start, size, order, sends.at[k], receives.at[k], hands.at[k], hands_got.at[k]
+        )
+        for k, (start, size, order) in enumerate(streams)
+    ]
+    for gather in gathers:
+        gather.step(0)
     spread(lambda peer: note, notes, note_sends, note_gets, me, shards)
     spread(lambda peer: bias, biases, bias_sends, bias_gets, me, shards)
+    swap.start()
+
+    def send_rows(b):
+        part = pl.ds(b * PICK, PICK)
+        return pltpu.make_async_remote_copy(
+            src_ref=rows.at[part, :],
+            dst_ref=got.at[part, :],
+            send_sem=row_sends.at[b],
+            recv_sem=row_gets.at[b],
+            device_id=across,
+            device_id_type=MESH,
+        )
+
+    def pick(b):
+        def one(t, carry):
+            stage[t] = table[ids[b * PICK + t]]
+            return carry
+
+        lax.fori_loop(0, PICK, one, 0, unroll=8)
+        choose = (
+            lax.broadcasted_iota(jnp.int32, (PICK, PICK * GROUP), 1)
+            == low_ref[b * PICK : (b + 1) * PICK, :]
+        )
+        rows[b * PICK : (b + 1) * PICK, :] = mm(choose.astype(F32).astype(BF), flat(stage)).astype(BF)
+        if b < batches:
+            send_rows(b).start()
+
+    def turn(k):
+        part = slice(k * 128, (k + 1) * 128)
+        et_ref[:, part] = e_ref[part, :].astype(F32).T.astype(BF)
+
+    def out_copies():
+        return (
+            pltpu.make_async_copy(e_ref, e_out, out_sems.at[0]),
+            pltpu.make_async_copy(et_ref, et_out, out_sems.at[1]),
+            pltpu.make_async_copy(rows.at[pl.ds(half, half), :], own_rows, out_sems.at[2]),
+        )
+
+    fill.wait()
+    done, turned = 0, 0
+    own_turns = slice_rows // 128
+    for index in range(1, ITEMS):
+        while done < 2 * batches and done < index * 3:
+            pick(done)
+            done += 1
+        if done == 2 * batches and turned < own_turns:
+            if turned == 0:
+                keep.wait()
+            turn(turned)
+            turned += 1
+        for gather in gathers:
+            gather.step(index)
+    swap.wait_recv()
+    for k in range(turned, e_ref.shape[0] // 128):
+        turn(k)
+    copies = out_copies()
+    for copy in copies:
+        copy.start()
+    for gather in gathers:
+        gather.finish()
     collect(lambda peer: note, notes, note_sends, note_gets, me, shards)
     collect(lambda peer: bias, biases, bias_sends, bias_gets, me, shards)
-    across.wait()
-    own_note.wait()
-    own_bias.wait()
-
-
-def start_exchange(rows, note, bias, shards):
+    for b in range(batches):
+        send_rows(b).wait()
+    swap.wait_send()
+    for copy in plain:
+        copy.wait()
+    for copy in copies:
+        copy.wait()
+
+
+def start_exchange(ids, low, table, chunk, note, bias, shards, slice_rows):
     anywhere = pl.BlockSpec(memory_space=pl.ANY)
+    cut = (chunk.shape[0] * 5 // 6 + 15) // 16 * 16
+    streams = ((0, cut, "xzy"), (cut, chunk.shape[0] - cut, "xyz"))
+    half = ids.shape[0] // 2
+    hidden = table.shape[1]
     shape = jax.ShapeDtypeStruct
     sems = pltpu.SemaphoreType.DMA
     return pl.pallas_call(
-        functools.partial(start_body, shards),
-        in_specs=[anywhere] * 3,
-        out_specs=[anywhere] * 3,
+        functools.partial(start_body, streams, shards),
+        in_specs=[
+            pl.BlockSpec(memory_space=pltpu.SMEM),
+            pl.BlockSpec(memory_space=pltpu.VMEM),
+        ]
+        + [anywhere] * 5,
+        out_specs=[anywhere] * 7,
         out_shape=[
-            shape(rows.shape, rows.dtype),
+            shape((shards, *chunk.shape), chunk.dtype),
+            shape((half, hidden), table.dtype),
+            shape((half, hidden), table.dtype),
             shape((shards, *note.shape), note.dtype),
             shape((shards, *bias.shape), bias.dtype),
+            shape((2 * slice_rows, hidden), table.dtype),
+            shape((hidden, 2 * slice_rows), table.dtype),
         ],
-        scratch_shapes=[sems((2,))] + [sems((shards,))] * 4 + [sems((2,))],
+        scratch_shapes=[
+            pltpu.VMEM((table.shape[0] // GROUP, GROUP, hidden), BF),
+            pltpu.VMEM((PICK, GROUP, hidden), BF),
+            pltpu.VMEM((2 * half, hidden), BF),
+            pltpu.VMEM((2 * slice_rows, hidden), BF),
+            pltpu.VMEM((hidden, 2 * slice_rows), BF),
+            sems((2, 4 * ITEMS)),
+            sems((2, 16)),
+            sems((2, ITEMS)),
+            sems((2, 16)),
+            sems((half // PICK,)),
+            sems((half // PICK,)),
+            sems((shards,)),
+            sems((shards,)),
+            sems((shards,)),
+            sems((shards,)),
+            sems((5,)),
+            sems((2,)),
+            sems((3,)),
+        ],
         compiler_params=params(collective_id=1, has_side_effects=True),
         name="start_exchange",
-    )(rows, note, bias)
+    )(ids, low, table.reshape(-1, GROUP, hidden), table, chunk, note, bias)
 
 
 def tail_body(shards, parts, dense, loss, total_ref, sums_ref, got, note, notes, send_a, get_a, send_b, get_b):
@@ -1235,40 +1476,49 @@
     wanted = jnp.concatenate([input_token_index[0], label_target_token[0]])
     dp_count = lax.axis_size("dp")
     group_ids = lax.all_gather(wanted, "dp", axis=0, tiled=False) - dp_index * table_rows
-    gathered = []
-    for chunk in chunks:
-        if gathered:
-            chunk, gathered[-1] = lax.optimization_barrier((chunk, gathered[-1]))
-        gathered.append(lax.all_gather(chunk, BOTH, axis=0, tiled=False))
-    first_full = gathered[0]
-
-    def look(ids):
-        inside = (ids >= 0) & (ids < table_rows)
-        found = embed[jnp.clip(ids, 0, table_rows - 1)]
-        return jnp.where(inside[:, None], found, jnp.zeros((), BF)), inside
-
+    later_full = [lax.all_gather(chunk, BOTH, axis=0, tiled=False) for chunk in chunks[1:]]
+    inside = (group_ids >= 0) & (group_ids < table_rows)
+    group_ids = jnp.clip(group_ids, 0, table_rows - 1)
+    mine = lax.dynamic_index_in_dim(inside, dp_index, 0, keepdims=False)
     task_range = jnp.arange(TASKS, dtype=jnp.int32)
     slice_rows = vocabulary_bias.shape[0]
     if grouped:
         pair_ids = jnp.concatenate(
             [
-                lax.dynamic_index_in_dim(group_ids, 1 - dp_index, 0, keepdims=False),
-                lax.dynamic_index_in_dim(group_ids, dp_index, 0, keepdims=False),
+                lax.dynamic_index_in_dim(group_ids, (dp_index + shift) % 2, 0, keepdims=False)
+                for shift in (1, 0)
             ]
         )
-        looked, inside = look(pair_ids)
+        low_ids = jnp.arange(pair_ids.size, dtype=jnp.int32) % PICK * GROUP + pair_ids % GROUP
         note = jnp.broadcast_to(sequence_task_index.astype(F32)[:, None], (8, 128))
         bias_rows = -(-slice_rows // 1024) * 8
         bias_block = jnp.pad(vocabulary_bias, (0, bias_rows * 128 - slice_rows)).reshape(bias_rows, 128)
-        got, notes, biases = start_exchange(looked[: wanted.size], note, bias_block, shards)
-        rows = jnp.where(inside[wanted.size :, None], looked[wanted.size :], got)
+        first_full, own_rows, got, notes, biases, own_vocab, own_turned = start_exchange(
+            pair_ids // GROUP, low_ids[:, None], embed, chunks[0], note, bias_block, shards, slice_rows
+        )
         every_task = notes[:, 0, 0].astype(jnp.int32)
         all_bias = biases.reshape(shards, -1)[:, :slice_rows].reshape(-1)
     else:
-        looked, inside = look(group_ids.reshape(-1))
-        rows = lax.psum_scatter(looked, "dp", scatter_dimension=0, tiled=True)
+        first_full = lax.all_gather(chunks[0], BOTH, axis=0, tiled=False)
+        looked = jnp.where(
+            inside.reshape(-1)[:, None], embed[group_ids.reshape(-1)], jnp.zeros((), BF)
+        )
+        own_rows = got = lax.psum_scatter(looked, "dp", scatter_dimension=0, tiled=True)
+        own_slice = lax.dynamic_slice_in_dim(embed, fsdp_index * slice_rows, slice_rows, 0)
+        own_vocab = jnp.concatenate(
+            [own_slice]
+            + [
+                lax.ppermute(
+                    own_slice, "dp", [(k, (k + shift) % dp_count) for k in range(dp_count)]
+                )
+                for shift in range(1, dp_count)
+            ],
+            0,
+        )
+        own_turned = own_vocab.T
         every_task = lax.all_gather(sequence_task_index, BOTH, axis=0, tiled=True)
         all_bias = lax.all_gather(vocabulary_bias, BOTH, axis=0, tiled=True)
+    gathered = [first_full, *later_full]
     counts = labels * jnp.sum((every_task[:, None] == task_range[None, :]).astype(F32), 0)
     task_hot = (sequence_task_index[:, None] == task_range[None, :]).astype(F32)
     row_weight = jnp.sum(task_hot[0] * (task_loss_weight / jnp.maximum(counts, 1.0)))
@@ -1293,20 +1543,25 @@
         .transpose(1, 2, 3, 0, 4)
         .reshape(layers, 2, rank, hidden)
     )
+    blank = jnp.zeros((rank, hidden), BF)
     adapters = [
-        jnp.zeros((128, 3 * hidden), BF)
-        .at[:rank, :hidden]
-        .set(2 * ups_full[layer, 0])
-        .at[rank : 2 * rank, 2 * hidden :]
-        .set(2 * ups_full[layer, 1])
+        jnp.pad(
+            jnp.concatenate(
+                [
+                    jnp.concatenate([2 * ups_full[layer, 0], blank, blank], 1),
+                    jnp.concatenate([blank, blank, 2 * ups_full[layer, 1]], 1),
+                ],
+                0,
+            ),
+            ((0, 128 - 2 * rank), (0, 0)),
+        )
         for layer in range(layers)
     ]
     downs = [
-        jnp.zeros((hidden, 128), BF)
-        .at[:, :rank]
-        .set(adapter_down_matrix[layer, 0])
-        .at[:, rank : 2 * rank]
-        .set(adapter_down_matrix[layer, 1])
+        jnp.pad(
+            jnp.concatenate([adapter_down_matrix[layer, 0], adapter_down_matrix[layer, 1]], 1),
+            ((0, 0), (0, 128 - 2 * rank)),
+        )
         for layer in range(layers)
     ]
     bias_of = []
@@ -1338,33 +1593,15 @@
         for layer in range(layers)
     ]
 
-    target_rows = rows[tokens:].astype(F32)
+    target_rows = jnp.where(mine[tokens:, None], own_rows[tokens:], got[tokens:]).astype(F32)
     segments = sentence_numbers[0]
-    place_hot = (
-        seg_positions(segments)[:, None]
-        == jnp.arange(position_embedding.shape[0], dtype=jnp.int32)[None, :]
-    ).astype(BF)
-    hidden_rows = layer_norm(
-        rows[:tokens].astype(F32)
-        + jnp.dot(place_hot, position_embedding, preferred_element_type=F32),
-        norm_gain_vector[0],
-        norm_bias_vector[0],
-    )
+    spot = seg_positions(segments)[:, None]
     seg_real = segments.astype(F32)
     seg_wide = jnp.broadcast_to(seg_real[:, None], (tokens, 128))
     seg_row = seg_real[None, :]
     place_row = label_positions
     place_col = jnp.broadcast_to(label_positions.reshape(labels, 1), (labels, 128))
 
-    own_slice = lax.dynamic_slice_in_dim(embed, fsdp_index * slice_rows, slice_rows, 0)
-    own_vocab = jnp.concatenate(
-        [own_slice]
-        + [
-            lax.ppermute(own_slice, "dp", [(k, (k + shift) % dp_count) for k in range(dp_count)])
-            for shift in range(1, dp_count)
-        ],
-        0,
-    )
     own_bias = jnp.concatenate(
         [
             lax.dynamic_slice_in_dim(
@@ -1378,13 +1615,16 @@
     )
     vocab_block = (
         own_vocab,
-        own_vocab.T,
+        own_turned,
         jnp.broadcast_to(own_bias[:, None], (own_bias.shape[0], 128)),
     )
     target_bias = all_bias[label_target_token[0]]
-    hidden_rows, vocab_block = lax.optimization_barrier((hidden_rows, vocab_block))
-
-    qkv, mid = project(hidden_rows, downs[0], in_weights[0], adapters[0], bias_of[0][0])
+
+    first_norm = jnp.concatenate([norm_gain_vector[:1], norm_bias_vector[:1]], 0)
+    qkv, mid, hidden_rows = project(
+        own_rows, got, mine[:tokens, None].astype(jnp.int32), spot, position_embedding, first_norm,
+        downs[0], in_weights[0], adapters[0], bias_of[0][0],
+    )
     context, logs = attend(qkv, seg_wide, seg_row)
     x_last, one, two, slope = after(
         context, hidden_rows, out_weights[0], *slabs[0], *bias_of[0][1:], norms_of[0]

time: 687 us -> 517 us (0.75)
  Pallas kernels: 315 us -> 427 us
  waiting for transfers between devices: 109 us -> 0.02 us
  local copies, waits for them, and re-layouts: 121 us -> 42.5 us
  blocking collectives: 69 us -> 5.37 us
  other arithmetic: 39.1 us -> 16.8 us
    pallas_call x2, Pallas kernels: 69.1 us -> 179 us  [the longest x1 166 us: start_exchange(): pl.pallas_call(functools.partial(start_body, streams, shards), in_specs=[...]
    all_gather x2 -> x1, waiting for transfers between devices: 109 us -> 0.01 us  [per_device(): lax.all_gather(chunk, BOTH, axis=0, tiled=False)]
    all_gather x1, blocking collectives: 69 us -> 5.37 us  [per_device(): lax.all_gather(wanted, 'dp', axis=0, tiled=False) - dp_index * table_rows]
    gather x1 -> x0, local copies, waits for them, and re-layouts: 41.4 us -> none  [look(): found = embed[jnp.clip(ids, 0, table_rows - 1)]]
    unnamed x83 -> x64, local copies, waits for them, and re-layouts: 13.8 us -> 0.94 us
    scatter x6 -> x0, local copies, waits for them, and re-layouts: 9.27 us -> none  [the longest x4 9.18 us: per_device(): downs = [jnp.zeros((hidden, 128), BF).at[:, :rank].set(adapter_down_matri...]
    optimization_barrier x1 -> x0, local copies, waits for them, and re-layouts: 7.65 us -> none  [per_device(): lax.optimization_barrier((hidden_rows, vocab_block))]
  transfers between devices with their start and end apart: 3 -> 1, of which waited for: 1 -> 0; matrix products, arithmetic and copies ran while one was open for 19% -> 6% of each run, Pallas kernels for 18% -> 45%
where the time goes in v4:
time: 517 us; the launch traced here: 511 us
  Pallas kernels  427 us (83%)
  local copies, waits for them, and re-layouts  42.5 us (8%)
  between operations  19.5 us (4%)
  other arithmetic  16.8 us (3%)
  blocking collectives  5.37 us (1%)
    pallas_call x1, Pallas kernels, start_exchange(): pl.pallas_call(functools.partial(start_body, streams, shards), in_specs=[...  166 us
    pallas_call x1, Pallas kernels, head(): pl.pallas_call(head_body, in_specs=[whole] + [anywhere] * 3, out_specs=[w...  67 us
    pallas_call x1, Pallas kernels, after_back_sum(): pl.pallas_call(functools.partial(after_back_sum_body, shards), grid=(rows...  36.7 us
    pallas_call x1, Pallas kernels, after(): pl.pallas_call(after_body, grid=(rows // tile,), in_specs=[row(width), ro...  29.2 us
    pallas_call x1, Pallas kernels, last_backward(): pl.pallas_call(functools.partial(last_backward_body, places=(up[1], dn[1]...  26.2 us
    pallas_call x1, Pallas kernels, attend_back(): pl.pallas_call(attend_back_body, grid=(pairs,), in_specs=[column(0), colu...  25.4 us
    pallas_call x1, Pallas kernels, tail(): pl.pallas_call(functools.partial(tail_body, shards), in_specs=[whole] * 3...  23.1 us
    pallas_call x1, Pallas kernels, attend(): pl.pallas_call(attend_body, grid=(pairs,), in_specs=[column(0), column(1)...  20.2 us
  transfers between devices with their start and end apart: 1, of which 0 were waited for; matrix products, arithmetic and copies ran while one was open for 6% of the time, Pallas kernels for 45%

profile of v4, /device:TPU:0, one launch (start us, length us, event | category | flops | bytes accessed | tf_op | source)
XLA Modules:
  0.0 511.4 jit_solution(14074344636641308860)
XLA Ops:
  7.2 0.9 slice_bitcast_fusion
  8.2 0.9 slice_bitcast_fusion.1
  9.1 0.9 slice_bitcast_fusion.2
  10.0 0.8 slice_bitcast_fusion.3
  10.8 0.8 pad_maximum_fusion
  11.7 5.4 %all-gather.2 = s32[2,1,1152]{2,1,0:T(1,128)S(1)} all-gather(s32[1,1,1152]{2,1,0:T(1,128)S(1)} %reshape.381), channel_id=2, replica_groups=mesh['dp'=2,'fsdp'=16] {'dp'}, dimensions={0}, use_global_device_ids=true | all-gather | bytes 13824 | tf_op jit(solution)/shard_map/all_gather | solution.py:1478
  17.2 0.4 copy.64
  17.6 0.5 copy.67
  19.1 0.8 pad.30.chunk
  19.9 0.6 pad_bitcast_fusion.1.bias
  20.5 0.6 add_select_fusion.2.ids
  21.1 1.6 fusion.1.low_ref
  22.8 0.6 broadcast_in_dim.29.note
  23.4 166.4 %start_exchange.1 = (bf16[32,320,768]{2,1,0:T(8,128)(2,1)}, bf16[1152,768]{1,0:T(8,128)(2,1)}, bf16[1152,768]{1,0:T(8,128)(2,1)}, f32[32,8,128]{2,1,0:T(8,128)},...) custom-call(s32[2304]{0:T(1024)} %add_select_fusion.2.ids, ...), custom_call_target="tpu_custom_call" | custom-call | tf_op jit(solution)/shard_map/start_exchange/pallas_call | solution.py:990
  189.7 4.0 slice.204
  193.7 1.2 slice_reduce_fusion
  194.9 0.4 reshape_reshape.9
  195.4 0.3 reshape.351
  195.8 0.9 pad.35.adapt_ref
  196.7 0.9 pad.33.up_ref
  197.6 1.0 copy.71.mine_ref
  198.9 0.7 pad.32.down_ref
  200.8 0.7 pad.34.down_ref
  201.5 0.6 broadcast_in_dim.34.hbias_ref
  203.1 0.6 pad_maximum_fusion.7.norm_ref
  203.7 0.6 fusion.30
  204.4 0.9 iota_subtract_fusion.spot_ref
  205.2 0.6 pad_maximum_fusion.6
  205.8 13.0 %project.1 = (bf16[1024,2304]{1,0:T(8,128)(2,1)}, bf16[1024,128]{1,0:T(8,128)(2,1)}, f32[1024,768]{1,0:T(8,128)}) custom-call(bf16[1152,768]{1,0:T(8,128)(2,1)} %get-tuple-element.47.own_ref, bf16[1152,768]{1,0:T(8,128)(2,1)} %get-tuple-element.48.got_ref, s32[1024,1]{1,0:T(8,128)} %copy.71.mine_ref, s32[1024,1]{1,0:T(8,128)} %iota_subtract_fusion.spot_ref, ...), custom_call_target="tpu_custom_call" | custom-call | tf_op jit(solution)/shard_map/project/pallas_call | solution.py:137
  218.9 1.0 broadcast_in_dim.31.seg_ref
  219.9 20.2 %attend.1 = (bf16[1024,768]{1,0:T(8,128)(2,1)}, f32[6,1,2048]{2,1,0:T(1,128)}) custom-call(bf16[1024,2304]{1,0:T(8,128)(2,1)} %get-tuple-element.50.q_ref.k_ref.v_ref, bf16[1024,2304]{1,0:T(8,128)(2,1)} %get-tuple-element.50.q_ref.k_ref.v_ref, bf16[1024,2304]{1,0:T(8,128)(2,1)} %get-tuple-element.50.q_ref.k_ref.v_ref, f32[1024,128]{1,0:T(8,128)} %broadcast_in_dim.31.seg_ref, ...), custom_call_target="tpu_custom_call" | custom-call | tf_op jit(solution)/shard_map/attend/pallas_call | solution.py:177
  240.1 1.1 gather_fusion
  241.3 0.6 concatenate.98.norm_ref.refs_7_
  241.9 0.6 concatenate.105.norm_ref
  242.5 3.2 fusion.28
  245.8 0.6 fusion.31
  246.4 29.2 %after.1 = (f32[1024,768]{1,0:T(8,128)}, f32[1024,768]{1,0:T(8,128)}, f32[1024,768]{1,0:T(8,128)}, bf16[1024,3072]{1,0:T(8,128)(2,1)}) custom-call(bf16[1024,768]{1,0:T(8,128)(2,1)} %get-tuple-element.52.ctx_ref, f32[1024,768]{1,0:T(8,128)} %get-tuple-element.53.x_ref, bf16[768,768]{1,0:T(8,128)(2,1)} %bitcast.118, ...), custom_call_target="tpu_custom_call" | custom-call | tf_op jit(solution)/shard_map/after/pallas_call | solution.py:244
  275.6 1.6 convert_reduce_fusion
  277.5 0.6 fusion.23
  278.1 4.1 slice.254
  282.2 2.4 slice.257
  284.6 0.7 broadcast_in_dim.33.place_ref
  285.3 20.1 %last_forward.1 = (bf16[1024,1536]{1,0:T(8,128)(2,1)}, bf16[128,768]{1,0:T(8,128)(2,1)}, bf16[1024,128]{1,0:T(8,128)(2,1)}, f32[6,256]{1,0:T(8,128)}, f32[128,76...) custom-call(f32[1024,768]{1,0:T(8,128)} %get-tuple-element.54.x_ref,, ...), custom_call_target="tpu_custom_call" | custom-call | tf_op jit(solution)/shard_map/last_forward/pallas_call | solution.py:360
  305.4 1.7 broadcast_in_dim.64.bias_any
  307.0 67.0 %head.1 = (f32[768,128]{1,0:T(8,128)}, f32[1,128]{1,0:T(1,128)}) custom-call(bf16[128,768]{1,0:T(8,128)(2,1)} %get-tuple-element.55.u_ref, bf16[3200,768]{1,0:T(8,128)(2,1)} %get-tuple-element.56.e_any, bf16[768,3200]{1,0:T(8,128)(2,1)} %get-tuple-element.57.et_any, f32[3200,128]{1,0:T(8,128)} %broadcast_in_dim.64.bias_any), custom_call_target="tpu_custom_call" | custom-call | tf_op jit(solution)/shard_map/head/pallas_call | solution.py:1356
  374.0 1.2 copy.73
  375.2 2.6 fusion.7
  377.8 0.6 fusion.25
  379.7 26.2 %last_backward.1 = (f32[1024,768]{1,0:T(8,128)}, f32[768,768]{1,0:T(8,128)}, f32[8,768]{1,0:T(8,128)}, f32[8,768]{1,0:T(8,128)}) custom-call(f32[128,768]{1,0:T(8,128)} %get-tuple-element.101.du_ref, bf16[1024,1536]{1,0:T(8,128)(2,1)} %get-tuple-element.60.kv_ref, bf16[128,768]{1,0:T(8,128)(2,1)} %get-tuple-element.61.q_ref, ...), custom_call_target="tpu_custom_call" | custom-call | tf_op jit(solution)/shard_map/last_backward/pallas_call | solution.py:527
  405.9 1.8 convert_element_type.82
  407.7 1.6 convert_element_type.83.refs_8_
  409.2 36.7 %after_back_sum.1 = (bf16[1024,768]{1,0:T(8,128)(2,1)}, f32[16,1152]{1,0:T(8,128)}) custom-call(f32[1024,768]{1,0:T(8,128)} %get-tuple-element.70.refs_0_, f32[1024,768]{1,0:T(8,128)} %get-tuple-element.71.refs_1_, f32[1024,768]{1,0:T(8,128)} %get-tuple-element.72.refs_2_, bf16[1024,3072]{1,0:T(8,128)(2,1)} %get-tuple-element.73.refs_3_, ...), custom_call_target="tpu_custom_call" | custom-call | tf_op jit(solution)/shard_map/after_back_sum/pallas_call | solution.py:595
  445.9 25.4 %attend_back.1 = (f32[8,768]{1,0:T(8,128)}, f32[8,768]{1,0:T(8,128)}) custom-call(bf16[1024,2304]{1,0:T(8,128)(2,1)} %get-tuple-element.50.q_ref.k_ref.v_ref, bf16[1024,2304]{1,0:T(8,128)(2,1)} %get-tuple-element.50.q_ref.k_ref.v_ref, bf16[1024,2304]{1,0:T(8,128)(2,1)} %get-tuple-element.50.q_ref.k_ref.v_ref, bf16[1024,768]{1,0:T(8,128)(2,1)} %get-tuple-element.75.dctx_ref, ...), custom_call_target="tpu_custom_call" | custom-call | tf_op jit(solution)/shard_map/attend_back/pallas_call | solution.py:661
  471.3 0.8 pad_maximum_fusion.1
  472.1 0.4 reshape_reshape.10
  472.5 0.3 copy.74
  473.1 0.7 copy.92
  473.8 0.7 reshape_reshape.11.dense
  474.4 0.6 broadcast_in_dim.67.loss
  475.0 23.1 %tail.1 = (f32[8,128]{1,0:T(8,128)}, f32[8,128]{1,0:T(8,128)}) custom-call(f32[32,8,128]{2,1,0:T(8,128)} %bitcast.125, f32[24,768]{1,0:T(8,128)} %reshape_reshape.11.dense, f32[8,128]{1,0:T(8,128)} %broadcast_in_dim.67.loss), custom_call_target="tpu_custom_call" | custom-call | tf_op jit(solution)/shard_map/tail/pallas_call | solution.py:1061
  498.1 1.3 fusion.34
  500.1 0.7 slice_multiply_fusion.4
  500.9 1.6 multiply_subtract_fusion
  502.5 0.6 multiply_subtract_fusion.1
  (106 shorter events, 2.8 us)
Async XLA Ops:
  7.2 4.5 copy-start.23
  7.2 4.5 copy-start.25
  7.2 270.9 %all-gather.5.cloned.1.call-start = ((), (), s32[]{:S(2)}) async-start(), calls=%async_computation | async-start | bytes 14598144 | tf_op jit(solution)/shard_map/all_gather | solution.py:1479
  11.6 7.2 %copy-start.10 = (f32[2,2,8,24]{3,2,1,0:T(8,128)S(1)}, f32[2,2,8,24]{3,2,1,0:T(8,128)}, u32[]{:S(2)}) copy-start(f32[2,2,8,24]{3,2,1,0:T(8,128)} %param.44) | copy-start | bytes 9220
  11.6 7.4 %copy-start.2 = (bf16[2,768,96]{1,2,0:T(8,128)(2,1)S(1)}, bf16[2,768,96]{1,2,0:T(8,128)(2,1)}, u32[]{:S(2)}) copy-start(bf16[2,768,96]{1,2,0:T(8,128)(2,1)} %param.38) | copy-start | bytes 884740
  11.6 7.4 %copy-start.3 = (bf16[2,96,768]{2,1,0:T(8,128)(2,1)S(1)}, bf16[2,96,768]{2,1,0:T(8,128)(2,1)}, u32[]{:S(2)}) copy-start(bf16[2,96,768]{2,1,0:T(8,128)(2,1)} %param.39) | copy-start | bytes 884740
  11.6 7.4 %copy-start.5 = (bf16[2,768,72]{1,2,0:T(8,128)(2,1)S(1)}, bf16[2,768,72]{1,2,0:T(8,128)(2,1)}, u32[]{:S(2)}) copy-start(bf16[2,768,72]{1,2,0:T(8,128)(2,1)} %param.36) | copy-start | bytes 663556
  17.2 1.8 copy-start.8
  17.2 1.9 copy-start.1
  17.6 2.3 copy-start.21
  195.4 3.2 copy-start.12
  196.7 2.9 copy-start.14
  197.6 3.9 copy-start.24
  197.6 4.4 copy-start.4
  199.6 19.3 %copy-start.11 = (f32[1,1024]{1,0:T(1,128)}, f32[1,1024]{1,0:T(1,128)S(1)}, u32[]{:S(2)}) copy-start(f32[1,1024]{1,0:T(1,128)S(1)} %convert_element_type.79.seg_row_ref) | copy-start | bytes 12292
  200.3 2.7 copy-start.19
  200.3 2.7 copy-start.20
  200.6 3.2 copy-start.13
  246.4 31.1 %copy-start.26 = (f32[4]{0:T(128)S(1)}, f32[4]{0:T(128)}, u32[]{:S(2)}) copy-start(f32[4]{0:T(128)} %param.30) | copy-start | bytes 52
  282.2 2.4 copy-start.22
  307.0 68.2 %copy-start = (bf16[128,768]{1,0:T(8,128)(2,1)S(1)}, bf16[128,768]{1,0:T(8,128)(2,1)}, u32[]{:S(2)}) copy-start(bf16[128,768]{1,0:T(8,128)(2,1)} %get-tuple-element.55.u_ref) | copy-start | bytes 589828
  374.0 3.8 copy-start.27
  445.9 25.4 %copy-start.15 = (f32[8,768]{1,0:T(8,128)S(1)}, f32[8,768]{1,0:T(8,128)}, u32[]{:S(2)}) copy-start(f32[8,768]{1,0:T(8,128)} %get-tuple-element.80) | copy-start | bytes 73732
  445.9 25.4 %copy-start.16 = (f32[8,768]{1,0:T(8,128)S(1)}, f32[8,768]{1,0:T(8,128)}, u32[]{:S(2)}) copy-start(f32[8,768]{1,0:T(8,128)} %get-tuple-element.81) | copy-start | bytes 73732
  472.5 1.3 copy-start.9
  472.5 28.4 %copy-start.6 = (f32[24,768]{1,0:T(8,128)S(1)}, f32[24,768]{1,0:T(8,128)}, u32[]{:S(2)}) copy-start(f32[24,768]{1,0:T(8,128)} %param.49) | copy-start | bytes 221188
  472.5 28.4 %copy-start.7 = (f32[24,768]{1,0:T(8,128)S(1)}, f32[24,768]{1,0:T(8,128)}, u32[]{:S(2)}) copy-start(f32[24,768]{1,0:T(8,128)} %param.48) | copy-start | bytes 221188
  472.8 29.7 %copy-start.17 = (f32[2,2,8,24]{3,2,1,0:T(8,128)S(1)}, f32[2,2,8,24]{3,2,1,0:T(8,128)}, u32[]{:S(2)}) copy-start(f32[2,2,8,24]{3,2,1,0:T(8,128)} %param.46) | copy-start | bytes 9220
  472.8 29.7 %copy-start.18 = (f32[2,2,8,24]{3,2,1,0:T(8,128)S(1)}, f32[2,2,8,24]{3,2,1,0:T(8,128)}, u32[]{:S(2)}) copy-start(f32[2,2,8,24]{3,2,1,0:T(8,128)} %param.45) | copy-start | bytes 9220
Sparse Core Ops, SparseCore 0:
  11.7 160.5 all-gather.4

commit v5 on v4

--- a/solution.py
+++ b/solution.py
@@ -441,8 +441,8 @@
 def last_backward_body(
     du_ref, kv_ref, q_ref, mid_ref, log_ref, one_ref, slope_ref, two_ref, low_ref, act_ref, hslope_ref,
     place_ref, place_row_ref, seg_ref, down_ref, w_ref, adapt_ref, wo_ref, up_any, dn_any, norm_ref, hb_ref,
-    dx_ref, gh_ref, gq_ref, gv_ref,
-    up_ref, dn_ref, dkv_ref, dq_ref, sems, *, places, rank,
+    dx_ref, gh_ref, g_ref,
+    up_ref, dn_ref, dkv_ref, dq_ref, sems, *, places, edge,
 ):
     copies = []
     for k, (source, target, place) in enumerate(
@@ -462,7 +462,14 @@
     scale = width**-0.5
     dact = norm_back(act_ref[...], norm_ref[4:5, :], du_ref[...])
     dz = (hslope_ref[...] * dact).astype(BF)
-    gh_ref[...] = mm_tn(low_ref[...], dz)
+    dense = mm_tn(low_ref[...], dz)
+    if len(gh_ref.shape) == 2:
+        gh_ref[...] = dense
+    else:
+        each = hidden // gh_ref.shape[0]
+        spare = jnp.zeros((gh_ref.shape[1] - each, hidden), F32)
+        for k in range(gh_ref.shape[0]):
+            gh_ref[k] = jnp.concatenate([dense[k * each : (k + 1) * each, :], spare], 0).astype(BF)
     dtwo = norm_back(two_ref[...], norm_ref[2:3, :], mm_nt(dz, hb_ref[...]))
     dtwo_low = dtwo.astype(BF)
     dmiddle = dtwo
@@ -498,8 +505,11 @@
         (lax.broadcasted_iota(jnp.int32, (labels, rows), 1) == place_ref[...][:, 0:1]).astype(F32).astype(BF),
         mid_ref[...],
     ).astype(BF)
-    gq_ref[...] = adapter_scale * mm_tn(own_mid, dq)[:rank, :]
-    gv_ref[...] = adapter_scale * mm_tn(mid_ref[...], dkv_ref[:, hidden:])[rank : 2 * rank, :]
+    g_ref[...] = adapter_scale * jnp.where(
+        lax.broadcasted_iota(jnp.int32, g_ref.shape, 1) < edge,
+        mm_tn(dq, own_mid),
+        mm_tn(dkv_ref[:, hidden:], mid_ref[...]),
+    )
     dmid_own = mm_nt(dq, adapt_ref[:, :hidden]).astype(BF)
     own = done + mm(dq, w_ref[:hidden, :]) + mm_nt(dmid_own, down_ref[...])
     spread = choose_t.astype(F32).astype(BF)
@@ -517,7 +527,7 @@
         )
 
 
-def last_backward(du, saved, place_col, place_row, seg_wide, down, w, adapt, wo, up, dn, norms, hb, rank):
+def last_backward(du, saved, place_col, place_row, seg_wide, down, w, adapt, wo, up, dn, norms, hb, edge, shards):
     kv = saved[0]
     rows = kv.shape[0]
     labels, hidden = du.shape
@@ -525,14 +535,15 @@
     anywhere = pl.BlockSpec(memory_space=pl.ANY)
     shape = jax.ShapeDtypeStruct
     return pl.pallas_call(
-        functools.partial(last_backward_body, places=(up[1], dn[1]), rank=rank),
+        functools.partial(last_backward_body, places=(up[1], dn[1]), edge=edge),
         in_specs=[whole] * 18 + [anywhere] * 2 + [whole] * 2,
-        out_specs=[whole] * 4,
+        out_specs=[whole] * 3,
         out_shape=[
             shape((rows, hidden), F32),
-            shape((hidden, hidden), F32),
-            shape((rank, hidden), F32),
-            shape((rank, hidden), F32),
+            shape((hidden, hidden), F32)
+            if shards is None
+            else shape((shards, -(-hidden // shards // 16) * 16, hidden), BF),
+            shape((hidden, down.shape[1]), F32),
         ],
         scratch_shapes=[
             slab_scratch(up),
@@ -544,32 +555,6 @@
         compiler_params=params(),
         name="last_backward",
     )(du, *saved, place_col, place_row, seg_wide, down, w, adapt, wo, up[0], dn[0], norms, hb)
-
-
-def after_back_sum_body(shards, *refs):
-    *plain, parts, dctx_ref, sum_ref, got, sends, gets = refs
-    step, last = pl.program_id(0), pl.num_programs(0) - 1
-    me = number_of(position())
-
-    @pl.when(step == 0)
-    def _():
-        greet_all(shards)
-        got[me] = parts[me]
-
-    @pl.when(step == jnp.minimum(1, last))
-    def _():
-        await_all(shards)
-        spread(lambda peer: parts.at[peer], got, sends, gets, me, shards)
-
-    after_back_body(*plain, dctx_ref)
-
-    @pl.when(step == last)
-    def _():
-        collect(lambda peer: parts.at[peer], got, sends, gets, me, shards)
-        total = got[0].astype(F32)
-        for k in range(1, shards):
-            total = total + got[k].astype(F32)
-        sum_ref[...] = total
 
 
 def after_back_body(dout_ref, one_ref, two_ref, slope_ref, wo_ref, up_ref, down_ref, norm_ref, dctx_ref):
@@ -585,27 +570,6 @@
         dmiddle = dmiddle + mm(dgate, rows_of(up_ref, start, step))
     done = norm_back(one_ref[...], norm_ref[0:1, :], dmiddle)
     dctx_ref[...] = mm(done.astype(BF), wo_ref[...]).astype(BF)
-
-
-def after_back_sum(dout, one, two, slope, wo, up, down, norms, parts, shards):
-    rows, width = dout.shape
-    tile = split_of(rows, 256, 16)
-    row = lambda n: pl.BlockSpec((tile, n), lambda i: (i, 0))
-    sems = pltpu.SemaphoreType.DMA
-    return pl.pallas_call(
-        functools.partial(after_back_sum_body, shards),
-        grid=(rows // tile,),
-        in_specs=[row(width), row(width), row(width), row(slope.shape[1]), full(wo.shape)]
-        + [slab_spec(up), slab_spec(down), full(norms.shape), full(parts.shape)],
-        out_specs=[row(width), full(parts.shape[1:])],
-        out_shape=[
-            jax.ShapeDtypeStruct((rows, width), BF),
-            jax.ShapeDtypeStruct(parts.shape[1:], F32),
-        ],
-        scratch_shapes=[pltpu.VMEM(parts.shape, BF), sems((shards,)), sems((shards,))],
-        compiler_params=params(collective_id=3, has_side_effects=True),
-        name="after_back_sum",
-    )(dout, one, two, slope, wo, up[0], down[0], norms, parts)
 
 
 def after_back(dout, one, two, slope, wo, up, down, norms):
@@ -625,12 +589,11 @@
 
 
 def attend_back_body(
-    q_ref, k_ref, v_ref, dctx_ref, log_ref, seg_ref, seg_row_ref, mid_ref, gq_ref, gv_ref, dv_ref
+    q_ref, k_ref, v_ref, dctx_ref, log_ref, seg_ref, seg_row_ref, mid_ref, g_ref, dv_ref, *, edge
 ):
     rows = q_ref.shape[0]
     width = q_ref.shape[1] // 2
     scale = width**-0.5
-    rank = gq_ref.shape[0]
     dv_ref[...] = jnp.zeros_like(dv_ref)
     gq = jnp.zeros((2 * width, mid_ref.shape[1]), F32)
     for start in range(0, rows, REACH):
@@ -648,18 +611,20 @@
         dv_ref[near, :] += mm(weights.astype(BF), outs)
         dq = (pair_join(mm_tn(keys, dscores), width) * scale).astype(BF)
         gq = gq + mm(dq, mid_ref[own, :])
-    gq_ref[...] = adapter_scale * gq.T[:rank, :]
-    gv_ref[...] = adapter_scale * mm_tn(mid_ref[...], dv_ref[...].astype(BF))[rank : 2 * rank, :]
-
-
-def attend_back(qkv, dctx, logs, seg_wide, seg_row, mid, rank):
+    gv = mm_tn(dv_ref[...].astype(BF), mid_ref[...])
+    g_ref[...] = adapter_scale * jnp.where(
+        lax.broadcasted_iota(jnp.int32, gq.shape, 1) < edge, gq, gv
+    )
+
+
+def attend_back(qkv, dctx, logs, seg_wide, seg_row, mid, edge):
     rows, total = qkv.shape
     hidden = total // 3
     lanes = 2 * (hidden // HEADS)
     pairs = hidden // lanes
     column = lambda kind: pl.BlockSpec((rows, lanes), lambda p: (0, kind * pairs + p))
     return pl.pallas_call(
-        attend_back_body,
+        functools.partial(attend_back_body, edge=edge),
         grid=(pairs,),
         in_specs=[
             column(0),
@@ -671,8 +636,8 @@
             full(seg_row.shape),
             full(mid.shape),
         ],
-        out_specs=[pl.BlockSpec((rank, lanes), lambda p: (0, p))] * 2,
-        out_shape=[jax.ShapeDtypeStruct((rank, hidden), F32)] * 2,
+        out_specs=pl.BlockSpec((lanes, mid.shape[1]), lambda p: (p, 0)),
+        out_shape=jax.ShapeDtypeStruct((hidden, mid.shape[1]), F32),
         scratch_shapes=[pltpu.VMEM((rows, lanes), F32)],
         compiler_params=params(),
         name="attend_back",
@@ -861,20 +826,16 @@
 
 
 def start_body(
-    streams, shards, ids, low_ref, groups_any, table_any, chunk, note, bias,
-    full_chunk, own_rows, got, notes, biases, e_out, et_out,
-    table, stage, rows, e_ref, et_ref,
-    sends, receives, hands, hands_got, row_sends, row_gets, note_sends, note_gets, bias_sends, bias_gets,
+    streams, shards, rows, table_any, chunk, note, bias,
+    full_chunk, got, notes, biases, e_out, et_out,
+    e_ref, et_ref,
+    sends, receives, hands, hands_got, row_sems, note_sends, note_gets, bias_sends, bias_gets,
     own_sems, e_sems, out_sems,
 ):
     here = position()
     me = number_of(here)
     across = device_of(dict(here, x=1 - here["x"]))
     slice_rows = e_ref.shape[0] // 2
-    half = own_rows.shape[0]
-    batches = half // PICK
-    fill = pltpu.make_async_copy(groups_any, table, own_sems.at[3])
-    fill.start()
     greet_all(shards)
     plain = [
         pltpu.make_async_copy(source, target, own_sems.at[k])
@@ -910,30 +871,15 @@
     spread(lambda peer: bias, biases, bias_sends, bias_gets, me, shards)
     swap.start()
 
-    def send_rows(b):
-        part = pl.ds(b * PICK, PICK)
-        return pltpu.make_async_remote_copy(
-            src_ref=rows.at[part, :],
-            dst_ref=got.at[part, :],
-            send_sem=row_sends.at[b],
-            recv_sem=row_gets.at[b],
-            device_id=across,
-            device_id_type=MESH,
-        )
-
-    def pick(b):
-        def one(t, carry):
-            stage[t] = table[ids[b * PICK + t]]
-            return carry
-
-        lax.fori_loop(0, PICK, one, 0, unroll=8)
-        choose = (
-            lax.broadcasted_iota(jnp.int32, (PICK, PICK * GROUP), 1)
-            == low_ref[b * PICK : (b + 1) * PICK, :]
-        )
-        rows[b * PICK : (b + 1) * PICK, :] = mm(choose.astype(F32).astype(BF), flat(stage)).astype(BF)
-        if b < batches:
-            send_rows(b).start()
+    send_rows = pltpu.make_async_remote_copy(
+        src_ref=rows,
+        dst_ref=got,
+        send_sem=row_sems.at[0],
+        recv_sem=row_sems.at[1],
+        device_id=across,
+        device_id_type=MESH,
+    )
+    send_rows.start()
 
     def turn(k):
         part = slice(k * 128, (k + 1) * 128)
@@ -943,17 +889,12 @@
         return (
             pltpu.make_async_copy(e_ref, e_out, out_sems.at[0]),
             pltpu.make_async_copy(et_ref, et_out, out_sems.at[1]),
-            pltpu.make_async_copy(rows.at[pl.ds(half, half), :], own_rows, out_sems.at[2]),
-        )
-
-    fill.wait()
-    done, turned = 0, 0
+        )
+
+    turned = 0
     own_turns = slice_rows // 128
     for index in range(1, ITEMS):
-        while done < 2 * batches and done < index * 3:
-            pick(done)
-            done += 1
-        if done == 2 * batches and turned < own_turns:
+        if turned < own_turns:
             if turned == 0:
                 keep.wait()
             turn(turned)
@@ -970,8 +911,7 @@
         gather.finish()
     collect(lambda peer: note, notes, note_sends, note_gets, me, shards)
     collect(lambda peer: bias, biases, bias_sends, bias_gets, me, shards)
-    for b in range(batches):
-        send_rows(b).wait()
+    send_rows.wait()
     swap.wait_send()
     for copy in plain:
         copy.wait()
@@ -979,99 +919,239 @@
         copy.wait()
 
 
-def start_exchange(ids, low, table, chunk, note, bias, shards, slice_rows):
+def start_exchange(rows, table, chunk, note, bias, shards, slice_rows):
     anywhere = pl.BlockSpec(memory_space=pl.ANY)
     cut = (chunk.shape[0] * 5 // 6 + 15) // 16 * 16
     streams = ((0, cut, "xzy"), (cut, chunk.shape[0] - cut, "xyz"))
-    half = ids.shape[0] // 2
     hidden = table.shape[1]
     shape = jax.ShapeDtypeStruct
     sems = pltpu.SemaphoreType.DMA
     return pl.pallas_call(
         functools.partial(start_body, streams, shards),
-        in_specs=[
-            pl.BlockSpec(memory_space=pltpu.SMEM),
-            pl.BlockSpec(memory_space=pltpu.VMEM),
-        ]
-        + [anywhere] * 5,
-        out_specs=[anywhere] * 7,
+        in_specs=[anywhere] * 5,
+        out_specs=[anywhere] * 6,
         out_shape=[
             shape((shards, *chunk.shape), chunk.dtype),
-            shape((half, hidden), table.dtype),
-            shape((half, hidden), table.dtype),
+            shape(rows.shape, rows.dtype),
             shape((shards, *note.shape), note.dtype),
             shape((shards, *bias.shape), bias.dtype),
             shape((2 * slice_rows, hidden), table.dtype),
             shape((hidden, 2 * slice_rows), table.dtype),
         ],
         scratch_shapes=[
-            pltpu.VMEM((table.shape[0] // GROUP, GROUP, hidden), BF),
-            pltpu.VMEM((PICK, GROUP, hidden), BF),
-            pltpu.VMEM((2 * half, hidden), BF),
             pltpu.VMEM((2 * slice_rows, hidden), BF),
             pltpu.VMEM((hidden, 2 * slice_rows), BF),
             sems((2, 4 * ITEMS)),
             sems((2, 16)),
             sems((2, ITEMS)),
             sems((2, 16)),
-            sems((half // PICK,)),
-            sems((half // PICK,)),
+            sems((2,)),
             sems((shards,)),
             sems((shards,)),
             sems((shards,)),
             sems((shards,)),
             sems((5,)),
             sems((2,)),
-            sems((3,)),
+            sems((2,)),
         ],
         compiler_params=params(collective_id=1, has_side_effects=True),
         name="start_exchange",
-    )(ids, low, table.reshape(-1, GROUP, hidden), table, chunk, note, bias)
-
-
-def tail_body(shards, parts, dense, loss, total_ref, sums_ref, got, note, notes, send_a, get_a, send_b, get_b):
+    )(rows, table, chunk, note, bias)
+
+
+def look_up_body(ids, low_ref, table, first_ref, second_ref, stage):
+    batches = first_ref.shape[0] // PICK
+    for k, out in enumerate((first_ref, second_ref)):
+
+        @pl.loop(0, batches)
+        def _(b, k=k, out=out):
+            at = (k * batches + b) * PICK
+
+            def one(t, carry):
+                stage[t] = table[ids[at + t]]
+                return carry
+
+            lax.fori_loop(0, PICK, one, 0, unroll=8)
+            choose = (
+                lax.broadcasted_iota(jnp.int32, (PICK, PICK * GROUP), 1)
+                == low_ref[pl.ds(pl.multiple_of(at, PICK), PICK), :]
+            )
+            out[pl.ds(pl.multiple_of(b * PICK, PICK), PICK), :] = mm(
+                choose.astype(F32).astype(BF), flat(stage)
+            ).astype(BF)
+
+
+def look_up(ids, table):
+    whole = pl.BlockSpec(memory_space=pltpu.VMEM)
+    hidden = table.shape[1]
+    low = jnp.arange(ids.size, dtype=jnp.int32) % PICK * GROUP + ids % GROUP
+    return pl.pallas_call(
+        look_up_body,
+        in_specs=[pl.BlockSpec(memory_space=pltpu.SMEM), whole, whole],
+        out_specs=[whole] * 2,
+        out_shape=[jax.ShapeDtypeStruct((ids.size // 2, hidden), table.dtype)] * 2,
+        scratch_shapes=[pltpu.VMEM((PICK, GROUP, hidden), table.dtype)],
+        compiler_params=params(),
+        name="look_up",
+    )(ids // GROUP, low[:, None], table.reshape(-1, GROUP, hidden))
+
+
+def adam(weight, gradient, moment_one, moment_two, fade_one, fade_two):
+    moment_one = beta_first * moment_one + (1.0 - beta_first) * gradient
+    moment_two = beta_second * moment_two + (1.0 - beta_second) * gradient * gradient
+    one_hat = moment_one / fade_one
+    two_hat = moment_two / fade_two
+    weight = weight - learn_rate * (one_hat / (jnp.sqrt(two_hat) + adam_eps) + decay_rate * weight)
+    return (weight, moment_one, moment_two)
+
+
+def finish_body(
+    shards, places, edge,
+    dout_any, one_any, two_any, slope_any, wo_any, up_any, dn_any, qkv_any, norm_ref, log_ref, seg_ref,
+    seg_row_ref, mid_ref, parts, late_ref, facts, head_w, head_m, head_v, adapt_w, adapt_m, adapt_v,
+    sums_ref, head_w_out, head_m_out, head_v_out, adapt_w_out, adapt_m_out, adapt_v_out,
+    dout, one, two, slope, wo, up, dn, qkv, dctx, dv, grad, dense_got, grad_got, note, notes,
+    tile_sems, load_sems, dense_send, dense_get, grad_send, grad_get, note_send, note_get,
+):
+    rows, hidden = dout.shape
+    tile = split_of(rows, 256, 16)
+    tiles = rows // tile
     me = number_of(position())
+
+    def tile_loads(i):
+        part = pl.ds(pl.multiple_of(i * tile, tile), tile)
+        return [
+            pltpu.make_async_copy(source.at[part, :], target.at[part, :], tile_sems.at[k, i])
+            for k, (source, target) in enumerate(
+                ((two_any, two), (dout_any, dout), (slope_any, slope), (one_any, one))
+            )
+        ]
+
+    def slab(source, target, place):
+        each = target.shape[1]
+        return source.at[:, pl.ds(place * each, each), :]
+
+    loads = [
+        pltpu.make_async_copy(source, target, load_sems.at[k])
+        for k, (source, target) in enumerate(
+            (
+                (slab(dn_any, dn, places[1]), dn),
+                (slab(up_any, up, places[0]), up),
+                (wo_any, wo),
+                (qkv_any, qkv),
+            )
+        )
+    ]
+    for copy in tile_loads(0) + loads[:3]:
+        copy.start()
+    for i in range(1, tiles):
+        for copy in tile_loads(i):
+            copy.start()
+    loads[3].start()
     greet_all(shards)
-    got[me] = parts[me]
-    await_all(shards)
-    spread(lambda peer: parts.at[peer], got, send_a, get_a, me, shards)
-    dense_square = jnp.sum(dense[...] * dense[...], keepdims=True)
-    collect(lambda peer: parts.at[peer], got, send_a, get_a, me, shards)
-    total = got[0]
+    dense_got[me] = parts[me]
+    for copy in loads[:3]:
+        copy.wait()
+
+    @pl.loop(0, tiles)
+    def _(i):
+        for copy in tile_loads(i):
+            copy.wait()
+        part = pl.ds(pl.multiple_of(i * tile, tile), tile)
+        after_back_body(
+            dout.at[part, :], one.at[part, :], two.at[part, :], slope.at[part, :], wo, up, dn, norm_ref,
+            dctx.at[part, :],
+        )
+
+        @pl.when(i == 0)
+        def _():
+            await_all(shards)
+            spread(lambda peer: parts.at[peer], dense_got, dense_send, dense_get, me, shards)
+
+    loads[3].wait()
+    lanes = 2 * (hidden // HEADS)
+    pairs = hidden // lanes
+
+    @pl.loop(0, pairs)
+    def _(p):
+        column = lambda kind: pl.ds(pl.multiple_of((kind * pairs + p) * lanes, lanes), lanes)
+        attend_back_body(
+            qkv.at[:, column(0)], qkv.at[:, column(1)], qkv.at[:, column(2)], dctx.at[:, column(0)],
+            log_ref.at[pl.ds(p, 1)], seg_ref, seg_row_ref, mid_ref, grad.at[column(0), :], dv, edge=edge,
+        )
+
+    grad[...] = grad[...] + late_ref[...]
+    each = hidden // shards
+    piece = lambda peer: grad.at[pl.ds(pl.multiple_of(peer * each, each), each), :]
+    grad_got[me] = piece(me)[...]
+    spread(piece, grad_got, grad_send, grad_get, me, shards)
+    collect(lambda peer: parts.at[peer], dense_got, dense_send, dense_get, me, shards)
+    dense = jnp.zeros((each, hidden), F32)
+    for k in range(shards):
+        dense = dense + dense_got[k].astype(F32)[:each, :]
+    square = jnp.sum(dense * dense, keepdims=True)
+    collect(piece, grad_got, grad_send, grad_get, me, shards)
+    total = grad_got[0]
     for k in range(1, shards):
-        total = total + got[k]
-    total_ref[...] = total
-    square = dense_square + jnp.sum(total * total, keepdims=True)
+        total = total + grad_got[k]
+    square = square + jnp.sum(total * total, keepdims=True)
     row = lax.broadcasted_iota(jnp.int32, note.shape, 0)
-    note[...] = jnp.where(row == 0, loss[...], jnp.where(row == 1, square, 0.0))
+    note[...] = jnp.where(row == 0, facts[...], jnp.where(row == 1, square, 0.0))
     notes[me] = note[...]
-    spread(lambda peer: note, notes, send_b, get_b, me, shards)
-    collect(lambda peer: note, notes, send_b, get_b, me, shards)
-    total = notes[0]
+    spread(lambda peer: note, notes, note_send, note_get, me, shards)
+    collect(lambda peer: note, notes, note_send, note_get, me, shards)
+    sums = notes[0]
     for k in range(1, shards):
-        total = total + notes[k]
-    sums_ref[...] = total
-
-
-def tail(parts, dense, loss, shards):
+        sums = sums + notes[k]
+    norm = jnp.sqrt(sums[1:2, :])
+    sums_ref[...] = jnp.where(row == 1, norm, sums)
+    factor = jnp.minimum(1.0, clip_limit / (norm + 1e-06))[:, 0:1]
+    fades = facts[1:2, 0:1], facts[2:3, 0:1]
+    new = adam(head_w[...], dense * factor, head_m[...], head_v[...], *fades)
+    head_w_out[...], head_m_out[...], head_v_out[...] = new
+    new = adam(adapt_w[...], total * factor, adapt_m[...], adapt_v[...], *fades)
+    adapt_w_out[...], adapt_m_out[...], adapt_v_out[...] = new
+
+
+def finish(back, qkv, logs, seg_wide, seg_row, mid, parts, late, facts, heads, adapts, edge, shards):
+    dout, one, two, slope, wo, up, dn, norms = back
+    rows, hidden = dout.shape
+    each = hidden // shards
     whole = pl.BlockSpec(memory_space=pltpu.VMEM)
-    block = parts.shape[1:]
+    anywhere = pl.BlockSpec(memory_space=pl.ANY)
     shape = jax.ShapeDtypeStruct
     sems = pltpu.SemaphoreType.DMA
+    tiles = rows // split_of(rows, 256, 16)
     return pl.pallas_call(
-        functools.partial(tail_body, shards),
-        in_specs=[whole] * 3,
-        out_specs=[whole] * 2,
-        out_shape=[shape(block, F32), shape((8, 128), F32)],
+        functools.partial(finish_body, shards, (up[1], dn[1]), edge),
+        in_specs=[anywhere] * 8 + [whole] * 14,
+        out_specs=[whole] * 7,
+        out_shape=[shape((8, 128), F32)]
+        + [shape(a.shape, F32) for a in heads]
+        + [shape(a.shape, F32) for a in adapts],
         scratch_shapes=[
-            pltpu.VMEM(parts.shape, F32),
+            pltpu.VMEM((rows, hidden), F32),
+            pltpu.VMEM((rows, hidden), F32),
+            pltpu.VMEM((rows, hidden), F32),
+            pltpu.VMEM(slope.shape, BF),
+            pltpu.VMEM(wo.shape, BF),
+            slab_scratch(up),
+            slab_scratch(dn),
+            pltpu.VMEM(qkv.shape, BF),
+            pltpu.VMEM((rows, hidden), BF),
+            pltpu.VMEM((rows, 2 * (hidden // HEADS)), F32),
+            pltpu.VMEM(late.shape, F32),
+            pltpu.VMEM(parts.shape, BF),
+            pltpu.VMEM((shards, each, late.shape[1]), F32),
             pltpu.VMEM((8, 128), F32),
             pltpu.VMEM((shards, 8, 128), F32),
+            sems((4, tiles)),
+            sems((4,)),
         ]
-        + [sems((shards,))] * 4,
+        + [sems((shards,))] * 6,
         compiler_params=params(collective_id=2, has_side_effects=True),
-        name="tail",
-    )(parts, dense, loss)
+        name="finish",
+    )(dout, one, two, slope, wo, up[0], dn[0], qkv, norms, logs, seg_wide, seg_row, mid, parts, late, facts, *heads, *adapts)
 
 
 HOPS = 3
@@ -1395,15 +1475,6 @@
     return index - starts
 
 
-def optimizer_update(weight, gradient, moment_one, moment_two, step_as_real):
-    moment_one = beta_first * moment_one + (1.0 - beta_first) * gradient
-    moment_two = beta_second * moment_two + (1.0 - beta_second) * gradient * gradient
-    one_hat = moment_one / (1.0 - beta_first**step_as_real)
-    two_hat = moment_two / (1.0 - beta_second**step_as_real)
-    weight = weight - learn_rate * (one_hat / (jnp.sqrt(two_hat) + adam_eps) + decay_rate * weight)
-    return (weight, moment_one, moment_two)
-
-
 def pad_rows(matrix, multiple):
     return jnp.pad(matrix, ((0, -matrix.shape[0] % multiple), (0, 0)))
 
@@ -1489,12 +1560,12 @@
                 for shift in (1, 0)
             ]
         )
-        low_ids = jnp.arange(pair_ids.size, dtype=jnp.int32) % PICK * GROUP + pair_ids % GROUP
+        other_rows, own_rows = look_up(pair_ids, embed)
         note = jnp.broadcast_to(sequence_task_index.astype(F32)[:, None], (8, 128))
         bias_rows = -(-slice_rows // 1024) * 8
         bias_block = jnp.pad(vocabulary_bias, (0, bias_rows * 128 - slice_rows)).reshape(bias_rows, 128)
-        first_full, own_rows, got, notes, biases, own_vocab, own_turned = start_exchange(
-            pair_ids // GROUP, low_ids[:, None], embed, chunks[0], note, bias_block, shards, slice_rows
+        first_full, got, notes, biases, own_vocab, own_turned = start_exchange(
+            other_rows, embed, chunks[0], note, bias_block, shards, slice_rows
         )
         every_task = notes[:, 0, 0].astype(jnp.int32)
         all_bias = biases.reshape(shards, -1)[:, :slice_rows].reshape(-1)
@@ -1553,14 +1624,14 @@
                 ],
                 0,
             ),
-            ((0, 128 - 2 * rank), (0, 0)),
+            ((2 * rank * layer, 128 - 2 * rank * (layer + 1)), (0, 0)),
         )
         for layer in range(layers)
     ]
     downs = [
         jnp.pad(
             jnp.concatenate([adapter_down_matrix[layer, 0], adapter_down_matrix[layer, 1]], 1),
-            ((0, 0), (0, 128 - 2 * rank)),
+            ((0, 0), (2 * rank * layer, 128 - 2 * rank * (layer + 1))),
         )
         for layer in range(layers)
     ]
@@ -1648,53 +1719,45 @@
     own_loss = row_weight * jnp.sum(own_logs - targets)
     feat_grad = row_weight * (mean_t.T - target_rows)
 
-    hidden_grad, dense_gradient, gq_last, gv_last = last_backward(
+    hidden_grad, dense_gradient, late = last_backward(
         feat_grad, saved, place_col, place_row, seg_wide, downs[1], in_weights[1], adapters[1],
-        out_weights[1], *slabs[1], norms_of[1], head_full, rank,
+        out_weights[1], *slabs[1], norms_of[1], head_full, 3 * rank, shards if grouped else None,
     )
     back = (hidden_grad, one, two, slope, out_weights[0], *slabs[0], norms_of[0])
+    step_as_real = optimizer_step_count[0].astype(F32)
+    fades = (1.0 - beta_first**step_as_real, 1.0 - beta_second**step_as_real)
+    adapts = (adapter_up_matrix, adapter_moment_first, adapter_moment_second)
+    heads = (head_projection, head_moment_first, head_moment_second)
     if grouped:
-        block = -(-head_rows * hidden // 2048) * 2048
-        dense_parts = jnp.pad(
-            dense_gradient.reshape(shards, -1).astype(BF), ((0, 0), (0, block - head_rows * hidden))
-        ).reshape(shards, 16, block // 16)
-        dctx, dense_sum = after_back_sum(*back, dense_parts, shards)
-        dense_portion = dense_sum.reshape(-1)[: head_rows * hidden].reshape(head_rows, hidden)
+        facts = jnp.concatenate(
+            [jnp.broadcast_to(value, (1, 128)) for value in (own_loss, *fades)]
+            + [jnp.zeros((5, 128), F32)]
+        )
+        turned = [
+            jnp.pad(a.reshape(-1, up_part).T, ((0, 0), (0, 128 - a.size // up_part))) for a in adapts
+        ]
+        sums, *new = finish(
+            back, qkv, logs, seg_wide, seg_row, mid, dense_gradient, late, facts, heads, turned, rank, shards
+        )
+        dense_new = new[:3]
+        adapter_new = [
+            a[:, : ups.size // up_part].T.reshape(adapter_up_matrix.shape) for a in new[3:]
+        ]
+        masked_task_loss, gradient_norm = sums[0, 0], sums[1, 0]
     else:
         dctx = after_back(*back)
+        first = attend_back(qkv, dctx, logs, seg_wide, seg_row, mid, rank)
+        adapter_gradient = (first + late)[:, : 2 * rank * layers].T.reshape(layers, 2, rank, hidden)
         dense_portion = lax.psum_scatter(dense_gradient, BOTH, scatter_dimension=0, tiled=True)
-    gq_first, gv_first = attend_back(qkv, dctx, logs, seg_wide, seg_row, mid, rank)
-    adapter_gradient = jnp.stack([gq_first, gv_first, gq_last, gv_last]).reshape(layers, 2, rank, hidden)
-    if grouped:
-        parts = adapter_gradient.reshape(-1, shards, up_part).transpose(1, 0, 2).reshape(shards, -1)
-        block = -(-ups.size // 1024) * 1024
-        parts = jnp.pad(parts, ((0, 0), (0, block - ups.size))).reshape(shards, block // 128, 128)
-        own_parts, sums = tail(parts, dense_portion, jnp.broadcast_to(own_loss, (8, 128)), shards)
-        adapter_portion = own_parts.reshape(-1)[: ups.size].reshape(adapter_up_matrix.shape)
-        masked_task_loss, norm_square = sums[0, 0], sums[1, 0]
-    else:
         adapter_portion = lax.psum_scatter(adapter_gradient, BOTH, scatter_dimension=3, tiled=True)
         squared_entries = jnp.sum(adapter_portion * adapter_portion) + jnp.sum(
             dense_portion * dense_portion
         )
         masked_task_loss, norm_square = lax.psum((own_loss, squared_entries), BOTH)
-    gradient_norm = jnp.sqrt(norm_square)
-    scale_factor = jnp.minimum(1.0, clip_limit / (gradient_norm + 1e-06))
-    step_as_real = optimizer_step_count[0].astype(F32)
-    adapter_new = optimizer_update(
-        adapter_up_matrix,
-        adapter_portion * scale_factor,
-        adapter_moment_first,
-        adapter_moment_second,
-        step_as_real,
-    )
-    dense_new = optimizer_update(
-        head_projection,
-        dense_portion * scale_factor,
-        head_moment_first,
-        head_moment_second,
-        step_as_real,
-    )
+        gradient_norm = jnp.sqrt(norm_square)
+        factor = jnp.minimum(1.0, clip_limit / (gradient_norm + 1e-06))
+        adapter_new = adam(adapts[0], adapter_portion * factor, *adapts[1:], *fades)
+        dense_new = adam(heads[0], dense_portion * factor, *heads[1:], *fades)
     return (masked_task_loss, gradient_norm, *adapter_new, *dense_new)
 
 

time: 517 us -> 510 us (0.986)
  local copies, waits for them, and re-layouts: 42.5 us -> 49.5 us
  other arithmetic: 16.8 us -> 11.5 us
    pallas_call x1, Pallas kernels: 166 us -> 143 us  [start_exchange(): pl.pallas_call(functools.partial(start_body, streams, shards), in_specs=[...]
    pallas_call x3 -> x2, Pallas kernels: 85.1 us -> 105 us  [the longest x1 70 us: finish(): pl.pallas_call(functools.partial(finish_body, shards, (up[1], dn[1]), edg...]
  transfers between devices with their start and end apart: 1 -> 1, of which waited for: 0 -> 0; matrix products, arithmetic and copies ran while one was open for 6% -> 6% of each run, Pallas kernels for 45% -> 48%
where the time goes in v5:
time: 510 us; the launch traced here: 506 us
  Pallas kernels  422 us (83%)
  local copies, waits for them, and re-layouts  49.5 us (10%)
  between operations  17.5 us (3%)
  other arithmetic  11.5 us (2%)
  blocking collectives  5.37 us (1%)
    pallas_call x1, Pallas kernels, start_exchange(): pl.pallas_call(functools.partial(start_body, streams, shards), in_specs=[...  143 us
    pallas_call x1, Pallas kernels, finish(): pl.pallas_call(functools.partial(finish_body, shards, (up[1], dn[1]), edg...  70 us
    pallas_call x1, Pallas kernels, head(): pl.pallas_call(head_body, in_specs=[whole] + [anywhere] * 3, out_specs=[w...  65 us
    pallas_call x1, Pallas kernels, look_up(): pl.pallas_call(look_up_body, in_specs=[pl.BlockSpec(memory_space=pltpu.SM...  35.1 us
    pallas_call x1, Pallas kernels, after(): pl.pallas_call(after_body, grid=(rows // tile,), in_specs=[row(width), ro...  29.2 us
    pallas_call x1, Pallas kernels, last_backward(): pl.pallas_call(functools.partial(last_backward_body, places=(up[1], dn[1]...  26.5 us
    pallas_call x1, Pallas kernels, attend(): pl.pallas_call(attend_body, grid=(pairs,), in_specs=[column(0), column(1)...  20.1 us
    pallas_call x1, Pallas kernels, last_forward(): pl.pallas_call(functools.partial(last_forward_body, places=(up[1], dn[1])...  20.1 us
  transfers between devices with their start and end apart: 1, of which 0 were waited for; matrix products, arithmetic and copies ran while one was open for 6% of the time, Pallas kernels for 48%

profile of v5, /device:TPU:0, one launch (start us, length us, event | category | flops | bytes accessed | tf_op | source)
XLA Modules:
  0.0 505.9 jit_solution(3496875616667500127)
XLA Ops:
  7.2 0.9 slice_bitcast_fusion
  8.2 0.9 slice_bitcast_fusion.1
  9.1 0.9 slice_bitcast_fusion.2
  10.0 0.8 slice_bitcast_fusion.3
  10.8 0.8 pad_maximum_fusion
  11.7 5.4 %all-gather.2 = s32[2,1,1152]{2,1,0:T(1,128)S(1)} all-gather(s32[1,1,1152]{2,1,0:T(1,128)S(1)} %reshape.386), channel_id=2, replica_groups=mesh['dp'=2,'fsdp'=16] {'dp'}, dimensions={0}, use_global_device_ids=true | all-gather | bytes 13824 | tf_op jit(solution)/shard_map/all_gather | solution.py:1549
  17.2 0.4 copy.79
  17.6 0.5 copy.82
  19.1 0.8 pad.38.chunk
  19.9 0.6 add_select_fusion.2.ids
  20.5 1.6 fusion.1.low_ref
  22.2 35.1 %look_up.1 = (bf16[1152,768]{1,0:T(8,128)(2,1)}, bf16[1152,768]{1,0:T(8,128)(2,1)}) custom-call(s32[2304]{0:T(1024)} %add_select_fusion.2.ids, s32[2304,1]{1,0:T(8,128)} %fusion.1.low_ref, bf16[1600,16,768]{2,1,0:T(8,128)(2,1)} %bitcast.120), custom_call_target="tpu_custom_call" | custom-call | tf_op jit(solution)/shard_map/look_up/pallas_call | solution.py:988
  57.3 0.6 pad_bitcast_fusion.bias
  57.9 0.6 broadcast_in_dim.35.note
  58.5 142.9 %start_exchange.1 = (bf16[32,320,768]{2,1,0:T(8,128)(2,1)}, bf16[1152,768]{1,0:T(8,128)(2,1)}, f32[32,8,128]{2,1,0:T(8,128)}, f32[32,16,128]{2,1,0:T(8,128)}, bf...) custom-call(bf16[1152,768]{1,0:T(8,128)(2,1)} %get-tuple-element.48.rows, bf16[25600,768]{1,0:T(8,128)(2,1)} %table_any.1, ...), custom_call_target="tpu_custom_call" | custom-call | tf_op jit(solution)/shard_map/start_exchange/pallas_call | solution.py:929
  201.4 4.0 slice.210
  205.3 1.2 slice_reduce_fusion
  206.6 0.4 reshape_reshape.3
  207.4 0.9 pad.43.adapt_ref
  208.3 0.9 pad.41.up_ref
  209.3 1.1 copy.86.mine_ref
  210.5 0.7 pad.40.down_ref
  212.5 0.8 pad.42.down_ref
  213.3 0.6 broadcast_in_dim.72.hbias_ref
  215.0 0.6 pad.44.adapt_w
  215.6 0.6 pad.45.adapt_m
  216.3 0.6 pad.46.adapt_v
  217.0 0.6 pad_maximum_fusion.6.norm_ref
  217.6 0.6 fusion.26
  218.2 0.9 iota_subtract_fusion.spot_ref
  219.0 0.6 pad_maximum_fusion.5
  219.7 13.1 %project.1 = (bf16[1024,2304]{1,0:T(8,128)(2,1)}, bf16[1024,128]{1,0:T(8,128)(2,1)}, f32[1024,768]{1,0:T(8,128)}) custom-call(bf16[1152,768]{1,0:T(8,128)(2,1)} %get-tuple-element.50.own_ref, bf16[1152,768]{1,0:T(8,128)(2,1)} %get-tuple-element.51.got_ref, s32[1024,1]{1,0:T(8,128)} %copy.86.mine_ref, s32[1024,1]{1,0:T(8,128)} %iota_subtract_fusion.spot_ref, ...), custom_call_target="tpu_custom_call" | custom-call | tf_op jit(solution)/shard_map/project/pallas_call | solution.py:137
  232.8 1.0 broadcast_in_dim.37.seg_ref
  233.8 20.1 %attend.1 = (bf16[1024,768]{1,0:T(8,128)(2,1)}, f32[6,1,2048]{2,1,0:T(1,128)}) custom-call(bf16[1024,2304]{1,0:T(8,128)(2,1)} %get-tuple-element.53.q_ref.k_ref.v_ref.qkv_any, bf16[1024,2304]{1,0:T(8,128)(2,1)} %get-tuple-element.53.q_ref.k_ref.v_ref.qkv_any, bf16[1024,2304]{1,0:T(8,128)(2,1)} %get-tuple-element.53.q_ref.k_ref.v_ref.qkv_any, ...), custom_call_target="tpu_custom_call" | custom-call | tf_op jit(solution)/shard_map/attend/pallas_call | solution.py:177
  254.0 1.1 gather_fusion
  255.1 0.6 concatenate.101.norm_ref
  255.8 0.6 concatenate.108.norm_ref
  256.4 3.2 fusion.24
  259.6 0.6 fusion.27
  260.3 29.2 %after.1 = (f32[1024,768]{1,0:T(8,128)}, f32[1024,768]{1,0:T(8,128)}, f32[1024,768]{1,0:T(8,128)}, bf16[1024,3072]{1,0:T(8,128)(2,1)}) custom-call(bf16[1024,768]{1,0:T(8,128)(2,1)} %get-tuple-element.54.ctx_ref, f32[1024,768]{1,0:T(8,128)} %get-tuple-element.55.x_ref, bf16[768,768]{1,0:T(8,128)(2,1)} %bitcast.126, ...), custom_call_target="tpu_custom_call" | custom-call | tf_op jit(solution)/shard_map/after/pallas_call | solution.py:244
  289.5 1.6 convert_reduce_fusion
  291.3 0.6 fusion.21
  291.9 4.1 slice.261
  296.0 2.4 slice.264
  298.4 0.7 broadcast_in_dim.71.place_ref
  299.1 20.1 %last_forward.1 = (bf16[1024,1536]{1,0:T(8,128)(2,1)}, bf16[128,768]{1,0:T(8,128)(2,1)}, bf16[1024,128]{1,0:T(8,128)(2,1)}, f32[6,256]{1,0:T(8,128)}, f32[128,76...) custom-call(f32[1024,768]{1,0:T(8,128)} %get-tuple-element.56.x_ref,, ...), custom_call_target="tpu_custom_call" | custom-call | tf_op jit(solution)/shard_map/last_forward/pallas_call | solution.py:360
  319.2 1.7 broadcast_in_dim.73.bias_any
  320.9 65.0 %head.1 = (f32[768,128]{1,0:T(8,128)}, f32[1,128]{1,0:T(1,128)}) custom-call(bf16[128,768]{1,0:T(8,128)(2,1)} %get-tuple-element.57.u_ref, bf16[3200,768]{1,0:T(8,128)(2,1)} %get-tuple-element.58.e_any, bf16[768,3200]{1,0:T(8,128)(2,1)} %get-tuple-element.59.et_any, f32[3200,128]{1,0:T(8,128)} %broadcast_in_dim.73.bias_any), custom_call_target="tpu_custom_call" | custom-call | tf_op jit(solution)/shard_map/head/pallas_call | solution.py:1436
  385.9 1.2 copy.88
  387.1 2.6 fusion.7
  389.7 0.6 fusion.23
  391.7 26.5 %last_backward.1 = (f32[1024,768]{1,0:T(8,128)}, bf16[32,32,768]{2,1,0:T(8,128)(2,1)}, f32[768,128]{1,0:T(8,128)}) custom-call(f32[128,768]{1,0:T(8,128)} %get-tuple-element.105.du_ref, bf16[1024,1536]{1,0:T(8,128)(2,1)} %get-tuple-element.62.kv_ref, bf16[128,768]{1,0:T(8,128)(2,1)} %get-tuple-element.63.q_ref, bf16[1024,128]{1,0:T(8,128)(2,1)} %get-tuple-element.64.mid_ref, ...), custom_call_target="tpu_custom_call" | custom-call | tf_op jit(solution)/shard_map/last_backward/pallas_call | solution.py:537
  418.1 0.7 broadcast.203.facts
  418.8 70.0 %finish.1 = (f32[8,128]{1,0:T(8,128)}, f32[24,768]{1,0:T(8,128)}, f32[24,768]{1,0:T(8,128)}, f32[24,768]{1,0:T(8,128)}, f32[24,128]{1,0:T(8,128)}, /*index=5*/f32[24,128]{1,0:T(8,128)}, f32[24,128]{1,0:T(8,128)}) custom-call(f32[1024,768]{1,0:T(8,128)} %get-tuple-element.72.dout_any, f32[1024,768]{1,0:T(8,128)} %get-tuple-element.73.one_any, ...), custom_call_target="tpu_custom_call" | custom-call | tf_op jit(solution)/shard_map/finish/pallas_call | solution.py:1125
  488.9 0.7 slice_bitcast_fusion.6
  489.6 0.7 copy.92
  490.3 0.7 slice_bitcast_fusion.5
  491.0 0.7 copy.93
  491.6 0.7 slice_bitcast_fusion.4
  492.4 0.7 copy.94
  493.0 1.3 fusion.30
  494.3 1.5 copy.124
  495.8 1.5 copy.125
  497.4 1.5 copy.126
  (99 shorter events, 3.0 us)
Async XLA Ops:
  7.2 4.5 copy-start.18
  7.2 4.5 copy-start.20
  7.2 284.7 %all-gather.5.cloned.1.call-start = ((), (), s32[]{:S(2)}) async-start(), calls=%async_computation | async-start | bytes 14598144 | tf_op jit(solution)/shard_map/all_gather | solution.py:1550
  11.6 7.2 %copy-start.7 = (f32[2,2,8,24]{3,2,1,0:T(8,128)S(1)}, f32[2,2,8,24]{3,2,1,0:T(8,128)}, u32[]{:S(2)}) copy-start(f32[2,2,8,24]{3,2,1,0:T(8,128)} %param.44) | copy-start | bytes 9220
  11.6 7.4 %copy-start.2 = (bf16[2,768,96]{1,2,0:T(8,128)(2,1)S(1)}, bf16[2,768,96]{1,2,0:T(8,128)(2,1)}, u32[]{:S(2)}) copy-start(bf16[2,768,96]{1,2,0:T(8,128)(2,1)} %param.38) | copy-start | bytes 884740
  11.6 7.4 %copy-start.3 = (bf16[2,96,768]{2,1,0:T(8,128)(2,1)S(1)}, bf16[2,96,768]{2,1,0:T(8,128)(2,1)}, u32[]{:S(2)}) copy-start(bf16[2,96,768]{2,1,0:T(8,128)(2,1)} %param.39) | copy-start | bytes 884740
  11.6 7.4 %copy-start.5 = (bf16[2,768,72]{1,2,0:T(8,128)(2,1)S(1)}, bf16[2,768,72]{1,2,0:T(8,128)(2,1)}, u32[]{:S(2)}) copy-start(bf16[2,768,72]{1,2,0:T(8,128)(2,1)} %param.36) | copy-start | bytes 663556
  17.2 1.8 copy-start.6
  17.2 1.8 copy-start.1
  22.2 35.1 %copy-start.16 = (f32[1600]{0:T(1024)S(1)}, f32[1600]{0:T(1024)}, u32[]{:S(2)}) copy-start(f32[1600]{0:T(1024)} %param.42) | copy-start | bytes 19204
  207.1 3.2 copy-start.9
  208.3 2.9 copy-start.11
  209.3 4.0 copy-start.19
  209.3 4.6 copy-start.4
  211.3 21.5 %copy-start.8 = (f32[1,1024]{1,0:T(1,128)}, f32[1,1024]{1,0:T(1,128)S(1)}, u32[]{:S(2)}) copy-start(f32[1,1024]{1,0:T(1,128)S(1)} %convert_element_type.76.seg_row_ref) | copy-start | bytes 12292
  212.0 2.9 copy-start.12
  212.2 4.0 copy-start.13
  212.3 4.6 copy-start.14
  212.3 4.6 copy-start.15
  212.3 5.3 %copy-start.10 = (f32[2,6144]{1,0:T(2,128)S(1)}, f32[2,6144]{1,0:T(2,128)}, u32[]{:S(2)}) copy-start(f32[2,6144]{1,0:T(2,128)} %param.40) | copy-start | bytes 147460
  260.3 31.0 %copy-start.21 = (f32[4]{0:T(128)S(1)}, f32[4]{0:T(128)}, u32[]{:S(2)}) copy-start(f32[4]{0:T(128)} %param.30) | copy-start | bytes 52
  296.0 2.4 copy-start.17
  320.9 66.2 %copy-start = (bf16[128,768]{1,0:T(8,128)(2,1)S(1)}, bf16[128,768]{1,0:T(8,128)(2,1)}, u32[]{:S(2)}) copy-start(bf16[128,768]{1,0:T(8,128)(2,1)} %get-tuple-element.57.u_ref) | copy-start | bytes 589828
  385.9 3.8 copy-start.22
Sparse Core Ops, SparseCore 0:
  11.7 144.9 all-gather.4

commit v6 on v5

--- a/solution.py
+++ b/solution.py
@@ -262,23 +262,54 @@
     return mm(choose, high) + mm(choose, middle) + mm(choose, low)
 
 
+def unpack_rows(slab_ref, targets):
+    shards = slab_ref.shape[0]
+
+    @pl.loop(0, shards // 2)
+    def _(k):
+        first, second = slab_ref[2 * k].astype(F32), slab_ref[2 * k + 1].astype(F32)
+        at = 0
+        for target in targets:
+            each = target.shape[0] // shards
+            both = jnp.concatenate([first[at : at + each], second[at : at + each]], 0)
+            target[pl.ds(pl.multiple_of(2 * each * k, 2 * each), 2 * each), :] = both.astype(BF)
+            at += each
+
+
 def last_forward_body(
-    x_ref, place_ref, place_row_ref, seg_ref, down_ref, w_ref, adapt_ref, bias_ref, wo_ref, up_any, dn_any,
-    bo_ref, b1_ref, b2_ref, norm_ref, hb_ref, hbias_ref,
-    kv_ref, q_ref, mid_ref, log_ref, one_ref, slope_ref, two_ref, low_ref, act_ref, hslope_ref, feat_ref,
-    up_ref, dn_ref, ctx_ref, sems, *, places,
+    x_ref, place_ref, place_row_ref, seg_ref, down_ref, adapt_ref, bias_ref, weights_any, up_any, dn_any,
+    bo_ref, b1_ref, b2_ref, norm_ref, hbias_ref,
+    kv_ref, q_ref, mid_ref, log_ref, one_ref, slope_ref, two_ref, low_ref, act_ref, hslope_ref, feat_ref, *more,
+    places, starts,
 ):
     copies = []
-    for k, (source, target, place) in enumerate(
-        ((up_any, up_ref, places[0]), (dn_any, dn_ref, places[1]))
-    ):
-        rows = target.shape[1]
-        copies.append(
-            pltpu.make_async_copy(
-                source.at[:, pl.ds(place * rows, rows), :], target, sems.at[k]
-            )
-        )
-        copies[-1].start()
+    if starts is None:
+        up_ref, dn_ref, ctx_ref, w_ref, wo_ref, hb_ref, sems = more
+        sources = zip(weights_any, (w_ref, wo_ref, hb_ref))
+    else:
+        w_out, wo_out, hb_out, up_ref, dn_ref, ctx_ref, w_ref, wo_ref, hb_ref, in_slab, hb_slab, sems = more
+        sources = [
+            (weights_any[0].at[:, pl.ds(start, slab.shape[1]), :], slab)
+            for start, slab in zip(starts, (in_slab, hb_slab))
+        ]
+    for source, target in sources:
+        copies.append((source, target))
+    early = len(copies)
+    for source, target, place in ((up_any, up_ref, places[0]), (dn_any, dn_ref, places[1])):
+        each = target.shape[1]
+        copies.append((source.at[:, pl.ds(place * each, each), :], target))
+    copies = [pltpu.make_async_copy(*ends, sems.at[k]) for k, ends in enumerate(copies)]
+    for copy in copies:
+        copy.start()
+    for copy in copies[:early]:
+        copy.wait()
+    copies = copies[early:]
+    if starts is not None:
+        unpack_rows(in_slab, (w_ref, wo_ref))
+        unpack_rows(hb_slab, (hb_ref,))
+        for k, ends in enumerate(((w_ref, w_out), (wo_ref, wo_out), (hb_ref, hb_out))):
+            copies.append(pltpu.make_async_copy(*ends, sems.at[4 + k]))
+            copies[-1].start()
     rows, hidden = x_ref.shape
     labels = place_ref.shape[0]
     lanes = 2 * (hidden // HEADS)
@@ -349,7 +380,9 @@
     return pltpu.VMEM((array.shape[0], rows, array.shape[2]), BF)
 
 
-def last_forward(x, place_col, place_row, seg_wide, down, w, adapt, bias, wo, up, dn, bo, b1, b2, norms, hb, hbias):
+def last_forward(
+    x, place_col, place_row, seg_wide, down, adapt, bias, weights, starts, up, dn, bo, b1, b2, norms, hbias
+):
     rows, hidden = x.shape
     labels = place_col.shape[0]
     units = b1.shape[1]
@@ -357,10 +390,25 @@
     anywhere = pl.BlockSpec(memory_space=pl.ANY)
     shape = jax.ShapeDtypeStruct
     pairs = HEADS // 2
+    matrices = [(3 * hidden, hidden), (hidden, hidden), (hidden, hidden)]
+    slabs = []
+    if starts is not None:
+        shards = weights[0].shape[0]
+        slabs = [
+            pltpu.VMEM((shards, 4 * hidden // shards, hidden), BF),
+            pltpu.VMEM((shards, weights[0].shape[1] - starts[1], hidden), BF),
+        ]
+
+    def body(*refs):
+        head, rest = refs[:7], refs[7:]
+        return last_forward_body(
+            *head, rest[: len(weights)], *rest[len(weights) :], places=(up[1], dn[1]), starts=starts
+        )
+
     return pl.pallas_call(
-        functools.partial(last_forward_body, places=(up[1], dn[1])),
-        in_specs=[whole] * 9 + [anywhere] * 2 + [whole] * 6,
-        out_specs=[whole] * 11,
+        body,
+        in_specs=[whole] * 7 + [anywhere] * (len(weights) + 2) + [whole] * 5,
+        out_specs=[whole] * 11 + ([anywhere] * 3 if slabs else []),
         out_shape=[
             shape((rows, 2 * hidden), BF),
             shape((labels, hidden), BF),
@@ -373,16 +421,19 @@
             shape((labels, hidden), F32),
             shape((labels, hidden), F32),
             shape((labels, hidden), BF),
-        ],
+        ]
+        + ([shape(m, BF) for m in matrices] if slabs else []),
         scratch_shapes=[
             slab_scratch(up),
             slab_scratch(dn),
             pltpu.VMEM((labels, hidden), BF),
-            pltpu.SemaphoreType.DMA((2,)),
+            *[pltpu.VMEM(m, BF) for m in matrices],
+            *slabs,
+            pltpu.SemaphoreType.DMA((7,)),
         ],
         compiler_params=params(),
         name="last_forward",
-    )(x, place_col, place_row, seg_wide, down, w, adapt, bias, wo, up[0], dn[0], bo, b1, b2, norms, hb, hbias)
+    )(x, place_col, place_row, seg_wide, down, adapt, bias, *weights, up[0], dn[0], bo, b1, b2, norms, hbias)
 
 
 def vocab_body(u_ref, e_ref, et_ref, bias_ref, num_ref, log_ref, scores, weights):
@@ -820,143 +871,278 @@
 ITEMS = 28
 
 
-ITEMS = 28
-PICK = 64
-GROUP = 16
-
-
-def start_body(
-    streams, shards, rows, table_any, chunk, note, bias,
-    full_chunk, got, notes, biases, e_out, et_out,
-    e_ref, et_ref,
-    sends, receives, hands, hands_got, row_sems, note_sends, note_gets, bias_sends, bias_gets,
-    own_sems, e_sems, out_sems,
+def start_body(shards, rows, fact, got, facts, row_sems, sends, receives, own_sem):
+    here = position()
+    me = number_of(here)
+    greet_all(shards)
+    own = pltpu.make_async_copy(fact, facts.at[me], own_sem.at[0])
+    own.start()
+    await_all(shards)
+    swap = pltpu.make_async_remote_copy(
+        src_ref=rows,
+        dst_ref=got,
+        send_sem=row_sems.at[0],
+        recv_sem=row_sems.at[1],
+        device_id=device_of(dict(here, x=1 - here["x"])),
+        device_id_type=MESH,
+    )
+    swap.start()
+    spread(lambda peer: fact, facts, sends, receives, me, shards)
+    collect(lambda peer: fact, facts, sends, receives, me, shards)
+    swap.wait()
+    own.wait()
+
+
+def start_exchange(rows, fact, shards):
+    anywhere = pl.BlockSpec(memory_space=pl.ANY)
+    shape = jax.ShapeDtypeStruct
+    sems = pltpu.SemaphoreType.DMA
+    return pl.pallas_call(
+        functools.partial(start_body, shards),
+        in_specs=[anywhere] * 2,
+        out_specs=[anywhere] * 2,
+        out_shape=[shape(rows.shape, rows.dtype), shape((shards, *fact.shape), fact.dtype)],
+        scratch_shapes=[sems((2,)), sems((shards,)), sems((shards,)), sems((1,))],
+        compiler_params=params(collective_id=1, has_side_effects=True),
+        name="start_exchange",
+    )(rows, fact)
+
+
+def first_layer_body(
+    streams, shards, places,
+    own_any, got_any, first_any, chunk, table_any, mine_ref, spot_ref, spots_ref, first_norm_ref, down_ref,
+    adapt_ref, bias_ref, seg_ref, seg_row_ref, bo_ref, b1_ref, b2_ref, norm_ref,
+    qkv_out, x_out, one_out, two_out, slope_out, wo_out, full_chunk, e_out, et_out, mid_ref, log_ref,
+    own, got, in_slab, w, wo, up, dn, x, qkv, ctx, two, out, slope, e_ref, et_ref,
+    load_sems, tile_sems, out_sems, swap_sems, sends, receives, hands, hands_got,
 ):
     here = position()
     me = number_of(here)
     across = device_of(dict(here, x=1 - here["x"]))
+    rows, hidden = x.shape
+    tile = split_of(rows, 256, 16)
+    tiles = rows // tile
+    lanes = 2 * (hidden // HEADS)
+    pairs = hidden // lanes
     slice_rows = e_ref.shape[0] // 2
-    greet_all(shards)
-    plain = [
-        pltpu.make_async_copy(source, target, own_sems.at[k])
+    own_slice = table_any.at[pl.ds(pl.multiple_of((me % 16) * slice_rows, 16), slice_rows), :]
+
+    def slab(target, place):
+        each = target.shape[1]
+        return first_any.at[:, pl.ds(place * each, each), :]
+
+    loads = [
+        pltpu.make_async_copy(source, target, load_sems.at[k])
         for k, (source, target) in enumerate(
-            ((chunk, full_chunk.at[me]), (note, notes.at[me]), (bias, biases.at[me]))
+            (
+                (own_any.at[pl.ds(0, rows), :], own),
+                (got_any.at[pl.ds(0, rows), :], got),
+                (first_any.at[:, pl.ds(places[2], in_slab.shape[1]), :], in_slab),
+                (slab(up, places[0]), up),
+                (slab(dn, places[1]), dn),
+                (own_slice, e_ref.at[pl.ds(0, slice_rows), :]),
+                (chunk, full_chunk.at[me]),
+            )
         )
     ]
-    for copy in plain:
+    for copy in loads:
         copy.start()
-    own_slice = table_any.at[
-        pl.ds(pl.multiple_of((me % 16) * slice_rows, 16), slice_rows), :
+    barrier = pltpu.get_barrier_semaphore()
+    peers = [
+        dict(here, c=1 - here["c"]),
+        dict(here, x=1 - here["x"]),
+        dict(here, y=1 - here["y"]),
+        *[dict(here, z=flip(here["z"], k)) for k in (1, 2, 3)],
     ]
-    keep = pltpu.make_async_copy(own_slice, e_ref.at[pl.ds(0, slice_rows), :], own_sems.at[4])
-    keep.start()
+    for peer in peers:
+        pl.semaphore_signal(barrier, inc=1, device_id=device_of(peer), device_id_type=MESH)
+    pl.semaphore_wait(barrier, len(peers))
+    gathers = [
+        Gather(
+            chunk, full_chunk, start, size, order, sends.at[k], receives.at[k], hands.at[k], hands_got.at[k]
+        )
+        for k, (start, size, order) in enumerate(streams)
+    ]
     swap = pltpu.make_async_remote_copy(
         src_ref=own_slice,
         dst_ref=e_ref.at[pl.ds(slice_rows, slice_rows), :],
-        send_sem=e_sems.at[0],
-        recv_sem=e_sems.at[1],
+        send_sem=swap_sems.at[0],
+        recv_sem=swap_sems.at[1],
         device_id=across,
         device_id_type=MESH,
     )
-    await_all(shards)
-    gathers = [
-        Gather(
-            chunk, full_chunk, start, size, order, sends.at[k], receives.at[k], hands.at[k], hands_got.at[k]
-        )
-        for k, (start, size, order) in enumerate(streams)
+
+    def advance(first, last):
+        for index in range(first, last + 1):
+            for gather in gathers:
+                gather.step(index)
+
+    advance(0, 0)
+    for copy in loads[:3]:
+        copy.wait()
+    unpack_rows(in_slab, (w, wo))
+
+    @pl.loop(0, tiles)
+    def _(i):
+        part = pl.ds(pl.multiple_of(i * tile, tile), tile)
+        project_body(
+            own.at[part, :], got.at[part, :], mine_ref.at[part, :], spot_ref.at[part, :], spots_ref,
+            first_norm_ref, down_ref, w, adapt_ref, bias_ref, qkv.at[part, :], mid_ref.at[part, :],
+            x.at[part, :],
+        )
+
+        @pl.when(i == tiles - 2)
+        def _():
+            advance(1, 4)
+            swap.start()
+
+    early = [
+        pltpu.make_async_copy(qkv, qkv_out, out_sems.at[0]),
+        pltpu.make_async_copy(wo, wo_out, out_sems.at[1]),
     ]
-    for gather in gathers:
-        gather.step(0)
-    spread(lambda peer: note, notes, note_sends, note_gets, me, shards)
-    spread(lambda peer: bias, biases, bias_sends, bias_gets, me, shards)
-    swap.start()
-
-    send_rows = pltpu.make_async_remote_copy(
-        src_ref=rows,
-        dst_ref=got,
-        send_sem=row_sems.at[0],
-        recv_sem=row_sems.at[1],
-        device_id=across,
-        device_id_type=MESH,
-    )
-    send_rows.start()
-
-    def turn(k):
-        part = slice(k * 128, (k + 1) * 128)
+    for copy in early:
+        copy.start()
+
+    @pl.loop(0, pairs)
+    def _(p):
+        column = lambda kind: pl.ds(pl.multiple_of((kind * pairs + p) * lanes, lanes), lanes)
+        attend_body(
+            qkv.at[:, column(0)], qkv.at[:, column(1)], qkv.at[:, column(2)], seg_ref, seg_row_ref,
+            ctx.at[:, column(0)], log_ref.at[pl.ds(p, 1)],
+        )
+
+        @pl.when(p == pairs // 2 - 1)
+        def _():
+            advance(5, 11)
+
+        @pl.when(p == pairs - 1)
+        def _():
+            advance(12, 15)
+
+    for copy in loads[3:5]:
+        copy.wait()
+
+    def tile_copies(i):
+        part = pl.ds(pl.multiple_of(i * tile, tile), tile)
+        turn = i % 2
+        return [
+            pltpu.make_async_copy(source, target.at[part, :], tile_sems.at[k, i])
+            for k, (source, target) in enumerate(
+                (
+                    (out.at[turn], x_out),
+                    (two.at[turn], two_out),
+                    (slope.at[turn], slope_out),
+                    (x.at[part, :], one_out),
+                )
+            )
+        ]
+
+    plan = {tiles - 4: (16, 19), tiles - 3: (20, 22), tiles - 2: (23, 25), tiles - 1: (26, 27)}
+
+    @pl.loop(0, tiles)
+    def _(i):
+        part = pl.ds(pl.multiple_of(i * tile, tile), tile)
+        turn = i % 2
+
+        @pl.when(i >= 2)
+        def _():
+            for copy in tile_copies(i - 2):
+                copy.wait()
+
+        after_body(
+            ctx.at[part, :], x.at[part, :], wo, up, dn, bo_ref, b1_ref, b2_ref, norm_ref, out.at[turn],
+            x.at[part, :], two.at[turn], slope.at[turn],
+        )
+        for copy in tile_copies(i):
+            copy.start()
+        for k, (first, last) in plan.items():
+            pl.when(i == k)(functools.partial(advance, first, last))
+
+    loads[5].wait()
+    swap.wait_recv()
+
+    @pl.loop(0, e_ref.shape[0] // 128)
+    def _(k):
+        part = pl.ds(pl.multiple_of(k * 128, 128), 128)
         et_ref[:, part] = e_ref[part, :].astype(F32).T.astype(BF)
 
-    def out_copies():
-        return (
-            pltpu.make_async_copy(e_ref, e_out, out_sems.at[0]),
-            pltpu.make_async_copy(et_ref, et_out, out_sems.at[1]),
-        )
-
-    turned = 0
-    own_turns = slice_rows // 128
-    for index in range(1, ITEMS):
-        if turned < own_turns:
-            if turned == 0:
-                keep.wait()
-            turn(turned)
-            turned += 1
-        for gather in gathers:
-            gather.step(index)
-    swap.wait_recv()
-    for k in range(turned, e_ref.shape[0] // 128):
-        turn(k)
-    copies = out_copies()
-    for copy in copies:
+    late = [
+        pltpu.make_async_copy(e_ref, e_out, out_sems.at[2]),
+        pltpu.make_async_copy(et_ref, et_out, out_sems.at[3]),
+    ]
+    for copy in late:
         copy.start()
     for gather in gathers:
         gather.finish()
-    collect(lambda peer: note, notes, note_sends, note_gets, me, shards)
-    collect(lambda peer: bias, biases, bias_sends, bias_gets, me, shards)
-    send_rows.wait()
+    for i in (tiles - 2, tiles - 1):
+        for copy in tile_copies(i):
+            copy.wait()
     swap.wait_send()
-    for copy in plain:
+    for copy in early + late + loads[6:]:
         copy.wait()
-    for copy in copies:
-        copy.wait()
-
-
-def start_exchange(rows, table, chunk, note, bias, shards, slice_rows):
+
+
+def first_layer(own, got, first, chunk, table, more, places, units, slice_rows, shards):
+    whole = pl.BlockSpec(memory_space=pltpu.VMEM)
     anywhere = pl.BlockSpec(memory_space=pl.ANY)
+    mine, down = more[0], more[4]
+    rows, hidden = mine.shape[0], table.shape[1]
+    tile = split_of(rows, 256, 16)
+    pairs = HEADS // 2
     cut = (chunk.shape[0] * 5 // 6 + 15) // 16 * 16
     streams = ((0, cut, "xzy"), (cut, chunk.shape[0] - cut, "xyz"))
-    hidden = table.shape[1]
+    each = units // shards
     shape = jax.ShapeDtypeStruct
     sems = pltpu.SemaphoreType.DMA
     return pl.pallas_call(
-        functools.partial(start_body, streams, shards),
-        in_specs=[anywhere] * 5,
-        out_specs=[anywhere] * 6,
+        functools.partial(first_layer_body, streams, shards, places),
+        in_specs=[anywhere] * 5 + [whole] * len(more),
+        out_specs=[anywhere] * 9 + [whole] * 2,
         out_shape=[
-            shape((shards, *chunk.shape), chunk.dtype),
-            shape(rows.shape, rows.dtype),
-            shape((shards, *note.shape), note.dtype),
-            shape((shards, *bias.shape), bias.dtype),
-            shape((2 * slice_rows, hidden), table.dtype),
-            shape((hidden, 2 * slice_rows), table.dtype),
+            shape((rows, 3 * hidden), BF),
+            shape((rows, hidden), F32),
+            shape((rows, hidden), F32),
+            shape((rows, hidden), F32),
+            shape((rows, units), BF),
+            shape((hidden, hidden), BF),
+            shape((shards, *chunk.shape), BF),
+            shape((2 * slice_rows, hidden), BF),
+            shape((hidden, 2 * slice_rows), BF),
+            shape((rows, down.shape[1]), BF),
+            shape((pairs, 1, 2 * rows), F32),
         ],
         scratch_shapes=[
+            pltpu.VMEM((rows, hidden), BF),
+            pltpu.VMEM((rows, hidden), BF),
+            pltpu.VMEM((shards, 4 * hidden // shards, hidden), BF),
+            pltpu.VMEM((3 * hidden, hidden), BF),
+            pltpu.VMEM((hidden, hidden), BF),
+            pltpu.VMEM((shards, each, hidden), BF),
+            pltpu.VMEM((shards, each, hidden), BF),
+            pltpu.VMEM((rows, hidden), F32),
+            pltpu.VMEM((rows, 3 * hidden), BF),
+            pltpu.VMEM((rows, hidden), BF),
+            pltpu.VMEM((2, tile, hidden), F32),
+            pltpu.VMEM((2, tile, hidden), F32),
+            pltpu.VMEM((2, tile, units), BF),
             pltpu.VMEM((2 * slice_rows, hidden), BF),
             pltpu.VMEM((hidden, 2 * slice_rows), BF),
+            sems((7,)),
+            sems((4, rows // tile)),
+            sems((4,)),
+            sems((2,)),
             sems((2, 4 * ITEMS)),
             sems((2, 16)),
             sems((2, ITEMS)),
             sems((2, 16)),
-            sems((2,)),
-            sems((shards,)),
-            sems((shards,)),
-            sems((shards,)),
-            sems((shards,)),
-            sems((5,)),
-            sems((2,)),
-            sems((2,)),
         ],
-        compiler_params=params(collective_id=1, has_side_effects=True),
-        name="start_exchange",
-    )(rows, table, chunk, note, bias)
+        compiler_params=params(collective_id=3, has_side_effects=True),
+        name="first_layer",
+    )(own, got, first, chunk, table, *more)
+
+
+PICK = 64
+GROUP = 16
 
 
 def look_up_body(ids, low_ref, table, first_ref, second_ref, stage):
@@ -1535,24 +1721,21 @@
         ]
         for layer in range(layers)
     ]
-    ups = adapter_up_matrix.astype(BF).reshape(-1)
-    up_rows = -(-ups.size // hidden)
-    chunks[0] += [
-        head_projection.astype(BF),
-        jnp.pad(ups, (0, up_rows * hidden - ups.size)).reshape(up_rows, hidden),
-    ]
+    chunks[-1].append(head_projection.astype(BF))
     chunks = [pad_rows(jnp.concatenate(pieces, 0), 32) for pieces in chunks]
+    first_full = lax.all_gather(chunks[0], BOTH, axis=0, tiled=False)
 
     table_rows = embed.shape[0]
     wanted = jnp.concatenate([input_token_index[0], label_target_token[0]])
     dp_count = lax.axis_size("dp")
     group_ids = lax.all_gather(wanted, "dp", axis=0, tiled=False) - dp_index * table_rows
-    later_full = [lax.all_gather(chunk, BOTH, axis=0, tiled=False) for chunk in chunks[1:]]
     inside = (group_ids >= 0) & (group_ids < table_rows)
     group_ids = jnp.clip(group_ids, 0, table_rows - 1)
     mine = lax.dynamic_index_in_dim(inside, dp_index, 0, keepdims=False)
+
     task_range = jnp.arange(TASKS, dtype=jnp.int32)
     slice_rows = vocabulary_bias.shape[0]
+    ups = adapter_up_matrix.reshape(-1)
     if grouped:
         pair_ids = jnp.concatenate(
             [
@@ -1561,55 +1744,28 @@
             ]
         )
         other_rows, own_rows = look_up(pair_ids, embed)
-        note = jnp.broadcast_to(sequence_task_index.astype(F32)[:, None], (8, 128))
-        bias_rows = -(-slice_rows // 1024) * 8
-        bias_block = jnp.pad(vocabulary_bias, (0, bias_rows * 128 - slice_rows)).reshape(bias_rows, 128)
-        first_full, got, notes, biases, own_vocab, own_turned = start_exchange(
-            other_rows, embed, chunks[0], note, bias_block, shards, slice_rows
-        )
-        every_task = notes[:, 0, 0].astype(jnp.int32)
-        all_bias = biases.reshape(shards, -1)[:, :slice_rows].reshape(-1)
+        fact = jnp.concatenate([vocabulary_bias, ups, sequence_task_index.astype(F32)])
+        fact_rows = -(-fact.size // 1024) * 8
+        got, facts = start_exchange(
+            other_rows, jnp.pad(fact, (0, fact_rows * 128 - fact.size)).reshape(fact_rows, 128), shards
+        )
+        facts = facts.reshape(shards, -1)
+        all_bias = facts[:, :slice_rows].reshape(-1)
+        every_up = facts[:, slice_rows : slice_rows + ups.size]
+        every_task = facts[:, slice_rows + ups.size].astype(jnp.int32)
     else:
-        first_full = lax.all_gather(chunks[0], BOTH, axis=0, tiled=False)
         looked = jnp.where(
             inside.reshape(-1)[:, None], embed[group_ids.reshape(-1)], jnp.zeros((), BF)
         )
         own_rows = got = lax.psum_scatter(looked, "dp", scatter_dimension=0, tiled=True)
-        own_slice = lax.dynamic_slice_in_dim(embed, fsdp_index * slice_rows, slice_rows, 0)
-        own_vocab = jnp.concatenate(
-            [own_slice]
-            + [
-                lax.ppermute(
-                    own_slice, "dp", [(k, (k + shift) % dp_count) for k in range(dp_count)]
-                )
-                for shift in range(1, dp_count)
-            ],
-            0,
-        )
-        own_turned = own_vocab.T
+        all_bias = lax.all_gather(vocabulary_bias, BOTH, axis=0, tiled=True)
+        every_up = lax.all_gather(ups, BOTH, axis=0, tiled=False)
         every_task = lax.all_gather(sequence_task_index, BOTH, axis=0, tiled=True)
-        all_bias = lax.all_gather(vocabulary_bias, BOTH, axis=0, tiled=True)
-    gathered = [first_full, *later_full]
     counts = labels * jnp.sum((every_task[:, None] == task_range[None, :]).astype(F32), 0)
     task_hot = (sequence_task_index[:, None] == task_range[None, :]).astype(F32)
     row_weight = jnp.sum(task_hot[0] * (task_loss_weight / jnp.maximum(counts, 1.0)))
-
-    slabs = [
-        (slab_of(gathered[layer], 0, ff_rows), slab_of(gathered[layer], ff_rows, ff_rows))
-        for layer in range(layers)
-    ]
-    in_weights, out_weights = [], []
-    for layer in range(layers):
-        at = 2 * ff_rows
-        in_weights.append(gathered[layer][:, at : at + qkv_rows].reshape(-1, hidden))
-        at += qkv_rows
-        out_weights.append(gathered[layer][:, at : at + out_rows].reshape(-1, hidden))
-    at = 2 * ff_rows + qkv_rows + out_rows
-    head_full = first_full[:, at : at + head_rows].reshape(-1, hidden)
-    at += head_rows
     ups_full = (
-        first_full[:, at : at + up_rows]
-        .reshape(shards, -1)[:, : ups.size]
+        every_up.astype(BF)
         .reshape(shards, layers, 2, rank, up_part)
         .transpose(1, 2, 3, 0, 4)
         .reshape(layers, 2, rank, hidden)
@@ -1684,31 +1840,62 @@
             for shift in range(dp_count)
         ]
     )
-    vocab_block = (
-        own_vocab,
-        own_turned,
-        jnp.broadcast_to(own_bias[:, None], (own_bias.shape[0], 128)),
-    )
+    bias_wide = jnp.broadcast_to(own_bias[:, None], (own_bias.shape[0], 128))
     target_bias = all_bias[label_target_token[0]]
 
     first_norm = jnp.concatenate([norm_gain_vector[:1], norm_bias_vector[:1]], 0)
-    qkv, mid, hidden_rows = project(
-        own_rows, got, mine[:tokens, None].astype(jnp.int32), spot, position_embedding, first_norm,
-        downs[0], in_weights[0], adapters[0], bias_of[0][0],
-    )
-    context, logs = attend(qkv, seg_wide, seg_row)
-    x_last, one, two, slope = after(
-        context, hidden_rows, out_weights[0], *slabs[0], *bias_of[0][1:], norms_of[0]
-    )
-    *saved, features = last_forward(
-        x_last, place_col, place_row, seg_wide, downs[1], in_weights[1], adapters[1], bias_of[1][0],
-        out_weights[1], *slabs[1], *bias_of[1][1:], norms_of[1], head_full, head_dense_bias[None, :],
-    )
+    mine_col = mine[:tokens, None].astype(jnp.int32)
+    in_start = 2 * ff_rows
+    slabs_of = lambda full_chunk: (slab_of(full_chunk, 0, ff_rows), slab_of(full_chunk, ff_rows, ff_rows))
+    slabs = [slabs_of(first_full)]
+    last_inputs = (place_col, place_row, seg_wide, downs[1], adapters[1], bias_of[1][0])
     if grouped:
-        mean_t, own_logs = head(features, *vocab_block)
+        more = (
+            mine_col, spot, position_embedding, first_norm, downs[0], adapters[0], bias_of[0][0],
+            seg_wide, seg_row, *bias_of[0][1:], norms_of[0],
+        )
+        qkv, x_last, one, two, slope, out_first, last_full, own_vocab, own_turned, mid, logs = first_layer(
+            own_rows, got, first_full, chunks[1], embed, more, (0, 1, in_start), shards * ff_rows, slice_rows,
+            shards,
+        )
+        slabs.append(slabs_of(last_full))
+        *saved, features, in_last, out_last, head_full = last_forward(
+            x_last, *last_inputs, (last_full,), (in_start, in_start + qkv_rows + out_rows),
+            *slabs[1], *bias_of[1][1:], norms_of[1], head_dense_bias[None, :],
+        )
+        mean_t, own_logs = head(features, own_vocab, own_turned, bias_wide)
     else:
+        last_full = lax.all_gather(chunks[1], BOTH, axis=0, tiled=False)
+        slabs.append(slabs_of(last_full))
+        taken = lambda full_chunk, start, size: full_chunk[:, start : start + size].reshape(-1, hidden)
+        in_first, in_last = [taken(f, in_start, qkv_rows) for f in (first_full, last_full)]
+        out_first, out_last = [taken(f, in_start + qkv_rows, out_rows) for f in (first_full, last_full)]
+        head_full = taken(last_full, in_start + qkv_rows + out_rows, head_rows)
+        qkv, mid, hidden_rows = project(
+            own_rows, got, mine_col, spot, position_embedding, first_norm, downs[0], in_first, adapters[0],
+            bias_of[0][0],
+        )
+        context, logs = attend(qkv, seg_wide, seg_row)
+        x_last, one, two, slope = after(
+            context, hidden_rows, out_first, *slabs[0], *bias_of[0][1:], norms_of[0]
+        )
+        *saved, features = last_forward(
+            x_last, *last_inputs, (in_last, out_last, head_full), None, *slabs[1], *bias_of[1][1:],
+            norms_of[1], head_dense_bias[None, :],
+        )
+        own_slice = lax.dynamic_slice_in_dim(embed, fsdp_index * slice_rows, slice_rows, 0)
+        own_vocab = jnp.concatenate(
+            [own_slice]
+            + [
+                lax.ppermute(
+                    own_slice, "dp", [(k, (k + shift) % dp_count) for k in range(dp_count)]
+                )
+                for shift in range(1, dp_count)
+            ],
+            0,
+        )
         every = lax.all_gather(features, "fsdp", axis=0, tiled=True)
-        means, local_logs = vocab(every, *vocab_block, labels)
+        means, local_logs = vocab(every, own_vocab, own_vocab.T, bias_wide, labels)
         local_logs = local_logs.reshape(-1, labels)
         all_logs = lax.all_gather(local_logs, "fsdp", axis=0, tiled=False)
         whole_logs = jax.nn.logsumexp(all_logs, axis=0)
@@ -1720,10 +1907,10 @@
     feat_grad = row_weight * (mean_t.T - target_rows)
 
     hidden_grad, dense_gradient, late = last_backward(
-        feat_grad, saved, place_col, place_row, seg_wide, downs[1], in_weights[1], adapters[1],
-        out_weights[1], *slabs[1], norms_of[1], head_full, 3 * rank, shards if grouped else None,
+        feat_grad, saved, place_col, place_row, seg_wide, downs[1], in_last, adapters[1],
+        out_last, *slabs[1], norms_of[1], head_full, 3 * rank, shards if grouped else None,
     )
-    back = (hidden_grad, one, two, slope, out_weights[0], *slabs[0], norms_of[0])
+    back = (hidden_grad, one, two, slope, out_first, *slabs[0], norms_of[0])
     step_as_real = optimizer_step_count[0].astype(F32)
     fades = (1.0 - beta_first**step_as_real, 1.0 - beta_second**step_as_real)
     adapts = (adapter_up_matrix, adapter_moment_first, adapter_moment_second)

time: 510 us -> 474 us (0.929)
  Pallas kernels: 422 us -> 401 us
  local copies, waits for them, and re-layouts: 49.5 us -> 35 us
    pallas_call x5 -> x3, Pallas kernels: 225 us -> 201 us  [the longest x1 103 us: first_layer(): pl.pallas_call(functools.partial(first_layer_body, streams, shards, place...]
    slice x7 -> x3, local copies, waits for them, and re-layouts: 15 us -> 0.17 us  [the longest x1 0.08 us: per_device(): every_up = facts[:, slice_rows:slice_rows + ups.size]]
  transfers between devices with their start and end apart: 1 -> 1, of which waited for: 0 -> 0; matrix products, arithmetic and copies ran while one was open for 6% -> 5% of each run, Pallas kernels for 48% -> 24%
where the time goes in v6:
time: 474 us; the launch traced here: 469 us
  Pallas kernels  401 us (85%)
  local copies, waits for them, and re-layouts  35 us (7%)
  between operations  17.5 us (4%)
  other arithmetic  10 us (2%)
  blocking collectives  5.23 us (1%)
    pallas_call x1, Pallas kernels, first_layer(): pl.pallas_call(functools.partial(first_layer_body, streams, shards, place...  103 us
    pallas_call x1, Pallas kernels, start_exchange(): pl.pallas_call(functools.partial(start_body, shards), in_specs=[anywhere]...  75.8 us
    pallas_call x1, Pallas kernels, finish(): pl.pallas_call(functools.partial(finish_body, shards, (up[1], dn[1]), edg...  69.9 us
    pallas_call x1, Pallas kernels, head(): pl.pallas_call(head_body, in_specs=[whole] + [anywhere] * 3, out_specs=[w...  68.6 us
    pallas_call x1, Pallas kernels, look_up(): pl.pallas_call(look_up_body, in_specs=[pl.BlockSpec(memory_space=pltpu.SM...  35.3 us
    pallas_call x1, Pallas kernels, last_backward(): pl.pallas_call(functools.partial(last_backward_body, places=(up[1], dn[1]...  26.3 us
    pallas_call x1, Pallas kernels, last_forward(): pl.pallas_call(body, in_specs=[whole] * 7 + [anywhere] * (len(weights) +...  22 us
  transfers between devices with their start and end apart: 1, of which 0 were waited for; matrix products, arithmetic and copies ran while one was open for 5% of the time, Pallas kernels for 24%

profile of v6, /device:TPU:0, one launch (start us, length us, event | category | flops | bytes accessed | tf_op | source)
XLA Modules:
  0.0 468.6 jit_solution(5600348630386862255)
XLA Ops:
  7.2 0.9 slice_bitcast_fusion
  8.2 0.9 slice_bitcast_fusion.1
  9.1 0.9 slice_bitcast_fusion.2
  10.0 0.8 slice_bitcast_fusion.3
  10.8 0.8 pad_maximum_fusion
  11.7 5.2 %all-gather.2 = s32[2,1,1152]{2,1,0:T(1,128)S(1)} all-gather(s32[1,1,1152]{2,1,0:T(1,128)S(1)} %reshape.361), channel_id=2, replica_groups=mesh['dp'=2,'fsdp'=16] {'dp'}, dimensions={0}, use_global_device_ids=true | all-gather | bytes 13824 | tf_op jit(solution)/shard_map/all_gather | solution.py:1731
  17.0 0.4 copy.95
  17.4 0.5 copy.98
  18.7 0.6 add_select_fusion.2.ids
  19.3 1.6 fusion.1.low_ref
  21.0 35.3 %look_up.1 = (bf16[1152,768]{1,0:T(8,128)(2,1)}, bf16[1152,768]{1,0:T(8,128)(2,1)}) custom-call(s32[2304]{0:T(1024)} %add_select_fusion.2.ids, s32[2304,1]{1,0:T(8,128)} %fusion.1.low_ref, bf16[1600,16,768]{2,1,0:T(8,128)(2,1)} %bitcast.108), custom_call_target="tpu_custom_call" | custom-call | tf_op jit(solution)/shard_map/look_up/pallas_call | solution.py:1174
  56.3 0.6 pad_bitcast_fusion.fact
  56.9 75.8 %start_exchange.1 = (bf16[1152,768]{1,0:T(8,128)(2,1)}, f32[32,24,128]{2,1,0:T(8,128)}) custom-call(bf16[1152,768]{1,0:T(8,128)(2,1)} %get-tuple-element.49.rows, f32[24,128]{1,0:T(8,128)} %pad_bitcast_fusion.fact), custom_call_target="tpu_custom_call" | custom-call | tf_op jit(solution)/shard_map/start_exchange/pallas_call | solution.py:900
  132.8 1.1 copy.129
  134.0 0.4 reshape.331
  134.5 0.3 reshape.332
  134.9 1.0 copy.102.mine_ref
  135.9 0.2 copy.100
  136.2 0.9 pad.41.adapt_ref
  137.1 0.7 pad.40.down_ref
  138.0 0.3 reduce-window.9
  138.5 0.2 copy.99
  139.0 0.8 pad.39.chunk
  139.8 0.9 pad.43.refs_5_.adapt_ref
  140.7 0.2 copy.103
  140.8 0.8 pad.42.refs_4_.down_ref
  141.7 0.6 broadcast_in_dim.62.refs_14_
  142.3 0.1 reshape.333
  143.3 0.6 pad.44.adapt_w
  143.9 0.6 pad.45.adapt_m
  144.6 0.6 pad.46.adapt_v
  145.2 1.1 gather_fusion
  146.4 0.6 concatenate.106.norm_ref
  147.0 0.6 concatenate.112.refs_13_.norm_ref
  147.7 0.2 fusion.14
  147.9 0.1 convert_reduce_fusion
  148.0 0.6 pad_maximum_fusion.6.first_norm_ref
  148.8 0.6 fusion.22
  149.4 0.6 fusion.26
  150.0 0.9 iota_subtract_fusion.spot_ref
  150.8 0.6 pad_maximum_fusion.5
  151.5 0.6 fusion.27
  152.1 1.0 broadcast_in_dim.31.seg_ref.refs_3_
  153.1 102.8 %first_layer.1 = (bf16[1024,2304]{1,0:T(8,128)(2,1)}, f32[1024,768]{1,0:T(8,128)}, f32[1024,768]{1,0:T(8,128)}, f32[1024,768]{1,0:T(8,128)}, bf16[1024,3072]{1,0...) custom-call(bf16[1152,768]{1,0:T(8,128)(2,1)} %get-tuple-element.51., ...), custom_call_target="tpu_custom_call" | custom-call | tf_op jit(solution)/shard_map/first_layer/pallas_call | solution.py:1097
  256.0 0.7 broadcast_in_dim.33.refs_1_.place_ref
  256.7 22.0 %last_forward.1 = (bf16[1024,1536]{1,0:T(8,128)(2,1)}, bf16[128,768]{1,0:T(8,128)(2,1)}, bf16[1024,128]{1,0:T(8,128)(2,1)}, f32[6,256]{1,0:T(8,128)}, f32[128,76...) custom-call(f32[1024,768]{1,0:T(8,128)} %get-tuple-element.53.refs_0, ...), custom_call_target="tpu_custom_call" | custom-call | tf_op jit(solution)/shard_map/last_forward/pallas_call | solution.py:408
  278.7 1.6 broadcast_in_dim.63.bias_any
  280.3 68.6 %head.1 = (f32[768,128]{1,0:T(8,128)}, f32[1,128]{1,0:T(1,128)}) custom-call(bf16[128,768]{1,0:T(8,128)(2,1)} %get-tuple-element.55.u_ref, bf16[3200,768]{1,0:T(8,128)(2,1)} %get-tuple-element.56.e_any, bf16[768,3200]{1,0:T(8,128)(2,1)} %get-tuple-element.57.et_any, f32[3200,128]{1,0:T(8,128)} %broadcast_in_dim.63.bias_any), custom_call_target="tpu_custom_call" | custom-call | tf_op jit(solution)/shard_map/head/pallas_call | solution.py:1622
  348.9 1.2 copy.104
  350.0 2.6 fusion.7
  352.6 0.6 fusion.24
  354.6 26.3 %last_backward.1 = (f32[1024,768]{1,0:T(8,128)}, bf16[32,32,768]{2,1,0:T(8,128)(2,1)}, f32[768,128]{1,0:T(8,128)}) custom-call(f32[128,768]{1,0:T(8,128)} %get-tuple-element.105.du_ref, bf16[1024,1536]{1,0:T(8,128)(2,1)} %get-tuple-element.59.kv_ref, bf16[128,768]{1,0:T(8,128)(2,1)} %get-tuple-element.60.q_ref, bf16[1024,128]{1,0:T(8,128)(2,1)} %get-tuple-element.61.mid_ref, ...), custom_call_target="tpu_custom_call" | custom-call | tf_op jit(solution)/shard_map/last_backward/pallas_call | solution.py:588
  380.9 0.7 broadcast.202.facts
  381.6 69.9 %finish.1 = (f32[8,128]{1,0:T(8,128)}, f32[24,768]{1,0:T(8,128)}, f32[24,768]{1,0:T(8,128)}, f32[24,768]{1,0:T(8,128)}, f32[24,128]{1,0:T(8,128)}, /*index=5*/f32[24,128]{1,0:T(8,128)}, f32[24,128]{1,0:T(8,128)}) custom-call(f32[1024,768]{1,0:T(8,128)} %get-tuple-element.72.dout_any, f32[1024,768]{1,0:T(8,128)} %get-tuple-element.73.one_any, ...), custom_call_target="tpu_custom_call" | custom-call | tf_op jit(solution)/shard_map/finish/pallas_call | solution.py:1311
  451.5 0.7 slice_bitcast_fusion.6
  452.2 0.7 copy.108
  452.9 0.7 slice_bitcast_fusion.5
  453.6 0.7 copy.109
  454.3 0.7 slice_bitcast_fusion.4
  455.0 0.7 copy.110
  455.6 1.3 fusion.30
  456.9 1.5 copy.139
  458.4 1.5 copy.140
  460.0 1.5 copy.141
  (88 shorter events, 1.7 us)
Async XLA Ops:
  7.2 4.5 copy-start.17
  7.2 4.5 copy-start.19
  7.2 144.9 %all-gather.5.cloned.1.call-start = ((), (), s32[]{:S(2)}) async-start(), calls=%async_computation | async-start | bytes 14598144 | tf_op jit(solution)/shard_map/all_gather | solution.py:1726
  11.6 7.0 %copy-start.7 = (f32[2,2,8,24]{3,2,1,0:T(8,128)S(1)}, f32[2,2,8,24]{3,2,1,0:T(8,128)}, u32[]{:S(2)}) copy-start(f32[2,2,8,24]{3,2,1,0:T(8,128)} %param.44) | copy-start | bytes 9220
  20.9 35.3 %copy-start.15 = (f32[1600]{0:T(1024)S(1)}, f32[1600]{0:T(1024)}, u32[]{:S(2)}) copy-start(f32[1600]{0:T(1024)} %param.42) | copy-start | bytes 19204
  133.8 2.1 copy-start.8
  134.8 3.0 copy-start.10
  135.9 2.9 copy-start.2
  136.1 2.7 copy-start.3
  136.1 2.7 copy-start.4
  136.2 2.7 copy-start.5
  136.2 2.7 copy-start.1
  137.8 14.3 %copy-start.6 = (f32[1,1024]{1,0:T(1,128)}, f32[1,1024]{1,0:T(1,128)S(1)}, u32[]{:S(2)}) copy-start(f32[1,1024]{1,0:T(1,128)S(1)} %convert_element_type.66.seg_row_ref) | copy-start | bytes 12292
  138.9 2.8 copy-start.18
  138.9 4.3 copy-start.11
  138.9 5.5 %copy-start.12 = (f32[2,2,8,24]{3,2,1,0:T(8,128)S(1)}, f32[2,2,8,24]{3,2,1,0:T(8,128)}, u32[]{:S(2)}) copy-start(f32[2,2,8,24]{3,2,1,0:T(8,128)} %param.46) | copy-start | bytes 9220
  139.8 6.6 %copy-start.13 = (f32[6,768]{1,0:T(8,128)S(1)}, f32[6,768]{1,0:T(8,128)}, u32[]{:S(2)}) copy-start(f32[6,768]{1,0:T(8,128)} %param.35) | copy-start | bytes 55300
  139.8 6.6 %copy-start.14 = (f32[6,768]{1,0:T(8,128)S(1)}, f32[6,768]{1,0:T(8,128)}, u32[]{:S(2)}) copy-start(f32[6,768]{1,0:T(8,128)} %param.34) | copy-start | bytes 55300
  140.7 8.1 %copy-start.20 = (f32[4]{0:T(128)S(1)}, f32[4]{0:T(128)}, u32[]{:S(2)}) copy-start(f32[4]{0:T(128)} %param.30) | copy-start | bytes 52
  140.7 8.7 %copy-start.9 = (f32[2,6144]{1,0:T(2,128)S(1)}, f32[2,6144]{1,0:T(2,128)}, u32[]{:S(2)}) copy-start(f32[2,6144]{1,0:T(2,128)} %param.40) | copy-start | bytes 147460
  153.1 102.8 %copy-start.16 = (s32[1,128]{1,0:T(1,128)S(1)}, s32[1,128]{1,0:T(1,128)}, u32[]{:S(2)}) copy-start(s32[1,128]{1,0:T(1,128)} %place_row_ref.1) | copy-start | bytes 1540
  280.3 69.7 %copy-start = (bf16[128,768]{1,0:T(8,128)(2,1)S(1)}, bf16[128,768]{1,0:T(8,128)(2,1)}, u32[]{:S(2)}) copy-start(bf16[128,768]{1,0:T(8,128)(2,1)} %get-tuple-element.55.u_ref) | copy-start | bytes 589828
  348.8 3.8 copy-start.21
Sparse Core Ops, SparseCore 0:
  11.7 136.9 all-gather.4

commit v7 on v6

--- a/solution.py
+++ b/solution.py
@@ -107,47 +107,61 @@
     )
 
 
+def qkv_bias(bias_ref, layer, start, size):
+    hidden = bias_ref.shape[1] // 8
+    if start >= 2 * hidden:
+        return bias_ref[layer : layer + 1, start - hidden : start - hidden + size]
+    return bias_ref[layer : layer + 1, start : start + size] if start < hidden else 0.0
+
+
+def norm_of(norm_refs, k):
+    return norm_refs[0][k : k + 1, :], norm_refs[1][k : k + 1, :]
+
+
 def project_body(
-    own_ref, got_ref, mine_ref, spot_ref, spots_ref, norm_ref, down_ref, w_ref, up_ref, bias_ref,
+    own_ref, got_ref, code_ref, spots_ref, gain_ref, shift_ref, down_ref, w_ref, up_ref, bias_ref,
     out_ref, mid_ref, x_ref,
 ):
-    choose = lax.broadcasted_iota(jnp.int32, (own_ref.shape[0], spots_ref.shape[0]), 1) == spot_ref[...]
+    mine = code_ref[...] % 2
+    choose = (
+        lax.broadcasted_iota(jnp.int32, (own_ref.shape[0], spots_ref.shape[0]), 1) == code_ref[...] // 2
+    )
     summed = jnp.where(
-        mine_ref[...] > 0, own_ref[...].astype(F32), got_ref[...].astype(F32)
+        mine > 0, own_ref[...].astype(F32), got_ref[...].astype(F32)
     ) + mm(choose.astype(F32).astype(BF), spots_ref[...])
-    x = layer_norm(summed, norm_ref[0:1, :], norm_ref[1:2, :])
+    x = layer_norm(summed, *norm_of((gain_ref, shift_ref), 0))
     x_ref[...] = x
     low = x.astype(BF)
-    mid = mm(low, down_ref[...]).astype(BF)
+    mid = mm(low, down_ref[0]).astype(BF)
     mid_ref[...] = mid
     total = w_ref.shape[0]
-    step = split_of(total, 768, 128)
+    step = total // 3
     for start in range(0, total, step):
         part = slice(start, start + step)
         out_ref[:, part] = (
-            mm_nt(low, w_ref[part, :]) + mm(mid, up_ref[:, part]) + bias_ref[:, part]
+            mm_nt(low, w_ref[part, :]) + mm(mid, up_ref[0, :, part]) + qkv_bias(bias_ref, 0, start, step)
         ).astype(BF)
 
 
-def project(own, got, mine, spot, spots, norms, down, w, up, bias):
-    rows, width = mine.shape[0], own.shape[1]
+def project(own, got, code, spots, gains, shifts, down, w, up, bias):
+    rows, width = code.shape[0], own.shape[1]
     tile = split_of(rows, 256, 16)
     total = w.shape[0]
     row = lambda n: pl.BlockSpec((tile, n), lambda i: (i, 0))
     return pl.pallas_call(
         project_body,
         grid=(rows // tile,),
-        in_specs=[row(width), row(width), row(1), row(1)]
-        + [full(a.shape) for a in (spots, norms, down, w, up, bias)],
-        out_specs=[row(total), row(down.shape[1]), row(width)],
+        in_specs=[row(width), row(width), row(1)]
+        + [full(a.shape) for a in (spots, gains, shifts, down, w, up, bias)],
+        out_specs=[row(total), row(down.shape[2]), row(width)],
         out_shape=[
             jax.ShapeDtypeStruct((rows, total), BF),
-            jax.ShapeDtypeStruct((rows, down.shape[1]), BF),
+            jax.ShapeDtypeStruct((rows, down.shape[2]), BF),
             jax.ShapeDtypeStruct((rows, width), F32),
         ],
         compiler_params=params(),
         name="project",
-    )(own, got, mine, spot, spots, norms, down, w, up, bias)
+    )(own, got, code, spots, gains, shifts, down, w, up, bias)
 
 
 def attend_body(q_ref, k_ref, v_ref, seg_ref, seg_row_ref, ctx_ref, log_ref):
@@ -212,23 +226,30 @@
     return units, (step if ref.shape[0] > 1 else split_of(units, 768, 128))
 
 
+def later_biases(bias_ref, layer):
+    hidden = bias_ref.shape[1] // 8
+    row = bias_ref[layer : layer + 1, :]
+    return row[:, 2 * hidden : 3 * hidden], row[:, 3 * hidden : 7 * hidden], row[:, 7 * hidden :]
+
+
 def after_body(
-    ctx_ref, x_ref, wo_ref, up_ref, down_ref, bo_ref, b1_ref, b2_ref, norm_ref,
+    ctx_ref, x_ref, wo_ref, up_ref, down_ref, bias_ref, gain_ref, shift_ref,
     out_ref, one_ref, two_ref, slope_ref,
 ):
-    one = x_ref[...] + (mm_nt(ctx_ref[...], wo_ref[...]) + bo_ref[...])
+    bo, b1, b2 = later_biases(bias_ref, 0)
+    one = x_ref[...] + (mm_nt(ctx_ref[...], wo_ref[...]) + bo)
     one_ref[...] = one
-    middle = layer_norm(one, norm_ref[0:1, :], norm_ref[1:2, :])
+    middle = layer_norm(one, *norm_of((gain_ref, shift_ref), 1))
     low = middle.astype(BF)
-    total = middle + b2_ref[...]
+    total = middle + b2
     units, step = feed_step(up_ref)
     for start in range(0, units, step):
         part = slice(start, start + step)
-        act, slope = gelu_pair(mm_nt(low, rows_of(up_ref, start, step)) + b1_ref[:, part])
+        act, slope = gelu_pair(mm_nt(low, rows_of(up_ref, start, step)) + b1[:, part])
         slope_ref[:, part] = slope.astype(BF)
         total = total + mm(act.astype(BF), rows_of(down_ref, start, step))
     two_ref[...] = total
-    out_ref[...] = layer_norm(total, norm_ref[2:3, :], norm_ref[3:4, :])
+    out_ref[...] = layer_norm(total, *norm_of((gain_ref, shift_ref), 2))
 
 
 def slab_spec(slab):
@@ -236,22 +257,22 @@
     return pl.BlockSpec((array.shape[0], rows, array.shape[2]), lambda *_: (0, place, 0))
 
 
-def after(ctx, x, wo, up, down, bo, b1, b2, norms):
+def after(ctx, x, wo, up, down, bias, gains, shifts):
     rows, width = x.shape
     tile = split_of(rows, 256, 16)
-    units = b1.shape[1]
+    units = 4 * width
     row = lambda n: pl.BlockSpec((tile, n), lambda i: (i, 0))
     return pl.pallas_call(
         after_body,
         grid=(rows // tile,),
         in_specs=[row(width), row(width), full(wo.shape), slab_spec(up), slab_spec(down)]
-        + [full(a.shape) for a in (bo, b1, b2, norms)],
+        + [full(a.shape) for a in (bias, gains, shifts)],
         out_specs=[row(width), row(width), row(width), row(units)],
         out_shape=[jax.ShapeDtypeStruct((rows, width), F32)] * 3
         + [jax.ShapeDtypeStruct((rows, units), BF)],
         compiler_params=params(),
         name="after",
-    )(ctx, x, wo, up[0], down[0], bo, b1, b2, norms)
+    )(ctx, x, wo, up[0], down[0], bias, gains, shifts)
 
 
 def exact_rows(choose, matrix):
@@ -278,7 +299,7 @@
 
 def last_forward_body(
     x_ref, place_ref, place_row_ref, seg_ref, down_ref, adapt_ref, bias_ref, weights_any, up_any, dn_any,
-    bo_ref, b1_ref, b2_ref, norm_ref, hbias_ref,
+    gain_ref, shift_ref, hbias_ref,
     kv_ref, q_ref, mid_ref, log_ref, one_ref, slope_ref, two_ref, low_ref, act_ref, hslope_ref, feat_ref, *more,
     places, starts,
 ):
@@ -315,13 +336,13 @@
     lanes = 2 * (hidden // HEADS)
     width = lanes // 2
     low = x_ref[...].astype(BF)
-    mid = mm(low, down_ref[...]).astype(BF)
+    mid = mm(low, down_ref[1]).astype(BF)
     mid_ref[...] = mid
-    step = split_of(2 * hidden, 512, 128)
+    step = split_of(hidden, 768, 128)
     for start in range(hidden, 3 * hidden, step):
         part = slice(start, start + step)
         kv_ref[:, start - hidden : start - hidden + step] = (
-            mm_nt(low, w_ref[part, :]) + mm(mid, adapt_ref[:, part]) + bias_ref[:, part]
+            mm_nt(low, w_ref[part, :]) + mm(mid, adapt_ref[1, :, part]) + qkv_bias(bias_ref, 1, start, step)
         ).astype(BF)
     choose = (
         lax.broadcasted_iota(jnp.int32, (labels, rows), 1) == place_ref[...][:, 0:1]
@@ -330,7 +351,9 @@
     own_low = own.astype(BF)
     own_mid = mm(choose, mid).astype(BF)
     q_ref[...] = (
-        mm_nt(own_low, w_ref[:hidden, :]) + mm(own_mid, adapt_ref[:, :hidden]) + bias_ref[:, :hidden]
+        mm_nt(own_low, w_ref[:hidden, :])
+        + mm(own_mid, adapt_ref[1, :, :hidden])
+        + qkv_bias(bias_ref, 1, 0, hidden)
     ).astype(BF)
     seg = seg_ref[...]
     seg_own = jnp.sum(
@@ -353,26 +376,28 @@
         ) * (1.0 / total)
         ctx_ref[:, part] = pair_join(context, width).T.astype(BF)
         log_ref[p : p + 1, :] = top + jnp.log(total)
-    one = own + (mm_nt(ctx_ref[...], wo_ref[...]) + bo_ref[...])
+    bo, b1, b2 = later_biases(bias_ref, 1)
+    norms = (gain_ref, shift_ref)
+    one = own + (mm_nt(ctx_ref[...], wo_ref[...]) + bo)
     one_ref[...] = one
-    middle = layer_norm(one, norm_ref[0:1, :], norm_ref[1:2, :])
+    middle = layer_norm(one, *norm_of(norms, 3))
     middle_low = middle.astype(BF)
-    sum_two = middle + b2_ref[...]
+    sum_two = middle + b2
     units, step = feed_step(up_ref)
     for copy in copies:
         copy.wait()
     for start in range(0, units, step):
         part = slice(start, start + step)
-        act, slope = gelu_pair(mm_nt(middle_low, rows_of(up_ref, start, step)) + b1_ref[:, part])
+        act, slope = gelu_pair(mm_nt(middle_low, rows_of(up_ref, start, step)) + b1[:, part])
         slope_ref[:, part] = slope.astype(BF)
         sum_two = sum_two + mm(act.astype(BF), rows_of(dn_ref, start, step))
     two_ref[...] = sum_two
-    out_low = layer_norm(sum_two, norm_ref[2:3, :], norm_ref[3:4, :]).astype(BF)
+    out_low = layer_norm(sum_two, *norm_of(norms, 4)).astype(BF)
     low_ref[...] = out_low
     act, slope = gelu_pair(mm(out_low, hb_ref[...]) + hbias_ref[...])
     act_ref[...] = act
     hslope_ref[...] = slope
-    feat_ref[...] = layer_norm(act, norm_ref[4:5, :], norm_ref[5:6, :]).astype(BF)
+    feat_ref[...] = layer_norm(act, *norm_of(norms, 5)).astype(BF)
 
 
 def slab_scratch(slab):
@@ -381,11 +406,11 @@
 
 
 def last_forward(
-    x, place_col, place_row, seg_wide, down, adapt, bias, weights, starts, up, dn, bo, b1, b2, norms, hbias
+    x, place_col, place_row, seg_wide, down, adapt, bias, weights, starts, up, dn, gains, shifts, hbias
 ):
     rows, hidden = x.shape
     labels = place_col.shape[0]
-    units = b1.shape[1]
+    units = 4 * hidden
     whole = pl.BlockSpec(memory_space=pltpu.VMEM)
     anywhere = pl.BlockSpec(memory_space=pl.ANY)
     shape = jax.ShapeDtypeStruct
@@ -407,12 +432,12 @@
 
     return pl.pallas_call(
         body,
-        in_specs=[whole] * 7 + [anywhere] * (len(weights) + 2) + [whole] * 5,
+        in_specs=[whole] * 7 + [anywhere] * (len(weights) + 2) + [whole] * 3,
         out_specs=[whole] * 11 + ([anywhere] * 3 if slabs else []),
         out_shape=[
             shape((rows, 2 * hidden), BF),
             shape((labels, hidden), BF),
-            shape((rows, down.shape[1]), BF),
+            shape((rows, down.shape[2]), BF),
             shape((pairs, 2 * labels), F32),
             shape((labels, hidden), F32),
             shape((labels, units), BF),
@@ -433,7 +458,7 @@
         ],
         compiler_params=params(),
         name="last_forward",
-    )(x, place_col, place_row, seg_wide, down, adapt, bias, *weights, up[0], dn[0], bo, b1, b2, norms, hbias)
+    )(x, place_col, place_row, seg_wide, down, adapt, bias, *weights, up[0], dn[0], gains, shifts, hbias)
 
 
 def vocab_body(u_ref, e_ref, et_ref, bias_ref, num_ref, log_ref, scores, weights):
@@ -490,9 +515,10 @@
 
 
 def last_backward_body(
-    du_ref, kv_ref, q_ref, mid_ref, log_ref, one_ref, slope_ref, two_ref, low_ref, act_ref, hslope_ref,
-    place_ref, place_row_ref, seg_ref, down_ref, w_ref, adapt_ref, wo_ref, up_any, dn_any, norm_ref, hb_ref,
-    dx_ref, gh_ref, g_ref,
+    mean_ref, all_log_ref, target_ref, fact_ref, kv_ref, q_ref, mid_ref, log_ref, one_ref, slope_ref, two_ref,
+    low_ref, act_ref, hslope_ref, feat_ref, place_ref, place_row_ref, seg_ref, down_ref, w_ref, adapt_ref, wo_ref,
+    up_any, dn_any, gain_ref, hb_ref,
+    dx_ref, gh_ref, g_ref, out_fact_ref,
     up_ref, dn_ref, dkv_ref, dq_ref, sems, *, places, edge,
 ):
     copies = []
@@ -507,11 +533,19 @@
         )
         copies[-1].start()
     rows = kv_ref.shape[0]
-    labels, hidden = du_ref.shape
+    labels, hidden = feat_ref.shape
     lanes = 2 * (hidden // HEADS)
     width = lanes // 2
     scale = width**-0.5
-    dact = norm_back(act_ref[...], norm_ref[4:5, :], du_ref[...])
+    targets = target_ref[...].astype(F32)
+    weight = fact_ref[0:1, 0:1]
+    chosen = jnp.sum(feat_ref[...].astype(F32) * targets, keepdims=True)
+    loss = weight * (jnp.sum(all_log_ref[...] - fact_ref[3:4, :labels], keepdims=True) - chosen)
+    out_fact_ref[...] = jnp.where(
+        lax.broadcasted_iota(jnp.int32, fact_ref.shape, 0) == 0, loss, fact_ref[...]
+    )
+    du = weight * (mean_ref[...].T - targets)
+    dact = norm_back(act_ref[...], gain_ref[5:6, :], du)
     dz = (hslope_ref[...] * dact).astype(BF)
     dense = mm_tn(low_ref[...], dz)
     if len(gh_ref.shape) == 2:
@@ -521,7 +555,7 @@
         spare = jnp.zeros((gh_ref.shape[1] - each, hidden), F32)
         for k in range(gh_ref.shape[0]):
             gh_ref[k] = jnp.concatenate([dense[k * each : (k + 1) * each, :], spare], 0).astype(BF)
-    dtwo = norm_back(two_ref[...], norm_ref[2:3, :], mm_nt(dz, hb_ref[...]))
+    dtwo = norm_back(two_ref[...], gain_ref[4:5, :], mm_nt(dz, hb_ref[...]))
     dtwo_low = dtwo.astype(BF)
     dmiddle = dtwo
     units, step = feed_step(up_ref)
@@ -533,7 +567,7 @@
             slope_ref[:, part].astype(F32) * mm_nt(dtwo_low, rows_of(dn_ref, start, step))
         ).astype(BF)
         dmiddle = dmiddle + mm(dgate, rows_of(up_ref, start, step))
-    done = norm_back(one_ref[...], norm_ref[0:1, :], dmiddle)
+    done = norm_back(one_ref[...], gain_ref[3:4, :], dmiddle)
     dctx = mm(done.astype(BF), wo_ref[...]).astype(BF)
     seg = seg_ref[...]
     choose_t = lax.broadcasted_iota(jnp.int32, (rows, labels), 0) == place_row_ref[...]
@@ -561,40 +595,43 @@
         mm_tn(dq, own_mid),
         mm_tn(dkv_ref[:, hidden:], mid_ref[...]),
     )
-    dmid_own = mm_nt(dq, adapt_ref[:, :hidden]).astype(BF)
-    own = done + mm(dq, w_ref[:hidden, :]) + mm_nt(dmid_own, down_ref[...])
+    dmid_own = mm_nt(dq, adapt_ref[1, :, :hidden]).astype(BF)
+    own = done + mm(dq, w_ref[:hidden, :]) + mm_nt(dmid_own, down_ref[1])
     spread = choose_t.astype(F32).astype(BF)
     own_high = own.astype(BF)
     own_rest = (own - own_high.astype(F32)).astype(BF)
-    dmid = mm_nt(dkv_ref[:, hidden:], adapt_ref[:, 2 * hidden :]).astype(BF)
+    dmid = mm_nt(dkv_ref[:, hidden:], adapt_ref[1, :, 2 * hidden :]).astype(BF)
     step = split_of(hidden, 256, 128)
     for start in range(0, hidden, step):
         part = slice(start, start + step)
         dx_ref[:, part] = (
             mm(dkv_ref[...], w_ref[hidden:, part])
-            + mm_nt(dmid, down_ref[part, :])
+            + mm_nt(dmid, down_ref[1, part, :])
             + mm(spread, own_high[:, part])
             + mm(spread, own_rest[:, part])
         )
 
 
-def last_backward(du, saved, place_col, place_row, seg_wide, down, w, adapt, wo, up, dn, norms, hb, edge, shards):
+def last_backward(
+    mean, logs, targets, facts, saved, place_col, place_row, seg_wide, down, w, adapt, wo, up, dn, gains, hb, edge, shards
+):
     kv = saved[0]
     rows = kv.shape[0]
-    labels, hidden = du.shape
+    labels, hidden = targets.shape
     whole = pl.BlockSpec(memory_space=pltpu.VMEM)
     anywhere = pl.BlockSpec(memory_space=pl.ANY)
     shape = jax.ShapeDtypeStruct
     return pl.pallas_call(
         functools.partial(last_backward_body, places=(up[1], dn[1]), edge=edge),
-        in_specs=[whole] * 18 + [anywhere] * 2 + [whole] * 2,
-        out_specs=[whole] * 3,
+        in_specs=[whole] * 22 + [anywhere] * 2 + [whole] * 2,
+        out_specs=[whole] * 4,
         out_shape=[
             shape((rows, hidden), F32),
             shape((hidden, hidden), F32)
             if shards is None
             else shape((shards, -(-hidden // shards // 16) * 16, hidden), BF),
-            shape((hidden, down.shape[1]), F32),
+            shape((hidden, down.shape[2]), F32),
+            shape(facts.shape, F32),
         ],
         scratch_shapes=[
             slab_scratch(up),
@@ -605,11 +642,11 @@
         ],
         compiler_params=params(),
         name="last_backward",
-    )(du, *saved, place_col, place_row, seg_wide, down, w, adapt, wo, up[0], dn[0], norms, hb)
-
-
-def after_back_body(dout_ref, one_ref, two_ref, slope_ref, wo_ref, up_ref, down_ref, norm_ref, dctx_ref):
-    dtwo = norm_back(two_ref[...], norm_ref[2:3, :], dout_ref[...])
+    )(mean, logs, targets, facts, *saved, place_col, place_row, seg_wide, down, w, adapt, wo, up[0], dn[0], gains, hb)
+
+
+def after_back_body(dout_ref, one_ref, two_ref, slope_ref, wo_ref, up_ref, down_ref, gain_ref, dctx_ref):
+    dtwo = norm_back(two_ref[...], gain_ref[2:3, :], dout_ref[...])
     low = dtwo.astype(BF)
     dmiddle = dtwo
     units, step = feed_step(up_ref)
@@ -619,7 +656,7 @@
             slope_ref[:, part].astype(F32) * mm_nt(low, rows_of(down_ref, start, step))
         ).astype(BF)
         dmiddle = dmiddle + mm(dgate, rows_of(up_ref, start, step))
-    done = norm_back(one_ref[...], norm_ref[0:1, :], dmiddle)
+    done = norm_back(one_ref[...], gain_ref[1:2, :], dmiddle)
     dctx_ref[...] = mm(done.astype(BF), wo_ref[...]).astype(BF)
 
 
@@ -730,32 +767,28 @@
     pl.semaphore_wait(pltpu.get_barrier_semaphore(), shards - 1)
 
 
-def direct_copy(source, target, sends, receives, me, k, shards):
+def direct_copy(source, target, sems, me, k, shards):
     return pltpu.make_async_remote_copy(
         src_ref=source,
         dst_ref=target,
-        send_sem=sends.at[k],
-        recv_sem=receives.at[me],
+        send_sem=sems.at[0],
+        recv_sem=sems.at[1],
         device_id=rank_device((me + k) % shards),
         device_id_type=MESH,
     )
 
 
-def spread(piece_of, buffer, sends, receives, me, shards):
+def spread(piece_of, buffer, sems, me, shards):
     @pl.loop(1, shards)
     def _(k):
-        direct_copy(piece_of((me + k) % shards), buffer.at[me], sends, receives, me, k, shards).start()
-
-
-def collect(piece_of, buffer, sends, receives, me, shards):
-    @pl.loop(1, shards)
-    def _(k):
-        source = (me + shards - k) % shards
-        direct_copy(buffer.at[source], buffer.at[source], sends, receives, source, k, shards).wait_recv()
-
-    @pl.loop(1, shards)
-    def _(k):
-        direct_copy(piece_of((me + k) % shards), buffer.at[me], sends, receives, me, k, shards).wait_send()
+        direct_copy(piece_of((me + k) % shards), buffer.at[me], sems, me, k, shards).start()
+
+
+def collect(buffer, sems, me, shards):
+    whole = buffer.at[pl.ds(0, shards - 1)]
+    copy = direct_copy(whole, whole, sems, me, 1, shards)
+    copy.wait_recv()
+    copy.wait_send()
 
 
 def relative_places(order):
@@ -871,13 +904,26 @@
 ITEMS = 28
 
 
-def start_body(shards, rows, fact, got, facts, row_sems, sends, receives, own_sem):
+def start_body(
+    streams, shards, rows, fact, chunk, got, facts, full_chunk,
+    row_sems, fact_sems, own_sems, sends, receives, hands, hands_got,
+):
     here = position()
     me = number_of(here)
     greet_all(shards)
-    own = pltpu.make_async_copy(fact, facts.at[me], own_sem.at[0])
-    own.start()
+    own = [
+        pltpu.make_async_copy(source, target, own_sems.at[k])
+        for k, (source, target) in enumerate(((fact, facts.at[me]), (chunk, full_chunk.at[me])))
+    ]
+    for copy in own:
+        copy.start()
     await_all(shards)
+    gathers = [
+        Gather(
+            chunk, full_chunk, start, size, order, sends.at[k], receives.at[k], hands.at[k], hands_got.at[k]
+        )
+        for k, (start, size, order) in enumerate(streams)
+    ]
     swap = pltpu.make_async_remote_copy(
         src_ref=rows,
         dst_ref=got,
@@ -886,32 +932,54 @@
         device_id=device_of(dict(here, x=1 - here["x"])),
         device_id_type=MESH,
     )
+    for gather in gathers:
+        gather.step(0)
     swap.start()
-    spread(lambda peer: fact, facts, sends, receives, me, shards)
-    collect(lambda peer: fact, facts, sends, receives, me, shards)
+    spread(lambda peer: fact, facts, fact_sems, me, shards)
+    for index in range(1, ITEMS):
+        for gather in gathers:
+            gather.step(index)
+    for gather in gathers:
+        gather.finish()
+    collect(facts, fact_sems, me, shards)
     swap.wait()
-    own.wait()
-
-
-def start_exchange(rows, fact, shards):
+    for copy in own:
+        copy.wait()
+
+
+def gather_sems():
+    sems = pltpu.SemaphoreType.DMA
+    return [sems((2, 4 * ITEMS)), sems((2, 16)), sems((2, ITEMS)), sems((2, 16))]
+
+
+def streams_of(rows):
+    cut = (rows * 5 // 6 + 15) // 16 * 16
+    return ((0, cut, "xzy"), (cut, rows - cut, "xyz"))
+
+
+def start_exchange(rows, fact, chunk, shards):
     anywhere = pl.BlockSpec(memory_space=pl.ANY)
     shape = jax.ShapeDtypeStruct
     sems = pltpu.SemaphoreType.DMA
     return pl.pallas_call(
-        functools.partial(start_body, shards),
-        in_specs=[anywhere] * 2,
-        out_specs=[anywhere] * 2,
-        out_shape=[shape(rows.shape, rows.dtype), shape((shards, *fact.shape), fact.dtype)],
-        scratch_shapes=[sems((2,)), sems((shards,)), sems((shards,)), sems((1,))],
+        functools.partial(start_body, streams_of(chunk.shape[0]), shards),
+        in_specs=[anywhere] * 3,
+        out_specs=[anywhere] * 3,
+        out_shape=[
+            shape(rows.shape, rows.dtype),
+            shape((shards, *fact.shape), fact.dtype),
+            shape((shards, *chunk.shape), chunk.dtype),
+        ],
+        scratch_shapes=[sems((2,)), sems((2,)), sems((2,)), *gather_sems()],
         compiler_params=params(collective_id=1, has_side_effects=True),
         name="start_exchange",
-    )(rows, fact)
+    )(rows, fact, chunk)
 
 
 def first_layer_body(
     streams, shards, places,
-    own_any, got_any, first_any, chunk, table_any, mine_ref, spot_ref, spots_ref, first_norm_ref, down_ref,
-    adapt_ref, bias_ref, seg_ref, seg_row_ref, bo_ref, b1_ref, b2_ref, norm_ref,
+    own_any, got_any, in_any, feed_any, chunk, table_any, code_ref, spots_ref, gain_ref, shift_ref, down_ref,
+    adapt_ref, bias_ref, seg_ref, seg_row_ref,
     qkv_out, x_out, one_out, two_out, slope_out, wo_out, full_chunk, e_out, et_out, mid_ref, log_ref,
     own, got, in_slab, w, wo, up, dn, x, qkv, ctx, two, out, slope, e_ref, et_ref,
     load_sems, tile_sems, out_sems, swap_sems, sends, receives, hands, hands_got,
@@ -929,7 +997,7 @@
 
     def slab(target, place):
         each = target.shape[1]
-        return first_any.at[:, pl.ds(place * each, each), :]
+        return feed_any.at[:, pl.ds(place * each, each), :]
 
     loads = [
         pltpu.make_async_copy(source, target, load_sems.at[k])
@@ -937,7 +1005,7 @@
             (
                 (own_any.at[pl.ds(0, rows), :], own),
                 (got_any.at[pl.ds(0, rows), :], got),
-                (first_any.at[:, pl.ds(places[2], in_slab.shape[1]), :], in_slab),
+                (in_any, in_slab),
                 (slab(up, places[0]), up),
                 (slab(dn, places[1]), dn),
                 (own_slice, e_ref.at[pl.ds(0, slice_rows), :]),
@@ -986,9 +1054,8 @@
     def _(i):
         part = pl.ds(pl.multiple_of(i * tile, tile), tile)
         project_body(
-            own.at[part, :], got.at[part, :], mine_ref.at[part, :], spot_ref.at[part, :], spots_ref,
-            first_norm_ref, down_ref, w, adapt_ref, bias_ref, qkv.at[part, :], mid_ref.at[part, :],
-            x.at[part, :],
+            own.at[part, :], got.at[part, :], code_ref.at[part, :], spots_ref, gain_ref, shift_ref, down_ref, w,
+            adapt_ref, bias_ref, qkv.at[part, :], mid_ref.at[part, :], x.at[part, :],
         )
 
         @pl.when(i == tiles - 2)
@@ -1050,7 +1117,7 @@
                 copy.wait()
 
         after_body(
-            ctx.at[part, :], x.at[part, :], wo, up, dn, bo_ref, b1_ref, b2_ref, norm_ref, out.at[turn],
+            ctx.at[part, :], x.at[part, :], wo, up, dn, bias_ref, gain_ref, shift_ref, out.at[turn],
             x.at[part, :], two.at[turn], slope.at[turn],
         )
         for copy in tile_copies(i):
@@ -1082,21 +1149,20 @@
         copy.wait()
 
 
-def first_layer(own, got, first, chunk, table, more, places, units, slice_rows, shards):
+def first_layer(own, got, first_in, feed, chunk, table, more, places, slice_rows, shards):
     whole = pl.BlockSpec(memory_space=pltpu.VMEM)
     anywhere = pl.BlockSpec(memory_space=pl.ANY)
-    mine, down = more[0], more[4]
-    rows, hidden = mine.shape[0], table.shape[1]
+    code, down = more[0], more[4]
+    rows, hidden = code.shape[0], table.shape[1]
     tile = split_of(rows, 256, 16)
     pairs = HEADS // 2
-    cut = (chunk.shape[0] * 5 // 6 + 15) // 16 * 16
-    streams = ((0, cut, "xzy"), (cut, chunk.shape[0] - cut, "xyz"))
+    units = 4 * hidden
     each = units // shards
     shape = jax.ShapeDtypeStruct
     sems = pltpu.SemaphoreType.DMA
     return pl.pallas_call(
-        functools.partial(first_layer_body, streams, shards, places),
-        in_specs=[anywhere] * 5 + [whole] * len(more),
+        functools.partial(first_layer_body, streams_of(chunk.shape[0]), shards, places),
+        in_specs=[anywhere] * 6 + [whole] * len(more),
         out_specs=[anywhere] * 9 + [whole] * 2,
         out_shape=[
             shape((rows, 3 * hidden), BF),
@@ -1108,7 +1174,7 @@
             shape((shards, *chunk.shape), BF),
             shape((2 * slice_rows, hidden), BF),
             shape((hidden, 2 * slice_rows), BF),
-            shape((rows, down.shape[1]), BF),
+            shape((rows, down.shape[2]), BF),
             shape((pairs, 1, 2 * rows), F32),
         ],
         scratch_shapes=[
@@ -1131,14 +1197,11 @@
             sems((4, rows // tile)),
             sems((4,)),
             sems((2,)),
-            sems((2, 4 * ITEMS)),
-            sems((2, 16)),
-            sems((2, ITEMS)),
-            sems((2, 16)),
+            *gather_sems(),
         ],
         compiler_params=params(collective_id=3, has_side_effects=True),
         name="first_layer",
-    )(own, got, first, chunk, table, *more)
+    )(own, got, first_in, feed, chunk, table, *more)
 
 
 PICK = 64
@@ -1191,16 +1254,19 @@
     return (weight, moment_one, moment_two)
 
 
+BACK_TILE = 512
+
+
 def finish_body(
     shards, places, edge,
-    dout_any, one_any, two_any, slope_any, wo_any, up_any, dn_any, qkv_any, norm_ref, log_ref, seg_ref,
-    seg_row_ref, mid_ref, parts, late_ref, facts, head_w, head_m, head_v, adapt_w, adapt_m, adapt_v,
-    sums_ref, head_w_out, head_m_out, head_v_out, adapt_w_out, adapt_m_out, adapt_v_out,
+    dout_any, one_any, two_any, slope_any, wo_any, up_any, dn_any, qkv_any, gain_ref, log_ref, seg_ref,
+    seg_row_ref, mid_ref, parts, late_ref, facts,
+    sums_ref, dense_ref, total_ref,
     dout, one, two, slope, wo, up, dn, qkv, dctx, dv, grad, dense_got, grad_got, note, notes,
-    tile_sems, load_sems, dense_send, dense_get, grad_send, grad_get, note_send, note_get,
+    tile_sems, load_sems, dense_sems, grad_sems, note_sems,
 ):
     rows, hidden = dout.shape
-    tile = split_of(rows, 256, 16)
+    tile = split_of(rows, BACK_TILE, 16)
     tiles = rows // tile
     me = number_of(position())
 
@@ -1245,14 +1311,14 @@
             copy.wait()
         part = pl.ds(pl.multiple_of(i * tile, tile), tile)
         after_back_body(
-            dout.at[part, :], one.at[part, :], two.at[part, :], slope.at[part, :], wo, up, dn, norm_ref,
+            dout.at[part, :], one.at[part, :], two.at[part, :], slope.at[part, :], wo, up, dn, gain_ref,
             dctx.at[part, :],
         )
 
         @pl.when(i == 0)
         def _():
             await_all(shards)
-            spread(lambda peer: parts.at[peer], dense_got, dense_send, dense_get, me, shards)
+            spread(lambda peer: parts.at[peer], dense_got, dense_sems, me, shards)
 
     loads[3].wait()
     lanes = 2 * (hidden // HEADS)
@@ -1270,51 +1336,83 @@
     each = hidden // shards
     piece = lambda peer: grad.at[pl.ds(pl.multiple_of(peer * each, each), each), :]
     grad_got[me] = piece(me)[...]
-    spread(piece, grad_got, grad_send, grad_get, me, shards)
-    collect(lambda peer: parts.at[peer], dense_got, dense_send, dense_get, me, shards)
+    spread(piece, grad_got, grad_sems, me, shards)
+    collect(dense_got, dense_sems, me, shards)
     dense = jnp.zeros((each, hidden), F32)
     for k in range(shards):
         dense = dense + dense_got[k].astype(F32)[:each, :]
+    dense_ref[...] = dense
     square = jnp.sum(dense * dense, keepdims=True)
-    collect(piece, grad_got, grad_send, grad_get, me, shards)
+    collect(grad_got, grad_sems, me, shards)
     total = grad_got[0]
     for k in range(1, shards):
         total = total + grad_got[k]
+    total_ref[...] = total
     square = square + jnp.sum(total * total, keepdims=True)
     row = lax.broadcasted_iota(jnp.int32, note.shape, 0)
     note[...] = jnp.where(row == 0, facts[...], jnp.where(row == 1, square, 0.0))
     notes[me] = note[...]
-    spread(lambda peer: note, notes, note_send, note_get, me, shards)
-    collect(lambda peer: note, notes, note_send, note_get, me, shards)
+    spread(lambda peer: note, notes, note_sems, me, shards)
+    collect(notes, note_sems, me, shards)
     sums = notes[0]
     for k in range(1, shards):
         sums = sums + notes[k]
-    norm = jnp.sqrt(sums[1:2, :])
-    sums_ref[...] = jnp.where(row == 1, norm, sums)
-    factor = jnp.minimum(1.0, clip_limit / (norm + 1e-06))[:, 0:1]
+    sums_ref[...] = sums
+
+
+def update_body(
+    sums_ref, dense_ref, total_ref, facts, head_w, head_m, head_v, adapt_w, adapt_m, adapt_v,
+    loss_out, norm_out, head_w_out, head_m_out, head_v_out, adapt_w_out, adapt_m_out, adapt_v_out,
+):
+    norm = jnp.sqrt(sums_ref[1:2, 0:1])
+    loss_out[...] = sums_ref[0:1, 0:1]
+    norm_out[...] = norm
+    factor = jnp.minimum(1.0, clip_limit / (norm + 1e-06))
     fades = facts[1:2, 0:1], facts[2:3, 0:1]
-    new = adam(head_w[...], dense * factor, head_m[...], head_v[...], *fades)
+    new = adam(head_w[...], dense_ref[...] * factor, head_m[...], head_v[...], *fades)
     head_w_out[...], head_m_out[...], head_v_out[...] = new
-    new = adam(adapt_w[...], total * factor, adapt_m[...], adapt_v[...], *fades)
-    adapt_w_out[...], adapt_m_out[...], adapt_v_out[...] = new
-
-
-def finish(back, qkv, logs, seg_wide, seg_row, mid, parts, late, facts, heads, adapts, edge, shards):
-    dout, one, two, slope, wo, up, dn, norms = back
+    grad = (total_ref[...] * factor).T
+    layers, kinds, rank, unused = adapt_w.shape
+    for layer in range(layers):
+        for kind in range(kinds):
+            at = (layer * kinds + kind) * rank
+            new = adam(
+                adapt_w[layer, kind], grad[at : at + rank], adapt_m[layer, kind], adapt_v[layer, kind], *fades
+            )
+            adapt_w_out[layer, kind], adapt_m_out[layer, kind], adapt_v_out[layer, kind] = new
+
+
+def update(sums, dense, total, facts, heads, adapts):
+    whole = pl.BlockSpec(memory_space=pltpu.VMEM)
+    shape = jax.ShapeDtypeStruct
+    return pl.pallas_call(
+        update_body,
+        in_specs=[whole] * 10,
+        out_specs=[whole] * 8,
+        out_shape=[shape((1, 1), F32)] * 2 + [shape(a.shape, F32) for a in (*heads, *adapts)],
+        compiler_params=params(),
+        name="update",
+    )(sums, dense, total, facts, *heads, *adapts)
+
+
+def finish(back, qkv, logs, seg_wide, seg_row, mid, parts, late, facts, edge, shards):
+    dout, one, two, slope, wo, up, dn, gains = back
     rows, hidden = dout.shape
     each = hidden // shards
     whole = pl.BlockSpec(memory_space=pltpu.VMEM)
     anywhere = pl.BlockSpec(memory_space=pl.ANY)
     shape = jax.ShapeDtypeStruct
     sems = pltpu.SemaphoreType.DMA
-    tiles = rows // split_of(rows, 256, 16)
+    tiles = rows // split_of(rows, BACK_TILE, 16)
     return pl.pallas_call(
         functools.partial(finish_body, shards, (up[1], dn[1]), edge),
-        in_specs=[anywhere] * 8 + [whole] * 14,
-        out_specs=[whole] * 7,
-        out_shape=[shape((8, 128), F32)]
-        + [shape(a.shape, F32) for a in heads]
-        + [shape(a.shape, F32) for a in adapts],
+        in_specs=[anywhere] * 8 + [whole] * 8,
+        out_specs=[whole] * 3,
+        out_shape=[
+            shape((8, 128), F32),
+            shape((each, hidden), F32),
+            shape((each, late.shape[1]), F32),
+        ],
         scratch_shapes=[
             pltpu.VMEM((rows, hidden), F32),
             pltpu.VMEM((rows, hidden), F32),
@@ -1333,11 +1431,13 @@
             pltpu.VMEM((shards, 8, 128), F32),
             sems((4, tiles)),
             sems((4,)),
-        ]
-        + [sems((shards,))] * 6,
+            sems((2,)),
+            sems((2,)),
+            sems((2,)),
+        ],
         compiler_params=params(collective_id=2, has_side_effects=True),
         name="finish",
-    )(dout, one, two, slope, wo, up[0], dn[0], qkv, norms, logs, seg_wide, seg_row, mid, parts, late, facts, *heads, *adapts)
+    )(dout, one, two, slope, wo, up[0], dn[0], qkv, gains, logs, seg_wide, seg_row, mid, parts, late, facts)
 
 
 HOPS = 3
@@ -1469,7 +1569,6 @@
     fills[1].wait()
     fills[2].wait()
     count = e_ref.shape[0]
-    step = split_of(count, 640, 128)
 
     def hand_part(s):
         return pltpu.make_async_remote_copy(
@@ -1483,7 +1582,7 @@
 
     def cross_part(k):
         return pltpu.make_async_remote_copy(
-            src_ref=packs.at[2 * k + 1, c],
+            src_ref=packs.at[cross_step(k), c],
             dst_ref=crossed.at[k],
             send_sem=p_send.at[k],
             recv_sem=p_get.at[k],
@@ -1501,15 +1600,25 @@
             device_id_type=MESH,
         )
 
+    def row_of(s):
+        return (s + 1) // 2 % 4
+
+    def other_of(s):
+        return (s % 2 + (7 - s) // 7 + s // 7) % 2
+
+    def cross_step(k):
+        return 2 * k - 1 + (3 - k) // 3
+
     def compute(s):
-        zt, yt = flip(z, s // 2), (y + s % 2) % 2
-
-        handed_here(zt, s % 2).wait_recv()
+        zt, yt = flip(z, row_of(s)), (y + other_of(s)) % 2
+        handed_here(zt, other_of(s)).wait_recv()
         first = slot_of(zt, yt, 0)
         u = feats[pl.ds(first, 2)].reshape(2 * labels, hidden)
         top = total = mean = None
-        for start in range(0, count, step):
-            part = slice(start, start + step)
+        for start in range(0, count, 1280):
+            if start == 1280:
+                between(s)
+            part = slice(start, min(start + 1280, count))
             bias = bias_ref[part, :]
             logits = mm_nt(e_ref[part, :], u) + jnp.concatenate([bias, bias], 1)
             high = jnp.max(logits, 0, keepdims=True)
@@ -1535,14 +1644,14 @@
         hand_part(s).wait_recv()
         pair = merged(unpack(packs[s, c], hidden), unpack(handed[s], hidden))
 
-        @pl.when(s % 2 == 1)
+        @pl.when(other_of(s) == 1)
         def _():
             store_packed(packs.at[s, c], pair, hidden)
-            cross_part(s // 2).start()
-
-        @pl.when(s % 2 == 0)
+            cross_part(row_of(s)).start()
+
+        @pl.when(other_of(s) == 0)
         def _():
-            store_packed(kept.at[s // 2], pair, hidden)
+            store_packed(kept.at[row_of(s)], pair, hidden)
 
     def finish(k):
         cross_part(k).wait_recv()
@@ -1559,22 +1668,23 @@
 
     steps = 8
 
+    def between(s):
+        @pl.when(s > 0)
+        def _():
+            settle(s - 1)
+
+        @pl.when((s >= 3) & (s % 2 == 1))
+        def _():
+            finish((s - 1) // 2)
+
     @pl.loop(0, steps)
     def _(s):
         for r in range(1, HOPS + 2):
-            pl.when(s == r)(functools.partial(later_round, r))
+            pl.when(s == r - 1)(functools.partial(later_round, r))
         compute(s)
 
-        @pl.when(s > 0)
-        def _():
-            settle(s - 1)
-
-        @pl.when((s >= 3) & (s % 2 == 1))
-        def _():
-            finish((s - 3) // 2)
-
     settle(steps - 1)
-    finish(steps // 2 - 1)
+    finish(0)
     total = unpack(zouts[0], hidden)
     for k in range(1, 4):
         line_part(k).wait_recv()
@@ -1712,18 +1822,13 @@
     head_rows = head_projection.shape[0]
 
     grouped = (lax.axis_size("dp"), lax.axis_size("fsdp")) == (2, 16)
-    chunks = [
-        [
-            feedforward_up[layer].T,
-            feedforward_down[layer],
-            attention_in_weight[layer].T,
-            attention_out_weight[layer].T,
-        ]
-        for layer in range(layers)
-    ]
-    chunks[-1].append(head_projection.astype(BF))
-    chunks = [pad_rows(jnp.concatenate(pieces, 0), 32) for pieces in chunks]
-    first_full = lax.all_gather(chunks[0], BOTH, axis=0, tiled=False)
+    feeds = [[feedforward_up[layer].T, feedforward_down[layer]] for layer in range(layers)]
+    attends = [[attention_in_weight[layer].T, attention_out_weight[layer].T] for layer in range(layers)]
+    first_in = lax.all_gather(jnp.concatenate(attends[0], 0), BOTH, axis=0, tiled=False)
+    feed_chunk = jnp.concatenate(feeds[0], 0)
+    last_chunk = pad_rows(
+        jnp.concatenate(feeds[1] + attends[1] + [head_projection.astype(BF)], 0), 32
+    )
 
     table_rows = embed.shape[0]
     wanted = jnp.concatenate([input_token_index[0], label_target_token[0]])
@@ -1746,8 +1851,11 @@
         other_rows, own_rows = look_up(pair_ids, embed)
         fact = jnp.concatenate([vocabulary_bias, ups, sequence_task_index.astype(F32)])
         fact_rows = -(-fact.size // 1024) * 8
-        got, facts = start_exchange(
-            other_rows, jnp.pad(fact, (0, fact_rows * 128 - fact.size)).reshape(fact_rows, 128), shards
+        got, facts, feed_full = start_exchange(
+            other_rows,
+            jnp.pad(fact, (0, fact_rows * 128 - fact.size)).reshape(fact_rows, 128),
+            feed_chunk,
+            shards,
         )
         facts = facts.reshape(shards, -1)
         all_bias = facts[:, :slice_rows].reshape(-1)
@@ -1771,58 +1879,33 @@
         .reshape(layers, 2, rank, hidden)
     )
     blank = jnp.zeros((rank, hidden), BF)
-    adapters = [
-        jnp.pad(
+    spare = lambda rows: jnp.zeros((rows, 3 * hidden), BF)
+    adapters = jnp.stack(
+        [
             jnp.concatenate(
                 [
+                    spare(2 * rank * layer),
                     jnp.concatenate([2 * ups_full[layer, 0], blank, blank], 1),
                     jnp.concatenate([blank, blank, 2 * ups_full[layer, 1]], 1),
+                    spare(128 - 2 * rank * (layer + 1)),
                 ],
                 0,
-            ),
-            ((2 * rank * layer, 128 - 2 * rank * (layer + 1)), (0, 0)),
-        )
-        for layer in range(layers)
-    ]
-    downs = [
-        jnp.pad(
-            jnp.concatenate([adapter_down_matrix[layer, 0], adapter_down_matrix[layer, 1]], 1),
-            ((0, 0), (2 * rank * layer, 128 - 2 * rank * (layer + 1))),
-        )
-        for layer in range(layers)
-    ]
-    bias_of = []
-    for layer in range(layers):
-        b = layer_bias_vector[layer][None, :]
-        ff = b.shape[1] - 4 * hidden
-        bias_of.append(
-            (
-                jnp.concatenate(
-                    [b[:, :hidden], jnp.zeros((1, hidden), F32), b[:, hidden : 2 * hidden]], 1
-                ),
-                b[:, 2 * hidden : 3 * hidden],
-                b[:, 3 * hidden : 3 * hidden + ff],
-                b[:, 3 * hidden + ff :],
             )
-        )
-    norms_of = [
-        jnp.concatenate(
-            [
-                norm_gain_vector[1 + 2 * layer][None],
-                norm_bias_vector[1 + 2 * layer][None],
-                norm_gain_vector[2 + 2 * layer][None],
-                norm_bias_vector[2 + 2 * layer][None],
-                norm_gain_vector[-1][None],
-                norm_bias_vector[-1][None],
-            ],
-            0,
-        )
-        for layer in range(layers)
-    ]
-
-    target_rows = jnp.where(mine[tokens:, None], own_rows[tokens:], got[tokens:]).astype(F32)
+            for layer in range(layers)
+        ]
+    )
+    downs = jnp.stack(
+        [
+            jnp.pad(
+                jnp.concatenate([adapter_down_matrix[layer, 0], adapter_down_matrix[layer, 1]], 1),
+                ((0, 0), (2 * rank * layer, 128 - 2 * rank * (layer + 1))),
+            )
+            for layer in range(layers)
+        ]
+    )
+    target_rows = jnp.where(mine[tokens:, None], own_rows[tokens:], got[tokens:])
     segments = sentence_numbers[0]
-    spot = seg_positions(segments)[:, None]
+    code = (2 * seg_positions(segments) + mine[:tokens].astype(jnp.int32))[:, None]
     seg_real = segments.astype(F32)
     seg_wide = jnp.broadcast_to(seg_real[:, None], (tokens, 128))
     seg_row = seg_real[None, :]
@@ -1843,46 +1926,44 @@
     bias_wide = jnp.broadcast_to(own_bias[:, None], (own_bias.shape[0], 128))
     target_bias = all_bias[label_target_token[0]]
 
-    first_norm = jnp.concatenate([norm_gain_vector[:1], norm_bias_vector[:1]], 0)
-    mine_col = mine[:tokens, None].astype(jnp.int32)
+    gains, shifts = norm_gain_vector, norm_bias_vector
+    last_inputs = (place_col, place_row, seg_wide, downs, adapters, layer_bias_vector)
     in_start = 2 * ff_rows
     slabs_of = lambda full_chunk: (slab_of(full_chunk, 0, ff_rows), slab_of(full_chunk, ff_rows, ff_rows))
-    slabs = [slabs_of(first_full)]
-    last_inputs = (place_col, place_row, seg_wide, downs[1], adapters[1], bias_of[1][0])
     if grouped:
         more = (
-            mine_col, spot, position_embedding, first_norm, downs[0], adapters[0], bias_of[0][0],
-            seg_wide, seg_row, *bias_of[0][1:], norms_of[0],
+            code, position_embedding, gains, shifts, downs, adapters, layer_bias_vector, seg_wide, seg_row,
         )
         qkv, x_last, one, two, slope, out_first, last_full, own_vocab, own_turned, mid, logs = first_layer(
-            own_rows, got, first_full, chunks[1], embed, more, (0, 1, in_start), shards * ff_rows, slice_rows,
-            shards,
-        )
-        slabs.append(slabs_of(last_full))
-        *saved, features, in_last, out_last, head_full = last_forward(
-            x_last, *last_inputs, (last_full,), (in_start, in_start + qkv_rows + out_rows),
-            *slabs[1], *bias_of[1][1:], norms_of[1], head_dense_bias[None, :],
-        )
-        mean_t, own_logs = head(features, own_vocab, own_turned, bias_wide)
+            own_rows, got, first_in, feed_full, last_chunk, embed, more, (0, 1), slice_rows, shards
+        )
+        slabs = [slabs_of(feed_full), slabs_of(last_full)]
+        *saved, in_last, out_last, head_full = last_forward(
+            x_last, *last_inputs, (last_full,), (in_start, in_start + qkv_rows + out_rows), *slabs[1], gains,
+            shifts, head_dense_bias[None, :],
+        )
+        mean_t, own_logs = head(saved[-1], own_vocab, own_turned, bias_wide)
     else:
-        last_full = lax.all_gather(chunks[1], BOTH, axis=0, tiled=False)
-        slabs.append(slabs_of(last_full))
+        feed_full = lax.all_gather(feed_chunk, BOTH, axis=0, tiled=False)
+        last_full = lax.all_gather(last_chunk, BOTH, axis=0, tiled=False)
+        slabs = [slabs_of(feed_full), slabs_of(last_full)]
         taken = lambda full_chunk, start, size: full_chunk[:, start : start + size].reshape(-1, hidden)
-        in_first, in_last = [taken(f, in_start, qkv_rows) for f in (first_full, last_full)]
-        out_first, out_last = [taken(f, in_start + qkv_rows, out_rows) for f in (first_full, last_full)]
+        in_first, out_first = taken(first_in, 0, qkv_rows), taken(first_in, qkv_rows, out_rows)
+        in_last = taken(last_full, in_start, qkv_rows)
+        out_last = taken(last_full, in_start + qkv_rows, out_rows)
         head_full = taken(last_full, in_start + qkv_rows + out_rows, head_rows)
         qkv, mid, hidden_rows = project(
-            own_rows, got, mine_col, spot, position_embedding, first_norm, downs[0], in_first, adapters[0],
-            bias_of[0][0],
+            own_rows, got, code, position_embedding, gains, shifts, downs, in_first, adapters, layer_bias_vector
         )
         context, logs = attend(qkv, seg_wide, seg_row)
         x_last, one, two, slope = after(
-            context, hidden_rows, out_first, *slabs[0], *bias_of[0][1:], norms_of[0]
-        )
-        *saved, features = last_forward(
-            x_last, *last_inputs, (in_last, out_last, head_full), None, *slabs[1], *bias_of[1][1:],
-            norms_of[1], head_dense_bias[None, :],
-        )
+            context, hidden_rows, out_first, *slabs[0], layer_bias_vector, gains, shifts
+        )
+        saved = last_forward(
+            x_last, *last_inputs, (in_last, out_last, head_full), None, *slabs[1], gains, shifts,
+            head_dense_bias[None, :],
+        )
+        features = saved[-1]
         own_slice = lax.dynamic_slice_in_dim(embed, fsdp_index * slice_rows, slice_rows, 0)
         own_vocab = jnp.concatenate(
             [own_slice]
@@ -1902,49 +1983,40 @@
         scaled = (means * jnp.exp(local_logs - whole_logs)[:, None, :]).astype(BF)
         mean_t = lax.psum_scatter(scaled, "fsdp", scatter_dimension=0, tiled=True)[0].astype(F32)
         own_logs = lax.dynamic_index_in_dim(whole_logs, fsdp_index, 0, keepdims=False)
-    targets = jnp.sum(features.astype(F32) * target_rows, 1) + target_bias
-    own_loss = row_weight * jnp.sum(own_logs - targets)
-    feat_grad = row_weight * (mean_t.T - target_rows)
-
-    hidden_grad, dense_gradient, late = last_backward(
-        feat_grad, saved, place_col, place_row, seg_wide, downs[1], in_last, adapters[1],
-        out_last, *slabs[1], norms_of[1], head_full, 3 * rank, shards if grouped else None,
-    )
-    back = (hidden_grad, one, two, slope, out_first, *slabs[0], norms_of[0])
+        own_logs = own_logs[None, :]
+
     step_as_real = optimizer_step_count[0].astype(F32)
     fades = (1.0 - beta_first**step_as_real, 1.0 - beta_second**step_as_real)
+    lanes = lambda value: jnp.pad(
+        jnp.broadcast_to(value, (1, value.size if value.ndim else 128)), ((0, 0), (0, 128))
+    )[:, :128]
+    facts = jnp.concatenate(
+        [lanes(value) for value in (row_weight, *fades, target_bias)] + [jnp.zeros((4, 128), F32)]
+    )
+    hidden_grad, dense_gradient, late, facts = last_backward(
+        mean_t, own_logs, target_rows, facts, saved, place_col, place_row, seg_wide, downs, in_last, adapters,
+        out_last, *slabs[1], gains, head_full, 3 * rank, shards if grouped else None,
+    )
+    back = (hidden_grad, one, two, slope, out_first, *slabs[0], gains)
     adapts = (adapter_up_matrix, adapter_moment_first, adapter_moment_second)
     heads = (head_projection, head_moment_first, head_moment_second)
     if grouped:
-        facts = jnp.concatenate(
-            [jnp.broadcast_to(value, (1, 128)) for value in (own_loss, *fades)]
-            + [jnp.zeros((5, 128), F32)]
-        )
-        turned = [
-            jnp.pad(a.reshape(-1, up_part).T, ((0, 0), (0, 128 - a.size // up_part))) for a in adapts
-        ]
-        sums, *new = finish(
-            back, qkv, logs, seg_wide, seg_row, mid, dense_gradient, late, facts, heads, turned, rank, shards
-        )
-        dense_new = new[:3]
-        adapter_new = [
-            a[:, : ups.size // up_part].T.reshape(adapter_up_matrix.shape) for a in new[3:]
-        ]
-        masked_task_loss, gradient_norm = sums[0, 0], sums[1, 0]
-    else:
-        dctx = after_back(*back)
-        first = attend_back(qkv, dctx, logs, seg_wide, seg_row, mid, rank)
-        adapter_gradient = (first + late)[:, : 2 * rank * layers].T.reshape(layers, 2, rank, hidden)
-        dense_portion = lax.psum_scatter(dense_gradient, BOTH, scatter_dimension=0, tiled=True)
-        adapter_portion = lax.psum_scatter(adapter_gradient, BOTH, scatter_dimension=3, tiled=True)
-        squared_entries = jnp.sum(adapter_portion * adapter_portion) + jnp.sum(
-            dense_portion * dense_portion
-        )
-        masked_task_loss, norm_square = lax.psum((own_loss, squared_entries), BOTH)
-        gradient_norm = jnp.sqrt(norm_square)
-        factor = jnp.minimum(1.0, clip_limit / (gradient_norm + 1e-06))
-        adapter_new = adam(adapts[0], adapter_portion * factor, *adapts[1:], *fades)
-        dense_new = adam(heads[0], dense_portion * factor, *heads[1:], *fades)
+        sums, dense_portion, adapter_portion = finish(
+            back, qkv, logs, seg_wide, seg_row, mid, dense_gradient, late, facts, rank, shards
+        )
+        loss, norm, *new = update(sums, dense_portion, adapter_portion, facts, heads, adapts)
+        return (loss[0, 0], norm[0, 0], *new[3:], *new[:3])
+    dctx = after_back(*back)
+    first = attend_back(qkv, dctx, logs, seg_wide, seg_row, mid, rank)
+    adapter_gradient = (first + late)[:, : 2 * rank * layers].T.reshape(layers, 2, rank, hidden)
+    dense_portion = lax.psum_scatter(dense_gradient, BOTH, scatter_dimension=0, tiled=True)
+    adapter_portion = lax.psum_scatter(adapter_gradient, BOTH, scatter_dimension=3, tiled=True)
+    squared_entries = jnp.sum(adapter_portion * adapter_portion) + jnp.sum(dense_portion * dense_portion)
+    masked_task_loss, norm_square = lax.psum((facts[0, 0], squared_entries), BOTH)
+    gradient_norm = jnp.sqrt(norm_square)
+    factor = jnp.minimum(1.0, clip_limit / (gradient_norm + 1e-06))
+    adapter_new = adam(adapts[0], adapter_portion * factor, *adapts[1:], *fades)
+    dense_new = adam(heads[0], dense_portion * factor, *heads[1:], *fades)
     return (masked_task_loss, gradient_norm, *adapter_new, *dense_new)
 
 

time: 474 us -> 459 us (0.968)
  local copies, waits for them, and re-layouts: 35 us -> 15.2 us
  Pallas kernels: 401 us -> 406 us
    pallas_call x2 -> x3, Pallas kernels: 179 us -> 182 us  [the longest x1 105 us: first_layer(): pl.pallas_call(functools.partial(first_layer_body, streams_of(chunk.shape...]
  transfers between devices with their start and end apart: 1 -> 1, of which waited for: 0 -> 0; matrix products, arithmetic and copies ran while one was open for 5% -> 4% of each run, Pallas kernels for 24% -> 24%
where the time goes in v7:
time: 459 us; the launch traced here: 453 us
  Pallas kernels  406 us (88%)
  between operations  16.1 us (4%)
  local copies, waits for them, and re-layouts  15.2 us (3%)
  other arithmetic  10.6 us (2%)
  blocking collectives  5.23 us (1%)
    pallas_call x1, Pallas kernels, first_layer(): pl.pallas_call(functools.partial(first_layer_body, streams_of(chunk.shape...  105 us
    pallas_call x1, Pallas kernels, start_exchange(): pl.pallas_call(functools.partial(start_body, streams_of(chunk.shape[0]),...  75.9 us
    pallas_call x1, Pallas kernels, finish(): pl.pallas_call(functools.partial(finish_body, shards, (up[1], dn[1]), edg...  71.5 us
    pallas_call x1, Pallas kernels, head(): pl.pallas_call(head_body, in_specs=[whole] + [anywhere] * 3, out_specs=[w...  67.7 us
    pallas_call x1, Pallas kernels, look_up(): pl.pallas_call(look_up_body, in_specs=[pl.BlockSpec(memory_space=pltpu.SM...  35 us
    pallas_call x1, Pallas kernels, last_backward(): pl.pallas_call(functools.partial(last_backward_body, places=(up[1], dn[1]...  26.8 us
    pallas_call x1, Pallas kernels, last_forward(): pl.pallas_call(body, in_specs=[whole] * 7 + [anywhere] * (len(weights) +...  22.4 us
  transfers between devices with their start and end apart: 1, of which 0 were waited for; matrix products, arithmetic and copies ran while one was open for 4% of the time, Pallas kernels for 24%

profile of v7, /device:TPU:0, one launch (start us, length us, event | category | flops | bytes accessed | tf_op | source)
XLA Modules:
  0.0 453.0 jit_solution(11889683665234219198)
XLA Ops:
  7.2 0.0 all-gather.5.cloned.1.call-start
  7.2 0.8 slice_bitcast_fusion.3
  8.0 0.9 slice_bitcast_fusion.2
  8.9 0.7 pad_maximum_fusion.3
  9.6 0.0 all-gather.5.cloned.1.call-update
  10.3 0.8 reshape.300
  11.1 0.7 pad_add_fusion.2
  11.8 5.2 %all-gather.2 = s32[2,1,1152]{2,1,0:T(1,128)S(1)} all-gather(s32[1,1,1152]{2,1,0:T(1,128)S(1)} %reshape.328), channel_id=2, replica_groups=mesh['dp'=2,'fsdp'=16] {'dp'}, dimensions={0}, use_global_device_ids=true | all-gather | bytes 13824 | tf_op jit(solution)/shard_map/all_gather | solution.py:1836
  17.1 0.5 copy.74
  17.7 0.4 copy.71
  18.1 0.1 concatenate.83
  18.2 0.6 add_select_fusion.2.ids
  18.8 1.6 fusion.1.low_ref
  20.4 35.0 %look_up.1 = (bf16[1152,768]{1,0:T(8,128)(2,1)}, bf16[1152,768]{1,0:T(8,128)(2,1)}) custom-call(s32[2304]{0:T(1024)} %add_select_fusion.2.ids, s32[2304,1]{1,0:T(8,128)} %fusion.1.low_ref, bf16[1600,16,768]{2,1,0:T(8,128)(2,1)} %bitcast.96), custom_call_target="tpu_custom_call" | custom-call | tf_op jit(solution)/shard_map/look_up/pallas_call | solution.py:1237
  55.4 0.6 pad_bitcast_fusion.2.fact
  56.1 0.7 pad_maximum_fusion.2.chunk
  56.8 75.9 %start_exchange.1 = (bf16[1152,768]{1,0:T(8,128)(2,1)}, f32[32,24,128]{2,1,0:T(8,128)}, bf16[32,192,768]{2,1,0:T(8,128)(2,1)}) custom-call(bf16[1152,768]{1,0:T(8,128)(2,1)} %get-tuple-element.56.rows, f32[24,128]{1,0:T(8,128)} %pad_bitcast_fusion.2.fact, bf16[192,768]{1,0:T(8,128)(2,1)} %pad_maximum_fusion.2.chunk), custom_call_target="tpu_custom_call" | custom-call | tf_op jit(solution)/shard_map/start_exchange/pallas_call | solution.py:964
  132.7 0.0 copy-start.7
  132.8 0.0 copy-start.6
  132.8 1.1 copy.108
  133.9 0.0 copy-start.4
  133.9 0.1 slice.168
  134.8 0.1 pad.48.clone
  134.9 0.1 pad.45.clone
  135.0 0.6 broadcast_in_dim.69.refs_12_
  135.5 0.1 compare_reduce_fusion
  135.6 0.1 add_select_fusion.3
  135.7 0.3 reduce-window.9
  136.0 0.1 slice.104
  136.2 0.2 copy.78
  136.3 0.2 copy.79
  136.6 0.8 pad.32.chunk
  137.5 0.2 copy.77
  137.7 0.1 slice_reduce_fusion
  137.8 0.1 broadcast_maximum_fusion
  137.9 0.2 copy.76
  138.1 0.1 slice_convert_fusion.1
  138.2 0.1 copy.106
  138.3 0.1 reshape.306
  138.4 0.4 reshape.304
  138.8 0.1 copy.80
  139.0 0.3 reshape.305
  139.3 0.9 add.122.code_ref
  140.2 1.1 gather_fusion
  141.3 0.1 convert_reduce_fusion
  141.4 0.6 fusion.27
  142.1 0.6 pad.35
  142.7 0.6 concatenate.98.fact_ref
  143.3 0.1 fusion.29
  143.4 0.1 pad_maximum_fusion.6
  143.5 0.1 pad_bitcast_fusion
  143.7 0.8 pad_maximum_fusion.1.down_ref.refs_4_
  144.5 1.8 slice_select_fusion.target_ref
  146.3 0.1 fusion.15
  146.4 1.2 pad_maximum_fusion.adapt_ref.refs_5_
  147.6 1.0 broadcast_in_dim.66.seg_ref.refs_3_
  148.6 104.5 %first_layer.1 = (bf16[1024,2304]{1,0:T(8,128)(2,1)}, f32[1024,768]{1,0:T(8,128)}, f32[1024,768]{1,0:T(8,128)}, f32[1024,768]{1,0:T(8,128)}, bf16[1024,3072]{1,0...) custom-call(bf16[1152,768]{1,0:T(8,128)(2,1)} %get-tuple-element.55., ...), custom_call_target="tpu_custom_call" | custom-call | tf_op jit(solution)/shard_map/first_layer/pallas_call | solution.py:1163
  253.1 0.7 broadcast_in_dim.68.refs_1_.place_ref
  253.8 22.4 %last_forward.1 = (bf16[1024,1536]{1,0:T(8,128)(2,1)}, bf16[128,768]{1,0:T(8,128)(2,1)}, bf16[1024,128]{1,0:T(8,128)(2,1)}, f32[6,256]{1,0:T(8,128)}, f32[128,76...) custom-call(f32[1024,768]{1,0:T(8,128)} %get-tuple-element.60.refs_0, ...), custom_call_target="tpu_custom_call" | custom-call | tf_op jit(solution)/shard_map/last_forward/pallas_call | solution.py:433
  276.3 1.8 broadcast_in_dim.70.bias_any
  278.1 67.7 %head.1 = (f32[768,128]{1,0:T(8,128)}, f32[1,128]{1,0:T(1,128)}) custom-call(bf16[128,768]{1,0:T(8,128)(2,1)} %get-tuple-element.62.u_ref.feat_ref, bf16[3200,768]{1,0:T(8,128)(2,1)} %get-tuple-element.63.e_any, bf16[768,3200]{1,0:T(8,128)(2,1)} %get-tuple-element.64.et_any, f32[3200,128]{1,0:T(8,128)} %broadcast_in_dim.70.bias_any), custom_call_target="tpu_custom_call" | custom-call | tf_op jit(solution)/shard_map/head/pallas_call | solution.py:1732
  345.8 26.8 %last_backward.1 = (f32[1024,768]{1,0:T(8,128)}, bf16[32,32,768]{2,1,0:T(8,128)(2,1)}, f32[768,128]{1,0:T(8,128)}, f32[8,128]{1,0:T(8,128)}) custom-call(f32[768,128]{1,0:T(8,128)} %get-tuple-element.65.mean_ref, f32[1,128]{1,0:T(1,128)} %get-tuple-element.66.all_log_ref, bf16[128,768]{1,0:T(8,128)(2,1)} %slice_select_fusion.target_ref, ...), custom_call_target="tpu_custom_call" | custom-call | tf_op jit(solution)/shard_map/last_backward/pallas_call | solution.py:624
  372.6 71.5 %finish.1 = (f32[8,128]{1,0:T(8,128)}, f32[24,768]{1,0:T(8,128)}, f32[24,128]{1,0:T(8,128)}) custom-call(f32[1024,768]{1,0:T(8,128)} %get-tuple-element.80.dout_any, f32[1024,768]{1,0:T(8,128)} %get-tuple-element.81.one_any, f32[1024,768]{1,0:T(8,128)} %get-tuple-element.82.two_any, bf16[1024,3072]{1,0:T(8,128)(2,1)} %get-tuple-element.83.slope_any, ...), custom_call_target="tpu_custom_call" | custom-call | tf_op jit(solution)/shard_map/finish/pallas_call | solution.py:1407
  444.1 1.8 update.1
  (55 shorter events, 0.4 us)
Async XLA Ops:
  7.2 140.4 %all-gather.5.cloned.1.call-start = ((), (), s32[]{:S(2)}) async-start(), calls=%async_computation | async-start | bytes 4866048 | tf_op jit(solution)/shard_map/all_gather | solution.py:1827
  8.0 10.1 %copy-start.8 = (f32[1600]{0:T(1024)S(1)}, f32[1600]{0:T(1024)}, u32[]{:S(2)}) copy-start(f32[1600]{0:T(1024)} %param.42) | copy-start | bytes 19204
  20.4 35.6 %copy-start = (bf16[2,768,96]{1,2,0:T(8,128)(2,1)S(1)}, bf16[2,768,96]{1,2,0:T(8,128)(2,1)}, u32[]{:S(2)}) copy-start(bf16[2,768,96]{1,2,0:T(8,128)(2,1)} %param.38) | copy-start | bytes 884740
  20.4 35.6 %copy-start.1 = (bf16[2,96,768]{2,1,0:T(8,128)(2,1)S(1)}, bf16[2,96,768]{2,1,0:T(8,128)(2,1)}, u32[]{:S(2)}) copy-start(bf16[2,96,768]{2,1,0:T(8,128)(2,1)} %param.39) | copy-start | bytes 884740
  132.7 2.2 copy-start.10
  132.7 2.8 copy-start.7
  132.8 3.4 copy-start.6
  132.8 3.8 copy-start.3
  133.9 2.7 copy-start.4
  133.9 2.7 copy-start.2
  135.5 12.0 %copy-start.5 = (f32[1,1024]{1,0:T(1,128)}, f32[1,1024]{1,0:T(1,128)S(1)}, u32[]{:S(2)}) copy-start(f32[1,1024]{1,0:T(1,128)S(1)} %convert_element_type.63.seg_row_ref) | copy-start | bytes 12292
  138.8 1.3 copy-start.11
  138.9 2.5 copy-start.12
  148.6 104.5 %copy-start.9 = (s32[1,128]{1,0:T(1,128)S(1)}, s32[1,128]{1,0:T(1,128)}, u32[]{:S(2)}) copy-start(s32[1,128]{1,0:T(1,128)} %place_row_ref.1) | copy-start | bytes 1540
Sparse Core Ops, SparseCore 0:
  10.9 77.4 all-gather.4
